TPU v7x, 32 devices: a whole 2x2x4 slice. The times are simulated.
32 devices in a mesh: row: 4 (over y, x), col: 8 (over z, core).
Axes of the slice: x: 2, y: 2, z: 4, core: 2. Of those that a mesh axis runs over, the one named last changes fastest.
Arguments:
- trailing: bfloat16 [16384, 16384], P('row', 'col'), may hold values from -0.0625 to 0.0625
- panel_vectors: bfloat16 [16384, 512], P(('row', 'col')), may hold values from -6 to 6
Outputs:
- sym_product: float32 [16384, 512], P(('row', 'col'))
All inputs are finite; a program needn't handle non-finite values.
Results may differ from a plain program's by a relative error of at most 0.0003.
Values may be sent and summed in bfloat16 or wider, within the bound.
No kernel may reach another device: no remote copies, remote signals or barrier semaphores. Data moves between devices by JAX's collectives and lax.ppermute only.
A program may use at most 128 MiB of HBM per device.

v0:
```python
import jax
import jax.numpy as jnp
from jax import lax
from jax.sharding import PartitionSpec as P


def from_root(shard, axis, root):
    mine = lax.axis_index(axis) == root
    return lax.psum(jnp.where(mine, shard, jnp.zeros_like(shard)), axis)


def shards(trailing, panel_vectors):
    rows_here, cols_here = trailing.shape
    shard_rows, width = panel_vectors.shape
    row_count = lax.axis_size("row")
    col_count = lax.axis_size("col")
    per_row = col_count // row_count
    row_id = lax.axis_index("row")
    col_id = lax.axis_index("col")
    row_panel = lax.all_gather(panel_vectors, "col", axis=0, tiled=True)
    slab_piece = lax.dynamic_slice_in_dim(row_panel, col_id % per_row * cols_here, cols_here, 0)
    col_panel = from_root(slab_piece, "row", col_id // per_row)
    global_rows = row_id * rows_here + lax.iota(jnp.int32, rows_here)
    global_cols = col_id * cols_here + lax.iota(jnp.int32, cols_here)
    empty = jnp.zeros((), trailing.dtype)
    lower_part = jnp.where(global_rows[:, None] >= global_cols[None, :], trailing, empty)
    strict_part = jnp.where(global_rows[:, None] > global_cols[None, :], trailing, empty)
    direct = jnp.dot(lower_part, col_panel, preferred_element_type=jnp.float32)
    mirrored = lax.dot_general(
        strict_part, row_panel, (((0,), (0,)), ((), ())), preferred_element_type=jnp.float32
    )
    column_total = lax.psum(mirrored, "row")
    own_rows = lax.psum_scatter(direct, "col", scatter_dimension=0, tiled=True)
    chosen = jnp.zeros((shard_rows, width), jnp.float32)
    offset = col_id % row_count * shard_rows
    for which in range(per_row):
        received = from_root(column_total, "col", row_id * per_row + which)
        segment = lax.dynamic_slice_in_dim(received, offset, shard_rows, 0)
        chosen = jnp.where(col_id // row_count == which, segment, chosen)
    return own_rows + chosen


def solution(mesh):
    in_specs = (P("row", "col"), P(("row", "col"), None))
    out_specs = P(("row", "col"), None)
    return jax.shard_map(shards, mesh=mesh, in_specs=in_specs, out_specs=out_specs, check_vma=False)
```

profile of v0, /device:TPU:7, one launch (start us, length us, event | category | flops | bytes accessed | tf_op | source)
XLA Modules:
  0.0 529.0 jit_solution(13884800279380477651)
XLA Ops:
  6.5 0.0 all-gather.2.cloned.1.call-start
  6.5 0.7 all-gather.2.cloned.1.call-update
  7.3 0.0 all-reduce.7.cloned.1.call-start
  7.3 50.4 %all-gather.2.cloned.1.call-done = bf16[4096,512]{1,0:T(8,128)(2,1)} async-done(((bf16[512,512]{1,0:T(8,128)(2,1)}), bf16[4096,512]{1,0:T(8,128)(2,1)}) %all-gather.2.cloned.1.call-update) | async-done | bytes 4194320 | tf_op jit(solution)/shard_map/all_gather | solution.py:20
  57.7 18.2 %fusion.1 = f32[2048,512]{1,0:T(8,128)} fusion(bf16[4096,512]{1,0:T(8,128)(2,1)} %all-gather.2.cloned.1.call-done, bf16[4096,2048]{1,0:T(8,128)(2,1)} %param.2, s32[2048]{0:T(1024)S(1)} %iota_add_fusion.1, s32[4096]{0:T(1024)S(1)} %iota_add_fusion), kind=kOutput, calls=%fused_computation.3 | convolution fusion | flops 8606711808 | bytes 25190400 | tf_op jit(solution)/shard_map/dot_general | solution.py:29
  75.9 0.0 all-reduce.7.cloned.1.call-update
  75.9 0.0 all-reduce.5.cloned.1.call-start
  76.0 3.3 dynamic-slice_select_fusion
  79.3 0.0 all-reduce.5.cloned.1.call-update
  79.3 0.0 all-reduce.9.cloned.1.call-start
  79.4 98.0 %all-reduce.7.cloned.1.call-done = f32[2048,512]{1,0:T(8,128)} async-done(((f32[2048,512]{1,0:T(8,128)}), f32[2048,512]{1,0:T(8,128)}) %all-reduce.7.cloned.1.call-update) | async-done | bytes 4194320 | tf_op jit(solution)/shard_map/psum | solution.py:32
  177.3 6.7 %broadcast_select_fusion.1 = (f32[2048,512]{1,0:T(8,128)}, f32[2048,512]{1,0:T(8,128)}) fusion(f32[2048,512]{1,0:T(8,128)} %all-reduce.7.cloned.1.call-done, pred[]{:T(512)S(6)} %eq.20, pred[]{:T(512)S(6)} %eq.22), kind=kLoop, calls=%fused_computation.11 | loop fusion | flops 2097152 | bytes 12582914 | tf_op jit(solution)/shard_map/jit(_where)/select_n | solution.py:9
  184.1 0.0 all-reduce.9.cloned.1.call-update
  184.1 0.2 reduce-scatter.2.cloned.1.call-start
  184.3 66.1 %all-reduce.5.cloned.1.call-done = bf16[2048,512]{1,0:T(8,128)(2,1)} async-done(((bf16[2048,512]{1,0:T(8,128)(2,1)}), bf16[2048,512]{1,0:T(8,128)(2,1)}) %all-reduce.5.cloned.1.call-update) | async-done | bytes 2097168 | tf_op jit(solution)/shard_map/psum | solution.py:9
  250.4 15.2 %fusion = f32[4096,512]{1,0:T(8,128)} fusion(bf16[2048,512]{1,0:T(8,128)(2,1)} %all-reduce.5.cloned.1.call-done, bf16[4096,2048]{1,0:T(8,128)(2,1)} %param.2, s32[2048]{0:T(1024)S(1)} %iota_add_fusion.1, s32[4096]{0:T(1024)S(1)} %iota_add_fusion), kind=kOutput, calls=%fused_computation.2 | convolution fusion | flops 8606711808 | bytes 27287552 | tf_op jit(solution)/shard_map/dot_general | solution.py:28
  265.6 0.0 reduce-scatter.2.cloned.1.call-update
  265.6 163.8 %all-reduce.9.cloned.1.call-done = (f32[2048,512]{1,0:T(8,128)}, f32[2048,512]{1,0:T(8,128)}) async-done(((f32[2048,512]{1,0:T(8,128)}, f32[2048,512]{1,0:T(8,128)}), (f32[2048,512]{1,0:T(8,128)}, f32[2048,512]{1,0:T(8,128)})) %all-reduce.9.cloned.1.call-update) | async-done | bytes 8388624 | tf_op jit(solution)/shard_map/psum | solution.py:9
  429.4 89.9 %reduce-scatter.2.cloned.1.call-done = f32[512,512]{1,0:T(8,128)} async-done(((f32[4096,512]{1,0:T(8,128)}), f32[512,512]{1,0:T(8,128)}) %reduce-scatter.2.cloned.1.call-update) | async-done | bytes 1048592 | tf_op jit(solution)/shard_map/reduce_scatter | solution.py:33
  519.3 3.2 select_add_fusion
  (2 shorter events, 0.0 us)
Async XLA Ops:
  6.5 51.2 %all-gather.2.cloned.1.call-start = ((), (), s32[]{:S(2)}) async-start(), calls=%async_computation.1 | async-start | bytes 4718592 | tf_op jit(solution)/shard_map/all_gather | solution.py:20
  7.3 170.1 %all-reduce.7.cloned.1.call-start = ((), (), s32[]{:S(2)}) async-start(), calls=%async_computation.4 | async-start | bytes 8388608 | tf_op jit(solution)/shard_map/psum | solution.py:32
  75.9 174.5 %all-reduce.5.cloned.1.call-start = ((), (), s32[]{:S(2)}) async-start(), calls=%async_computation.2 | async-start | bytes 4194304 | tf_op jit(solution)/shard_map/psum | solution.py:9
  79.3 350.1 %all-reduce.9.cloned.1.call-start = ((), (), s32[]{:S(2)}) async-start(), calls=%async_computation.5 | async-start | bytes 16777216 | tf_op jit(solution)/shard_map/psum | solution.py:9
  184.1 335.2 %reduce-scatter.2.cloned.1.call-start = ((), (), s32[]{:S(2)}) async-start(), calls=%async_computation.3 | async-start | bytes 9437184 | tf_op jit(solution)/shard_map/reduce_scatter | solution.py:33
Sparse Core Ops, SparseCore 0:
  9.0 48.7 all-gather.1
  76.0 101.2 all-reduce.6
  180.7 69.6 all-reduce.4
  252.7 176.7 all-reduce.8
  431.6 87.6 reduce-scatter.1
where the time goes:
time: 533 us; the launch traced here: 529 us
  waiting for transfers between devices  469 us (88%)
  matrix products  33.4 us (6%)
  other arithmetic  13.2 us (2%)
  between operations  13.2 us (2%)
    psum x2, waiting for transfers between devices, from_root(): return lax.psum(jnp.where(mine, shard, jnp.zeros_like(shard)), axis)  230 us
    psum x1, waiting for transfers between devices, shards(): column_total = lax.psum(mirrored, 'row')  98 us
    reduce_scatter x1, waiting for transfers between devices, shards(): own_rows = lax.psum_scatter(direct, 'col', scatter_dimension=0, tiled=True)  89.9 us
    all_gather x1, waiting for transfers between devices, shards(): row_panel = lax.all_gather(panel_vectors, 'col', axis=0, tiled=True)  50.4 us
    dot_general x1, matrix products, shards(): lax.dot_general(strict_part, row_panel, (((0,), (0,)), ((), ())), preferr...  18.2 us
    dot_general x1, matrix products, shards(): direct = jnp.dot(lower_part, col_panel, preferred_element_type=jnp.float32)  15.2 us
  transfers between devices with their start and end apart: 5, of which 5 were waited for; matrix products, arithmetic and copies ran while one was open for 5% of the time, Pallas kernels for 0%

commit v1 on v0

v1 whole, which is shorter than its diff:
```python
import functools

import jax
import jax.numpy as jnp
from jax import lax
from jax.experimental import pallas as pl
from jax.experimental.pallas import tpu as pltpu
from jax.sharding import PartitionSpec as P

TOP = 40000.0
TAIL = 16
VMEM = 12 * 2**20


def scale_for(largest):
    scale = TOP / jnp.maximum(largest, 1e-30)
    return scale.astype(jnp.bfloat16).astype(jnp.float32)


def encode(values, scale):
    x = values * scale
    x2 = x * x
    x4 = x2 * x2
    return (x * jnp.abs(x) * x2 * x4).astype(jnp.bfloat16)


def decode(coded, scale):
    y = coded.astype(jnp.float32)
    back = jnp.where(scale > 0, 1.0 / scale, 0.0)
    return y * jnp.exp2(-0.875 * jnp.log2(jnp.maximum(jnp.abs(y), 2.0**-126))) * back


def scale_of(message, rows, block):
    return message[pl.ds(rows + block * TAIL, TAIL), :][0:1, 0:1].astype(jnp.float32)


def put_scale(message, rows, block, scale):
    spread = jnp.full((TAIL, message.shape[1]), scale, jnp.float32).astype(jnp.bfloat16)
    message[pl.ds(rows + block * TAIL, TAIL), :] = spread


def local(kernel, out_shape, name, *operands, after=(), cost=None, **options):
    count, skipped = len(operands), len(after)

    def body(*refs):
        kernel(*refs[:count], *refs[count + skipped :])

    return pl.pallas_call(
        body,
        out_shape=out_shape,
        in_specs=[pl.BlockSpec(memory_space=pltpu.SMEM)]
        + [pl.BlockSpec(memory_space=pltpu.VMEM)] * (count - 1)
        + [pl.BlockSpec(memory_space=pl.ANY)] * skipped,
        out_specs=jax.tree.map(lambda _: pl.BlockSpec(memory_space=pltpu.VMEM), out_shape),
        compiler_params=pltpu.CompilerParams(vmem_limit_bytes=VMEM),
        cost_estimate=cost,
        name=name,
        **options,
    )(*operands, *after)


def load_kernel(ids, a_ref, out_ref, sem):
    height, cols = a_ref.shape
    block = cols // 4

    @pl.when(ids[1] <= ids[0])
    def _():
        copy = pltpu.make_async_copy(a_ref, out_ref, sem)
        copy.start()
        copy.wait()

    for part in range(4):
        here = pl.ds(part * block, block)

        @pl.when(ids[1] == ids[0])
        def _():
            @pl.loop(0, height // block)
            def _(at):
                first = ids[3] + at * block
                rows = pl.ds(pl.multiple_of(at * block, block), block)

                @pl.when(first < part * block)
                def _():
                    out_ref[rows, here] = jnp.zeros((block, block), out_ref.dtype)

                @pl.when(first == part * block)
                def _():
                    tile = out_ref[rows, here]
                    kept = lax.broadcasted_iota(jnp.int32, tile.shape, 0) >= lax.broadcasted_iota(
                        jnp.int32, tile.shape, 1
                    )
                    out_ref[rows, here] = jnp.where(kept, tile, jnp.zeros_like(tile))


def load(ids, trailing):
    return pl.pallas_call(
        load_kernel,
        out_shape=jax.ShapeDtypeStruct(trailing.shape, trailing.dtype),
        in_specs=[pl.BlockSpec(memory_space=pltpu.SMEM), pl.BlockSpec(memory_space=pl.ANY)],
        out_specs=pl.BlockSpec(memory_space=pltpu.VMEM),
        scratch_shapes=[pltpu.SemaphoreType.DMA],
        compiler_params=pltpu.CompilerParams(vmem_limit_bytes=VMEM),
        cost_estimate=pl.CostEstimate(flops=0, bytes_accessed=trailing.size * 4, transcendentals=0),
        name="load",
    )(ids, trailing)


def line_kernel(ids, *refs):
    *came, out_ref = refs
    height = came[0].shape[0]
    for step, piece in enumerate(came):
        chip = lax.rem(ids[1] + len(came) - step, len(came))
        out_ref[pl.ds(pl.multiple_of(chip * height, height), height), :] = piece[...]


def line(ids, came, after):
    height, width = came[0].shape
    out_shape = jax.ShapeDtypeStruct((height * len(came), width), came[0].dtype)
    return local(line_kernel, out_shape, "line", ids, *came, after=after)


def half_kernel(height, ids, mine, other, out_ref):
    count = out_ref.shape[0] // height
    for at in range(count // 2):
        chip = ids[2] * (count // 2) + at
        rows = pl.ds(pl.multiple_of(chip * height, height), height)
        for core, ref in ((ids[2], mine), (1 - ids[2], other)):
            out_ref[pl.ds(pl.multiple_of((2 * at + core) * height, height), height), :] = ref[rows, :]


def half(ids, mine, other, height):
    out_shape = jax.ShapeDtypeStruct(mine.shape, mine.dtype)
    return local(functools.partial(half_kernel, height), out_shape, "half", ids, mine, other)


def mirrored_kernel(piece, ids, a_ref, mine, other, m_ref, msg_ref, turned):
    height, cols = a_ref.shape
    block = cols // 4
    used = ids[1] <= ids[0]

    @pl.loop(0, height // piece // 2)
    def _(at):
        rows = pl.ds(pl.multiple_of(at * piece, piece), piece)
        for core, ref in ((ids[2], mine), (1 - ids[2], other)):
            turned[:, pl.ds(pl.multiple_of((2 * at + core) * piece, piece), piece)] = ref[rows, :].T

    @pl.loop(0, 4)
    def _(part):
        here = pl.ds(pl.multiple_of(part * block, block), block)

        @pl.when(used)
        def _():
            m_ref[here, :] = jnp.dot(turned[...], a_ref[:, here], preferred_element_type=jnp.float32).T

        @pl.when(jnp.logical_not(used))
        def _():
            m_ref[here, :] = jnp.zeros((block, m_ref.shape[1]), jnp.float32)

        @pl.when(ids[1] == ids[0])
        def _():
            rows = pl.ds(pl.multiple_of(part * block - ids[3], block), block)
            tile = a_ref[rows, here]
            kept = lax.broadcasted_iota(jnp.int32, tile.shape, 0) == lax.broadcasted_iota(jnp.int32, tile.shape, 1)
            tile = jnp.where(kept, tile, jnp.zeros_like(tile))
            m_ref[here, :] -= jnp.dot(turned[:, rows], tile, preferred_element_type=jnp.float32).T

        total = m_ref[here, :]
        scale = scale_for(jnp.max(jnp.abs(total), keepdims=True))
        msg_ref[here, :] = encode(total, scale)
        put_scale(msg_ref, cols, part, scale)


def mirrored_product(ids, trailing, mine, other, piece, after):
    rows, cols = trailing.shape
    width = mine.shape[1]
    out_shape = [
        jax.ShapeDtypeStruct((cols, width), jnp.float32),
        jax.ShapeDtypeStruct((cols + 4 * TAIL, width), jnp.bfloat16),
    ]
    cost = pl.CostEstimate(flops=4 * rows * cols * width, bytes_accessed=rows * cols * 2, transcendentals=0)
    return local(
        functools.partial(mirrored_kernel, piece), out_shape, "mirrored_product",
        ids, trailing, mine, other, after=after, cost=cost,
        scratch_shapes=[pltpu.VMEM((width, rows), jnp.bfloat16)],
    )


def relay_kernel(ids, m_ref, *refs):
    *messages, msg_ref = refs
    rows, width = m_ref.shape
    height = rows // 4

    @pl.loop(0, 4)
    def _(part):
        at = pl.ds(pl.multiple_of(part * height, height), height)
        total = m_ref[at, :]
        for message in messages:
            total += decode(message[at, :], scale_of(message, rows, part))
        scale = scale_for(jnp.max(jnp.abs(total), keepdims=True))
        msg_ref[at, :] = encode(total, scale)
        put_scale(msg_ref, rows, part, scale)


def relay(ids, partial, messages, after):
    cost = pl.CostEstimate(flops=0, bytes_accessed=partial.size * 8, transcendentals=0)
    out_shape = jax.ShapeDtypeStruct(messages[0].shape, messages[0].dtype)
    return local(relay_kernel, out_shape, "relay", ids, partial, *messages, after=after, cost=cost)


def direct_kernel(places, ids, a_ref, m_ref, *refs):
    panels = refs[:places]
    messages = refs[places:-4]
    *outs, panel, sem = refs[-4:]
    height = outs[0].shape[0] // places
    cols = a_ref.shape[1]
    blocks = cols // height
    core = ids[2]
    used = ids[1] <= ids[0]

    for place in range(places):

        @pl.when(ids[4] == place)
        def _():
            copy = pltpu.make_async_copy(panels[place], panel, sem)
            copy.start()
            copy.wait()

    @pl.loop(0, outs[0].shape[0] // height)
    def _(piece):
        to = pl.ds(pl.multiple_of(piece * height, height), height)
        for other, out_ref in enumerate(outs):
            step = 2 * piece + (core ^ other)
            rows = pl.ds(pl.multiple_of(step * height, height), height)

            @pl.when(used)
            def _():
                out_ref[to, :] = jnp.dot(a_ref[rows, :], panel[...], preferred_element_type=jnp.float32)

            inside = step - core * blocks

            @pl.when((ids[1] == ids[0]) & (inside >= 0) & (inside < blocks))
            def _():
                block = jnp.clip(inside, 0, blocks - 1)
                at = pl.ds(pl.multiple_of(block * height, height), height)
                total = out_ref[to, :] + m_ref[at, :]
                for message in messages:
                    total += decode(message[at, :], scale_of(message, cols, lax.div(block * 4, blocks)))
                out_ref[to, :] = total


def direct_product(ids, trailing, partial, panels, messages, height, after):
    rows, cols = trailing.shape
    width = partial.shape[1]
    out_shape = [jax.ShapeDtypeStruct((rows // 2, width), jnp.float32)] * 2
    cost = pl.CostEstimate(flops=4 * rows * cols * width, bytes_accessed=rows * cols * 2, transcendentals=0)
    return local(
        functools.partial(direct_kernel, len(panels)), out_shape, "direct_product",
        ids, trailing, partial, *panels, *messages, after=after, cost=cost,
        scratch_shapes=[pltpu.VMEM((cols, width), jnp.bfloat16), pltpu.SemaphoreType.DMA],
    )


def pack_kernel(ids, a_ref, b_ref, own_ref, *msgs):
    height = own_ref.shape[0]
    chips = 1 + len(msgs)
    for step in range(chips):
        rows = pl.ds(pl.multiple_of(lax.rem(ids[1] + step, chips) * height, height), height)
        total = a_ref[rows, :] + b_ref[rows, :]
        if step == 0:
            own_ref[...] = jnp.where(ids[1] <= ids[0], total, 0.0)
        else:
            msg = msgs[step - 1]
            scale = scale_for(jnp.max(jnp.abs(total), keepdims=True))
            msg[pl.ds(0, height), :] = encode(total, scale)
            put_scale(msg, height, 0, scale)


def pack(ids, mine, theirs, chips, after):
    rows, width = mine.shape
    height = rows // chips
    out_shape = [
        jax.ShapeDtypeStruct((height, width), jnp.float32),
        *[jax.ShapeDtypeStruct((height + TAIL, width), jnp.bfloat16)] * (chips - 1),
    ]
    return local(pack_kernel, out_shape, "pack", ids, mine, theirs, after=after)


def finish_kernel(ids, before, own, *refs):
    *messages, out_ref = refs
    height, width = own.shape
    total = own[...]
    for message in messages:
        total += decode(message[pl.ds(0, height), :], scale_of(message, height, 0))
    done = out_ref.shape[1] - width
    if done:
        out_ref[:, pl.ds(0, done)] = before[:, pl.ds(0, done)]
    out_ref[:, pl.ds(done, width)] = total


def finish(ids, before, arrays, after):
    height, width = arrays[0].shape
    done = 0 if before is None else before.shape[1]
    out_shape = jax.ShapeDtypeStruct((height, done + width), jnp.float32)
    return local(finish_kernel, out_shape, "finish", ids, arrays[0] if before is None else before, *arrays, after=after)


def shards(trailing, panel_vectors):
    rows_here, cols_here = trailing.shape
    piece = panel_vectors.shape[0]
    count = lax.axis_size("row")
    devices_along = lax.axis_size("col")
    chips = devices_along // 2
    bits = count.bit_length() - 1
    row, col = lax.axis_index("row"), lax.axis_index("col")
    chip, core = col // 2, col % 2

    def at(row, chip, core):
        return (row * chips + chip) * 2 + core

    def turned(place, core):
        if core == 0:
            return place
        return sum(((place >> b) & 1) << (bits - 1 - b) for b in range(bits))

    def send(x, pairs):
        return lax.ppermute(x, ("row", "col"), [(at(*s), at(*d)) for s, d in pairs])

    offset = row ^ chip
    reverse = sum(((offset >> b) & 1) << (bits - 1 - b) for b in range(bits))
    place = jnp.where(core == 0, offset, reverse)
    ids = jnp.stack([row, chip, core, row * rows_here - col * cols_here, place]).astype(jnp.int32)

    def needed(chip, core, place, bit):
        rest = range(0, count, 2 ** (bit + 1))
        return any(chip ^ turned(place | r, core) > chip for r in rest)

    everyone = [(k, c) for k in range(chips) for c in range(2)]

    width = panel_vectors.shape[1] // 2
    active = [(r, k, c) for r in range(count) for k in range(r + 1) for c in range(2)]

    def spread(place, source):
        bit = place.bit_length() - 1
        before = place - (1 << bit)
        pairs = [
            ((k ^ turned(before, c), k, c), (k ^ turned(place, c), k, c))
            for k, c in everyone
            if needed(k, c, place, bit)
        ]
        return send(source, pairs)

    def collect(bit, message):
        pairs = [
            ((k ^ turned(p, c), k, c), (k ^ turned(p - (1 << bit), c), k, c))
            for k, c in everyone
            for p in range(1 << bit, 2 << bit)
            if needed(k, c, p, bit)
        ]
        return send(message, pairs)

    matrix = load(ids, trailing)

    def gather(block):
        came = [block]
        for step in range(1, chips):
            pairs = [
                ((r, k, c), (r, (k + step) % chips, c))
                for r in range(count)
                for k in range(chips)
                for c in range(2)
                if (k + step) % chips <= r
            ]
            came.append(send(block, pairs))
        return came

    swap = [((r, k, c), (r, k, 1 - c)) for r, k, c in active]

    def opening(came, beside):
        mine = line(ids, came, [])
        other = send(mine, swap)
        panels = [half(ids, mine, other, piece)]
        panels.append(spread(1, panels[0]))
        partial, message = mirrored_product(ids, matrix, mine, other, piece, [panels[0]])
        message, panels[1], *beside = lax.optimization_barrier((message, panels[1], *beside))
        messages = [collect(bits - 1, message)]
        return panels, partial, messages, message, beside

    def relaying(panels, partial, messages, after):
        panels[0], panels[1] = lax.optimization_barrier((panels[0], panels[1]))
        for place in range(2, count):
            panels.append(spread(place, panels[place - (1 << (place.bit_length() - 1))]))
        for bit in reversed(range(bits - 1)):
            message = relay(ids, partial, messages, [panels[1], *after])
            message, *panels[2:] = lax.optimization_barrier((message, *panels[2:]))
            messages.append(collect(bit, message))
        return message

    def product(panels, partial, messages, after):
        keep, give = direct_product(ids, matrix, partial, panels, messages, piece, after)
        got = send(give, swap)
        return keep, got

    def deliver(keep, got, after):
        own, *out = pack(ids, keep, got, chips, after)
        arrays = [own]
        for step, x in enumerate(out, 1):
            arrays.append(send(x, [((r, k, c), (r, (k + step) % chips, c)) for r, k, c in active]))
        return arrays

    came_a = gather(panel_vectors[:, :width])
    came_a, block_b, matrix = lax.optimization_barrier((came_a, panel_vectors[:, width:], matrix))
    came_b = gather(block_b)
    first = opening(came_a, came_b[1:-1])
    came_b[1:-1] = first[4]
    relayed = relaying(*first[:3], [came_b[-1]])
    second = opening(came_b, [relayed])
    keep_a, got_a = product(*first[:3], [second[3], second[0][1]])
    relayed = relaying(*second[:3], [keep_a])
    arrays_a = deliver(keep_a, got_a, [relayed])
    keep_b, give_b = direct_product(ids, matrix, second[1], second[0], second[2], piece, [arrays_a[0]])
    give_b, *arrays_a[1:-1] = lax.optimization_barrier((give_b, *arrays_a[1:-1]))
    arrays_b = deliver(keep_b, send(give_b, swap), [])
    result = finish(ids, None, arrays_a, [arrays_b[0]])
    return finish(ids, result, arrays_b, [])


def solution(mesh):
    in_specs = (P("row", "col"), P(("row", "col"), None))
    out_specs = P(("row", "col"), None)
    return jax.shard_map(shards, mesh=mesh, in_specs=in_specs, out_specs=out_specs, check_vma=False)
```

time: 533 us -> 182 us (0.34)
  the two profiles are of different devices: /device:TPU:7 before, /device:TPU:15 now
where the time goes in v1:
time: 182 us; the launch traced here: 181 us
  starting transfers between devices  63.4 us (35%)
  waiting for transfers between devices  63 us (35%)
  Pallas kernels  47.1 us (26%)
  local copies, waits for them, and re-layouts  6.92 us (4%)
    ppermute x26, starting transfers between devices, send(): return lax.ppermute(x, ('row', 'col'), [(at(*s), at(*d)) for s, d in pairs])  63.4 us
    ppermute x26, waiting for transfers between devices, send(): return lax.ppermute(x, ('row', 'col'), [(at(*s), at(*d)) for s, d in pairs])  63 us
    pallas_call x14, Pallas kernels, local(): pl.pallas_call(body, out_shape=out_shape, in_specs=[pl.BlockSpec(memory_s...  45.4 us
    unnamed x2, local copies, waits for them, and re-layouts  5.77 us
  transfers between devices with their start and end apart: 26, of which 13 were waited for; matrix products, arithmetic and copies ran while one was open for 0% of the time, Pallas kernels for 24%

profile of v1, /device:TPU:15, one launch (start us, length us, event | category | flops | bytes accessed | tf_op | source)
XLA Modules:
  0.0 180.9 jit_solution(11242847474266497242)
XLA Ops:
  1.1 3.2 %collective-permute-start = (bf16[512,256]{1,0:T(8,128)(2,1)S(1)}, bf16[512,256]{1,0:T(8,128)(2,1)S(1)}, u32[]{:S(2)}, u32[]{:S(2)}) collective-permute-start(bf16[512,256]{1,0:T(8,128)(2,1)S(1)} %get-tuple-element.47.refs_1_), channel_id=1, source_target_pairs={{6,0},{7,1},{8,10},{9,11},{14,8},{15,9},{16,18},{17,19},{18,20},{1... | collective-permute-start | bytes 786440 | tf_op jit(solution)/shard_map/ppermute | solution.py:326
  4.3 2.9 %collective-permute-start.1 = (bf16[512,256]{1,0:T(8,128)(2,1)S(1)}, bf16[512,256]{1,0:T(8,128)(2,1)S(1)}, u32[]{:S(2)}, u32[]{:S(2)}) collective-permute-start(bf16[512,256]{1,0:T(8,128)(2,1)S(1)} %get-tuple-element.47.refs_1_), channel_id=1, source_target_pairs={{4,0},{5,1},{12,8},{13,9},{14,10},{15,11},{16,20},{17,21},{20,16},... | collective-permute-start | bytes 786440 | tf_op jit(solution)/shard_map/ppermute | solution.py:326
  7.2 3.4 %collective-permute-start.2 = (bf16[512,256]{1,0:T(8,128)(2,1)S(1)}, bf16[512,256]{1,0:T(8,128)(2,1)S(1)}, u32[]{:S(2)}, u32[]{:S(2)}) collective-permute-start(bf16[512,256]{1,0:T(8,128)(2,1)S(1)} %get-tuple-element.47.refs_1_), channel_id=1, source_target_pairs={{2,0},{3,1},{10,8},{11,9},{12,10},{13,11},{18,16},{19,17},{20,18},... | collective-permute-start | bytes 786440 | tf_op jit(solution)/shard_map/ppermute | solution.py:326
  10.7 5.8 %copy-done = bf16[4096,2048]{1,0:T(8,128)(2,1)S(1)} copy-done((bf16[4096,2048]{1,0:T(8,128)(2,1)S(1)}, bf16[4096,2048]{1,0:T(8,128)(2,1)}, u32[]{:S(2)}) %copy-start) | copy-done | bytes 16777240
  18.2 7.9 %collective-permute-done.1.refs_3_ = bf16[512,256]{1,0:T(8,128)(2,1)S(1)} collective-permute-done((bf16[512,256]{1,0:T(8,128)(2,1)S(1)}, bf16[512,256]{1,0:T(8,128)(2,1)S(1)}, u32[]{:S(2)}, u32[]{:S(2)}) %collective-permute-start.1) | collective-permute-done | bytes 262176 | tf_op jit(solution)/shard_map/ppermute | solution.py:326
  26.1 2.9 %collective-permute-done.2.refs_4_ = bf16[512,256]{1,0:T(8,128)(2,1)S(1)} collective-permute-done((bf16[512,256]{1,0:T(8,128)(2,1)S(1)}, bf16[512,256]{1,0:T(8,128)(2,1)S(1)}, u32[]{:S(2)}, u32[]{:S(2)}) %collective-permute-start.2) | collective-permute-done | bytes 262176 | tf_op jit(solution)/shard_map/ppermute | solution.py:326
  29.6 2.4 %collective-permute-start.3 = (bf16[2048,256]{1,0:T(8,128)(2,1)S(1)}, bf16[2048,256]{1,0:T(8,128)(2,1)S(1)}, u32[]{:S(2)}, u32[]{:S(2)}) collective-permute-start(bf16[2048,256]{1,0:T(8,128)(2,1)S(1)} %line.2.refs_1_.refs_2_), channel_id=1, source_target_pairs={{0,1},{1,0},{8,9},{9,8},{10,11},{11,10},{16,17},{17,16},{18,19},{1... | collective-permute-start | bytes 3145736 | tf_op jit(solution)/shard_map/ppermute | solution.py:326
  32.0 2.3 %collective-permute-done.3.refs_2_.refs_3_ = bf16[2048,256]{1,0:T(8,128)(2,1)S(1)} collective-permute-done((bf16[2048,256]{1,0:T(8,128)(2,1)S(1)}, bf16[2048,256]{1,0:T(8,128)(2,1)S(1)}, u32[]{:S(2)}, u32[]{:S(2)}) %collective-permute-start.3) | collective-permute-done | bytes 1048608 | tf_op jit(solution)/shard_map/ppermute | solution.py:326
  36.2 1.9 %collective-permute-start.5 = (bf16[512,256]{1,0:T(8,128)(2,1)S(1)}, bf16[512,256]{1,0:T(8,128)(2,1)S(1)}, u32[]{:S(2)}, u32[]{:S(2)}) collective-permute-start(bf16[512,256]{1,0:T(8,128)(2,1)S(1)} %get-tuple-element.53.refs_1_), channel_id=1, source_target_pairs={{6,0},{7,1},{8,10},{9,11},{14,8},{15,9},{16,18},{17,19},{18,20},{1... | collective-permute-start | bytes 786440 | tf_op jit(solution)/shard_map/ppermute | solution.py:326
  38.1 2.6 %collective-permute-start.6 = (bf16[512,256]{1,0:T(8,128)(2,1)S(1)}, bf16[512,256]{1,0:T(8,128)(2,1)S(1)}, u32[]{:S(2)}, u32[]{:S(2)}) collective-permute-start(bf16[512,256]{1,0:T(8,128)(2,1)S(1)} %get-tuple-element.53.refs_1_), channel_id=1, source_target_pairs={{4,0},{5,1},{12,8},{13,9},{14,10},{15,11},{16,20},{17,21},{20,16},... | collective-permute-start | bytes 786440 | tf_op jit(solution)/shard_map/ppermute | solution.py:326
  40.7 3.4 %collective-permute-start.8 = (bf16[512,256]{1,0:T(8,128)(2,1)S(1)}, bf16[512,256]{1,0:T(8,128)(2,1)S(1)}, u32[]{:S(2)}, u32[]{:S(2)}) collective-permute-start(bf16[512,256]{1,0:T(8,128)(2,1)S(1)} %get-tuple-element.53.refs_1_), channel_id=1, source_target_pairs={{2,0},{3,1},{10,8},{11,9},{12,10},{13,11},{18,16},{19,17},{20,18},... | collective-permute-start | bytes 786440 | tf_op jit(solution)/shard_map/ppermute | solution.py:326
  44.1 8.7 %mirrored_product.2 = (f32[2048,256]{1,0:T(8,128)S(1)}, bf16[2112,256]{1,0:T(8,128)(2,1)S(1)}) custom-call(s32[5]{0:T(128)S(1)} %stack.23.ids.refs_0_, bf16[4096,2048]{1,0:T(8,128)(2,1)S(1)} %load.1.refs_1_, bf16[2048,256]{1,0:T(8,128)(2,1)S(1)} %line.2.refs_1_.refs_2_, bf16[2048,256]{1,0:T(8,128)(2,1)S(1)} %collective-permute-done.3.refs_2_.refs_3_, ...), custom_call_target="tpu_custom_call" | custom-call | flops 8589934592 | bytes 16777216 | tf_op jit(solution)/shard_map/mirrored_product/pallas_call | solution.py:48
  52.8 8.1 %collective-permute-done.6.refs_3_ = bf16[512,256]{1,0:T(8,128)(2,1)S(1)} collective-permute-done((bf16[512,256]{1,0:T(8,128)(2,1)S(1)}, bf16[512,256]{1,0:T(8,128)(2,1)S(1)}, u32[]{:S(2)}, u32[]{:S(2)}) %collective-permute-start.6) | collective-permute-done | bytes 262176 | tf_op jit(solution)/shard_map/ppermute | solution.py:326
  63.0 4.1 %collective-permute-start.10 = (bf16[2048,256]{1,0:T(8,128)(2,1)S(1)}, bf16[2048,256]{1,0:T(8,128)(2,1)S(1)}, u32[]{:S(2)}, u32[]{:S(2)}) collective-permute-start(bf16[2048,256]{1,0:T(8,128)(2,1)S(1)} %collective-permute-done.4.refs_3_.refs_4_), channel_id=1, source_target_pairs={{8,24},{17,25},{2,18},{27,19}} | collective-permute-start | bytes 3145736 | tf_op jit(solution)/shard_map/ppermute | solution.py:326
  67.7 1.9 %collective-permute-start.12 = (bf16[2048,256]{1,0:T(8,128)(2,1)S(1)}, bf16[2048,256]{1,0:T(8,128)(2,1)S(1)}, u32[]{:S(2)}, u32[]{:S(2)}) collective-permute-start(bf16[2048,256]{1,0:T(8,128)(2,1)S(1)} %line.3.refs_1_.refs_2_), channel_id=1, source_target_pairs={{0,1},{1,0},{8,9},{9,8},{10,11},{11,10},{16,17},{17,16},{18,19},{1... | collective-permute-start | bytes 3145736 | tf_op jit(solution)/shard_map/ppermute | solution.py:326
  69.7 7.5 %collective-permute-done.7.refs_2_.refs_7_ = bf16[2112,256]{1,0:T(8,128)(2,1)S(1)} collective-permute-done((bf16[2112,256]{1,0:T(8,128)(2,1)S(1)}, bf16[2112,256]{1,0:T(8,128)(2,1)S(1)}, u32[]{:S(2)}, u32[]{:S(2)}) %collective-permute-start.7) | collective-permute-done | bytes 1081376 | tf_op jit(solution)/shard_map/ppermute | solution.py:326
  77.1 2.8 %relay.2 = bf16[2112,256]{1,0:T(8,128)(2,1)S(1)} custom-call(s32[5]{0:T(128)S(1)} %stack.23.ids.refs_0_, f32[2048,256]{1,0:T(8,128)S(1)} %get-tuple-element.51.refs_1_.refs_2_, bf16[2112,256]{1,0:T(8,128)(2,1)S(1)} %collective-permute-done.7.refs_2_.refs_7_, bf16[2048,256]{1,0:T(8,128)(2,1)S(1)} %collective-permute-done.4.refs_3_.refs_4_, ...), custom_call_target="tpu_custom_call" | custom-call | bytes 4194304 | tf_op jit(solution)/shard_map/relay/pallas_call | solution.py:48
  83.3 8.7 %mirrored_product.3 = (f32[2048,256]{1,0:T(8,128)S(1)}, bf16[2112,256]{1,0:T(8,128)(2,1)S(1)}) custom-call(s32[5]{0:T(128)S(1)} %stack.23.ids.refs_0_, bf16[4096,2048]{1,0:T(8,128)(2,1)S(1)} %load.1.refs_1_, bf16[2048,256]{1,0:T(8,128)(2,1)S(1)} %line.3.refs_1_.refs_2_, bf16[2048,256]{1,0:T(8,128)(2,1)S(1)} %collective-permute-done.12.refs_2_.refs_3_, ...), custom_call_target="tpu_custom_call" | custom-call | flops 8589934592 | bytes 16777216 | tf_op jit(solution)/shard_map/mirrored_product/pallas_call | solution.py:48
  92.0 5.5 %collective-permute-done.13.refs_10_.refs_3_.refs_4_ = bf16[2048,256]{1,0:T(8,128)(2,1)S(1)} collective-permute-done((bf16[2048,256]{1,0:T(8,128)(2,1)S(1)}, bf16[2048,256]{1,0:T(8,128)(2,1)S(1)}, u32[]{:S(2)}, u32[]{:S(2)}) %collective-permute-start.13) | collective-permute-done | bytes 1048608 | tf_op jit(solution)/shard_map/ppermute | solution.py:326
  99.6 4.1 %collective-permute-start.17 = (bf16[2048,256]{1,0:T(8,128)(2,1)S(1)}, bf16[2048,256]{1,0:T(8,128)(2,1)S(1)}, u32[]{:S(2)}, u32[]{:S(2)}) collective-permute-start(bf16[2048,256]{1,0:T(8,128)(2,1)S(1)} %collective-permute-done.13.refs_10_.refs_3_.refs_4_), channel_id=1, source_target_pairs={{8,24},{17,25},{2,18},{27,19}} | collective-permute-start | bytes 3145736 | tf_op jit(solution)/shard_map/ppermute | solution.py:326
  103.7 6.5 %direct_product.2 = (f32[2048,256]{1,0:T(8,128)S(1)}, f32[2048,256]{1,0:T(8,128)S(1)}) custom-call(s32[5]{0:T(128)S(1)} %stack.23.ids.refs_0_, bf16[4096,2048]{1,0:T(8,128)(2,1)S(1)} %load.1.refs_1_, f32[2048,256]{1,0:T(8,128)S(1)} %get-tuple-element.51.refs_1_.refs_2_, bf16[2048,256]{1,0:T(8,128)(2,1)S(1)} %half.2.refs_4_.refs_3_, ...), custom_call_target="tpu_custom_call" | custom-call | flops 8589934592 | bytes 16777216 | tf_op jit(solution)/shard_map/direct_product/pallas_call | solution.py:48
  110.1 1.9 %collective-permute-start.14 = (f32[2048,256]{1,0:T(8,128)S(1)}, f32[2048,256]{1,0:T(8,128)S(1)}, u32[]{:S(2)}, u32[]{:S(2)}) collective-permute-start(f32[2048,256]{1,0:T(8,128)S(1)} %get-tuple-element.67), channel_id=1, source_target_pairs={{0,1},{1,0},{8,9},{9,8},{10,11},{11,10},{16,17},{17,16},{18,19},{1... | collective-permute-start | bytes 6291464 | tf_op jit(solution)/shard_map/ppermute | solution.py:326
  113.7 2.8 %relay.3.refs_3_ = bf16[2112,256]{1,0:T(8,128)(2,1)S(1)} custom-call(s32[5]{0:T(128)S(1)} %stack.23.ids.refs_0_, f32[2048,256]{1,0:T(8,128)S(1)} %get-tuple-element.68.refs_1_.refs_2_, bf16[2112,256]{1,0:T(8,128)(2,1)S(1)} %collective-permute-done.15.refs_2_.refs_7_, bf16[2048,256]{1,0:T(8,128)(2,1)S(1)} %collective-permute-done.13.refs_10_.refs_3_.refs_4_, ...), custom_call_target="tpu_custom_call" | custom-call | bytes 4194304 | tf_op jit(solution)/shard_map/relay/pallas_call | solution.py:48
  116.6 4.9 %collective-permute-start.18 = (bf16[2112,256]{1,0:T(8,128)(2,1)S(1)}, bf16[2112,256]{1,0:T(8,128)(2,1)S(1)}, u32[]{:S(2)}, u32[]{:S(2)}) collective-permute-start(bf16[2112,256]{1,0:T(8,128)(2,1)S(1)} %relay.3.refs_3_), channel_id=1, source_target_pairs={{8,0},{17,1},{2,10},{27,11},{28,20}} | collective-permute-start | bytes 3244040 | tf_op jit(solution)/shard_map/ppermute | solution.py:326
  127.0 6.3 %collective-permute-done.18.refs_8_ = bf16[2112,256]{1,0:T(8,128)(2,1)S(1)} collective-permute-done((bf16[2112,256]{1,0:T(8,128)(2,1)S(1)}, bf16[2112,256]{1,0:T(8,128)(2,1)S(1)}, u32[]{:S(2)}, u32[]{:S(2)}) %collective-permute-start.18) | collective-permute-done | bytes 1081376 | tf_op jit(solution)/shard_map/ppermute | solution.py:326
  133.3 6.4 %direct_product.3 = (f32[2048,256]{1,0:T(8,128)S(1)}, f32[2048,256]{1,0:T(8,128)S(1)}) custom-call(s32[5]{0:T(128)S(1)} %stack.23.ids.refs_0_, bf16[4096,2048]{1,0:T(8,128)(2,1)S(1)} %load.1.refs_1_, f32[2048,256]{1,0:T(8,128)S(1)} %get-tuple-element.68.refs_1_.refs_2_, bf16[2048,256]{1,0:T(8,128)(2,1)S(1)} %half.3.refs_4_.refs_3_, ...), custom_call_target="tpu_custom_call" | custom-call | flops 8589934592 | bytes 16777216 | tf_op jit(solution)/shard_map/direct_product/pallas_call | solution.py:48
  142.7 2.9 %collective-permute-start.21 = (bf16[528,256]{1,0:T(8,128)(2,1)S(1)}, bf16[528,256]{1,0:T(8,128)(2,1)S(1)}, u32[]{:S(2)}, u32[]{:S(2)}) collective-permute-start(bf16[528,256]{1,0:T(8,128)(2,1)S(1)} %get-tuple-element.80), channel_id=1, source_target_pairs={{0,6},{1,7},{8,14},{9,15},{10,8},{11,9},{16,22},{17,23},{18,16},{1... | collective-permute-start | bytes 811016 | tf_op jit(solution)/shard_map/ppermute | solution.py:326
  148.5 1.9 %collective-permute-start.23 = (bf16[528,256]{1,0:T(8,128)(2,1)S(1)}, bf16[528,256]{1,0:T(8,128)(2,1)S(1)}, u32[]{:S(2)}, u32[]{:S(2)}) collective-permute-start(bf16[528,256]{1,0:T(8,128)(2,1)S(1)} %get-tuple-element.84), channel_id=1, source_target_pairs={{0,2},{1,3},{8,10},{9,11},{10,12},{11,13},{16,18},{17,19},{18,20},... | collective-permute-start | bytes 811016 | tf_op jit(solution)/shard_map/ppermute | solution.py:326
  150.4 5.8 %collective-permute-start.24 = (bf16[528,256]{1,0:T(8,128)(2,1)S(1)}, bf16[528,256]{1,0:T(8,128)(2,1)S(1)}, u32[]{:S(2)}, u32[]{:S(2)}) collective-permute-start(bf16[528,256]{1,0:T(8,128)(2,1)S(1)} %get-tuple-element.85), channel_id=1, source_target_pairs={{0,4},{1,5},{8,12},{9,13},{10,14},{11,15},{16,20},{17,21},{18,22},... | collective-permute-start | bytes 811016 | tf_op jit(solution)/shard_map/ppermute | solution.py:326
  156.2 2.3 %collective-permute-start.25 = (bf16[528,256]{1,0:T(8,128)(2,1)S(1)}, bf16[528,256]{1,0:T(8,128)(2,1)S(1)}, u32[]{:S(2)}, u32[]{:S(2)}) collective-permute-start(bf16[528,256]{1,0:T(8,128)(2,1)S(1)} %get-tuple-element.86), channel_id=1, source_target_pairs={{0,6},{1,7},{8,14},{9,15},{10,8},{11,9},{16,22},{17,23},{18,16},{1... | collective-permute-start | bytes 811016 | tf_op jit(solution)/shard_map/ppermute | solution.py:326
  160.7 17.0 %collective-permute-done.24.refs_4_ = bf16[528,256]{1,0:T(8,128)(2,1)S(1)} collective-permute-done((bf16[528,256]{1,0:T(8,128)(2,1)S(1)}, bf16[528,256]{1,0:T(8,128)(2,1)S(1)}, u32[]{:S(2)}, u32[]{:S(2)}) %collective-permute-start.24) | collective-permute-done | bytes 270368 | tf_op jit(solution)/shard_map/ppermute | solution.py:326
  178.6 2.3 %finish.3 = f32[512,512]{1,0:T(8,128)} custom-call(s32[5]{0:T(128)S(1)} %stack.23.ids.refs_0_, f32[512,256]{1,0:T(8,128)S(1)} %finish.2.refs_1_, f32[512,256]{1,0:T(8,128)S(1)} %get-tuple-element.83.refs_6_.refs_2_, bf16[528,256]{1,0:T(8,128)(2,1)S(1)} %collective-permute-done.23.refs_3_, bf16[528,256]{1,0:T(8,128)(2,1)S(1)} %collective-permute-done.24.refs_4_, ...), custom_call_target="tpu_custom_call" | custom-call | tf_op jit(solution)/shard_map/finish/pallas_call | solution.py:48
  (39 shorter events, 29.3 us)
Async XLA Ops:
  1.1 17.2 %collective-permute-start = (bf16[512,256]{1,0:T(8,128)(2,1)S(1)}, bf16[512,256]{1,0:T(8,128)(2,1)S(1)}, u32[]{:S(2)}, u32[]{:S(2)}) collective-permute-start(bf16[512,256]{1,0:T(8,128)(2,1)S(1)} %get-tuple-element.47.refs_1_), channel_id=1, source_target_pairs={{6,0},{7,1},{8,10},{9,11},{14,8},{15,9},{16,18},{17,19},{18,20},{1... | collective-permute-start | bytes 786440 | tf_op jit(solution)/shard_map/ppermute | solution.py:326
  4.3 21.8 %collective-permute-start.1 = (bf16[512,256]{1,0:T(8,128)(2,1)S(1)}, bf16[512,256]{1,0:T(8,128)(2,1)S(1)}, u32[]{:S(2)}, u32[]{:S(2)}) collective-permute-start(bf16[512,256]{1,0:T(8,128)(2,1)S(1)} %get-tuple-element.47.refs_1_), channel_id=1, source_target_pairs={{4,0},{5,1},{12,8},{13,9},{14,10},{15,11},{16,20},{17,21},{20,16},... | collective-permute-start | bytes 786440 | tf_op jit(solution)/shard_map/ppermute | solution.py:326
  7.2 21.7 %collective-permute-start.2 = (bf16[512,256]{1,0:T(8,128)(2,1)S(1)}, bf16[512,256]{1,0:T(8,128)(2,1)S(1)}, u32[]{:S(2)}, u32[]{:S(2)}) collective-permute-start(bf16[512,256]{1,0:T(8,128)(2,1)S(1)} %get-tuple-element.47.refs_1_), channel_id=1, source_target_pairs={{2,0},{3,1},{10,8},{11,9},{12,10},{13,11},{18,16},{19,17},{20,18},... | collective-permute-start | bytes 786440 | tf_op jit(solution)/shard_map/ppermute | solution.py:326
  10.7 5.8 %copy-start = (bf16[4096,2048]{1,0:T(8,128)(2,1)S(1)}, bf16[4096,2048]{1,0:T(8,128)(2,1)}, u32[]{:S(2)}) copy-start(bf16[4096,2048]{1,0:T(8,128)(2,1)} %a_ref.1) | copy-start | bytes 50331652
  29.6 4.7 %collective-permute-start.3 = (bf16[2048,256]{1,0:T(8,128)(2,1)S(1)}, bf16[2048,256]{1,0:T(8,128)(2,1)S(1)}, u32[]{:S(2)}, u32[]{:S(2)}) collective-permute-start(bf16[2048,256]{1,0:T(8,128)(2,1)S(1)} %line.2.refs_1_.refs_2_), channel_id=1, source_target_pairs={{0,1},{1,0},{8,9},{9,8},{10,11},{11,10},{16,17},{17,16},{18,19},{1... | collective-permute-start | bytes 3145736 | tf_op jit(solution)/shard_map/ppermute | solution.py:326
  34.9 26.1 %collective-permute-start.4 = (bf16[2048,256]{1,0:T(8,128)(2,1)S(1)}, bf16[2048,256]{1,0:T(8,128)(2,1)S(1)}, u32[]{:S(2)}, u32[]{:S(2)}) collective-permute-start(bf16[2048,256]{1,0:T(8,128)(2,1)S(1)} %half.2.refs_4_.refs_3_), channel_id=1, source_target_pairs={{0,8},{1,17},{10,2},{11,27},{20,28}} | collective-permute-start | bytes 3145736 | tf_op jit(solution)/shard_map/ppermute | solution.py:326
  36.2 16.7 %collective-permute-start.5 = (bf16[512,256]{1,0:T(8,128)(2,1)S(1)}, bf16[512,256]{1,0:T(8,128)(2,1)S(1)}, u32[]{:S(2)}, u32[]{:S(2)}) collective-permute-start(bf16[512,256]{1,0:T(8,128)(2,1)S(1)} %get-tuple-element.53.refs_1_), channel_id=1, source_target_pairs={{6,0},{7,1},{8,10},{9,11},{14,8},{15,9},{16,18},{17,19},{18,20},{1... | collective-permute-start | bytes 786440 | tf_op jit(solution)/shard_map/ppermute | solution.py:326
  38.1 22.9 %collective-permute-start.6 = (bf16[512,256]{1,0:T(8,128)(2,1)S(1)}, bf16[512,256]{1,0:T(8,128)(2,1)S(1)}, u32[]{:S(2)}, u32[]{:S(2)}) collective-permute-start(bf16[512,256]{1,0:T(8,128)(2,1)S(1)} %get-tuple-element.53.refs_1_), channel_id=1, source_target_pairs={{4,0},{5,1},{12,8},{13,9},{14,10},{15,11},{16,20},{17,21},{20,16},... | collective-permute-start | bytes 786440 | tf_op jit(solution)/shard_map/ppermute | solution.py:326
  40.7 26.4 %collective-permute-start.8 = (bf16[512,256]{1,0:T(8,128)(2,1)S(1)}, bf16[512,256]{1,0:T(8,128)(2,1)S(1)}, u32[]{:S(2)}, u32[]{:S(2)}) collective-permute-start(bf16[512,256]{1,0:T(8,128)(2,1)S(1)} %get-tuple-element.53.refs_1_), channel_id=1, source_target_pairs={{2,0},{3,1},{10,8},{11,9},{12,10},{13,11},{18,16},{19,17},{20,18},... | collective-permute-start | bytes 786440 | tf_op jit(solution)/shard_map/ppermute | solution.py:326
  61.0 16.2 %collective-permute-start.7 = (bf16[2112,256]{1,0:T(8,128)(2,1)S(1)}, bf16[2112,256]{1,0:T(8,128)(2,1)S(1)}, u32[]{:S(2)}, u32[]{:S(2)}) collective-permute-start(bf16[2112,256]{1,0:T(8,128)(2,1)S(1)} %get-tuple-element.57), channel_id=1, source_target_pairs={{16,0},{24,8},{9,1},{25,17},{26,10},{18,2},{19,27},{29,21}} | collective-permute-start | bytes 3244040 | tf_op jit(solution)/shard_map/ppermute | solution.py:326
  62.2 17.7 %collective-permute-start.9 = (bf16[2048,256]{1,0:T(8,128)(2,1)S(1)}, bf16[2048,256]{1,0:T(8,128)(2,1)S(1)}, u32[]{:S(2)}, u32[]{:S(2)}) collective-permute-start(bf16[2048,256]{1,0:T(8,128)(2,1)S(1)} %half.2.refs_4_.refs_3_), channel_id=1, source_target_pairs={{0,16},{1,9},{10,26},{21,29}} | collective-permute-start | bytes 3145736 | tf_op jit(solution)/shard_map/ppermute | solution.py:326
  63.0 17.0 %collective-permute-start.10 = (bf16[2048,256]{1,0:T(8,128)(2,1)S(1)}, bf16[2048,256]{1,0:T(8,128)(2,1)S(1)}, u32[]{:S(2)}, u32[]{:S(2)}) collective-permute-start(bf16[2048,256]{1,0:T(8,128)(2,1)S(1)} %collective-permute-done.4.refs_3_.refs_4_), channel_id=1, source_target_pairs={{8,24},{17,25},{2,18},{27,19}} | collective-permute-start | bytes 3145736 | tf_op jit(solution)/shard_map/ppermute | solution.py:326
  67.7 13.6 %collective-permute-start.12 = (bf16[2048,256]{1,0:T(8,128)(2,1)S(1)}, bf16[2048,256]{1,0:T(8,128)(2,1)S(1)}, u32[]{:S(2)}, u32[]{:S(2)}) collective-permute-start(bf16[2048,256]{1,0:T(8,128)(2,1)S(1)} %line.3.refs_1_.refs_2_), channel_id=1, source_target_pairs={{0,1},{1,0},{8,9},{9,8},{10,11},{11,10},{16,17},{17,16},{18,19},{1... | collective-permute-start | bytes 3145736 | tf_op jit(solution)/shard_map/ppermute | solution.py:326
  80.0 23.7 %collective-permute-start.11 = (bf16[2112,256]{1,0:T(8,128)(2,1)S(1)}, bf16[2112,256]{1,0:T(8,128)(2,1)S(1)}, u32[]{:S(2)}, u32[]{:S(2)}) collective-permute-start(bf16[2112,256]{1,0:T(8,128)(2,1)S(1)} %relay.2), channel_id=1, source_target_pairs={{8,0},{17,1},{2,10},{27,11},{28,20}} | collective-permute-start | bytes 3244040 | tf_op jit(solution)/shard_map/ppermute | solution.py:326
  82.0 15.5 %collective-permute-start.13 = (bf16[2048,256]{1,0:T(8,128)(2,1)S(1)}, bf16[2048,256]{1,0:T(8,128)(2,1)S(1)}, u32[]{:S(2)}, u32[]{:S(2)}) collective-permute-start(bf16[2048,256]{1,0:T(8,128)(2,1)S(1)} %half.3.refs_4_.refs_3_), channel_id=1, source_target_pairs={{0,8},{1,17},{10,2},{11,27},{20,28}} | collective-permute-start | bytes 3145736 | tf_op jit(solution)/shard_map/ppermute | solution.py:326
  97.5 16.2 %collective-permute-start.15 = (bf16[2112,256]{1,0:T(8,128)(2,1)S(1)}, bf16[2112,256]{1,0:T(8,128)(2,1)S(1)}, u32[]{:S(2)}, u32[]{:S(2)}) collective-permute-start(bf16[2112,256]{1,0:T(8,128)(2,1)S(1)} %get-tuple-element.64.refs_9_), channel_id=1, source_target_pairs={{16,0},{24,8},{9,1},{25,17},{26,10},{18,2},{19,27},{29,21}} | collective-permute-start | bytes 3244040 | tf_op jit(solution)/shard_map/ppermute | solution.py:326
  98.8 17.7 %collective-permute-start.16 = (bf16[2048,256]{1,0:T(8,128)(2,1)S(1)}, bf16[2048,256]{1,0:T(8,128)(2,1)S(1)}, u32[]{:S(2)}, u32[]{:S(2)}) collective-permute-start(bf16[2048,256]{1,0:T(8,128)(2,1)S(1)} %half.3.refs_4_.refs_3_), channel_id=1, source_target_pairs={{0,16},{1,9},{10,26},{21,29}} | collective-permute-start | bytes 3145736 | tf_op jit(solution)/shard_map/ppermute | solution.py:326
  99.6 17.0 %collective-permute-start.17 = (bf16[2048,256]{1,0:T(8,128)(2,1)S(1)}, bf16[2048,256]{1,0:T(8,128)(2,1)S(1)}, u32[]{:S(2)}, u32[]{:S(2)}) collective-permute-start(bf16[2048,256]{1,0:T(8,128)(2,1)S(1)} %collective-permute-done.13.refs_10_.refs_3_.refs_4_), channel_id=1, source_target_pairs={{8,24},{17,25},{2,18},{27,19}} | collective-permute-start | bytes 3145736 | tf_op jit(solution)/shard_map/ppermute | solution.py:326
  110.1 11.4 %collective-permute-start.14 = (f32[2048,256]{1,0:T(8,128)S(1)}, f32[2048,256]{1,0:T(8,128)S(1)}, u32[]{:S(2)}, u32[]{:S(2)}) collective-permute-start(f32[2048,256]{1,0:T(8,128)S(1)} %get-tuple-element.67), channel_id=1, source_target_pairs={{0,1},{1,0},{8,9},{9,8},{10,11},{11,10},{16,17},{17,16},{18,19},{1... | collective-permute-start | bytes 6291464 | tf_op jit(solution)/shard_map/ppermute | solution.py:326
  116.6 16.8 %collective-permute-start.18 = (bf16[2112,256]{1,0:T(8,128)(2,1)S(1)}, bf16[2112,256]{1,0:T(8,128)(2,1)S(1)}, u32[]{:S(2)}, u32[]{:S(2)}) collective-permute-start(bf16[2112,256]{1,0:T(8,128)(2,1)S(1)} %relay.3.refs_3_), channel_id=1, source_target_pairs={{8,0},{17,1},{2,10},{27,11},{28,20}} | collective-permute-start | bytes 3244040 | tf_op jit(solution)/shard_map/ppermute | solution.py:326
  123.2 16.6 %collective-permute-start.19 = (bf16[528,256]{1,0:T(8,128)(2,1)S(1)}, bf16[528,256]{1,0:T(8,128)(2,1)S(1)}, u32[]{:S(2)}, u32[]{:S(2)}) collective-permute-start(bf16[528,256]{1,0:T(8,128)(2,1)S(1)} %get-tuple-element.76), channel_id=1, source_target_pairs={{0,2},{1,3},{8,10},{9,11},{10,12},{11,13},{16,18},{17,19},{18,20},... | collective-permute-start | bytes 811016 | tf_op jit(solution)/shard_map/ppermute | solution.py:326
  125.1 15.7 %collective-permute-start.20 = (bf16[528,256]{1,0:T(8,128)(2,1)S(1)}, bf16[528,256]{1,0:T(8,128)(2,1)S(1)}, u32[]{:S(2)}, u32[]{:S(2)}) collective-permute-start(bf16[528,256]{1,0:T(8,128)(2,1)S(1)} %get-tuple-element.77), channel_id=1, source_target_pairs={{0,4},{1,5},{8,12},{9,13},{10,14},{11,15},{16,20},{17,21},{18,22},... | collective-permute-start | bytes 811016 | tf_op jit(solution)/shard_map/ppermute | solution.py:326
  140.8 6.0 %collective-permute-start.22 = (f32[2048,256]{1,0:T(8,128)S(1)}, f32[2048,256]{1,0:T(8,128)S(1)}, u32[]{:S(2)}, u32[]{:S(2)}) collective-permute-start(f32[2048,256]{1,0:T(8,128)S(1)} %get-tuple-element.82), channel_id=1, source_target_pairs={{0,1},{1,0},{8,9},{9,8},{10,11},{11,10},{16,17},{17,16},{18,19},{1... | collective-permute-start | bytes 6291464 | tf_op jit(solution)/shard_map/ppermute | solution.py:326
  142.7 15.9 %collective-permute-start.21 = (bf16[528,256]{1,0:T(8,128)(2,1)S(1)}, bf16[528,256]{1,0:T(8,128)(2,1)S(1)}, u32[]{:S(2)}, u32[]{:S(2)}) collective-permute-start(bf16[528,256]{1,0:T(8,128)(2,1)S(1)} %get-tuple-element.80), channel_id=1, source_target_pairs={{0,6},{1,7},{8,14},{9,15},{10,8},{11,9},{16,22},{17,23},{18,16},{1... | collective-permute-start | bytes 811016 | tf_op jit(solution)/shard_map/ppermute | solution.py:326
  148.5 12.2 %collective-permute-start.23 = (bf16[528,256]{1,0:T(8,128)(2,1)S(1)}, bf16[528,256]{1,0:T(8,128)(2,1)S(1)}, u32[]{:S(2)}, u32[]{:S(2)}) collective-permute-start(bf16[528,256]{1,0:T(8,128)(2,1)S(1)} %get-tuple-element.84), channel_id=1, source_target_pairs={{0,2},{1,3},{8,10},{9,11},{10,12},{11,13},{16,18},{17,19},{18,20},... | collective-permute-start | bytes 811016 | tf_op jit(solution)/shard_map/ppermute | solution.py:326
  150.4 27.3 %collective-permute-start.24 = (bf16[528,256]{1,0:T(8,128)(2,1)S(1)}, bf16[528,256]{1,0:T(8,128)(2,1)S(1)}, u32[]{:S(2)}, u32[]{:S(2)}) collective-permute-start(bf16[528,256]{1,0:T(8,128)(2,1)S(1)} %get-tuple-element.85), channel_id=1, source_target_pairs={{0,4},{1,5},{8,12},{9,13},{10,14},{11,15},{16,20},{17,21},{18,22},... | collective-permute-start | bytes 811016 | tf_op jit(solution)/shard_map/ppermute | solution.py:326
  156.2 22.4 %collective-permute-start.25 = (bf16[528,256]{1,0:T(8,128)(2,1)S(1)}, bf16[528,256]{1,0:T(8,128)(2,1)S(1)}, u32[]{:S(2)}, u32[]{:S(2)}) collective-permute-start(bf16[528,256]{1,0:T(8,128)(2,1)S(1)} %get-tuple-element.86), channel_id=1, source_target_pairs={{0,6},{1,7},{8,14},{9,15},{10,8},{11,9},{16,22},{17,23},{18,16},{1... | collective-permute-start | bytes 811016 | tf_op jit(solution)/shard_map/ppermute | solution.py:326

commit v2 on v1

v2 whole, which is shorter than its diff:
```python
import functools

import jax
import jax.numpy as jnp
from jax import lax
from jax.experimental import pallas as pl
from jax.experimental.pallas import tpu as pltpu
from jax.sharding import PartitionSpec as P

TOP = 40000.0
TAIL = 16
VMEM = 6 * 2**20


def scale_for(largest):
    scale = TOP / jnp.maximum(largest, 1e-30)
    return scale.astype(jnp.bfloat16).astype(jnp.float32)


def encode(values, scale):
    x = values * scale
    x2 = x * x
    x4 = x2 * x2
    return (x * jnp.abs(x) * x2 * x4).astype(jnp.bfloat16)


def decode(coded, scale):
    y = coded.astype(jnp.float32)
    back = jnp.where(scale > 0, 1.0 / scale, 0.0)
    return y * jnp.exp2(-0.875 * jnp.log2(jnp.maximum(jnp.abs(y), 2.0**-126))) * back


def scale_of(message, rows, block):
    return message[pl.ds(rows + block * TAIL, TAIL), :][0:1, 0:1].astype(jnp.float32)


def put_scale(message, rows, block, scale):
    spread = jnp.full((TAIL, message.shape[1]), scale, jnp.float32).astype(jnp.bfloat16)
    message[pl.ds(rows + block * TAIL, TAIL), :] = spread


def local(kernel, out_shape, name, *operands, after=(), **options):
    count, skipped = len(operands), len(after)

    def body(*refs):
        kernel(*refs[:count], *refs[count + skipped :])

    return pl.pallas_call(
        body,
        out_shape=out_shape,
        in_specs=[pl.BlockSpec(memory_space=pltpu.SMEM)]
        + [pl.BlockSpec(memory_space=pltpu.VMEM)] * (count - 1)
        + [pl.BlockSpec(memory_space=pl.ANY)] * skipped,
        out_specs=jax.tree.map(lambda _: pl.BlockSpec(memory_space=pltpu.VMEM), out_shape),
        compiler_params=pltpu.CompilerParams(vmem_limit_bytes=VMEM),
        name=name,
        **options,
    )(*operands, *after)


def load_kernel(ids, a_ref, out_ref, diagonal, sem):
    height, cols = a_ref.shape
    block = cols // 4
    diagonal[...] = jnp.zeros_like(diagonal)

    @pl.when(ids[1] <= ids[0])
    def _():
        copy = pltpu.make_async_copy(a_ref, out_ref, sem)
        copy.start()
        copy.wait()

    for part in range(4):
        here = pl.ds(part * block, block)

        @pl.when(ids[1] == ids[0])
        def _():
            @pl.loop(0, height // block)
            def _(at):
                first = ids[3] + at * block
                rows = pl.ds(pl.multiple_of(at * block, block), block)

                @pl.when(first < part * block)
                def _():
                    out_ref[rows, here] = jnp.zeros((block, block), out_ref.dtype)

                @pl.when(first == part * block)
                def _():
                    tile = out_ref[rows, here]
                    empty = jnp.zeros_like(tile)
                    row = lax.broadcasted_iota(jnp.int32, tile.shape, 0)
                    col = lax.broadcasted_iota(jnp.int32, tile.shape, 1)
                    out_ref[rows, here] = jnp.where(row >= col, tile, empty)
                    on = jnp.where(row == col, tile, empty).astype(jnp.float32)
                    diagonal[:, here] = jnp.broadcast_to(jnp.sum(on, axis=0, keepdims=True), (8, block))


def load(ids, trailing):
    return pl.pallas_call(
        load_kernel,
        out_shape=[
            jax.ShapeDtypeStruct(trailing.shape, trailing.dtype),
            jax.ShapeDtypeStruct((8, trailing.shape[1]), jnp.float32),
        ],
        in_specs=[pl.BlockSpec(memory_space=pltpu.SMEM), pl.BlockSpec(memory_space=pltpu.HBM)],
        out_specs=[pl.BlockSpec(memory_space=pltpu.VMEM)] * 2,
        scratch_shapes=[pltpu.SemaphoreType.DMA],
        compiler_params=pltpu.CompilerParams(vmem_limit_bytes=VMEM),
        name="load",
    )(ids, trailing)


def line_kernel(places, ids, *refs):
    *came, out_ref = refs
    height = came[0].shape[0]
    for place, piece in zip(places, came):
        chip, there = place(ids[1])

        @pl.when(there)
        def _():
            out_ref[pl.ds(pl.multiple_of(chip * height, height), height), :] = piece[...]


def line(ids, came, places, after):
    height, width = came[0].shape
    chips = 4 if len(came) == 5 else len(came)
    out_shape = jax.ShapeDtypeStruct((height * chips, width), came[0].dtype)
    return local(functools.partial(line_kernel, places), out_shape, "line", ids, *came, after=after)


def half_kernel(height, ids, mine, other, out_ref):
    count = out_ref.shape[0] // height
    for at in range(count // 2):
        chip = ids[2] * (count // 2) + at
        here = pl.ds(pl.multiple_of(chip * height, height), height)
        for core, ref in ((ids[2], mine), (1 - ids[2], other)):
            out_ref[pl.ds(pl.multiple_of((2 * at + core) * height, height), height), :] = ref[here, :]


def half(ids, mine, other, height):
    out_shape = jax.ShapeDtypeStruct(mine.shape, mine.dtype)
    return local(functools.partial(half_kernel, height), out_shape, "half", ids, mine, other)


def mirrored_kernel(piece, ids, a_ref, diagonal, mine, other, m_ref, msg_ref, turned):
    height, cols = a_ref.shape
    block = cols // 4
    used = ids[1] <= ids[0]

    @pl.loop(0, height // piece // 2)
    def _(at):
        rows = pl.ds(pl.multiple_of(at * piece, piece), piece)
        for core, ref in ((ids[2], mine), (1 - ids[2], other)):
            turned[:, pl.ds(pl.multiple_of((2 * at + core) * piece, piece), piece)] = ref[rows, :].T

    @pl.loop(0, 4)
    def _(part):
        here = pl.ds(pl.multiple_of(part * block, block), block)

        @pl.when(used)
        def _():
            m_ref[here, :] = jnp.dot(turned[...], a_ref[:, here], preferred_element_type=jnp.float32).T

        @pl.when(jnp.logical_not(used))
        def _():
            m_ref[here, :] = jnp.zeros((block, m_ref.shape[1]), jnp.float32)

        @pl.when(ids[1] == ids[0])
        def _():
            rows = pl.ds(pl.multiple_of(part * block - ids[3], block), block)
            m_ref[here, :] -= (turned[:, rows].astype(jnp.float32) * diagonal[0:1, here]).T

        total = m_ref[here, :]
        scale = scale_for(jnp.max(jnp.abs(total), keepdims=True))
        msg_ref[here, :] = encode(total, scale)
        put_scale(msg_ref, cols, part, scale)


def mirrored_product(ids, matrix, diagonal, mine, other, piece, after):
    rows, cols = matrix.shape
    width = mine.shape[1]
    out_shape = [
        jax.ShapeDtypeStruct((cols, width), jnp.float32),
        jax.ShapeDtypeStruct((cols + 4 * TAIL, width), jnp.bfloat16),
    ]
    return local(
        functools.partial(mirrored_kernel, piece), out_shape, "mirrored_product",
        ids, matrix, diagonal, mine, other, after=after,
        scratch_shapes=[pltpu.VMEM((width, rows), jnp.bfloat16)],
    )


def relay_kernel(ids, m_ref, in_ref, sum_ref, msg_ref):
    rows, width = m_ref.shape
    height = rows // 4

    @pl.loop(0, 4)
    def _(part):
        at = pl.ds(pl.multiple_of(part * height, height), height)
        total = m_ref[at, :] + decode(in_ref[at, :], scale_of(in_ref, rows, part))
        scale = scale_for(jnp.max(jnp.abs(total), keepdims=True))
        sum_ref[at, :] = total
        msg_ref[at, :] = encode(total, scale)
        put_scale(msg_ref, rows, part, scale)


def relay(ids, partial, message, after):
    out_shape = [jax.ShapeDtypeStruct(x.shape, x.dtype) for x in (partial, message)]
    return local(relay_kernel, out_shape, "relay", ids, partial, message, after=after)


def pick(ids, panels, panel, sem):
    for place, ref in enumerate(panels):

        @pl.when(ids[4] == place)
        def _():
            copy = pltpu.make_async_copy(ref, panel, sem)
            copy.start()
            copy.wait()


def give_kernel(ids, a_ref, *refs):
    *panels, give_ref, give_too, panel, sem = refs
    pick(ids, panels, panel, sem)
    rows_kernel(ids, a_ref, panel, give_ref, core=1 - ids[2], of=2)
    rows_kernel(ids, a_ref, panel, give_too, core=1 - ids[2], at=1, of=2)


def direct_kernel(ids, a_ref, *refs):
    *panels, keep_ref, give_ref, give_too, panel, sem = refs
    pick(ids, panels, panel, sem)
    rows_kernel(ids, a_ref, panel, give_ref, core=1 - ids[2], of=2)
    rows_kernel(ids, a_ref, panel, give_too, core=1 - ids[2], at=1, of=2)
    rows_kernel(ids, a_ref, panel, keep_ref)


def rows_kernel(ids, a_ref, panel, out_ref, core=None, at=0, of=1):
    core = ids[2] if core is None else core
    rows = out_ref.shape[0]
    height = rows * of // 4
    skip = at * rows

    @pl.when(ids[1] <= ids[0])
    def _():
        @pl.loop(0, 4 // of)
        def _(part):
            at = pl.ds(pl.multiple_of(core * rows * of + skip + part * height, height), height)
            to = pl.ds(pl.multiple_of(part * height, height), height)
            out_ref[to, :] = jnp.dot(a_ref[at, :], panel[...], preferred_element_type=jnp.float32)


def direct_product(ids, matrix, panels, after):
    rows, cols = matrix.shape
    width = panels[0].shape[1]
    out_shape = [jax.ShapeDtypeStruct((rows // parts, width), jnp.float32) for parts in (2, 4, 4)]
    return local(
        direct_kernel, out_shape, "direct_product", ids, matrix, *panels, after=after,
        scratch_shapes=[pltpu.VMEM((cols, width), jnp.bfloat16), pltpu.SemaphoreType.DMA],
    )


def give_product(ids, matrix, panels, after):
    rows, cols = matrix.shape
    width = panels[0].shape[1]
    out_shape = [
        *[jax.ShapeDtypeStruct((rows // 4, width), jnp.float32)] * 2,
        jax.ShapeDtypeStruct((cols, width), jnp.bfloat16),
    ]
    return local(
        give_kernel, out_shape, "give_product", ids, matrix, *panels, after=after,
        scratch_shapes=[pltpu.SemaphoreType.DMA],
    )


def keep_product(ids, matrix, panel, after):
    rows, cols = matrix.shape
    width = panel.shape[1]
    out_shape = jax.ShapeDtypeStruct((rows // 2, width), jnp.float32)
    return local(
        rows_kernel, out_shape, "keep_product", ids, matrix, panel, after=after
    )


def pack_kernel(count, ids, a_ref, *refs):
    theirs, (sum_ref, in_ref, own_ref, *msgs, total) = refs[:count], refs[count:]
    height = own_ref.shape[0]
    chips = len(msgs)
    rows = chips * height
    tile = rows // 4
    chip, core = ids[1], ids[2]

    for part in range(4):
        at = pl.ds(part * tile, tile)
        b_ref, where = theirs[part * count // 4], part * tile % theirs[0].shape[0]
        total[at, :] = a_ref[at, :] + b_ref[pl.ds(where, tile), :]

    @pl.when(ids[0] == chip)
    def _():
        @pl.loop(0, 4)
        def _(part):
            at = pl.ds(pl.multiple_of(part * tile, tile), tile)
            total[at, :] += sum_ref[at, :] + decode(in_ref[at, :], scale_of(in_ref, rows, part))

    for step, msg in enumerate(msgs):
        at = pl.ds(pl.multiple_of(lax.rem(chip + step, chips) * height, height), height)
        values = total[at, :]
        scale = scale_for(jnp.max(jnp.abs(values), keepdims=True))
        msg[pl.ds(0, height), :] = encode(values, scale)
        put_scale(msg, height, 0, scale)

    stays = (chip <= ids[0]) & (lax.div(chip, chips // 2) == core)

    @pl.when(stays)
    def _():
        at = pl.ds(pl.multiple_of((2 * lax.rem(chip, chips // 2) + core) * height, height), height)
        own_ref[...] = total[at, :]

    @pl.when(jnp.logical_not(stays))
    def _():
        own_ref[...] = jnp.zeros_like(own_ref)


def pack(ids, mine, theirs, partial, message, chips, after):
    rows, width = mine.shape
    height = rows // chips
    out_shape = [
        jax.ShapeDtypeStruct((height, width), jnp.float32),
        *[jax.ShapeDtypeStruct((height + TAIL, width), jnp.bfloat16)] * chips,
    ]
    return local(
        functools.partial(pack_kernel, len(theirs)), out_shape, "pack", ids, mine, *theirs, partial, message, after=after,
        scratch_shapes=[pltpu.VMEM((rows, width), jnp.float32)],
    )


def finish_kernel(ids, before, own, *refs):
    *messages, out_ref = refs
    height, width = own.shape
    total = own[...]
    for message in messages:
        total += decode(message[pl.ds(0, height), :], scale_of(message, height, 0))
    done = out_ref.shape[1] - width
    if done:
        out_ref[:, pl.ds(0, done)] = before[:, pl.ds(0, done)]
    out_ref[:, pl.ds(done, width)] = total


def finish(ids, before, arrays, after):
    height, width = arrays[0].shape
    done = 0 if before is None else before.shape[1]
    out_shape = jax.ShapeDtypeStruct((height, done + width), jnp.float32)
    return local(finish_kernel, out_shape, "finish", ids, arrays[0] if before is None else before, *arrays, after=after)


def shards(trailing, panel_vectors):
    rows_here, cols_here = trailing.shape
    piece = panel_vectors.shape[0]
    count = lax.axis_size("row")
    devices_along = lax.axis_size("col")
    chips = devices_along // 2
    bits = count.bit_length() - 1
    row, col = lax.axis_index("row"), lax.axis_index("col")
    chip, core = col // 2, col % 2

    def at(row, chip, core):
        return (row * chips + chip) * 2 + core

    def turned(place, core):
        if core == 0:
            return place
        return sum(((place >> b) & 1) << (bits - 1 - b) for b in range(bits))

    def send(x, pairs):
        return lax.ppermute(x, ("row", "col"), [(at(*s), at(*d)) for s, d in pairs])

    offset = row ^ chip
    reverse = sum(((offset >> b) & 1) << (bits - 1 - b) for b in range(bits))
    place = jnp.where(core == 0, offset, reverse)
    ids = jnp.stack([row, chip, core, row * rows_here - col * cols_here, place]).astype(jnp.int32)

    def needed(chip, core, place, bit):
        rest = range(0, count, 2 ** (bit + 1))
        return any(chip ^ turned(place | r, core) > chip for r in rest)

    everyone = [(k, c) for k in range(chips) for c in range(2)]

    width = panel_vectors.shape[1] // 2
    active = [(r, k, c) for r in range(count) for k in range(r + 1) for c in range(2)]

    def spread(place, source):
        bit = place.bit_length() - 1
        before = place - (1 << bit)
        pairs = [
            ((k ^ turned(before, c), k, c), (k ^ turned(place, c), k, c))
            for k, c in everyone
            if needed(k, c, place, bit)
        ]
        return send(source, pairs)

    def collect(bit, message):
        pairs = [
            ((k ^ turned(p, c), k, c), (k ^ turned(p - (1 << bit), c), k, c))
            for k, c in everyone
            for p in range(1 << bit, 2 << bit)
            if needed(k, c, p, bit)
        ]
        return send(message, pairs)

    matrix, diagonal = load(ids, trailing)

    line_of = [(r, k, c) for r in range(count) for k in range(chips) for c in range(2)]

    def step(x, to, wanted):
        return send(x, [((r, k, c), (r, to(k), c)) for r, k, c in line_of if wanted(r, k)])

    def by_distance(block):
        came, places = [block], [lambda chip: (chip, chip >= 0)]
        for by in range(1, chips):
            came.append(step(block, lambda k: (k + by) % chips, lambda r, k: (k + by) % chips <= r))
            places.append(lambda chip, by=by: (lax.rem(chip + chips - by, chips), chip >= 0))
        return came, places

    four = [
        lambda chip: (chip, chip >= 0),
        lambda chip: (chip ^ 2, chip >= 0),
        lambda chip: (jnp.maximum(chip - 1, 0), chip > 0),
        lambda chip: (jnp.minimum(chip + 1, 3), chip < 3),
        lambda chip: (3 - chip, (chip == 0) | (chip == 3)),
    ]

    def two_away(block):
        return step(block, lambda k: k ^ 2, lambda r, k: k >= 2 or k + 2 <= r)

    def next_ones(block):
        up = step(block, lambda k: k + 1, lambda r, k: k + 1 <= r and k < 3)
        return [up, step(block, lambda k: k - 1, lambda r, k: 0 <= k - 1 <= r)]

    def ends(two):
        return step(two, lambda k: 3 * (k - 1), lambda r, k: k == 1 or (k == 2 and r == 3))

    swap = [((r, k, c), (r, k, 1 - c)) for r, k, c in active]

    def widen(panels, after):
        panels[0], panels[1] = lax.optimization_barrier((panels[0], panels[1]))
        for place in range(2, count):
            panels.append(spread(place, panels[place - (1 << (place.bit_length() - 1))]))

    def relaying(partial, came, panels, after):
        for bit in reversed(range(bits - 1)):
            partial, message = relay(ids, partial, came, after)
            if panels:
                message, *panels[2:] = lax.optimization_barrier((message, *panels[2:]))
            came = collect(bit, message)
        return partial, came, message

    def deliver(keep, got, partial, came, after):
        own, *out = pack(ids, keep, got, partial, came, chips, after)
        arrays = [own]
        for step, x in enumerate(out):
            pairs = []
            for r, k, c in active:
                at = c * chips + (k + step) % chips
                if (at // 2, at % 2) != (k, c):
                    pairs.append(((r, k, c), (r, at // 2, at % 2)))
            arrays.append(send(x, pairs))
        return arrays

    block_a, block_b = panel_vectors[:, :width], panel_vectors[:, width:]
    if chips == 4:
        two_a, two_b = two_away(block_a), two_away(block_b)
        came_a = [block_a, two_a, *next_ones(block_a)]
        two_a, matrix = lax.optimization_barrier((two_a, matrix))
        came_a.append(ends(two_a))
        mine_a = line(ids, came_a, four, [two_b])
        came_b, places = [block_b, two_b, *next_ones(block_b), ends(two_b)], four
    else:
        came_a, places = by_distance(block_a)
        came_b, places = by_distance(block_b)
        mine_a = line(ids, came_a, places, [])
    other_a = send(mine_a, swap)
    panels_a = [half(ids, mine_a, other_a, piece)]
    panels_a.append(spread(1, panels_a[0]))
    partial_a, message_a = mirrored_product(ids, matrix, diagonal, mine_a, other_a, piece, [panels_a[0]])
    message_a, panels_a[1], *came_b[2:] = lax.optimization_barrier((message_a, panels_a[1], *came_b[2:]))
    to_a = collect(bits - 1, message_a)
    widen(panels_a, [])

    mine_b = line(ids, came_b, places, [])
    other_b = send(mine_b, swap)
    panels_b = [half(ids, mine_b, other_b, piece)]
    panels_b.append(spread(1, panels_b[0]))
    partial_b, message_b = mirrored_product(ids, matrix, diagonal, mine_b, other_b, piece, [panels_b[0]])
    to_b = collect(bits - 1, message_b)
    partial_a, to_a, relayed = relaying(partial_a, to_a, panels_a, [message_b])
    keep_a, *give_a = direct_product(ids, matrix, panels_a, [relayed, panels_b[1]])
    got_a = [send(x, swap) for x in give_a]
    partial_b, to_b, relayed = relaying(partial_b, to_b, [], [keep_a, to_a])
    widen(panels_b, [])
    arrays_a = deliver(keep_a, got_a, partial_a, to_a, [relayed])
    *give_b, panel_b = give_product(ids, matrix, panels_b, [arrays_a[0]])
    give_b, arrays_a[1] = lax.optimization_barrier((give_b, arrays_a[1]))
    got_b = [send(x, swap) for x in give_b]
    keep_b = keep_product(ids, matrix, panel_b, [to_b])
    arrays_b = deliver(keep_b, got_b, partial_b, to_b, [])
    result = finish(ids, None, arrays_a, [arrays_b[0]])
    return finish(ids, result, arrays_b, [])


def solution(mesh):
    in_specs = (P("row", "col"), P(("row", "col"), None))
    out_specs = P(("row", "col"), None)
    return jax.shard_map(shards, mesh=mesh, in_specs=in_specs, out_specs=out_specs, check_vma=False)
```

time: 182 us -> 179 us (0.984)
  the two profiles are of different devices: /device:TPU:15 before, /device:TPU:7 now
where the time goes in v2:
time: 179 us; the launch traced here: 178 us
  starting transfers between devices  84 us (47%)
  Pallas kernels  48.9 us (27%)
  waiting for transfers between devices  37.8 us (21%)
  local copies, waits for them, and re-layouts  6.92 us (4%)
    ppermute x32, starting transfers between devices, send(): return lax.ppermute(x, ('row', 'col'), [(at(*s), at(*d)) for s, d in pairs])  84 us
    pallas_call x15, Pallas kernels, local(): pl.pallas_call(body, out_shape=out_shape, in_specs=[pl.BlockSpec(memory_s...  47.2 us
    ppermute x32, waiting for transfers between devices, send(): return lax.ppermute(x, ('row', 'col'), [(at(*s), at(*d)) for s, d in pairs])  37.8 us
    unnamed x2, local copies, waits for them, and re-layouts  5.77 us
  transfers between devices with their start and end apart: 32, of which 8 were waited for; matrix products, arithmetic and copies ran while one was open for 0% of the time, Pallas kernels for 25%

profile of v2, /device:TPU:7, one launch (start us, length us, event | category | flops | bytes accessed | tf_op | source)
XLA Modules:
  0.0 178.2 jit_solution(16575453056232228153)
XLA Ops:
  1.1 4.2 %collective-permute-start = (bf16[512,256]{1,0:T(8,128)(2,1)S(1)}, bf16[512,256]{1,0:T(8,128)(2,1)S(1)}, u32[]{:S(2)}, u32[]{:S(2)}) collective-permute-start(bf16[512,256]{1,0:T(8,128)(2,1)S(1)} %get-tuple-element.92.refs_1_), channel_id=1, source_target_pairs={{4,0},{5,1},{6,2},{7,3},{12,8},{13,9},{14,10},{15,11},{16,20},{17,... | collective-permute-start | bytes 786440 | tf_op jit(solution)/shard_map/ppermute | solution.py:373
  5.3 3.2 %collective-permute-start.1 = (bf16[512,256]{1,0:T(8,128)(2,1)S(1)}, bf16[512,256]{1,0:T(8,128)(2,1)S(1)}, u32[]{:S(2)}, u32[]{:S(2)}) collective-permute-start(bf16[512,256]{1,0:T(8,128)(2,1)S(1)} %get-tuple-element.92.refs_1_), channel_id=1, source_target_pairs={{8,10},{9,11},{16,18},{17,19},{18,20},{19,21},{24,26},{25,27},{26,... | collective-permute-start | bytes 786440 | tf_op jit(solution)/shard_map/ppermute | solution.py:373
  9.8 3.7 %collective-permute-start.4 = (bf16[512,256]{1,0:T(8,128)(2,1)S(1)}, bf16[512,256]{1,0:T(8,128)(2,1)S(1)}, u32[]{:S(2)}, u32[]{:S(2)}) collective-permute-start(bf16[512,256]{1,0:T(8,128)(2,1)S(1)} %get-tuple-element.91.refs_1_), channel_id=1, source_target_pairs={{4,0},{5,1},{6,2},{7,3},{12,8},{13,9},{14,10},{15,11},{16,20},{17,... | collective-permute-start | bytes 786440 | tf_op jit(solution)/shard_map/ppermute | solution.py:373
  13.6 5.8 %copy-done = bf16[4096,2048]{1,0:T(8,128)(2,1)S(1)} copy-done((bf16[4096,2048]{1,0:T(8,128)(2,1)S(1)}, bf16[4096,2048]{1,0:T(8,128)(2,1)}, u32[]{:S(2)}) %copy-start) | copy-done | bytes 16777240
  22.9 10.7 %collective-permute-done.4.refs_6_.refs_2_ = bf16[512,256]{1,0:T(8,128)(2,1)S(1)} collective-permute-done((bf16[512,256]{1,0:T(8,128)(2,1)S(1)}, bf16[512,256]{1,0:T(8,128)(2,1)S(1)}, u32[]{:S(2)}, u32[]{:S(2)}) %collective-permute-start.4) | collective-permute-done | bytes 262176 | tf_op jit(solution)/shard_map/ppermute | solution.py:373
  34.3 6.1 %collective-permute-start.5 = (bf16[2048,256]{1,0:T(8,128)(2,1)S(1)}, bf16[2048,256]{1,0:T(8,128)(2,1)S(1)}, u32[]{:S(2)}, u32[]{:S(2)}) collective-permute-start(bf16[2048,256]{1,0:T(8,128)(2,1)S(1)} %line.2.refs_1_.refs_3_), channel_id=1, source_target_pairs={{0,1},{1,0},{8,9},{9,8},{10,11},{11,10},{16,17},{17,16},{18,19},{1... | collective-permute-start | bytes 3145736 | tf_op jit(solution)/shard_map/ppermute | solution.py:373
  40.4 2.3 %collective-permute-done.5.refs_2_.refs_4_ = bf16[2048,256]{1,0:T(8,128)(2,1)S(1)} collective-permute-done((bf16[2048,256]{1,0:T(8,128)(2,1)S(1)}, bf16[2048,256]{1,0:T(8,128)(2,1)S(1)}, u32[]{:S(2)}, u32[]{:S(2)}) %collective-permute-start.5) | collective-permute-done | bytes 1048608 | tf_op jit(solution)/shard_map/ppermute | solution.py:373
  48.4 8.7 %mirrored_product.2 = (f32[2048,256]{1,0:T(8,128)S(1)}, bf16[2112,256]{1,0:T(8,128)(2,1)S(1)}) custom-call(s32[5]{0:T(128)S(1)} %stack.23.ids.refs_0_, bf16[4096,2048]{1,0:T(8,128)(2,1)S(1)} %get-tuple-element.49.refs_1_, f32[8,2048]{1,0:T(8,128)S(1)} %get-tuple-element.51.refs_2_, bf16[2048,256]{1,0:T(8,128)(2,1)S(1)} %line.2.refs_1_.refs_3_, ...), custom_call_target="tpu_custom_call" | custom-call | tf_op jit(solution)/shard_map/mirrored_product/pallas_call | solution.py:48
  57.1 3.9 %collective-permute-done.9.refs_5_ = bf16[512,256]{1,0:T(8,128)(2,1)S(1)} collective-permute-done((bf16[512,256]{1,0:T(8,128)(2,1)S(1)}, bf16[512,256]{1,0:T(8,128)(2,1)S(1)}, u32[]{:S(2)}, u32[]{:S(2)}) %collective-permute-start.9) | collective-permute-done | bytes 262176 | tf_op jit(solution)/shard_map/ppermute | solution.py:373
  61.6 3.8 %collective-permute-start.11 = (bf16[2048,256]{1,0:T(8,128)(2,1)S(1)}, bf16[2048,256]{1,0:T(8,128)(2,1)S(1)}, u32[]{:S(2)}, u32[]{:S(2)}) collective-permute-start(bf16[2048,256]{1,0:T(8,128)(2,1)S(1)} %line.3.refs_1_.refs_3_), channel_id=1, source_target_pairs={{0,1},{1,0},{8,9},{9,8},{10,11},{11,10},{16,17},{17,16},{18,19},{1... | collective-permute-start | bytes 3145736 | tf_op jit(solution)/shard_map/ppermute | solution.py:373
  70.3 8.7 %mirrored_product.3 = (f32[2048,256]{1,0:T(8,128)S(1)}, bf16[2112,256]{1,0:T(8,128)(2,1)S(1)}) custom-call(s32[5]{0:T(128)S(1)} %stack.23.ids.refs_0_, bf16[4096,2048]{1,0:T(8,128)(2,1)S(1)} %get-tuple-element.49.refs_1_, f32[8,2048]{1,0:T(8,128)S(1)} %get-tuple-element.51.refs_2_, bf16[2048,256]{1,0:T(8,128)(2,1)S(1)} %line.3.refs_1_.refs_3_, ...), custom_call_target="tpu_custom_call" | custom-call | tf_op jit(solution)/shard_map/mirrored_product/pallas_call | solution.py:48
  79.0 4.7 %collective-permute-start.18 = (bf16[2112,256]{1,0:T(8,128)(2,1)S(1)}, bf16[2112,256]{1,0:T(8,128)(2,1)S(1)}, u32[]{:S(2)}, u32[]{:S(2)}) collective-permute-start(bf16[2112,256]{1,0:T(8,128)(2,1)S(1)} %get-tuple-element.61.refs_3_), channel_id=1, source_target_pairs={{16,0},{24,8},{9,1},{25,17},{26,10},{18,2},{19,27},{29,21}} | collective-permute-start | bytes 3244040 | tf_op jit(solution)/shard_map/ppermute | solution.py:373
  83.7 2.8 %relay.2 = (f32[2048,256]{1,0:T(8,128)S(1)}, bf16[2112,256]{1,0:T(8,128)(2,1)S(1)}) custom-call(s32[5]{0:T(128)S(1)} %stack.23.ids.refs_0_, f32[2048,256]{1,0:T(8,128)S(1)} %get-tuple-element.56.refs_1_, bf16[2112,256]{1,0:T(8,128)(2,1)S(1)} %collective-permute-done.10.refs_2_, bf16[2112,256]{1,0:T(8,128)(2,1)S(1)} %get-tuple-element.61.refs_3_), custom_call_target="tpu_custom_call" | custom-call | tf_op jit(solution)/shard_map/relay/pallas_call | solution.py:48
  87.3 6.4 %direct_product.1 = (f32[2048,256]{1,0:T(8,128)S(1)}, f32[1024,256]{1,0:T(8,128)S(1)}, f32[1024,256]{1,0:T(8,128)S(1)}) custom-call(s32[5]{0:T(128)S(1)} %stack.23.ids.refs_0_, bf16[4096,2048]{1,0:T(8,128)(2,1)S(1)} %get-tuple-element.49.refs_1_, bf16[2048,256]{1,0:T(8,128)(2,1)S(1)} %half.2.refs_5_.refs_2_, ...), custom_call_target="tpu_custom_call" | custom-call | tf_op jit(solution)/shard_map/direct_product/pallas_call | solution.py:48
  93.7 4.5 %collective-permute-start.15 = (f32[1024,256]{1,0:T(8,128)S(1)}, f32[1024,256]{1,0:T(8,128)S(1)}, u32[]{:S(2)}, u32[]{:S(2)}) collective-permute-start(f32[1024,256]{1,0:T(8,128)S(1)} %get-tuple-element.67), channel_id=1, source_target_pairs={{0,1},{1,0},{8,9},{9,8},{10,11},{11,10},{16,17},{17,16},{18,19},{1... | collective-permute-start | bytes 3145736 | tf_op jit(solution)/shard_map/ppermute | solution.py:373
  102.2 2.8 %relay.3 = (f32[2048,256]{1,0:T(8,128)S(1)}, bf16[2112,256]{1,0:T(8,128)(2,1)S(1)}) custom-call(s32[5]{0:T(128)S(1)} %stack.23.ids.refs_0_, f32[2048,256]{1,0:T(8,128)S(1)} %get-tuple-element.70.refs_1_, bf16[2112,256]{1,0:T(8,128)(2,1)S(1)} %collective-permute-done.18.refs_2_, f32[2048,256]{1,0:T(8,128)S(1)} %get-tuple-element.66.refs_3_.refs_1_, ...), custom_call_target="tpu_custom_call" | custom-call | tf_op jit(solution)/shard_map/relay/pallas_call | solution.py:48
  105.1 2.2 %pack.2 = (f32[512,256]{1,0:T(8,128)S(1)}, bf16[528,256]{1,0:T(8,128)(2,1)S(1)}, bf16[528,256]{1,0:T(8,128)(2,1)S(1)}, bf16[528,256]{1,0:T(8,128)(2,1)S(1)}, bf16[528,256]{1,0:T(8,128)(2,1)S(1)}) custom-call(s32[5]{0:T(128)S(1)} %stack.23.ids.refs_0_, f32[2048,256]{1,0:T(8,128)S(1)} %get-tuple-element.66.refs_3_.refs_1_, ...), custom_call_target="tpu_custom_call" | custom-call | tf_op jit(solution)/shard_map/pack/pallas_call | solution.py:48
  107.3 10.5 %collective-permute-start.21 = (bf16[528,256]{1,0:T(8,128)(2,1)S(1)}, bf16[528,256]{1,0:T(8,128)(2,1)S(1)}, u32[]{:S(2)}, u32[]{:S(2)}) collective-permute-start(bf16[528,256]{1,0:T(8,128)(2,1)S(1)} %get-tuple-element.77), channel_id=1, source_target_pairs={{1,4},{9,12},{10,9},{11,13},{17,20},{18,17},{19,21},{20,18},{21,22... | collective-permute-start | bytes 811016 | tf_op jit(solution)/shard_map/ppermute | solution.py:373
  118.5 2.7 %collective-permute-done.20.refs_5_ = bf16[2048,256]{1,0:T(8,128)(2,1)S(1)} collective-permute-done((bf16[2048,256]{1,0:T(8,128)(2,1)S(1)}, bf16[2048,256]{1,0:T(8,128)(2,1)S(1)}, u32[]{:S(2)}, u32[]{:S(2)}) %collective-permute-start.20) | collective-permute-done | bytes 1048608 | tf_op jit(solution)/shard_map/ppermute | solution.py:373
  121.2 3.5 %give_product.1 = (f32[1024,256]{1,0:T(8,128)S(1)}, f32[1024,256]{1,0:T(8,128)S(1)}, bf16[2048,256]{1,0:T(8,128)(2,1)S(1)}) custom-call(s32[5]{0:T(128)S(1)} %stack.23.ids.refs_0_, bf16[4096,2048]{1,0:T(8,128)(2,1)S(1)} %get-tuple-element.49.refs_1_, bf16[2048,256]{1,0:T(8,128)(2,1)S(1)} %half.3.refs_5_.refs_2_, ...), custom_call_target="tpu_custom_call" | custom-call | tf_op jit(solution)/shard_map/give_product/pallas_call | solution.py:48
  124.7 2.4 %collective-permute-start.26 = (f32[1024,256]{1,0:T(8,128)S(1)}, f32[1024,256]{1,0:T(8,128)S(1)}, u32[]{:S(2)}, u32[]{:S(2)}) collective-permute-start(f32[1024,256]{1,0:T(8,128)S(1)} %get-tuple-element.83), channel_id=1, source_target_pairs={{0,1},{1,0},{8,9},{9,8},{10,11},{11,10},{16,17},{17,16},{18,19},{1... | collective-permute-start | bytes 3145736 | tf_op jit(solution)/shard_map/ppermute | solution.py:373
  127.2 1.9 %collective-permute-start.27 = (f32[1024,256]{1,0:T(8,128)S(1)}, f32[1024,256]{1,0:T(8,128)S(1)}, u32[]{:S(2)}, u32[]{:S(2)}) collective-permute-start(f32[1024,256]{1,0:T(8,128)S(1)} %get-tuple-element.84), channel_id=1, source_target_pairs={{0,1},{1,0},{8,9},{9,8},{10,11},{11,10},{16,17},{17,16},{18,19},{1... | collective-permute-start | bytes 3145736 | tf_op jit(solution)/shard_map/ppermute | solution.py:373
  129.1 4.1 %collective-permute-start.22 = (bf16[528,256]{1,0:T(8,128)(2,1)S(1)}, bf16[528,256]{1,0:T(8,128)(2,1)S(1)}, u32[]{:S(2)}, u32[]{:S(2)}) collective-permute-start(bf16[528,256]{1,0:T(8,128)(2,1)S(1)} %get-tuple-element.79), channel_id=1, source_target_pairs={{0,1},{1,5},{8,9},{9,13},{11,14},{16,17},{17,21},{19,22},{20,19},{... | collective-permute-start | bytes 811016 | tf_op jit(solution)/shard_map/ppermute | solution.py:373
  133.2 3.6 %collective-permute-start.23 = (bf16[528,256]{1,0:T(8,128)(2,1)S(1)}, bf16[528,256]{1,0:T(8,128)(2,1)S(1)}, u32[]{:S(2)}, u32[]{:S(2)}) collective-permute-start(bf16[528,256]{1,0:T(8,128)(2,1)S(1)} %get-tuple-element.80), channel_id=1, source_target_pairs={{0,2},{1,6},{8,10},{9,14},{10,11},{11,15},{16,18},{17,22},{18,19},... | collective-permute-start | bytes 811016 | tf_op jit(solution)/shard_map/ppermute | solution.py:373
  138.8 3.4 %keep_product.1.refs_1_ = f32[2048,256]{1,0:T(8,128)S(1)} custom-call(s32[5]{0:T(128)S(1)} %stack.23.ids.refs_0_, bf16[4096,2048]{1,0:T(8,128)(2,1)S(1)} %get-tuple-element.49.refs_1_, bf16[2048,256]{1,0:T(8,128)(2,1)S(1)} %get-tuple-element.82.refs_2_, bf16[2112,256]{1,0:T(8,128)(2,1)S(1)} %collective-permute-done.25.refs_3_.refs_5_), custom_call_target="tpu_custom_call" | custom-call | tf_op jit(solution)/shard_map/keep_product/pallas_call | solution.py:48
  142.2 2.0 %pack.3 = (f32[512,256]{1,0:T(8,128)S(1)}, bf16[528,256]{1,0:T(8,128)(2,1)S(1)}, bf16[528,256]{1,0:T(8,128)(2,1)S(1)}, bf16[528,256]{1,0:T(8,128)(2,1)S(1)}, bf16[528,256]{1,0:T(8,128)(2,1)S(1)}) custom-call(s32[5]{0:T(128)S(1)} %stack.23.ids.refs_0_, f32[2048,256]{1,0:T(8,128)S(1)} %keep_product.1.refs_1_, f32[1024,256]{1,0:T(8,128)S(1)} %collective-permute-done.26.refs_2_, ...), custom_call_target="tpu_custom_call" | custom-call | tf_op jit(solution)/shard_map/pack/pallas_call | solution.py:48
  144.2 4.5 %collective-permute-start.28 = (bf16[528,256]{1,0:T(8,128)(2,1)S(1)}, bf16[528,256]{1,0:T(8,128)(2,1)S(1)}, u32[]{:S(2)}, u32[]{:S(2)}) collective-permute-start(bf16[528,256]{1,0:T(8,128)(2,1)S(1)} %get-tuple-element.87), channel_id=1, source_target_pairs={{1,4},{9,12},{10,9},{11,13},{17,20},{18,17},{19,21},{20,18},{21,22... | collective-permute-start | bytes 811016 | tf_op jit(solution)/shard_map/ppermute | solution.py:373
  148.8 2.4 %collective-permute-start.29 = (bf16[528,256]{1,0:T(8,128)(2,1)S(1)}, bf16[528,256]{1,0:T(8,128)(2,1)S(1)}, u32[]{:S(2)}, u32[]{:S(2)}) collective-permute-start(bf16[528,256]{1,0:T(8,128)(2,1)S(1)} %get-tuple-element.88), channel_id=1, source_target_pairs={{0,1},{1,5},{8,9},{9,13},{11,14},{16,17},{17,21},{19,22},{20,19},{... | collective-permute-start | bytes 811016 | tf_op jit(solution)/shard_map/ppermute | solution.py:373
  153.1 3.1 %collective-permute-start.31 = (bf16[528,256]{1,0:T(8,128)(2,1)S(1)}, bf16[528,256]{1,0:T(8,128)(2,1)S(1)}, u32[]{:S(2)}, u32[]{:S(2)}) collective-permute-start(bf16[528,256]{1,0:T(8,128)(2,1)S(1)} %get-tuple-element.90), channel_id=1, source_target_pairs={{0,3},{1,7},{8,11},{9,15},{10,8},{11,12},{16,19},{17,23},{18,16},{... | collective-permute-start | bytes 811016 | tf_op jit(solution)/shard_map/ppermute | solution.py:373
  159.1 5.7 %collective-permute-done.30.refs_5_ = bf16[528,256]{1,0:T(8,128)(2,1)S(1)} collective-permute-done((bf16[528,256]{1,0:T(8,128)(2,1)S(1)}, bf16[528,256]{1,0:T(8,128)(2,1)S(1)}, u32[]{:S(2)}, u32[]{:S(2)}) %collective-permute-start.30) | collective-permute-done | bytes 270368 | tf_op jit(solution)/shard_map/ppermute | solution.py:373
  164.8 10.8 %collective-permute-done.31.refs_6_ = bf16[528,256]{1,0:T(8,128)(2,1)S(1)} collective-permute-done((bf16[528,256]{1,0:T(8,128)(2,1)S(1)}, bf16[528,256]{1,0:T(8,128)(2,1)S(1)}, u32[]{:S(2)}, u32[]{:S(2)}) %collective-permute-start.31) | collective-permute-done | bytes 270368 | tf_op jit(solution)/shard_map/ppermute | solution.py:373
  175.6 2.6 %finish.3 = f32[512,512]{1,0:T(8,128)} custom-call(s32[5]{0:T(128)S(1)} %stack.23.ids.refs_0_, f32[512,256]{1,0:T(8,128)S(1)} %finish.2.refs_1_, f32[512,256]{1,0:T(8,128)S(1)} %get-tuple-element.86.refs_7_.refs_2_, bf16[528,256]{1,0:T(8,128)(2,1)S(1)} %collective-permute-done.28.refs_3_, bf16[528,256]{1,0:T(8,128)(2,1)S(1)} %collective-permute-done.29.refs_4_, ...), custom_call_target="tpu_custom_call" | custom-call | tf_op jit(solution)/shard_map/finish/pallas_call | solution.py:48
  (52 shorter events, 29.9 us)
Async XLA Ops:
  1.1 20.1 %collective-permute-start = (bf16[512,256]{1,0:T(8,128)(2,1)S(1)}, bf16[512,256]{1,0:T(8,128)(2,1)S(1)}, u32[]{:S(2)}, u32[]{:S(2)}) collective-permute-start(bf16[512,256]{1,0:T(8,128)(2,1)S(1)} %get-tuple-element.92.refs_1_), channel_id=1, source_target_pairs={{4,0},{5,1},{6,2},{7,3},{12,8},{13,9},{14,10},{15,11},{16,20},{17,... | collective-permute-start | bytes 786440 | tf_op jit(solution)/shard_map/ppermute | solution.py:373
  5.3 17.2 %collective-permute-start.1 = (bf16[512,256]{1,0:T(8,128)(2,1)S(1)}, bf16[512,256]{1,0:T(8,128)(2,1)S(1)}, u32[]{:S(2)}, u32[]{:S(2)}) collective-permute-start(bf16[512,256]{1,0:T(8,128)(2,1)S(1)} %get-tuple-element.92.refs_1_), channel_id=1, source_target_pairs={{8,10},{9,11},{16,18},{17,19},{18,20},{19,21},{24,26},{25,27},{26,... | collective-permute-start | bytes 786440 | tf_op jit(solution)/shard_map/ppermute | solution.py:373
  8.5 14.4 %collective-permute-start.2 = (bf16[512,256]{1,0:T(8,128)(2,1)S(1)}, bf16[512,256]{1,0:T(8,128)(2,1)S(1)}, u32[]{:S(2)}, u32[]{:S(2)}) collective-permute-start(bf16[512,256]{1,0:T(8,128)(2,1)S(1)} %get-tuple-element.92.refs_1_), channel_id=1, source_target_pairs={{2,0},{3,1},{10,8},{11,9},{12,10},{13,11},{18,16},{19,17},{20,18},... | collective-permute-start | bytes 786440 | tf_op jit(solution)/shard_map/ppermute | solution.py:373
  9.8 23.8 %collective-permute-start.4 = (bf16[512,256]{1,0:T(8,128)(2,1)S(1)}, bf16[512,256]{1,0:T(8,128)(2,1)S(1)}, u32[]{:S(2)}, u32[]{:S(2)}) collective-permute-start(bf16[512,256]{1,0:T(8,128)(2,1)S(1)} %get-tuple-element.91.refs_1_), channel_id=1, source_target_pairs={{4,0},{5,1},{6,2},{7,3},{12,8},{13,9},{14,10},{15,11},{16,20},{17,... | collective-permute-start | bytes 786440 | tf_op jit(solution)/shard_map/ppermute | solution.py:373
  21.2 12.4 %collective-permute-start.3 = (bf16[512,256]{1,0:T(8,128)(2,1)S(1)}, bf16[512,256]{1,0:T(8,128)(2,1)S(1)}, u32[]{:S(2)}, u32[]{:S(2)}) collective-permute-start(bf16[512,256]{1,0:T(8,128)(2,1)S(1)} %collective-permute-done.refs_2_), channel_id=1, source_target_pairs={{2,0},{3,1},{10,8},{11,9},{18,16},{19,17},{26,24},{27,25},{28,30},... | collective-permute-start | bytes 786440 | tf_op jit(solution)/shard_map/ppermute | solution.py:373
  34.3 8.4 %collective-permute-start.5 = (bf16[2048,256]{1,0:T(8,128)(2,1)S(1)}, bf16[2048,256]{1,0:T(8,128)(2,1)S(1)}, u32[]{:S(2)}, u32[]{:S(2)}) collective-permute-start(bf16[2048,256]{1,0:T(8,128)(2,1)S(1)} %line.2.refs_1_.refs_3_), channel_id=1, source_target_pairs={{0,1},{1,0},{8,9},{9,8},{10,11},{11,10},{16,17},{17,16},{18,19},{1... | collective-permute-start | bytes 3145736 | tf_op jit(solution)/shard_map/ppermute | solution.py:373
  43.3 17.7 %collective-permute-start.6 = (bf16[2048,256]{1,0:T(8,128)(2,1)S(1)}, bf16[2048,256]{1,0:T(8,128)(2,1)S(1)}, u32[]{:S(2)}, u32[]{:S(2)}) collective-permute-start(bf16[2048,256]{1,0:T(8,128)(2,1)S(1)} %half.2.refs_5_.refs_2_), channel_id=1, source_target_pairs={{0,8},{1,17},{10,2},{11,27},{20,28}} | collective-permute-start | bytes 3145736 | tf_op jit(solution)/shard_map/ppermute | solution.py:373
  44.0 13.1 %collective-permute-start.7 = (bf16[512,256]{1,0:T(8,128)(2,1)S(1)}, bf16[512,256]{1,0:T(8,128)(2,1)S(1)}, u32[]{:S(2)}, u32[]{:S(2)}) collective-permute-start(bf16[512,256]{1,0:T(8,128)(2,1)S(1)} %get-tuple-element.91.refs_1_), channel_id=1, source_target_pairs={{8,10},{9,11},{16,18},{17,19},{18,20},{19,21},{24,26},{25,27},{26,... | collective-permute-start | bytes 786440 | tf_op jit(solution)/shard_map/ppermute | solution.py:373
  45.8 11.3 %collective-permute-start.8 = (bf16[512,256]{1,0:T(8,128)(2,1)S(1)}, bf16[512,256]{1,0:T(8,128)(2,1)S(1)}, u32[]{:S(2)}, u32[]{:S(2)}) collective-permute-start(bf16[512,256]{1,0:T(8,128)(2,1)S(1)} %get-tuple-element.91.refs_1_), channel_id=1, source_target_pairs={{2,0},{3,1},{10,8},{11,9},{12,10},{13,11},{18,16},{19,17},{20,18},... | collective-permute-start | bytes 786440 | tf_op jit(solution)/shard_map/ppermute | solution.py:373
  47.1 13.9 %collective-permute-start.9 = (bf16[512,256]{1,0:T(8,128)(2,1)S(1)}, bf16[512,256]{1,0:T(8,128)(2,1)S(1)}, u32[]{:S(2)}, u32[]{:S(2)}) collective-permute-start(bf16[512,256]{1,0:T(8,128)(2,1)S(1)} %collective-permute-done.4.refs_6_.refs_2_), channel_id=1, source_target_pairs={{2,0},{3,1},{10,8},{11,9},{18,16},{19,17},{26,24},{27,25},{28,30},... | collective-permute-start | bytes 786440 | tf_op jit(solution)/shard_map/ppermute | solution.py:373
  61.6 7.3 %collective-permute-start.11 = (bf16[2048,256]{1,0:T(8,128)(2,1)S(1)}, bf16[2048,256]{1,0:T(8,128)(2,1)S(1)}, u32[]{:S(2)}, u32[]{:S(2)}) collective-permute-start(bf16[2048,256]{1,0:T(8,128)(2,1)S(1)} %line.3.refs_1_.refs_3_), channel_id=1, source_target_pairs={{0,1},{1,0},{8,9},{9,8},{10,11},{11,10},{16,17},{17,16},{18,19},{1... | collective-permute-start | bytes 3145736 | tf_op jit(solution)/shard_map/ppermute | solution.py:373
  65.4 18.3 %collective-permute-start.10 = (bf16[2112,256]{1,0:T(8,128)(2,1)S(1)}, bf16[2112,256]{1,0:T(8,128)(2,1)S(1)}, u32[]{:S(2)}, u32[]{:S(2)}) collective-permute-start(bf16[2112,256]{1,0:T(8,128)(2,1)S(1)} %get-tuple-element.57), channel_id=1, source_target_pairs={{16,0},{24,8},{9,1},{25,17},{26,10},{18,2},{19,27},{29,21}} | collective-permute-start | bytes 3244040 | tf_op jit(solution)/shard_map/ppermute | solution.py:373
  66.9 19.6 %collective-permute-start.12 = (bf16[2048,256]{1,0:T(8,128)(2,1)S(1)}, bf16[2048,256]{1,0:T(8,128)(2,1)S(1)}, u32[]{:S(2)}, u32[]{:S(2)}) collective-permute-start(bf16[2048,256]{1,0:T(8,128)(2,1)S(1)} %half.2.refs_5_.refs_2_), channel_id=1, source_target_pairs={{0,16},{1,9},{10,26},{21,29}} | collective-permute-start | bytes 3145736 | tf_op jit(solution)/shard_map/ppermute | solution.py:373
  67.7 18.9 %collective-permute-start.13 = (bf16[2048,256]{1,0:T(8,128)(2,1)S(1)}, bf16[2048,256]{1,0:T(8,128)(2,1)S(1)}, u32[]{:S(2)}, u32[]{:S(2)}) collective-permute-start(bf16[2048,256]{1,0:T(8,128)(2,1)S(1)} %collective-permute-done.6.refs_3_), channel_id=1, source_target_pairs={{8,24},{17,25},{2,18},{27,19}} | collective-permute-start | bytes 3145736 | tf_op jit(solution)/shard_map/ppermute | solution.py:373
  69.6 17.7 %collective-permute-start.14 = (bf16[2048,256]{1,0:T(8,128)(2,1)S(1)}, bf16[2048,256]{1,0:T(8,128)(2,1)S(1)}, u32[]{:S(2)}, u32[]{:S(2)}) collective-permute-start(bf16[2048,256]{1,0:T(8,128)(2,1)S(1)} %half.3.refs_5_.refs_2_), channel_id=1, source_target_pairs={{0,8},{1,17},{10,2},{11,27},{20,28}} | collective-permute-start | bytes 3145736 | tf_op jit(solution)/shard_map/ppermute | solution.py:373
  79.0 21.9 %collective-permute-start.18 = (bf16[2112,256]{1,0:T(8,128)(2,1)S(1)}, bf16[2112,256]{1,0:T(8,128)(2,1)S(1)}, u32[]{:S(2)}, u32[]{:S(2)}) collective-permute-start(bf16[2112,256]{1,0:T(8,128)(2,1)S(1)} %get-tuple-element.61.refs_3_), channel_id=1, source_target_pairs={{16,0},{24,8},{9,1},{25,17},{26,10},{18,2},{19,27},{29,21}} | collective-permute-start | bytes 3244040 | tf_op jit(solution)/shard_map/ppermute | solution.py:373
  86.6 15.7 %collective-permute-start.17 = (bf16[2112,256]{1,0:T(8,128)(2,1)S(1)}, bf16[2112,256]{1,0:T(8,128)(2,1)S(1)}, u32[]{:S(2)}, u32[]{:S(2)}) collective-permute-start(bf16[2112,256]{1,0:T(8,128)(2,1)S(1)} %get-tuple-element.65.refs_6_), channel_id=1, source_target_pairs={{8,0},{17,1},{2,10},{27,11},{28,20}} | collective-permute-start | bytes 3244040 | tf_op jit(solution)/shard_map/ppermute | solution.py:373
  93.7 11.4 %collective-permute-start.15 = (f32[1024,256]{1,0:T(8,128)S(1)}, f32[1024,256]{1,0:T(8,128)S(1)}, u32[]{:S(2)}, u32[]{:S(2)}) collective-permute-start(f32[1024,256]{1,0:T(8,128)S(1)} %get-tuple-element.67), channel_id=1, source_target_pairs={{0,1},{1,0},{8,9},{9,8},{10,11},{11,10},{16,17},{17,16},{18,19},{1... | collective-permute-start | bytes 3145736 | tf_op jit(solution)/shard_map/ppermute | solution.py:373
  98.3 6.8 %collective-permute-start.16 = (f32[1024,256]{1,0:T(8,128)S(1)}, f32[1024,256]{1,0:T(8,128)S(1)}, u32[]{:S(2)}, u32[]{:S(2)}) collective-permute-start(f32[1024,256]{1,0:T(8,128)S(1)} %get-tuple-element.68), channel_id=1, source_target_pairs={{0,1},{1,0},{8,9},{9,8},{10,11},{11,10},{16,17},{17,16},{18,19},{1... | collective-permute-start | bytes 3145736 | tf_op jit(solution)/shard_map/ppermute | solution.py:373
  100.2 18.3 %collective-permute-start.19 = (bf16[2048,256]{1,0:T(8,128)(2,1)S(1)}, bf16[2048,256]{1,0:T(8,128)(2,1)S(1)}, u32[]{:S(2)}, u32[]{:S(2)}) collective-permute-start(bf16[2048,256]{1,0:T(8,128)(2,1)S(1)} %half.3.refs_5_.refs_2_), channel_id=1, source_target_pairs={{0,16},{1,9},{10,26},{21,29}} | collective-permute-start | bytes 3145736 | tf_op jit(solution)/shard_map/ppermute | solution.py:373
  100.9 20.3 %collective-permute-start.20 = (bf16[2048,256]{1,0:T(8,128)(2,1)S(1)}, bf16[2048,256]{1,0:T(8,128)(2,1)S(1)}, u32[]{:S(2)}, u32[]{:S(2)}) collective-permute-start(bf16[2048,256]{1,0:T(8,128)(2,1)S(1)} %collective-permute-done.14.refs_7_.refs_3_), channel_id=1, source_target_pairs={{8,24},{17,25},{2,18},{27,19}} | collective-permute-start | bytes 3145736 | tf_op jit(solution)/shard_map/ppermute | solution.py:373
  107.3 17.4 %collective-permute-start.21 = (bf16[528,256]{1,0:T(8,128)(2,1)S(1)}, bf16[528,256]{1,0:T(8,128)(2,1)S(1)}, u32[]{:S(2)}, u32[]{:S(2)}) collective-permute-start(bf16[528,256]{1,0:T(8,128)(2,1)S(1)} %get-tuple-element.77), channel_id=1, source_target_pairs={{1,4},{9,12},{10,9},{11,13},{17,20},{18,17},{19,21},{20,18},{21,22... | collective-permute-start | bytes 811016 | tf_op jit(solution)/shard_map/ppermute | solution.py:373
  117.8 19.1 %collective-permute-start.25 = (bf16[2112,256]{1,0:T(8,128)(2,1)S(1)}, bf16[2112,256]{1,0:T(8,128)(2,1)S(1)}, u32[]{:S(2)}, u32[]{:S(2)}) collective-permute-start(bf16[2112,256]{1,0:T(8,128)(2,1)S(1)} %get-tuple-element.71.refs_6_), channel_id=1, source_target_pairs={{8,0},{17,1},{2,10},{27,11},{28,20}} | collective-permute-start | bytes 3244040 | tf_op jit(solution)/shard_map/ppermute | solution.py:373
  124.7 17.5 %collective-permute-start.26 = (f32[1024,256]{1,0:T(8,128)S(1)}, f32[1024,256]{1,0:T(8,128)S(1)}, u32[]{:S(2)}, u32[]{:S(2)}) collective-permute-start(f32[1024,256]{1,0:T(8,128)S(1)} %get-tuple-element.83), channel_id=1, source_target_pairs={{0,1},{1,0},{8,9},{9,8},{10,11},{11,10},{16,17},{17,16},{18,19},{1... | collective-permute-start | bytes 3145736 | tf_op jit(solution)/shard_map/ppermute | solution.py:373
  127.2 15.0 %collective-permute-start.27 = (f32[1024,256]{1,0:T(8,128)S(1)}, f32[1024,256]{1,0:T(8,128)S(1)}, u32[]{:S(2)}, u32[]{:S(2)}) collective-permute-start(f32[1024,256]{1,0:T(8,128)S(1)} %get-tuple-element.84), channel_id=1, source_target_pairs={{0,1},{1,0},{8,9},{9,8},{10,11},{11,10},{16,17},{17,16},{18,19},{1... | collective-permute-start | bytes 3145736 | tf_op jit(solution)/shard_map/ppermute | solution.py:373
  129.1 22.1 %collective-permute-start.22 = (bf16[528,256]{1,0:T(8,128)(2,1)S(1)}, bf16[528,256]{1,0:T(8,128)(2,1)S(1)}, u32[]{:S(2)}, u32[]{:S(2)}) collective-permute-start(bf16[528,256]{1,0:T(8,128)(2,1)S(1)} %get-tuple-element.79), channel_id=1, source_target_pairs={{0,1},{1,5},{8,9},{9,13},{11,14},{16,17},{17,21},{19,22},{20,19},{... | collective-permute-start | bytes 811016 | tf_op jit(solution)/shard_map/ppermute | solution.py:373
  133.2 19.9 %collective-permute-start.23 = (bf16[528,256]{1,0:T(8,128)(2,1)S(1)}, bf16[528,256]{1,0:T(8,128)(2,1)S(1)}, u32[]{:S(2)}, u32[]{:S(2)}) collective-permute-start(bf16[528,256]{1,0:T(8,128)(2,1)S(1)} %get-tuple-element.80), channel_id=1, source_target_pairs={{0,2},{1,6},{8,10},{9,14},{10,11},{11,15},{16,18},{17,22},{18,19},... | collective-permute-start | bytes 811016 | tf_op jit(solution)/shard_map/ppermute | solution.py:373
  136.9 20.7 %collective-permute-start.24 = (bf16[528,256]{1,0:T(8,128)(2,1)S(1)}, bf16[528,256]{1,0:T(8,128)(2,1)S(1)}, u32[]{:S(2)}, u32[]{:S(2)}) collective-permute-start(bf16[528,256]{1,0:T(8,128)(2,1)S(1)} %get-tuple-element.81), channel_id=1, source_target_pairs={{0,3},{1,7},{8,11},{9,15},{10,8},{11,12},{16,19},{17,23},{18,16},{... | collective-permute-start | bytes 811016 | tf_op jit(solution)/shard_map/ppermute | solution.py:373
  144.2 14.8 %collective-permute-start.28 = (bf16[528,256]{1,0:T(8,128)(2,1)S(1)}, bf16[528,256]{1,0:T(8,128)(2,1)S(1)}, u32[]{:S(2)}, u32[]{:S(2)}) collective-permute-start(bf16[528,256]{1,0:T(8,128)(2,1)S(1)} %get-tuple-element.87), channel_id=1, source_target_pairs={{1,4},{9,12},{10,9},{11,13},{17,20},{18,17},{19,21},{20,18},{21,22... | collective-permute-start | bytes 811016 | tf_op jit(solution)/shard_map/ppermute | solution.py:373
  148.8 10.3 %collective-permute-start.29 = (bf16[528,256]{1,0:T(8,128)(2,1)S(1)}, bf16[528,256]{1,0:T(8,128)(2,1)S(1)}, u32[]{:S(2)}, u32[]{:S(2)}) collective-permute-start(bf16[528,256]{1,0:T(8,128)(2,1)S(1)} %get-tuple-element.88), channel_id=1, source_target_pairs={{0,1},{1,5},{8,9},{9,13},{11,14},{16,17},{17,21},{19,22},{20,19},{... | collective-permute-start | bytes 811016 | tf_op jit(solution)/shard_map/ppermute | solution.py:373
  151.2 13.6 %collective-permute-start.30 = (bf16[528,256]{1,0:T(8,128)(2,1)S(1)}, bf16[528,256]{1,0:T(8,128)(2,1)S(1)}, u32[]{:S(2)}, u32[]{:S(2)}) collective-permute-start(bf16[528,256]{1,0:T(8,128)(2,1)S(1)} %get-tuple-element.89), channel_id=1, source_target_pairs={{0,2},{1,6},{8,10},{9,14},{10,11},{11,15},{16,18},{17,22},{18,19},... | collective-permute-start | bytes 811016 | tf_op jit(solution)/shard_map/ppermute | solution.py:373
  153.1 22.5 %collective-permute-start.31 = (bf16[528,256]{1,0:T(8,128)(2,1)S(1)}, bf16[528,256]{1,0:T(8,128)(2,1)S(1)}, u32[]{:S(2)}, u32[]{:S(2)}) collective-permute-start(bf16[528,256]{1,0:T(8,128)(2,1)S(1)} %get-tuple-element.90), channel_id=1, source_target_pairs={{0,3},{1,7},{8,11},{9,15},{10,8},{11,12},{16,19},{17,23},{18,16},{... | collective-permute-start | bytes 811016 | tf_op jit(solution)/shard_map/ppermute | solution.py:373
  (1 other events, 5.8 us)

commit v3 on v2

--- a/solution.py
+++ b/solution.py
@@ -127,30 +127,35 @@
     return local(functools.partial(line_kernel, places), out_shape, "line", ids, *came, after=after)
 
 
-def half_kernel(height, ids, mine, other, out_ref):
-    count = out_ref.shape[0] // height
+def half_kernel(height, ids, mine, other, *outs):
+    rows, width = outs[0].shape
+    count = rows // height
     for at in range(count // 2):
         chip = ids[2] * (count // 2) + at
         here = pl.ds(pl.multiple_of(chip * height, height), height)
         for core, ref in ((ids[2], mine), (1 - ids[2], other)):
-            out_ref[pl.ds(pl.multiple_of((2 * at + core) * height, height), height), :] = ref[here, :]
+            to = pl.ds(pl.multiple_of((2 * at + core) * height, height), height)
+            for part, out_ref in enumerate(outs):
+                out_ref[to, :] = ref[here, pl.ds(part * width, width)]
 
 
 def half(ids, mine, other, height):
-    out_shape = jax.ShapeDtypeStruct(mine.shape, mine.dtype)
+    rows, width = mine.shape
+    out_shape = [jax.ShapeDtypeStruct((rows, width // 2), mine.dtype)] * 2
     return local(functools.partial(half_kernel, height), out_shape, "half", ids, mine, other)
 
 
-def mirrored_kernel(piece, ids, a_ref, diagonal, mine, other, m_ref, msg_ref, turned):
+def mirrored_kernel(piece, part_at, ids, a_ref, diagonal, mine, other, m_ref, msg_ref, turned):
     height, cols = a_ref.shape
     block = cols // 4
     used = ids[1] <= ids[0]
+    these = pl.ds(part_at * m_ref.shape[1], m_ref.shape[1])
 
     @pl.loop(0, height // piece // 2)
     def _(at):
         rows = pl.ds(pl.multiple_of(at * piece, piece), piece)
         for core, ref in ((ids[2], mine), (1 - ids[2], other)):
-            turned[:, pl.ds(pl.multiple_of((2 * at + core) * piece, piece), piece)] = ref[rows, :].T
+            turned[:, pl.ds(pl.multiple_of((2 * at + core) * piece, piece), piece)] = ref[rows, these].T
 
     @pl.loop(0, 4)
     def _(part):
@@ -175,15 +180,15 @@
         put_scale(msg_ref, cols, part, scale)
 
 
-def mirrored_product(ids, matrix, diagonal, mine, other, piece, after):
+def mirrored_product(ids, matrix, diagonal, mine, other, piece, part_at, after):
     rows, cols = matrix.shape
-    width = mine.shape[1]
+    width = mine.shape[1] // 2
     out_shape = [
         jax.ShapeDtypeStruct((cols, width), jnp.float32),
         jax.ShapeDtypeStruct((cols + 4 * TAIL, width), jnp.bfloat16),
     ]
     return local(
-        functools.partial(mirrored_kernel, piece), out_shape, "mirrored_product",
+        functools.partial(mirrored_kernel, piece, part_at), out_shape, "mirrored_product",
         ids, matrix, diagonal, mine, other, after=after,
         scratch_shapes=[pltpu.VMEM((width, rows), jnp.bfloat16)],
     )
@@ -383,7 +388,6 @@
 
     everyone = [(k, c) for k in range(chips) for c in range(2)]
 
-    width = panel_vectors.shape[1] // 2
     active = [(r, k, c) for r in range(count) for k in range(r + 1) for c in range(2)]
 
     def spread(place, source):
@@ -464,34 +468,26 @@
             arrays.append(send(x, pairs))
         return arrays
 
-    block_a, block_b = panel_vectors[:, :width], panel_vectors[:, width:]
     if chips == 4:
-        two_a, two_b = two_away(block_a), two_away(block_b)
-        came_a = [block_a, two_a, *next_ones(block_a)]
-        two_a, matrix = lax.optimization_barrier((two_a, matrix))
-        came_a.append(ends(two_a))
-        mine_a = line(ids, came_a, four, [two_b])
-        came_b, places = [block_b, two_b, *next_ones(block_b), ends(two_b)], four
+        two = two_away(panel_vectors)
+        came, places = [panel_vectors, two, *next_ones(panel_vectors)], four
+        two, matrix = lax.optimization_barrier((two, matrix))
+        came.append(ends(two))
     else:
-        came_a, places = by_distance(block_a)
-        came_b, places = by_distance(block_b)
-        mine_a = line(ids, came_a, places, [])
-    other_a = send(mine_a, swap)
-    panels_a = [half(ids, mine_a, other_a, piece)]
+        came, places = by_distance(panel_vectors)
+    mine = line(ids, came, places, [])
+    other = send(mine, swap)
+    panels_a, panels_b = ([x] for x in half(ids, mine, other, piece))
     panels_a.append(spread(1, panels_a[0]))
-    partial_a, message_a = mirrored_product(ids, matrix, diagonal, mine_a, other_a, piece, [panels_a[0]])
-    message_a, panels_a[1], *came_b[2:] = lax.optimization_barrier((message_a, panels_a[1], *came_b[2:]))
+    partial_a, message_a = mirrored_product(ids, matrix, diagonal, mine, other, piece, 0, [panels_a[0]])
+    message_a, panels_a[1] = lax.optimization_barrier((message_a, panels_a[1]))
     to_a = collect(bits - 1, message_a)
     widen(panels_a, [])
-
-    mine_b = line(ids, came_b, places, [])
-    other_b = send(mine_b, swap)
-    panels_b = [half(ids, mine_b, other_b, piece)]
+    partial_b, message_b = mirrored_product(ids, matrix, diagonal, mine, other, piece, 1, [message_a])
+    to_b = collect(bits - 1, message_b)
     panels_b.append(spread(1, panels_b[0]))
-    partial_b, message_b = mirrored_product(ids, matrix, diagonal, mine_b, other_b, piece, [panels_b[0]])
-    to_b = collect(bits - 1, message_b)
     partial_a, to_a, relayed = relaying(partial_a, to_a, panels_a, [message_b])
-    keep_a, *give_a = direct_product(ids, matrix, panels_a, [relayed, panels_b[1]])
+    keep_a, *give_a = direct_product(ids, matrix, panels_a, [relayed])
     got_a = [send(x, swap) for x in give_a]
     partial_b, to_b, relayed = relaying(partial_b, to_b, [], [keep_a, to_a])
     widen(panels_b, [])

time: 179 us -> 175 us (0.978)
  starting transfers between devices: 84 us -> 69 us
  waiting for transfers between devices: 37.8 us -> 51.2 us
    ppermute x32 -> x27, starting transfers between devices: 84 us -> 69 us  [send(): return lax.ppermute(x, ('row', 'col'), [(at(*s), at(*d)) for s, d in pairs])]
    ppermute x32 -> x27, waiting for transfers between devices: 37.8 us -> 51.2 us  [send(): return lax.ppermute(x, ('row', 'col'), [(at(*s), at(*d)) for s, d in pairs])]
    pallas_call x15 -> x13, Pallas kernels: 47.2 us -> 46.1 us  [local(): pl.pallas_call(body, out_shape=out_shape, in_specs=[pl.BlockSpec(memory_s...]
    unnamed x2 -> x4, local copies, waits for them, and re-layouts: 5.77 us -> 5.77 us
  transfers between devices with their start and end apart: 32 -> 27, of which waited for: 8 -> 8; matrix products, arithmetic and copies ran while one was open for 0% -> 0% of each run, Pallas kernels for 25% -> 25%
where the time goes in v3:
time: 175 us; the launch traced here: 174 us
  starting transfers between devices  69 us (39%)
  waiting for transfers between devices  51.2 us (29%)
  Pallas kernels  47.8 us (27%)
  local copies, waits for them, and re-layouts  5.86 us (3%)
    ppermute x27, starting transfers between devices, send(): return lax.ppermute(x, ('row', 'col'), [(at(*s), at(*d)) for s, d in pairs])  69 us
    ppermute x27, waiting for transfers between devices, send(): return lax.ppermute(x, ('row', 'col'), [(at(*s), at(*d)) for s, d in pairs])  51.2 us
    pallas_call x13, Pallas kernels, local(): pl.pallas_call(body, out_shape=out_shape, in_specs=[pl.BlockSpec(memory_s...  46.1 us
    unnamed x4, local copies, waits for them, and re-layouts  5.77 us
  transfers between devices with their start and end apart: 27, of which 8 were waited for; matrix products, arithmetic and copies ran while one was open for 0% of the time, Pallas kernels for 25%

profile of v3, /device:TPU:7, one launch (start us, length us, event | category | flops | bytes accessed | tf_op | source)
XLA Modules:
  0.0 174.3 jit_solution(14481466545882935585)
XLA Ops:
  0.0 4.2 %collective-permute-start = (bf16[512,512]{1,0:T(8,128)(2,1)}, bf16[512,512]{1,0:T(8,128)(2,1)S(1)}, u32[]{:S(2)}, u32[]{:S(2)}) collective-permute-start(bf16[512,512]{1,0:T(8,128)(2,1)} %refs_1_.1), channel_id=1, source_target_pairs={{4,0},{5,1},{6,2},{7,3},{12,8},{13,9},{14,10},{15,11},{16,20},{17,... | collective-permute-start | bytes 1572872 | tf_op jit(solution)/shard_map/ppermute | solution.py:378
  4.2 3.2 %collective-permute-start.1 = (bf16[512,512]{1,0:T(8,128)(2,1)}, bf16[512,512]{1,0:T(8,128)(2,1)S(1)}, u32[]{:S(2)}, u32[]{:S(2)}) collective-permute-start(bf16[512,512]{1,0:T(8,128)(2,1)} %refs_1_.1), channel_id=1, source_target_pairs={{8,10},{9,11},{16,18},{17,19},{18,20},{19,21},{24,26},{25,27},{26,... | collective-permute-start | bytes 1572872 | tf_op jit(solution)/shard_map/ppermute | solution.py:378
  8.9 5.8 %copy-done = bf16[4096,2048]{1,0:T(8,128)(2,1)S(1)} copy-done((bf16[4096,2048]{1,0:T(8,128)(2,1)S(1)}, bf16[4096,2048]{1,0:T(8,128)(2,1)}, u32[]{:S(2)}) %copy-start) | copy-done | bytes 16777240
  16.4 10.7 %collective-permute-done.refs_2_ = bf16[512,512]{1,0:T(8,128)(2,1)S(1)} collective-permute-done((bf16[512,512]{1,0:T(8,128)(2,1)}, bf16[512,512]{1,0:T(8,128)(2,1)S(1)}, u32[]{:S(2)}, u32[]{:S(2)}) %collective-permute-start) | collective-permute-done | bytes 524320 | tf_op jit(solution)/shard_map/ppermute | solution.py:378
  28.4 3.5 %collective-permute-done.2.refs_4_ = bf16[512,512]{1,0:T(8,128)(2,1)S(1)} collective-permute-done((bf16[512,512]{1,0:T(8,128)(2,1)}, bf16[512,512]{1,0:T(8,128)(2,1)S(1)}, u32[]{:S(2)}, u32[]{:S(2)}) %collective-permute-start.2) | collective-permute-done | bytes 524320 | tf_op jit(solution)/shard_map/ppermute | solution.py:378
  31.9 11.2 %collective-permute-done.3.refs_5_ = bf16[512,512]{1,0:T(8,128)(2,1)S(1)} collective-permute-done((bf16[512,512]{1,0:T(8,128)(2,1)S(1)}, bf16[512,512]{1,0:T(8,128)(2,1)S(1)}, u32[]{:S(2)}, u32[]{:S(2)}) %collective-permute-start.3) | collective-permute-done | bytes 524320 | tf_op jit(solution)/shard_map/ppermute | solution.py:378
  43.8 4.1 %collective-permute-start.4 = (bf16[2048,512]{1,0:T(8,128)(2,1)S(1)}, bf16[2048,512]{1,0:T(8,128)(2,1)S(1)}, u32[]{:S(2)}, u32[]{:S(2)}) collective-permute-start(bf16[2048,512]{1,0:T(8,128)(2,1)S(1)} %line.1.refs_1_.refs_3_), channel_id=1, source_target_pairs={{0,1},{1,0},{8,9},{9,8},{10,11},{11,10},{16,17},{17,16},{18,19},{1... | collective-permute-start | bytes 6291464 | tf_op jit(solution)/shard_map/ppermute | solution.py:378
  47.9 3.8 %collective-permute-done.4.refs_2_.refs_4_ = bf16[2048,512]{1,0:T(8,128)(2,1)S(1)} collective-permute-done((bf16[2048,512]{1,0:T(8,128)(2,1)S(1)}, bf16[2048,512]{1,0:T(8,128)(2,1)S(1)}, u32[]{:S(2)}, u32[]{:S(2)}) %collective-permute-start.4) | collective-permute-done | bytes 2097184 | tf_op jit(solution)/shard_map/ppermute | solution.py:378
  53.1 8.7 %mirrored_product.2 = (f32[2048,256]{1,0:T(8,128)S(1)}, bf16[2112,256]{1,0:T(8,128)(2,1)S(1)}) custom-call(s32[5]{0:T(128)S(1)} %stack.23.ids.refs_0_, bf16[4096,2048]{1,0:T(8,128)(2,1)S(1)} %get-tuple-element.48.refs_1_, f32[8,2048]{1,0:T(8,128)S(1)} %get-tuple-element.51.refs_2_, bf16[2048,512]{1,0:T(8,128)(2,1)S(1)} %line.1.refs_1_.refs_3_, ...), custom_call_target="tpu_custom_call" | custom-call | tf_op jit(solution)/shard_map/mirrored_product/pallas_call | solution.py:48
  61.8 6.4 %collective-permute-start.6 = (bf16[2112,256]{1,0:T(8,128)(2,1)S(1)}, bf16[2112,256]{1,0:T(8,128)(2,1)S(1)}, u32[]{:S(2)}, u32[]{:S(2)}) collective-permute-start(bf16[2112,256]{1,0:T(8,128)(2,1)S(1)} %get-tuple-element.57.refs_5_), channel_id=1, source_target_pairs={{16,0},{24,8},{9,1},{25,17},{26,10},{18,2},{19,27},{29,21}} | collective-permute-start | bytes 3244040 | tf_op jit(solution)/shard_map/ppermute | solution.py:378
  70.2 8.7 %mirrored_product.3 = (f32[2048,256]{1,0:T(8,128)S(1)}, bf16[2112,256]{1,0:T(8,128)(2,1)S(1)}) custom-call(s32[5]{0:T(128)S(1)} %stack.23.ids.refs_0_, bf16[4096,2048]{1,0:T(8,128)(2,1)S(1)} %get-tuple-element.48.refs_1_, f32[8,2048]{1,0:T(8,128)S(1)} %get-tuple-element.51.refs_2_, bf16[2048,512]{1,0:T(8,128)(2,1)S(1)} %line.1.refs_1_.refs_3_, ...), custom_call_target="tpu_custom_call" | custom-call | tf_op jit(solution)/shard_map/mirrored_product/pallas_call | solution.py:48
  79.0 4.1 %collective-permute-start.12 = (bf16[2112,256]{1,0:T(8,128)(2,1)S(1)}, bf16[2112,256]{1,0:T(8,128)(2,1)S(1)}, u32[]{:S(2)}, u32[]{:S(2)}) collective-permute-start(bf16[2112,256]{1,0:T(8,128)(2,1)S(1)} %get-tuple-element.58.refs_3_), channel_id=1, source_target_pairs={{16,0},{24,8},{9,1},{25,17},{26,10},{18,2},{19,27},{29,21}} | collective-permute-start | bytes 3244040 | tf_op jit(solution)/shard_map/ppermute | solution.py:378
  83.8 2.8 %relay.2 = (f32[2048,256]{1,0:T(8,128)S(1)}, bf16[2112,256]{1,0:T(8,128)(2,1)S(1)}) custom-call(s32[5]{0:T(128)S(1)} %stack.23.ids.refs_0_, f32[2048,256]{1,0:T(8,128)S(1)} %get-tuple-element.56.refs_1_, bf16[2112,256]{1,0:T(8,128)(2,1)S(1)} %collective-permute-done.6.refs_2_, bf16[2112,256]{1,0:T(8,128)(2,1)S(1)} %get-tuple-element.58.refs_3_), custom_call_target="tpu_custom_call" | custom-call | tf_op jit(solution)/shard_map/relay/pallas_call | solution.py:48
  87.4 6.4 %direct_product.1 = (f32[2048,256]{1,0:T(8,128)S(1)}, f32[1024,256]{1,0:T(8,128)S(1)}, f32[1024,256]{1,0:T(8,128)S(1)}) custom-call(s32[5]{0:T(128)S(1)} %stack.23.ids.refs_0_, bf16[4096,2048]{1,0:T(8,128)(2,1)S(1)} %get-tuple-element.48.refs_1_, bf16[2048,256]{1,0:T(8,128)(2,1)S(1)} %get-tuple-element.54.refs_5_.refs_2_, ...), custom_call_target="tpu_custom_call" | custom-call | tf_op jit(solution)/shard_map/direct_product/pallas_call | solution.py:48
  93.8 4.2 %collective-permute-start.9 = (f32[1024,256]{1,0:T(8,128)S(1)}, f32[1024,256]{1,0:T(8,128)S(1)}, u32[]{:S(2)}, u32[]{:S(2)}) collective-permute-start(f32[1024,256]{1,0:T(8,128)S(1)} %get-tuple-element.64), channel_id=1, source_target_pairs={{0,1},{1,0},{8,9},{9,8},{10,11},{11,10},{16,17},{17,16},{18,19},{1... | collective-permute-start | bytes 3145736 | tf_op jit(solution)/shard_map/ppermute | solution.py:378
  98.0 1.9 %collective-permute-start.10 = (f32[1024,256]{1,0:T(8,128)S(1)}, f32[1024,256]{1,0:T(8,128)S(1)}, u32[]{:S(2)}, u32[]{:S(2)}) collective-permute-start(f32[1024,256]{1,0:T(8,128)S(1)} %get-tuple-element.65), channel_id=1, source_target_pairs={{0,1},{1,0},{8,9},{9,8},{10,11},{11,10},{16,17},{17,16},{18,19},{1... | collective-permute-start | bytes 3145736 | tf_op jit(solution)/shard_map/ppermute | solution.py:378
  102.0 2.8 %relay.3 = (f32[2048,256]{1,0:T(8,128)S(1)}, bf16[2112,256]{1,0:T(8,128)(2,1)S(1)}) custom-call(s32[5]{0:T(128)S(1)} %stack.23.ids.refs_0_, f32[2048,256]{1,0:T(8,128)S(1)} %get-tuple-element.67.refs_1_, bf16[2112,256]{1,0:T(8,128)(2,1)S(1)} %collective-permute-done.12.refs_2_, f32[2048,256]{1,0:T(8,128)S(1)} %get-tuple-element.63.refs_3_.refs_1_, ...), custom_call_target="tpu_custom_call" | custom-call | tf_op jit(solution)/shard_map/relay/pallas_call | solution.py:48
  104.9 2.2 %pack.2 = (f32[512,256]{1,0:T(8,128)S(1)}, bf16[528,256]{1,0:T(8,128)(2,1)S(1)}, bf16[528,256]{1,0:T(8,128)(2,1)S(1)}, bf16[528,256]{1,0:T(8,128)(2,1)S(1)}, bf16[528,256]{1,0:T(8,128)(2,1)S(1)}) custom-call(s32[5]{0:T(128)S(1)} %stack.23.ids.refs_0_, f32[2048,256]{1,0:T(8,128)S(1)} %get-tuple-element.63.refs_3_.refs_1_, ...), custom_call_target="tpu_custom_call" | custom-call | tf_op jit(solution)/shard_map/pack/pallas_call | solution.py:48
  107.1 3.8 %collective-permute-start.16 = (bf16[528,256]{1,0:T(8,128)(2,1)S(1)}, bf16[528,256]{1,0:T(8,128)(2,1)S(1)}, u32[]{:S(2)}, u32[]{:S(2)}) collective-permute-start(bf16[528,256]{1,0:T(8,128)(2,1)S(1)} %get-tuple-element.75), channel_id=1, source_target_pairs={{1,4},{9,12},{10,9},{11,13},{17,20},{18,17},{19,21},{20,18},{21,22... | collective-permute-start | bytes 811016 | tf_op jit(solution)/shard_map/ppermute | solution.py:378
  111.6 4.9 %collective-permute-done.15.refs_5_ = bf16[2048,256]{1,0:T(8,128)(2,1)S(1)} collective-permute-done((bf16[2048,256]{1,0:T(8,128)(2,1)S(1)}, bf16[2048,256]{1,0:T(8,128)(2,1)S(1)}, u32[]{:S(2)}, u32[]{:S(2)}) %collective-permute-start.15) | collective-permute-done | bytes 1048608 | tf_op jit(solution)/shard_map/ppermute | solution.py:378
  116.5 3.5 %give_product.1 = (f32[1024,256]{1,0:T(8,128)S(1)}, f32[1024,256]{1,0:T(8,128)S(1)}, bf16[2048,256]{1,0:T(8,128)(2,1)S(1)}) custom-call(s32[5]{0:T(128)S(1)} %stack.23.ids.refs_0_, bf16[4096,2048]{1,0:T(8,128)(2,1)S(1)} %get-tuple-element.48.refs_1_, bf16[2048,256]{1,0:T(8,128)(2,1)S(1)} %get-tuple-element.71.refs_2_, ...), custom_call_target="tpu_custom_call" | custom-call | tf_op jit(solution)/shard_map/give_product/pallas_call | solution.py:48
  120.1 4.4 %collective-permute-start.21 = (f32[1024,256]{1,0:T(8,128)S(1)}, f32[1024,256]{1,0:T(8,128)S(1)}, u32[]{:S(2)}, u32[]{:S(2)}) collective-permute-start(f32[1024,256]{1,0:T(8,128)S(1)} %get-tuple-element.81), channel_id=1, source_target_pairs={{0,1},{1,0},{8,9},{9,8},{10,11},{11,10},{16,17},{17,16},{18,19},{1... | collective-permute-start | bytes 3145736 | tf_op jit(solution)/shard_map/ppermute | solution.py:378
  124.5 1.9 %collective-permute-start.22 = (f32[1024,256]{1,0:T(8,128)S(1)}, f32[1024,256]{1,0:T(8,128)S(1)}, u32[]{:S(2)}, u32[]{:S(2)}) collective-permute-start(f32[1024,256]{1,0:T(8,128)S(1)} %get-tuple-element.82), channel_id=1, source_target_pairs={{0,1},{1,0},{8,9},{9,8},{10,11},{11,10},{16,17},{17,16},{18,19},{1... | collective-permute-start | bytes 3145736 | tf_op jit(solution)/shard_map/ppermute | solution.py:378
  128.4 5.8 %collective-permute-start.18 = (bf16[528,256]{1,0:T(8,128)(2,1)S(1)}, bf16[528,256]{1,0:T(8,128)(2,1)S(1)}, u32[]{:S(2)}, u32[]{:S(2)}) collective-permute-start(bf16[528,256]{1,0:T(8,128)(2,1)S(1)} %get-tuple-element.78), channel_id=1, source_target_pairs={{0,2},{1,6},{8,10},{9,14},{10,11},{11,15},{16,18},{17,22},{18,19},... | collective-permute-start | bytes 811016 | tf_op jit(solution)/shard_map/ppermute | solution.py:378
  136.2 3.4 %keep_product.1.refs_1_ = f32[2048,256]{1,0:T(8,128)S(1)} custom-call(s32[5]{0:T(128)S(1)} %stack.23.ids.refs_0_, bf16[4096,2048]{1,0:T(8,128)(2,1)S(1)} %get-tuple-element.48.refs_1_, bf16[2048,256]{1,0:T(8,128)(2,1)S(1)} %get-tuple-element.80.refs_2_, bf16[2112,256]{1,0:T(8,128)(2,1)S(1)} %collective-permute-done.20.refs_3_.refs_5_), custom_call_target="tpu_custom_call" | custom-call | tf_op jit(solution)/shard_map/keep_product/pallas_call | solution.py:48
  139.6 2.0 %pack.3 = (f32[512,256]{1,0:T(8,128)S(1)}, bf16[528,256]{1,0:T(8,128)(2,1)S(1)}, bf16[528,256]{1,0:T(8,128)(2,1)S(1)}, bf16[528,256]{1,0:T(8,128)(2,1)S(1)}, bf16[528,256]{1,0:T(8,128)(2,1)S(1)}) custom-call(s32[5]{0:T(128)S(1)} %stack.23.ids.refs_0_, f32[2048,256]{1,0:T(8,128)S(1)} %keep_product.1.refs_1_, f32[1024,256]{1,0:T(8,128)S(1)} %collective-permute-done.21.refs_2_, ...), custom_call_target="tpu_custom_call" | custom-call | tf_op jit(solution)/shard_map/pack/pallas_call | solution.py:48
  141.6 4.5 %collective-permute-start.23 = (bf16[528,256]{1,0:T(8,128)(2,1)S(1)}, bf16[528,256]{1,0:T(8,128)(2,1)S(1)}, u32[]{:S(2)}, u32[]{:S(2)}) collective-permute-start(bf16[528,256]{1,0:T(8,128)(2,1)S(1)} %get-tuple-element.85), channel_id=1, source_target_pairs={{1,4},{9,12},{10,9},{11,13},{17,20},{18,17},{19,21},{20,18},{21,22... | collective-permute-start | bytes 811016 | tf_op jit(solution)/shard_map/ppermute | solution.py:378
  146.1 1.9 %collective-permute-start.24 = (bf16[528,256]{1,0:T(8,128)(2,1)S(1)}, bf16[528,256]{1,0:T(8,128)(2,1)S(1)}, u32[]{:S(2)}, u32[]{:S(2)}) collective-permute-start(bf16[528,256]{1,0:T(8,128)(2,1)S(1)} %get-tuple-element.86), channel_id=1, source_target_pairs={{0,1},{1,5},{8,9},{9,13},{11,14},{16,17},{17,21},{19,22},{20,19},{... | collective-permute-start | bytes 811016 | tf_op jit(solution)/shard_map/ppermute | solution.py:378
  150.0 3.1 %collective-permute-start.26 = (bf16[528,256]{1,0:T(8,128)(2,1)S(1)}, bf16[528,256]{1,0:T(8,128)(2,1)S(1)}, u32[]{:S(2)}, u32[]{:S(2)}) collective-permute-start(bf16[528,256]{1,0:T(8,128)(2,1)S(1)} %get-tuple-element.88), channel_id=1, source_target_pairs={{0,3},{1,7},{8,11},{9,15},{10,8},{11,12},{16,19},{17,23},{18,16},{... | collective-permute-start | bytes 811016 | tf_op jit(solution)/shard_map/ppermute | solution.py:378
  156.3 4.4 %collective-permute-done.25.refs_5_ = bf16[528,256]{1,0:T(8,128)(2,1)S(1)} collective-permute-done((bf16[528,256]{1,0:T(8,128)(2,1)S(1)}, bf16[528,256]{1,0:T(8,128)(2,1)S(1)}, u32[]{:S(2)}, u32[]{:S(2)}) %collective-permute-start.25) | collective-permute-done | bytes 270368 | tf_op jit(solution)/shard_map/ppermute | solution.py:378
  160.6 11.1 %collective-permute-done.26.refs_6_ = bf16[528,256]{1,0:T(8,128)(2,1)S(1)} collective-permute-done((bf16[528,256]{1,0:T(8,128)(2,1)S(1)}, bf16[528,256]{1,0:T(8,128)(2,1)S(1)}, u32[]{:S(2)}, u32[]{:S(2)}) %collective-permute-start.26) | collective-permute-done | bytes 270368 | tf_op jit(solution)/shard_map/ppermute | solution.py:378
  171.8 2.6 %finish.3 = f32[512,512]{1,0:T(8,128)} custom-call(s32[5]{0:T(128)S(1)} %stack.23.ids.refs_0_, f32[512,256]{1,0:T(8,128)S(1)} %finish.2.refs_1_, f32[512,256]{1,0:T(8,128)S(1)} %get-tuple-element.84.refs_7_.refs_2_, bf16[528,256]{1,0:T(8,128)(2,1)S(1)} %collective-permute-done.23.refs_3_, bf16[528,256]{1,0:T(8,128)(2,1)S(1)} %collective-permute-done.24.refs_4_, ...), custom_call_target="tpu_custom_call" | custom-call | tf_op jit(solution)/shard_map/finish/pallas_call | solution.py:48
  (41 shorter events, 21.7 us)
Async XLA Ops:
  0.0 27.1 %collective-permute-start = (bf16[512,512]{1,0:T(8,128)(2,1)}, bf16[512,512]{1,0:T(8,128)(2,1)S(1)}, u32[]{:S(2)}, u32[]{:S(2)}) collective-permute-start(bf16[512,512]{1,0:T(8,128)(2,1)} %refs_1_.1), channel_id=1, source_target_pairs={{4,0},{5,1},{6,2},{7,3},{12,8},{13,9},{14,10},{15,11},{16,20},{17,... | collective-permute-start | bytes 1572872 | tf_op jit(solution)/shard_map/ppermute | solution.py:378
  4.2 24.2 %collective-permute-start.1 = (bf16[512,512]{1,0:T(8,128)(2,1)}, bf16[512,512]{1,0:T(8,128)(2,1)S(1)}, u32[]{:S(2)}, u32[]{:S(2)}) collective-permute-start(bf16[512,512]{1,0:T(8,128)(2,1)} %refs_1_.1), channel_id=1, source_target_pairs={{8,10},{9,11},{16,18},{17,19},{18,20},{19,21},{24,26},{25,27},{26,... | collective-permute-start | bytes 1572872 | tf_op jit(solution)/shard_map/ppermute | solution.py:378
  7.5 24.4 %collective-permute-start.2 = (bf16[512,512]{1,0:T(8,128)(2,1)}, bf16[512,512]{1,0:T(8,128)(2,1)S(1)}, u32[]{:S(2)}, u32[]{:S(2)}) collective-permute-start(bf16[512,512]{1,0:T(8,128)(2,1)} %refs_1_.1), channel_id=1, source_target_pairs={{2,0},{3,1},{10,8},{11,9},{12,10},{13,11},{18,16},{19,17},{20,18},... | collective-permute-start | bytes 1572872 | tf_op jit(solution)/shard_map/ppermute | solution.py:378
  8.9 5.8 %copy-start = (bf16[4096,2048]{1,0:T(8,128)(2,1)S(1)}, bf16[4096,2048]{1,0:T(8,128)(2,1)}, u32[]{:S(2)}) copy-start(bf16[4096,2048]{1,0:T(8,128)(2,1)} %a_ref.1) | copy-start | bytes 50331652
  14.6 28.5 %copy-start.1 = (bf16[512,512]{1,0:T(8,128)(2,1)S(1)}, bf16[512,512]{1,0:T(8,128)(2,1)}, u32[]{:S(2)}) copy-start(bf16[512,512]{1,0:T(8,128)(2,1)} %refs_1_.1) | copy-start | bytes 1572868
  27.1 16.0 %collective-permute-start.3 = (bf16[512,512]{1,0:T(8,128)(2,1)S(1)}, bf16[512,512]{1,0:T(8,128)(2,1)S(1)}, u32[]{:S(2)}, u32[]{:S(2)}) collective-permute-start(bf16[512,512]{1,0:T(8,128)(2,1)S(1)} %collective-permute-done.refs_2_), channel_id=1, source_target_pairs={{2,0},{3,1},{10,8},{11,9},{18,16},{19,17},{26,24},{27,25},{28,30},... | collective-permute-start | bytes 1572872 | tf_op jit(solution)/shard_map/ppermute | solution.py:378
  43.8 7.8 %collective-permute-start.4 = (bf16[2048,512]{1,0:T(8,128)(2,1)S(1)}, bf16[2048,512]{1,0:T(8,128)(2,1)S(1)}, u32[]{:S(2)}, u32[]{:S(2)}) collective-permute-start(bf16[2048,512]{1,0:T(8,128)(2,1)S(1)} %line.1.refs_1_.refs_3_), channel_id=1, source_target_pairs={{0,1},{1,0},{8,9},{9,8},{10,11},{11,10},{16,17},{17,16},{18,19},{1... | collective-permute-start | bytes 6291464 | tf_op jit(solution)/shard_map/ppermute | solution.py:378
  52.4 9.4 %collective-permute-start.5 = (bf16[2048,256]{1,0:T(8,128)(2,1)S(1)}, bf16[2048,256]{1,0:T(8,128)(2,1)S(1)}, u32[]{:S(2)}, u32[]{:S(2)}) collective-permute-start(bf16[2048,256]{1,0:T(8,128)(2,1)S(1)} %get-tuple-element.54.refs_5_.refs_2_), channel_id=1, source_target_pairs={{0,8},{1,17},{10,2},{11,27},{20,28}} | collective-permute-start | bytes 3145736 | tf_op jit(solution)/shard_map/ppermute | solution.py:378
  61.8 22.0 %collective-permute-start.6 = (bf16[2112,256]{1,0:T(8,128)(2,1)S(1)}, bf16[2112,256]{1,0:T(8,128)(2,1)S(1)}, u32[]{:S(2)}, u32[]{:S(2)}) collective-permute-start(bf16[2112,256]{1,0:T(8,128)(2,1)S(1)} %get-tuple-element.57.refs_5_), channel_id=1, source_target_pairs={{16,0},{24,8},{9,1},{25,17},{26,10},{18,2},{19,27},{29,21}} | collective-permute-start | bytes 3244040 | tf_op jit(solution)/shard_map/ppermute | solution.py:378
  68.2 18.4 %collective-permute-start.7 = (bf16[2048,256]{1,0:T(8,128)(2,1)S(1)}, bf16[2048,256]{1,0:T(8,128)(2,1)S(1)}, u32[]{:S(2)}, u32[]{:S(2)}) collective-permute-start(bf16[2048,256]{1,0:T(8,128)(2,1)S(1)} %get-tuple-element.54.refs_5_.refs_2_), channel_id=1, source_target_pairs={{0,16},{1,9},{10,26},{21,29}} | collective-permute-start | bytes 3145736 | tf_op jit(solution)/shard_map/ppermute | solution.py:378
  68.9 17.7 %collective-permute-start.8 = (bf16[2048,256]{1,0:T(8,128)(2,1)S(1)}, bf16[2048,256]{1,0:T(8,128)(2,1)S(1)}, u32[]{:S(2)}, u32[]{:S(2)}) collective-permute-start(bf16[2048,256]{1,0:T(8,128)(2,1)S(1)} %collective-permute-done.5.refs_3_), channel_id=1, source_target_pairs={{8,24},{17,25},{2,18},{27,19}} | collective-permute-start | bytes 3145736 | tf_op jit(solution)/shard_map/ppermute | solution.py:378
  79.0 21.7 %collective-permute-start.12 = (bf16[2112,256]{1,0:T(8,128)(2,1)S(1)}, bf16[2112,256]{1,0:T(8,128)(2,1)S(1)}, u32[]{:S(2)}, u32[]{:S(2)}) collective-permute-start(bf16[2112,256]{1,0:T(8,128)(2,1)S(1)} %get-tuple-element.58.refs_3_), channel_id=1, source_target_pairs={{16,0},{24,8},{9,1},{25,17},{26,10},{18,2},{19,27},{29,21}} | collective-permute-start | bytes 3244040 | tf_op jit(solution)/shard_map/ppermute | solution.py:378
  83.1 16.9 %collective-permute-start.13 = (bf16[2048,256]{1,0:T(8,128)(2,1)S(1)}, bf16[2048,256]{1,0:T(8,128)(2,1)S(1)}, u32[]{:S(2)}, u32[]{:S(2)}) collective-permute-start(bf16[2048,256]{1,0:T(8,128)(2,1)S(1)} %get-tuple-element.71.refs_2_), channel_id=1, source_target_pairs={{0,8},{1,17},{10,2},{11,27},{20,28}} | collective-permute-start | bytes 3145736 | tf_op jit(solution)/shard_map/ppermute | solution.py:378
  86.7 15.3 %collective-permute-start.11 = (bf16[2112,256]{1,0:T(8,128)(2,1)S(1)}, bf16[2112,256]{1,0:T(8,128)(2,1)S(1)}, u32[]{:S(2)}, u32[]{:S(2)}) collective-permute-start(bf16[2112,256]{1,0:T(8,128)(2,1)S(1)} %get-tuple-element.62.refs_6_), channel_id=1, source_target_pairs={{8,0},{17,1},{2,10},{27,11},{28,20}} | collective-permute-start | bytes 3244040 | tf_op jit(solution)/shard_map/ppermute | solution.py:378
  93.8 11.0 %collective-permute-start.9 = (f32[1024,256]{1,0:T(8,128)S(1)}, f32[1024,256]{1,0:T(8,128)S(1)}, u32[]{:S(2)}, u32[]{:S(2)}) collective-permute-start(f32[1024,256]{1,0:T(8,128)S(1)} %get-tuple-element.64), channel_id=1, source_target_pairs={{0,1},{1,0},{8,9},{9,8},{10,11},{11,10},{16,17},{17,16},{18,19},{1... | collective-permute-start | bytes 3145736 | tf_op jit(solution)/shard_map/ppermute | solution.py:378
  98.0 6.8 %collective-permute-start.10 = (f32[1024,256]{1,0:T(8,128)S(1)}, f32[1024,256]{1,0:T(8,128)S(1)}, u32[]{:S(2)}, u32[]{:S(2)}) collective-permute-start(f32[1024,256]{1,0:T(8,128)S(1)} %get-tuple-element.65), channel_id=1, source_target_pairs={{0,1},{1,0},{8,9},{9,8},{10,11},{11,10},{16,17},{17,16},{18,19},{1... | collective-permute-start | bytes 3145736 | tf_op jit(solution)/shard_map/ppermute | solution.py:378
  100.0 11.7 %collective-permute-start.14 = (bf16[2048,256]{1,0:T(8,128)(2,1)S(1)}, bf16[2048,256]{1,0:T(8,128)(2,1)S(1)}, u32[]{:S(2)}, u32[]{:S(2)}) collective-permute-start(bf16[2048,256]{1,0:T(8,128)(2,1)S(1)} %get-tuple-element.71.refs_2_), channel_id=1, source_target_pairs={{0,16},{1,9},{10,26},{21,29}} | collective-permute-start | bytes 3145736 | tf_op jit(solution)/shard_map/ppermute | solution.py:378
  100.7 15.8 %collective-permute-start.15 = (bf16[2048,256]{1,0:T(8,128)(2,1)S(1)}, bf16[2048,256]{1,0:T(8,128)(2,1)S(1)}, u32[]{:S(2)}, u32[]{:S(2)}) collective-permute-start(bf16[2048,256]{1,0:T(8,128)(2,1)S(1)} %collective-permute-done.13.refs_3_), channel_id=1, source_target_pairs={{8,24},{17,25},{2,18},{27,19}} | collective-permute-start | bytes 3145736 | tf_op jit(solution)/shard_map/ppermute | solution.py:378
  107.1 13.0 %collective-permute-start.16 = (bf16[528,256]{1,0:T(8,128)(2,1)S(1)}, bf16[528,256]{1,0:T(8,128)(2,1)S(1)}, u32[]{:S(2)}, u32[]{:S(2)}) collective-permute-start(bf16[528,256]{1,0:T(8,128)(2,1)S(1)} %get-tuple-element.75), channel_id=1, source_target_pairs={{1,4},{9,12},{10,9},{11,13},{17,20},{18,17},{19,21},{20,18},{21,22... | collective-permute-start | bytes 811016 | tf_op jit(solution)/shard_map/ppermute | solution.py:378
  110.9 23.3 %collective-permute-start.20 = (bf16[2112,256]{1,0:T(8,128)(2,1)S(1)}, bf16[2112,256]{1,0:T(8,128)(2,1)S(1)}, u32[]{:S(2)}, u32[]{:S(2)}) collective-permute-start(bf16[2112,256]{1,0:T(8,128)(2,1)S(1)} %get-tuple-element.68.refs_6_), channel_id=1, source_target_pairs={{8,0},{17,1},{2,10},{27,11},{28,20}} | collective-permute-start | bytes 3244040 | tf_op jit(solution)/shard_map/ppermute | solution.py:378
  120.1 19.5 %collective-permute-start.21 = (f32[1024,256]{1,0:T(8,128)S(1)}, f32[1024,256]{1,0:T(8,128)S(1)}, u32[]{:S(2)}, u32[]{:S(2)}) collective-permute-start(f32[1024,256]{1,0:T(8,128)S(1)} %get-tuple-element.81), channel_id=1, source_target_pairs={{0,1},{1,0},{8,9},{9,8},{10,11},{11,10},{16,17},{17,16},{18,19},{1... | collective-permute-start | bytes 3145736 | tf_op jit(solution)/shard_map/ppermute | solution.py:378
  124.5 15.0 %collective-permute-start.22 = (f32[1024,256]{1,0:T(8,128)S(1)}, f32[1024,256]{1,0:T(8,128)S(1)}, u32[]{:S(2)}, u32[]{:S(2)}) collective-permute-start(f32[1024,256]{1,0:T(8,128)S(1)} %get-tuple-element.82), channel_id=1, source_target_pairs={{0,1},{1,0},{8,9},{9,8},{10,11},{11,10},{16,17},{17,16},{18,19},{1... | collective-permute-start | bytes 3145736 | tf_op jit(solution)/shard_map/ppermute | solution.py:378
  126.5 21.6 %collective-permute-start.17 = (bf16[528,256]{1,0:T(8,128)(2,1)S(1)}, bf16[528,256]{1,0:T(8,128)(2,1)S(1)}, u32[]{:S(2)}, u32[]{:S(2)}) collective-permute-start(bf16[528,256]{1,0:T(8,128)(2,1)S(1)} %get-tuple-element.77), channel_id=1, source_target_pairs={{0,1},{1,5},{8,9},{9,13},{11,14},{16,17},{17,21},{19,22},{20,19},{... | collective-permute-start | bytes 811016 | tf_op jit(solution)/shard_map/ppermute | solution.py:378
  128.4 21.6 %collective-permute-start.18 = (bf16[528,256]{1,0:T(8,128)(2,1)S(1)}, bf16[528,256]{1,0:T(8,128)(2,1)S(1)}, u32[]{:S(2)}, u32[]{:S(2)}) collective-permute-start(bf16[528,256]{1,0:T(8,128)(2,1)S(1)} %get-tuple-element.78), channel_id=1, source_target_pairs={{0,2},{1,6},{8,10},{9,14},{10,11},{11,15},{16,18},{17,22},{18,19},... | collective-permute-start | bytes 811016 | tf_op jit(solution)/shard_map/ppermute | solution.py:378
  134.2 20.4 %collective-permute-start.19 = (bf16[528,256]{1,0:T(8,128)(2,1)S(1)}, bf16[528,256]{1,0:T(8,128)(2,1)S(1)}, u32[]{:S(2)}, u32[]{:S(2)}) collective-permute-start(bf16[528,256]{1,0:T(8,128)(2,1)S(1)} %get-tuple-element.79), channel_id=1, source_target_pairs={{0,3},{1,7},{8,11},{9,15},{10,8},{11,12},{16,19},{17,23},{18,16},{... | collective-permute-start | bytes 811016 | tf_op jit(solution)/shard_map/ppermute | solution.py:378
  141.6 14.6 %collective-permute-start.23 = (bf16[528,256]{1,0:T(8,128)(2,1)S(1)}, bf16[528,256]{1,0:T(8,128)(2,1)S(1)}, u32[]{:S(2)}, u32[]{:S(2)}) collective-permute-start(bf16[528,256]{1,0:T(8,128)(2,1)S(1)} %get-tuple-element.85), channel_id=1, source_target_pairs={{1,4},{9,12},{10,9},{11,13},{17,20},{18,17},{19,21},{20,18},{21,22... | collective-permute-start | bytes 811016 | tf_op jit(solution)/shard_map/ppermute | solution.py:378
  146.1 10.1 %collective-permute-start.24 = (bf16[528,256]{1,0:T(8,128)(2,1)S(1)}, bf16[528,256]{1,0:T(8,128)(2,1)S(1)}, u32[]{:S(2)}, u32[]{:S(2)}) collective-permute-start(bf16[528,256]{1,0:T(8,128)(2,1)S(1)} %get-tuple-element.86), channel_id=1, source_target_pairs={{0,1},{1,5},{8,9},{9,13},{11,14},{16,17},{17,21},{19,22},{20,19},{... | collective-permute-start | bytes 811016 | tf_op jit(solution)/shard_map/ppermute | solution.py:378
  148.1 12.5 %collective-permute-start.25 = (bf16[528,256]{1,0:T(8,128)(2,1)S(1)}, bf16[528,256]{1,0:T(8,128)(2,1)S(1)}, u32[]{:S(2)}, u32[]{:S(2)}) collective-permute-start(bf16[528,256]{1,0:T(8,128)(2,1)S(1)} %get-tuple-element.87), channel_id=1, source_target_pairs={{0,2},{1,6},{8,10},{9,14},{10,11},{11,15},{16,18},{17,22},{18,19},... | collective-permute-start | bytes 811016 | tf_op jit(solution)/shard_map/ppermute | solution.py:378
  150.0 21.7 %collective-permute-start.26 = (bf16[528,256]{1,0:T(8,128)(2,1)S(1)}, bf16[528,256]{1,0:T(8,128)(2,1)S(1)}, u32[]{:S(2)}, u32[]{:S(2)}) collective-permute-start(bf16[528,256]{1,0:T(8,128)(2,1)S(1)} %get-tuple-element.88), channel_id=1, source_target_pairs={{0,3},{1,7},{8,11},{9,15},{10,8},{11,12},{16,19},{17,23},{18,16},{... | collective-permute-start | bytes 811016 | tf_op jit(solution)/shard_map/ppermute | solution.py:378

commit v4 on v3

--- a/solution.py
+++ b/solution.py
@@ -7,7 +7,7 @@
 from jax.experimental.pallas import tpu as pltpu
 from jax.sharding import PartitionSpec as P
 
-TOP = 40000.0
+TOP = 1400.0
 TAIL = 16
 VMEM = 6 * 2**20
 
@@ -21,13 +21,13 @@
     x = values * scale
     x2 = x * x
     x4 = x2 * x2
-    return (x * jnp.abs(x) * x2 * x4).astype(jnp.bfloat16)
+    return (x * jnp.abs(x) * x2 * (x4 * x4)).astype(jnp.bfloat16)
 
 
 def decode(coded, scale):
     y = coded.astype(jnp.float32)
     back = jnp.where(scale > 0, 1.0 / scale, 0.0)
-    return y * jnp.exp2(-0.875 * jnp.log2(jnp.maximum(jnp.abs(y), 2.0**-126))) * back
+    return y * jnp.exp2(-11 / 12 * jnp.log2(jnp.maximum(jnp.abs(y), 2.0**-126))) * back
 
 
 def scale_of(message, rows, block):
@@ -288,8 +288,8 @@
 def pack_kernel(count, ids, a_ref, *refs):
     theirs, (sum_ref, in_ref, own_ref, *msgs, total) = refs[:count], refs[count:]
     height = own_ref.shape[0]
-    chips = len(msgs)
-    rows = chips * height
+    rounds = len(msgs)
+    rows = rounds * height
     tile = rows // 4
     chip, core = ids[1], ids[2]
 
@@ -306,30 +306,30 @@
             total[at, :] += sum_ref[at, :] + decode(in_ref[at, :], scale_of(in_ref, rows, part))
 
     for step, msg in enumerate(msgs):
-        at = pl.ds(pl.multiple_of(lax.rem(chip + step, chips) * height, height), height)
+        at = pl.ds(pl.multiple_of(lax.rem(chip + step, rounds) * height, height), height)
         values = total[at, :]
         scale = scale_for(jnp.max(jnp.abs(values), keepdims=True))
         msg[pl.ds(0, height), :] = encode(values, scale)
         put_scale(msg, height, 0, scale)
 
-    stays = (chip <= ids[0]) & (lax.div(chip, chips // 2) == core)
+    stays = (chip <= ids[0]) & (lax.div(chip, rounds // 2) == core)
 
     @pl.when(stays)
     def _():
-        at = pl.ds(pl.multiple_of((2 * lax.rem(chip, chips // 2) + core) * height, height), height)
-        own_ref[...] = total[at, :]
+        place = 2 * lax.rem(chip, rounds // 2) + core
+        own_ref[...] = total[pl.ds(pl.multiple_of(place * height, height), height), :]
 
     @pl.when(jnp.logical_not(stays))
     def _():
         own_ref[...] = jnp.zeros_like(own_ref)
 
 
-def pack(ids, mine, theirs, partial, message, chips, after):
+def pack(ids, mine, theirs, partial, message, rounds, after):
     rows, width = mine.shape
-    height = rows // chips
+    height = rows // rounds
     out_shape = [
         jax.ShapeDtypeStruct((height, width), jnp.float32),
-        *[jax.ShapeDtypeStruct((height + TAIL, width), jnp.bfloat16)] * chips,
+        *[jax.ShapeDtypeStruct((height + TAIL, width), jnp.bfloat16)] * rounds,
     ]
     return local(
         functools.partial(pack_kernel, len(theirs)), out_shape, "pack", ids, mine, *theirs, partial, message, after=after,
@@ -444,7 +444,7 @@
     swap = [((r, k, c), (r, k, 1 - c)) for r, k, c in active]
 
     def widen(panels, after):
-        panels[0], panels[1] = lax.optimization_barrier((panels[0], panels[1]))
+        panels[0], panels[1], *_ = lax.optimization_barrier((panels[0], panels[1], *after))
         for place in range(2, count):
             panels.append(spread(place, panels[place - (1 << (place.bit_length() - 1))]))
 
@@ -479,23 +479,22 @@
     other = send(mine, swap)
     panels_a, panels_b = ([x] for x in half(ids, mine, other, piece))
     panels_a.append(spread(1, panels_a[0]))
-    partial_a, message_a = mirrored_product(ids, matrix, diagonal, mine, other, piece, 0, [panels_a[0]])
-    message_a, panels_a[1] = lax.optimization_barrier((message_a, panels_a[1]))
+    partial_a, message_a = mirrored_product(ids, matrix, diagonal, mine, other, piece, 0, [])
     to_a = collect(bits - 1, message_a)
-    widen(panels_a, [])
     partial_b, message_b = mirrored_product(ids, matrix, diagonal, mine, other, piece, 1, [message_a])
     to_b = collect(bits - 1, message_b)
+    widen(panels_a, [message_b])
     panels_b.append(spread(1, panels_b[0]))
-    partial_a, to_a, relayed = relaying(partial_a, to_a, panels_a, [message_b])
+    partial_a, to_a, relayed = relaying(partial_a, to_a, [], [message_b])
     keep_a, *give_a = direct_product(ids, matrix, panels_a, [relayed])
     got_a = [send(x, swap) for x in give_a]
     partial_b, to_b, relayed = relaying(partial_b, to_b, [], [keep_a, to_a])
     widen(panels_b, [])
     arrays_a = deliver(keep_a, got_a, partial_a, to_a, [relayed])
     *give_b, panel_b = give_product(ids, matrix, panels_b, [arrays_a[0]])
-    give_b, arrays_a[1] = lax.optimization_barrier((give_b, arrays_a[1]))
+    give_b, to_b, *arrays_a[1:3] = lax.optimization_barrier((give_b, to_b, *arrays_a[1:3]))
     got_b = [send(x, swap) for x in give_b]
-    keep_b = keep_product(ids, matrix, panel_b, [to_b])
+    keep_b = keep_product(ids, matrix, panel_b, [])
     arrays_b = deliver(keep_b, got_b, partial_b, to_b, [])
     result = finish(ids, None, arrays_a, [arrays_b[0]])
     return finish(ids, result, arrays_b, [])

time: 175 us -> 179 us (1.023)
  waiting for transfers between devices: 51.2 us -> 60.8 us
  starting transfers between devices: 69 us -> 62.7 us
    ppermute x27, waiting for transfers between devices: 51.2 us -> 60.8 us  [send(): return lax.ppermute(x, ('row', 'col'), [(at(*s), at(*d)) for s, d in pairs])]
    ppermute x27, starting transfers between devices: 69 us -> 62.7 us  [send(): return lax.ppermute(x, ('row', 'col'), [(at(*s), at(*d)) for s, d in pairs])]
where the time goes in v4:
time: 179 us; the launch traced here: 178 us
  starting transfers between devices  62.7 us (35%)
  waiting for transfers between devices  60.8 us (34%)
  Pallas kernels  48.5 us (27%)
  local copies, waits for them, and re-layouts  5.86 us (3%)
    ppermute x27, starting transfers between devices, send(): return lax.ppermute(x, ('row', 'col'), [(at(*s), at(*d)) for s, d in pairs])  62.7 us
    ppermute x27, waiting for transfers between devices, send(): return lax.ppermute(x, ('row', 'col'), [(at(*s), at(*d)) for s, d in pairs])  60.8 us
    pallas_call x13, Pallas kernels, local(): pl.pallas_call(body, out_shape=out_shape, in_specs=[pl.BlockSpec(memory_s...  46.8 us
    unnamed x4, local copies, waits for them, and re-layouts  5.77 us
  transfers between devices with their start and end apart: 27, of which 8 were waited for; matrix products, arithmetic and copies ran while one was open for 0% of the time, Pallas kernels for 25%

profile of v4, /device:TPU:7, one launch (start us, length us, event | category | flops | bytes accessed | tf_op | source)
XLA Modules:
  0.0 178.4 jit_solution(16329239068286732143)
XLA Ops:
  0.0 4.2 %collective-permute-start = (bf16[512,512]{1,0:T(8,128)(2,1)}, bf16[512,512]{1,0:T(8,128)(2,1)S(1)}, u32[]{:S(2)}, u32[]{:S(2)}) collective-permute-start(bf16[512,512]{1,0:T(8,128)(2,1)} %refs_1_.1), channel_id=1, source_target_pairs={{4,0},{5,1},{6,2},{7,3},{12,8},{13,9},{14,10},{15,11},{16,20},{17,... | collective-permute-start | bytes 1572872 | tf_op jit(solution)/shard_map/ppermute | solution.py:378
  4.2 3.2 %collective-permute-start.1 = (bf16[512,512]{1,0:T(8,128)(2,1)}, bf16[512,512]{1,0:T(8,128)(2,1)S(1)}, u32[]{:S(2)}, u32[]{:S(2)}) collective-permute-start(bf16[512,512]{1,0:T(8,128)(2,1)} %refs_1_.1), channel_id=1, source_target_pairs={{8,10},{9,11},{16,18},{17,19},{18,20},{19,21},{24,26},{25,27},{26,... | collective-permute-start | bytes 1572872 | tf_op jit(solution)/shard_map/ppermute | solution.py:378
  8.9 5.8 %copy-done = bf16[4096,2048]{1,0:T(8,128)(2,1)S(1)} copy-done((bf16[4096,2048]{1,0:T(8,128)(2,1)S(1)}, bf16[4096,2048]{1,0:T(8,128)(2,1)}, u32[]{:S(2)}) %copy-start) | copy-done | bytes 16777240
  16.4 10.7 %collective-permute-done.refs_2_ = bf16[512,512]{1,0:T(8,128)(2,1)S(1)} collective-permute-done((bf16[512,512]{1,0:T(8,128)(2,1)}, bf16[512,512]{1,0:T(8,128)(2,1)S(1)}, u32[]{:S(2)}, u32[]{:S(2)}) %collective-permute-start) | collective-permute-done | bytes 524320 | tf_op jit(solution)/shard_map/ppermute | solution.py:378
  28.4 3.5 %collective-permute-done.2.refs_4_ = bf16[512,512]{1,0:T(8,128)(2,1)S(1)} collective-permute-done((bf16[512,512]{1,0:T(8,128)(2,1)}, bf16[512,512]{1,0:T(8,128)(2,1)S(1)}, u32[]{:S(2)}, u32[]{:S(2)}) %collective-permute-start.2) | collective-permute-done | bytes 524320 | tf_op jit(solution)/shard_map/ppermute | solution.py:378
  31.9 11.2 %collective-permute-done.3.refs_5_ = bf16[512,512]{1,0:T(8,128)(2,1)S(1)} collective-permute-done((bf16[512,512]{1,0:T(8,128)(2,1)S(1)}, bf16[512,512]{1,0:T(8,128)(2,1)S(1)}, u32[]{:S(2)}, u32[]{:S(2)}) %collective-permute-start.3) | collective-permute-done | bytes 524320 | tf_op jit(solution)/shard_map/ppermute | solution.py:378
  43.8 4.1 %collective-permute-start.4 = (bf16[2048,512]{1,0:T(8,128)(2,1)S(1)}, bf16[2048,512]{1,0:T(8,128)(2,1)S(1)}, u32[]{:S(2)}, u32[]{:S(2)}) collective-permute-start(bf16[2048,512]{1,0:T(8,128)(2,1)S(1)} %line.1.refs_1_.refs_3_), channel_id=1, source_target_pairs={{0,1},{1,0},{8,9},{9,8},{10,11},{11,10},{16,17},{17,16},{18,19},{1... | collective-permute-start | bytes 6291464 | tf_op jit(solution)/shard_map/ppermute | solution.py:378
  47.9 3.8 %collective-permute-done.4.refs_2_.refs_4_ = bf16[2048,512]{1,0:T(8,128)(2,1)S(1)} collective-permute-done((bf16[2048,512]{1,0:T(8,128)(2,1)S(1)}, bf16[2048,512]{1,0:T(8,128)(2,1)S(1)}, u32[]{:S(2)}, u32[]{:S(2)}) %collective-permute-start.4) | collective-permute-done | bytes 2097184 | tf_op jit(solution)/shard_map/ppermute | solution.py:378
  53.1 8.8 %mirrored_product.2 = (f32[2048,256]{1,0:T(8,128)S(1)}, bf16[2112,256]{1,0:T(8,128)(2,1)S(1)}) custom-call(s32[5]{0:T(128)S(1)} %stack.23.ids.refs_0_, bf16[4096,2048]{1,0:T(8,128)(2,1)S(1)} %get-tuple-element.45.refs_1_, f32[8,2048]{1,0:T(8,128)S(1)} %get-tuple-element.48.refs_2_, bf16[2048,512]{1,0:T(8,128)(2,1)S(1)} %line.1.refs_1_.refs_3_, ...), custom_call_target="tpu_custom_call" | custom-call | tf_op jit(solution)/shard_map/mirrored_product/pallas_call | solution.py:48
  63.3 8.8 %mirrored_product.3 = (f32[2048,256]{1,0:T(8,128)S(1)}, bf16[2112,256]{1,0:T(8,128)(2,1)S(1)}) custom-call(s32[5]{0:T(128)S(1)} %stack.23.ids.refs_0_, bf16[4096,2048]{1,0:T(8,128)(2,1)S(1)} %get-tuple-element.45.refs_1_, f32[8,2048]{1,0:T(8,128)S(1)} %get-tuple-element.48.refs_2_, bf16[2048,512]{1,0:T(8,128)(2,1)S(1)} %line.1.refs_1_.refs_3_, ...), custom_call_target="tpu_custom_call" | custom-call | tf_op jit(solution)/shard_map/mirrored_product/pallas_call | solution.py:48
  74.2 4.1 %collective-permute-start.12 = (bf16[2112,256]{1,0:T(8,128)(2,1)S(1)}, bf16[2112,256]{1,0:T(8,128)(2,1)S(1)}, u32[]{:S(2)}, u32[]{:S(2)}) collective-permute-start(bf16[2112,256]{1,0:T(8,128)(2,1)S(1)} %get-tuple-element.50.refs_3_), channel_id=1, source_target_pairs={{16,0},{24,8},{9,1},{25,17},{26,10},{18,2},{19,27},{29,21}} | collective-permute-start | bytes 3244040 | tf_op jit(solution)/shard_map/ppermute | solution.py:378
  78.3 2.9 %relay.2 = (f32[2048,256]{1,0:T(8,128)S(1)}, bf16[2112,256]{1,0:T(8,128)(2,1)S(1)}) custom-call(s32[5]{0:T(128)S(1)} %stack.23.ids.refs_0_, f32[2048,256]{1,0:T(8,128)S(1)} %get-tuple-element.53.refs_1_, bf16[2112,256]{1,0:T(8,128)(2,1)S(1)} %collective-permute-done.8.refs_2_, bf16[2112,256]{1,0:T(8,128)(2,1)S(1)} %get-tuple-element.50.refs_3_), custom_call_target="tpu_custom_call" | custom-call | tf_op jit(solution)/shard_map/relay/pallas_call | solution.py:48
  82.7 6.0 %collective-permute-done.7.refs_5_ = bf16[2048,256]{1,0:T(8,128)(2,1)S(1)} collective-permute-done((bf16[2048,256]{1,0:T(8,128)(2,1)S(1)}, bf16[2048,256]{1,0:T(8,128)(2,1)S(1)}, u32[]{:S(2)}, u32[]{:S(2)}) %collective-permute-start.7) | collective-permute-done | bytes 1048608 | tf_op jit(solution)/shard_map/ppermute | solution.py:378
  88.7 6.4 %direct_product.1 = (f32[2048,256]{1,0:T(8,128)S(1)}, f32[1024,256]{1,0:T(8,128)S(1)}, f32[1024,256]{1,0:T(8,128)S(1)}) custom-call(s32[5]{0:T(128)S(1)} %stack.23.ids.refs_0_, bf16[4096,2048]{1,0:T(8,128)(2,1)S(1)} %get-tuple-element.45.refs_1_, bf16[2048,256]{1,0:T(8,128)(2,1)S(1)} %get-tuple-element.51.refs_2_, ...), custom_call_target="tpu_custom_call" | custom-call | tf_op jit(solution)/shard_map/direct_product/pallas_call | solution.py:48
  95.1 3.2 %collective-permute-start.9 = (f32[1024,256]{1,0:T(8,128)S(1)}, f32[1024,256]{1,0:T(8,128)S(1)}, u32[]{:S(2)}, u32[]{:S(2)}) collective-permute-start(f32[1024,256]{1,0:T(8,128)S(1)} %get-tuple-element.56), channel_id=1, source_target_pairs={{0,1},{1,0},{8,9},{9,8},{10,11},{11,10},{16,17},{17,16},{18,19},{1... | collective-permute-start | bytes 3145736 | tf_op jit(solution)/shard_map/ppermute | solution.py:378
  100.2 2.9 %relay.3 = (f32[2048,256]{1,0:T(8,128)S(1)}, bf16[2112,256]{1,0:T(8,128)(2,1)S(1)}) custom-call(s32[5]{0:T(128)S(1)} %stack.23.ids.refs_0_, f32[2048,256]{1,0:T(8,128)S(1)} %get-tuple-element.59.refs_1_, bf16[2112,256]{1,0:T(8,128)(2,1)S(1)} %collective-permute-done.12.refs_2_, f32[2048,256]{1,0:T(8,128)S(1)} %get-tuple-element.55.refs_3_.refs_1_, ...), custom_call_target="tpu_custom_call" | custom-call | tf_op jit(solution)/shard_map/relay/pallas_call | solution.py:48
  106.0 2.3 %pack.2 = (f32[512,256]{1,0:T(8,128)S(1)}, bf16[528,256]{1,0:T(8,128)(2,1)S(1)}, bf16[528,256]{1,0:T(8,128)(2,1)S(1)}, bf16[528,256]{1,0:T(8,128)(2,1)S(1)}, bf16[528,256]{1,0:T(8,128)(2,1)S(1)}) custom-call(s32[5]{0:T(128)S(1)} %stack.23.ids.refs_0_, f32[2048,256]{1,0:T(8,128)S(1)} %get-tuple-element.55.refs_3_.refs_1_, ...), custom_call_target="tpu_custom_call" | custom-call | tf_op jit(solution)/shard_map/pack/pallas_call | solution.py:48
  108.3 7.4 %collective-permute-start.17 = (bf16[528,256]{1,0:T(8,128)(2,1)S(1)}, bf16[528,256]{1,0:T(8,128)(2,1)S(1)}, u32[]{:S(2)}, u32[]{:S(2)}) collective-permute-start(bf16[528,256]{1,0:T(8,128)(2,1)S(1)} %get-tuple-element.67), channel_id=1, source_target_pairs={{1,4},{9,12},{10,9},{11,13},{17,20},{18,17},{19,21},{20,18},{21,22... | collective-permute-start | bytes 811016 | tf_op jit(solution)/shard_map/ppermute | solution.py:378
  117.6 9.7 %collective-permute-done.15.refs_5_ = bf16[2048,256]{1,0:T(8,128)(2,1)S(1)} collective-permute-done((bf16[2048,256]{1,0:T(8,128)(2,1)S(1)}, bf16[2048,256]{1,0:T(8,128)(2,1)S(1)}, u32[]{:S(2)}, u32[]{:S(2)}) %collective-permute-start.15) | collective-permute-done | bytes 1048608 | tf_op jit(solution)/shard_map/ppermute | solution.py:378
  127.3 3.5 %give_product.1 = (f32[1024,256]{1,0:T(8,128)S(1)}, f32[1024,256]{1,0:T(8,128)S(1)}, bf16[2048,256]{1,0:T(8,128)(2,1)S(1)}) custom-call(s32[5]{0:T(128)S(1)} %stack.23.ids.refs_0_, bf16[4096,2048]{1,0:T(8,128)(2,1)S(1)} %get-tuple-element.45.refs_1_, bf16[2048,256]{1,0:T(8,128)(2,1)S(1)} %get-tuple-element.63.refs_2_, ...), custom_call_target="tpu_custom_call" | custom-call | tf_op jit(solution)/shard_map/give_product/pallas_call | solution.py:48
  130.9 1.9 %collective-permute-start.21 = (f32[1024,256]{1,0:T(8,128)S(1)}, f32[1024,256]{1,0:T(8,128)S(1)}, u32[]{:S(2)}, u32[]{:S(2)}) collective-permute-start(f32[1024,256]{1,0:T(8,128)S(1)} %get-tuple-element.74), channel_id=1, source_target_pairs={{0,1},{1,0},{8,9},{9,8},{10,11},{11,10},{16,17},{17,16},{18,19},{1... | collective-permute-start | bytes 3145736 | tf_op jit(solution)/shard_map/ppermute | solution.py:378
  132.8 2.4 %collective-permute-start.22 = (f32[1024,256]{1,0:T(8,128)S(1)}, f32[1024,256]{1,0:T(8,128)S(1)}, u32[]{:S(2)}, u32[]{:S(2)}) collective-permute-start(f32[1024,256]{1,0:T(8,128)S(1)} %get-tuple-element.75), channel_id=1, source_target_pairs={{0,1},{1,0},{8,9},{9,8},{10,11},{11,10},{16,17},{17,16},{18,19},{1... | collective-permute-start | bytes 3145736 | tf_op jit(solution)/shard_map/ppermute | solution.py:378
  135.2 2.3 %collective-permute-start.19 = (bf16[528,256]{1,0:T(8,128)(2,1)S(1)}, bf16[528,256]{1,0:T(8,128)(2,1)S(1)}, u32[]{:S(2)}, u32[]{:S(2)}) collective-permute-start(bf16[528,256]{1,0:T(8,128)(2,1)S(1)} %get-tuple-element.71), channel_id=1, source_target_pairs={{0,2},{1,6},{8,10},{9,14},{10,11},{11,15},{16,18},{17,22},{18,19},... | collective-permute-start | bytes 811016 | tf_op jit(solution)/shard_map/ppermute | solution.py:378
  139.5 3.4 %keep_product.1.refs_1_ = f32[2048,256]{1,0:T(8,128)S(1)} custom-call(s32[5]{0:T(128)S(1)} %stack.23.ids.refs_0_, bf16[4096,2048]{1,0:T(8,128)(2,1)S(1)} %get-tuple-element.45.refs_1_, bf16[2048,256]{1,0:T(8,128)(2,1)S(1)} %get-tuple-element.73.refs_2_), custom_call_target="tpu_custom_call" | custom-call | tf_op jit(solution)/shard_map/keep_product/pallas_call | solution.py:48
  142.9 2.1 %pack.3 = (f32[512,256]{1,0:T(8,128)S(1)}, bf16[528,256]{1,0:T(8,128)(2,1)S(1)}, bf16[528,256]{1,0:T(8,128)(2,1)S(1)}, bf16[528,256]{1,0:T(8,128)(2,1)S(1)}, bf16[528,256]{1,0:T(8,128)(2,1)S(1)}) custom-call(s32[5]{0:T(128)S(1)} %stack.23.ids.refs_0_, f32[2048,256]{1,0:T(8,128)S(1)} %keep_product.1.refs_1_, f32[1024,256]{1,0:T(8,128)S(1)} %collective-permute-done.21.refs_2_, ...), custom_call_target="tpu_custom_call" | custom-call | tf_op jit(solution)/shard_map/pack/pallas_call | solution.py:48
  145.0 4.5 %collective-permute-start.23 = (bf16[528,256]{1,0:T(8,128)(2,1)S(1)}, bf16[528,256]{1,0:T(8,128)(2,1)S(1)}, u32[]{:S(2)}, u32[]{:S(2)}) collective-permute-start(bf16[528,256]{1,0:T(8,128)(2,1)S(1)} %get-tuple-element.79), channel_id=1, source_target_pairs={{1,4},{9,12},{10,9},{11,13},{17,20},{18,17},{19,21},{20,18},{21,22... | collective-permute-start | bytes 811016 | tf_op jit(solution)/shard_map/ppermute | solution.py:378
  149.6 3.7 %collective-permute-start.24 = (bf16[528,256]{1,0:T(8,128)(2,1)S(1)}, bf16[528,256]{1,0:T(8,128)(2,1)S(1)}, u32[]{:S(2)}, u32[]{:S(2)}) collective-permute-start(bf16[528,256]{1,0:T(8,128)(2,1)S(1)} %get-tuple-element.80), channel_id=1, source_target_pairs={{0,1},{1,5},{8,9},{9,13},{11,14},{16,17},{17,21},{19,22},{20,19},{... | collective-permute-start | bytes 811016 | tf_op jit(solution)/shard_map/ppermute | solution.py:378
  153.3 2.3 %collective-permute-start.25 = (bf16[528,256]{1,0:T(8,128)(2,1)S(1)}, bf16[528,256]{1,0:T(8,128)(2,1)S(1)}, u32[]{:S(2)}, u32[]{:S(2)}) collective-permute-start(bf16[528,256]{1,0:T(8,128)(2,1)S(1)} %get-tuple-element.81), channel_id=1, source_target_pairs={{0,2},{1,6},{8,10},{9,14},{10,11},{11,15},{16,18},{17,22},{18,19},... | collective-permute-start | bytes 811016 | tf_op jit(solution)/shard_map/ppermute | solution.py:378
  155.6 2.8 %collective-permute-start.26 = (bf16[528,256]{1,0:T(8,128)(2,1)S(1)}, bf16[528,256]{1,0:T(8,128)(2,1)S(1)}, u32[]{:S(2)}, u32[]{:S(2)}) collective-permute-start(bf16[528,256]{1,0:T(8,128)(2,1)S(1)} %get-tuple-element.82), channel_id=1, source_target_pairs={{0,3},{1,7},{8,11},{9,15},{10,8},{11,12},{16,19},{17,23},{18,16},{... | collective-permute-start | bytes 811016 | tf_op jit(solution)/shard_map/ppermute | solution.py:378
  160.0 7.6 %collective-permute-done.25.refs_5_ = bf16[528,256]{1,0:T(8,128)(2,1)S(1)} collective-permute-done((bf16[528,256]{1,0:T(8,128)(2,1)S(1)}, bf16[528,256]{1,0:T(8,128)(2,1)S(1)}, u32[]{:S(2)}, u32[]{:S(2)}) %collective-permute-start.25) | collective-permute-done | bytes 270368 | tf_op jit(solution)/shard_map/ppermute | solution.py:378
  167.5 8.2 %collective-permute-done.26.refs_6_ = bf16[528,256]{1,0:T(8,128)(2,1)S(1)} collective-permute-done((bf16[528,256]{1,0:T(8,128)(2,1)S(1)}, bf16[528,256]{1,0:T(8,128)(2,1)S(1)}, u32[]{:S(2)}, u32[]{:S(2)}) %collective-permute-start.26) | collective-permute-done | bytes 270368 | tf_op jit(solution)/shard_map/ppermute | solution.py:378
  175.8 2.6 %finish.3 = f32[512,512]{1,0:T(8,128)} custom-call(s32[5]{0:T(128)S(1)} %stack.23.ids.refs_0_, f32[512,256]{1,0:T(8,128)S(1)} %finish.2.refs_1_, f32[512,256]{1,0:T(8,128)S(1)} %get-tuple-element.78.refs_7_.refs_2_, bf16[528,256]{1,0:T(8,128)(2,1)S(1)} %collective-permute-done.23.refs_3_, bf16[528,256]{1,0:T(8,128)(2,1)S(1)} %collective-permute-done.24.refs_4_, ...), custom_call_target="tpu_custom_call" | custom-call | tf_op jit(solution)/shard_map/finish/pallas_call | solution.py:48
  (41 shorter events, 21.5 us)
Async XLA Ops:
  0.0 27.1 %collective-permute-start = (bf16[512,512]{1,0:T(8,128)(2,1)}, bf16[512,512]{1,0:T(8,128)(2,1)S(1)}, u32[]{:S(2)}, u32[]{:S(2)}) collective-permute-start(bf16[512,512]{1,0:T(8,128)(2,1)} %refs_1_.1), channel_id=1, source_target_pairs={{4,0},{5,1},{6,2},{7,3},{12,8},{13,9},{14,10},{15,11},{16,20},{17,... | collective-permute-start | bytes 1572872 | tf_op jit(solution)/shard_map/ppermute | solution.py:378
  4.2 24.2 %collective-permute-start.1 = (bf16[512,512]{1,0:T(8,128)(2,1)}, bf16[512,512]{1,0:T(8,128)(2,1)S(1)}, u32[]{:S(2)}, u32[]{:S(2)}) collective-permute-start(bf16[512,512]{1,0:T(8,128)(2,1)} %refs_1_.1), channel_id=1, source_target_pairs={{8,10},{9,11},{16,18},{17,19},{18,20},{19,21},{24,26},{25,27},{26,... | collective-permute-start | bytes 1572872 | tf_op jit(solution)/shard_map/ppermute | solution.py:378
  7.5 24.4 %collective-permute-start.2 = (bf16[512,512]{1,0:T(8,128)(2,1)}, bf16[512,512]{1,0:T(8,128)(2,1)S(1)}, u32[]{:S(2)}, u32[]{:S(2)}) collective-permute-start(bf16[512,512]{1,0:T(8,128)(2,1)} %refs_1_.1), channel_id=1, source_target_pairs={{2,0},{3,1},{10,8},{11,9},{12,10},{13,11},{18,16},{19,17},{20,18},... | collective-permute-start | bytes 1572872 | tf_op jit(solution)/shard_map/ppermute | solution.py:378
  8.9 5.8 %copy-start = (bf16[4096,2048]{1,0:T(8,128)(2,1)S(1)}, bf16[4096,2048]{1,0:T(8,128)(2,1)}, u32[]{:S(2)}) copy-start(bf16[4096,2048]{1,0:T(8,128)(2,1)} %a_ref.1) | copy-start | bytes 50331652
  14.6 28.5 %copy-start.1 = (bf16[512,512]{1,0:T(8,128)(2,1)S(1)}, bf16[512,512]{1,0:T(8,128)(2,1)}, u32[]{:S(2)}) copy-start(bf16[512,512]{1,0:T(8,128)(2,1)} %refs_1_.1) | copy-start | bytes 1572868
  27.1 16.0 %collective-permute-start.3 = (bf16[512,512]{1,0:T(8,128)(2,1)S(1)}, bf16[512,512]{1,0:T(8,128)(2,1)S(1)}, u32[]{:S(2)}, u32[]{:S(2)}) collective-permute-start(bf16[512,512]{1,0:T(8,128)(2,1)S(1)} %collective-permute-done.refs_2_), channel_id=1, source_target_pairs={{2,0},{3,1},{10,8},{11,9},{18,16},{19,17},{26,24},{27,25},{28,30},... | collective-permute-start | bytes 1572872 | tf_op jit(solution)/shard_map/ppermute | solution.py:378
  43.8 7.8 %collective-permute-start.4 = (bf16[2048,512]{1,0:T(8,128)(2,1)S(1)}, bf16[2048,512]{1,0:T(8,128)(2,1)S(1)}, u32[]{:S(2)}, u32[]{:S(2)}) collective-permute-start(bf16[2048,512]{1,0:T(8,128)(2,1)S(1)} %line.1.refs_1_.refs_3_), channel_id=1, source_target_pairs={{0,1},{1,0},{8,9},{9,8},{10,11},{11,10},{16,17},{17,16},{18,19},{1... | collective-permute-start | bytes 6291464 | tf_op jit(solution)/shard_map/ppermute | solution.py:378
  52.4 19.8 %collective-permute-start.5 = (bf16[2048,256]{1,0:T(8,128)(2,1)S(1)}, bf16[2048,256]{1,0:T(8,128)(2,1)S(1)}, u32[]{:S(2)}, u32[]{:S(2)}) collective-permute-start(bf16[2048,256]{1,0:T(8,128)(2,1)S(1)} %get-tuple-element.51.refs_2_), channel_id=1, source_target_pairs={{0,8},{1,17},{10,2},{11,27},{20,28}} | collective-permute-start | bytes 3145736 | tf_op jit(solution)/shard_map/ppermute | solution.py:378
  61.9 16.4 %collective-permute-start.8 = (bf16[2112,256]{1,0:T(8,128)(2,1)S(1)}, bf16[2112,256]{1,0:T(8,128)(2,1)S(1)}, u32[]{:S(2)}, u32[]{:S(2)}) collective-permute-start(bf16[2112,256]{1,0:T(8,128)(2,1)S(1)} %get-tuple-element.49.refs_5_), channel_id=1, source_target_pairs={{16,0},{24,8},{9,1},{25,17},{26,10},{18,2},{19,27},{29,21}} | collective-permute-start | bytes 3244040 | tf_op jit(solution)/shard_map/ppermute | solution.py:378
  72.1 10.6 %collective-permute-start.6 = (bf16[2048,256]{1,0:T(8,128)(2,1)S(1)}, bf16[2048,256]{1,0:T(8,128)(2,1)S(1)}, u32[]{:S(2)}, u32[]{:S(2)}) collective-permute-start(bf16[2048,256]{1,0:T(8,128)(2,1)S(1)} %get-tuple-element.51.refs_2_), channel_id=1, source_target_pairs={{0,16},{1,9},{10,26},{21,29}} | collective-permute-start | bytes 3145736 | tf_op jit(solution)/shard_map/ppermute | solution.py:378
  72.9 15.8 %collective-permute-start.7 = (bf16[2048,256]{1,0:T(8,128)(2,1)S(1)}, bf16[2048,256]{1,0:T(8,128)(2,1)S(1)}, u32[]{:S(2)}, u32[]{:S(2)}) collective-permute-start(bf16[2048,256]{1,0:T(8,128)(2,1)S(1)} %collective-permute-done.5.refs_3_), channel_id=1, source_target_pairs={{8,24},{17,25},{2,18},{27,19}} | collective-permute-start | bytes 3145736 | tf_op jit(solution)/shard_map/ppermute | solution.py:378
  74.2 26.0 %collective-permute-start.12 = (bf16[2112,256]{1,0:T(8,128)(2,1)S(1)}, bf16[2112,256]{1,0:T(8,128)(2,1)S(1)}, u32[]{:S(2)}, u32[]{:S(2)}) collective-permute-start(bf16[2112,256]{1,0:T(8,128)(2,1)S(1)} %get-tuple-element.50.refs_3_), channel_id=1, source_target_pairs={{16,0},{24,8},{9,1},{25,17},{26,10},{18,2},{19,27},{29,21}} | collective-permute-start | bytes 3244040 | tf_op jit(solution)/shard_map/ppermute | solution.py:378
  81.2 19.0 %collective-permute-start.11 = (bf16[2112,256]{1,0:T(8,128)(2,1)S(1)}, bf16[2112,256]{1,0:T(8,128)(2,1)S(1)}, u32[]{:S(2)}, u32[]{:S(2)}) collective-permute-start(bf16[2112,256]{1,0:T(8,128)(2,1)S(1)} %get-tuple-element.54.refs_6_), channel_id=1, source_target_pairs={{8,0},{17,1},{2,10},{27,11},{28,20}} | collective-permute-start | bytes 3244040 | tf_op jit(solution)/shard_map/ppermute | solution.py:378
  82.0 21.9 %collective-permute-start.13 = (bf16[2048,256]{1,0:T(8,128)(2,1)S(1)}, bf16[2048,256]{1,0:T(8,128)(2,1)S(1)}, u32[]{:S(2)}, u32[]{:S(2)}) collective-permute-start(bf16[2048,256]{1,0:T(8,128)(2,1)S(1)} %get-tuple-element.63.refs_2_), channel_id=1, source_target_pairs={{0,8},{1,17},{10,2},{11,27},{20,28}} | collective-permute-start | bytes 3145736 | tf_op jit(solution)/shard_map/ppermute | solution.py:378
  95.1 10.9 %collective-permute-start.9 = (f32[1024,256]{1,0:T(8,128)S(1)}, f32[1024,256]{1,0:T(8,128)S(1)}, u32[]{:S(2)}, u32[]{:S(2)}) collective-permute-start(f32[1024,256]{1,0:T(8,128)S(1)} %get-tuple-element.56), channel_id=1, source_target_pairs={{0,1},{1,0},{8,9},{9,8},{10,11},{11,10},{16,17},{17,16},{18,19},{1... | collective-permute-start | bytes 3145736 | tf_op jit(solution)/shard_map/ppermute | solution.py:378
  98.3 7.7 %collective-permute-start.10 = (f32[1024,256]{1,0:T(8,128)S(1)}, f32[1024,256]{1,0:T(8,128)S(1)}, u32[]{:S(2)}, u32[]{:S(2)}) collective-permute-start(f32[1024,256]{1,0:T(8,128)S(1)} %get-tuple-element.57), channel_id=1, source_target_pairs={{0,1},{1,0},{8,9},{9,8},{10,11},{11,10},{16,17},{17,16},{18,19},{1... | collective-permute-start | bytes 3145736 | tf_op jit(solution)/shard_map/ppermute | solution.py:378
  103.2 27.7 %collective-permute-start.16 = (bf16[2112,256]{1,0:T(8,128)(2,1)S(1)}, bf16[2112,256]{1,0:T(8,128)(2,1)S(1)}, u32[]{:S(2)}, u32[]{:S(2)}) collective-permute-start(bf16[2112,256]{1,0:T(8,128)(2,1)S(1)} %get-tuple-element.60.refs_6_), channel_id=1, source_target_pairs={{8,0},{17,1},{2,10},{27,11},{28,20}} | collective-permute-start | bytes 3244040 | tf_op jit(solution)/shard_map/ppermute | solution.py:378
  103.9 13.7 %collective-permute-start.14 = (bf16[2048,256]{1,0:T(8,128)(2,1)S(1)}, bf16[2048,256]{1,0:T(8,128)(2,1)S(1)}, u32[]{:S(2)}, u32[]{:S(2)}) collective-permute-start(bf16[2048,256]{1,0:T(8,128)(2,1)S(1)} %get-tuple-element.63.refs_2_), channel_id=1, source_target_pairs={{0,16},{1,9},{10,26},{21,29}} | collective-permute-start | bytes 3145736 | tf_op jit(solution)/shard_map/ppermute | solution.py:378
  104.6 22.7 %collective-permute-start.15 = (bf16[2048,256]{1,0:T(8,128)(2,1)S(1)}, bf16[2048,256]{1,0:T(8,128)(2,1)S(1)}, u32[]{:S(2)}, u32[]{:S(2)}) collective-permute-start(bf16[2048,256]{1,0:T(8,128)(2,1)S(1)} %collective-permute-done.13.refs_3_), channel_id=1, source_target_pairs={{8,24},{17,25},{2,18},{27,19}} | collective-permute-start | bytes 3145736 | tf_op jit(solution)/shard_map/ppermute | solution.py:378
  108.3 22.6 %collective-permute-start.17 = (bf16[528,256]{1,0:T(8,128)(2,1)S(1)}, bf16[528,256]{1,0:T(8,128)(2,1)S(1)}, u32[]{:S(2)}, u32[]{:S(2)}) collective-permute-start(bf16[528,256]{1,0:T(8,128)(2,1)S(1)} %get-tuple-element.67), channel_id=1, source_target_pairs={{1,4},{9,12},{10,9},{11,13},{17,20},{18,17},{19,21},{20,18},{21,22... | collective-permute-start | bytes 811016 | tf_op jit(solution)/shard_map/ppermute | solution.py:378
  115.7 15.2 %collective-permute-start.18 = (bf16[528,256]{1,0:T(8,128)(2,1)S(1)}, bf16[528,256]{1,0:T(8,128)(2,1)S(1)}, u32[]{:S(2)}, u32[]{:S(2)}) collective-permute-start(bf16[528,256]{1,0:T(8,128)(2,1)S(1)} %get-tuple-element.68), channel_id=1, source_target_pairs={{0,1},{1,5},{8,9},{9,13},{11,14},{16,17},{17,21},{19,22},{20,19},{... | collective-permute-start | bytes 811016 | tf_op jit(solution)/shard_map/ppermute | solution.py:378
  130.9 12.0 %collective-permute-start.21 = (f32[1024,256]{1,0:T(8,128)S(1)}, f32[1024,256]{1,0:T(8,128)S(1)}, u32[]{:S(2)}, u32[]{:S(2)}) collective-permute-start(f32[1024,256]{1,0:T(8,128)S(1)} %get-tuple-element.74), channel_id=1, source_target_pairs={{0,1},{1,0},{8,9},{9,8},{10,11},{11,10},{16,17},{17,16},{18,19},{1... | collective-permute-start | bytes 3145736 | tf_op jit(solution)/shard_map/ppermute | solution.py:378
  132.8 10.1 %collective-permute-start.22 = (f32[1024,256]{1,0:T(8,128)S(1)}, f32[1024,256]{1,0:T(8,128)S(1)}, u32[]{:S(2)}, u32[]{:S(2)}) collective-permute-start(f32[1024,256]{1,0:T(8,128)S(1)} %get-tuple-element.75), channel_id=1, source_target_pairs={{0,1},{1,0},{8,9},{9,8},{10,11},{11,10},{16,17},{17,16},{18,19},{1... | collective-permute-start | bytes 3145736 | tf_op jit(solution)/shard_map/ppermute | solution.py:378
  135.2 20.4 %collective-permute-start.19 = (bf16[528,256]{1,0:T(8,128)(2,1)S(1)}, bf16[528,256]{1,0:T(8,128)(2,1)S(1)}, u32[]{:S(2)}, u32[]{:S(2)}) collective-permute-start(bf16[528,256]{1,0:T(8,128)(2,1)S(1)} %get-tuple-element.71), channel_id=1, source_target_pairs={{0,2},{1,6},{8,10},{9,14},{10,11},{11,15},{16,18},{17,22},{18,19},... | collective-permute-start | bytes 811016 | tf_op jit(solution)/shard_map/ppermute | solution.py:378
  137.5 20.8 %collective-permute-start.20 = (bf16[528,256]{1,0:T(8,128)(2,1)S(1)}, bf16[528,256]{1,0:T(8,128)(2,1)S(1)}, u32[]{:S(2)}, u32[]{:S(2)}) collective-permute-start(bf16[528,256]{1,0:T(8,128)(2,1)S(1)} %get-tuple-element.72), channel_id=1, source_target_pairs={{0,3},{1,7},{8,11},{9,15},{10,8},{11,12},{16,19},{17,23},{18,16},{... | collective-permute-start | bytes 811016 | tf_op jit(solution)/shard_map/ppermute | solution.py:378
  145.0 14.9 %collective-permute-start.23 = (bf16[528,256]{1,0:T(8,128)(2,1)S(1)}, bf16[528,256]{1,0:T(8,128)(2,1)S(1)}, u32[]{:S(2)}, u32[]{:S(2)}) collective-permute-start(bf16[528,256]{1,0:T(8,128)(2,1)S(1)} %get-tuple-element.79), channel_id=1, source_target_pairs={{1,4},{9,12},{10,9},{11,13},{17,20},{18,17},{19,21},{20,18},{21,22... | collective-permute-start | bytes 811016 | tf_op jit(solution)/shard_map/ppermute | solution.py:378
  149.6 10.4 %collective-permute-start.24 = (bf16[528,256]{1,0:T(8,128)(2,1)S(1)}, bf16[528,256]{1,0:T(8,128)(2,1)S(1)}, u32[]{:S(2)}, u32[]{:S(2)}) collective-permute-start(bf16[528,256]{1,0:T(8,128)(2,1)S(1)} %get-tuple-element.80), channel_id=1, source_target_pairs={{0,1},{1,5},{8,9},{9,13},{11,14},{16,17},{17,21},{19,22},{20,19},{... | collective-permute-start | bytes 811016 | tf_op jit(solution)/shard_map/ppermute | solution.py:378
  153.3 14.2 %collective-permute-start.25 = (bf16[528,256]{1,0:T(8,128)(2,1)S(1)}, bf16[528,256]{1,0:T(8,128)(2,1)S(1)}, u32[]{:S(2)}, u32[]{:S(2)}) collective-permute-start(bf16[528,256]{1,0:T(8,128)(2,1)S(1)} %get-tuple-element.81), channel_id=1, source_target_pairs={{0,2},{1,6},{8,10},{9,14},{10,11},{11,15},{16,18},{17,22},{18,19},... | collective-permute-start | bytes 811016 | tf_op jit(solution)/shard_map/ppermute | solution.py:378
  155.6 20.2 %collective-permute-start.26 = (bf16[528,256]{1,0:T(8,128)(2,1)S(1)}, bf16[528,256]{1,0:T(8,128)(2,1)S(1)}, u32[]{:S(2)}, u32[]{:S(2)}) collective-permute-start(bf16[528,256]{1,0:T(8,128)(2,1)S(1)} %get-tuple-element.82), channel_id=1, source_target_pairs={{0,3},{1,7},{8,11},{9,15},{10,8},{11,12},{16,19},{17,23},{18,16},{... | collective-permute-start | bytes 811016 | tf_op jit(solution)/shard_map/ppermute | solution.py:378

commit v5 on v4

--- a/solution.py
+++ b/solution.py
@@ -223,13 +223,6 @@
             copy.wait()
 
 
-def give_kernel(ids, a_ref, *refs):
-    *panels, give_ref, give_too, panel, sem = refs
-    pick(ids, panels, panel, sem)
-    rows_kernel(ids, a_ref, panel, give_ref, core=1 - ids[2], of=2)
-    rows_kernel(ids, a_ref, panel, give_too, core=1 - ids[2], at=1, of=2)
-
-
 def direct_kernel(ids, a_ref, *refs):
     *panels, keep_ref, give_ref, give_too, panel, sem = refs
     pick(ids, panels, panel, sem)
@@ -260,28 +253,6 @@
     return local(
         direct_kernel, out_shape, "direct_product", ids, matrix, *panels, after=after,
         scratch_shapes=[pltpu.VMEM((cols, width), jnp.bfloat16), pltpu.SemaphoreType.DMA],
-    )
-
-
-def give_product(ids, matrix, panels, after):
-    rows, cols = matrix.shape
-    width = panels[0].shape[1]
-    out_shape = [
-        *[jax.ShapeDtypeStruct((rows // 4, width), jnp.float32)] * 2,
-        jax.ShapeDtypeStruct((cols, width), jnp.bfloat16),
-    ]
-    return local(
-        give_kernel, out_shape, "give_product", ids, matrix, *panels, after=after,
-        scratch_shapes=[pltpu.SemaphoreType.DMA],
-    )
-
-
-def keep_product(ids, matrix, panel, after):
-    rows, cols = matrix.shape
-    width = panel.shape[1]
-    out_shape = jax.ShapeDtypeStruct((rows // 2, width), jnp.float32)
-    return local(
-        rows_kernel, out_shape, "keep_product", ids, matrix, panel, after=after
     )
 
 
@@ -479,22 +450,21 @@
     other = send(mine, swap)
     panels_a, panels_b = ([x] for x in half(ids, mine, other, piece))
     panels_a.append(spread(1, panels_a[0]))
+    panels_b.append(spread(1, panels_b[0]))
     partial_a, message_a = mirrored_product(ids, matrix, diagonal, mine, other, piece, 0, [])
     to_a = collect(bits - 1, message_a)
     partial_b, message_b = mirrored_product(ids, matrix, diagonal, mine, other, piece, 1, [message_a])
     to_b = collect(bits - 1, message_b)
-    widen(panels_a, [message_b])
-    panels_b.append(spread(1, panels_b[0]))
+    widen(panels_a, [message_b, panels_b[1]])
+    widen(panels_b, [panels_a[1]])
     partial_a, to_a, relayed = relaying(partial_a, to_a, [], [message_b])
     keep_a, *give_a = direct_product(ids, matrix, panels_a, [relayed])
     got_a = [send(x, swap) for x in give_a]
-    partial_b, to_b, relayed = relaying(partial_b, to_b, [], [keep_a, to_a])
-    widen(panels_b, [])
+    keep_b, *give_b = direct_product(ids, matrix, panels_b, [keep_a])
+    got_b = [send(x, swap) for x in give_b]
+    partial_b, to_b, relayed = relaying(partial_b, to_b, [], [keep_b, to_a])
     arrays_a = deliver(keep_a, got_a, partial_a, to_a, [relayed])
-    *give_b, panel_b = give_product(ids, matrix, panels_b, [arrays_a[0]])
-    give_b, to_b, *arrays_a[1:3] = lax.optimization_barrier((give_b, to_b, *arrays_a[1:3]))
-    got_b = [send(x, swap) for x in give_b]
-    keep_b = keep_product(ids, matrix, panel_b, [])
+    keep_b, *arrays_a[1:3] = lax.optimization_barrier((keep_b, *arrays_a[1:3]))
     arrays_b = deliver(keep_b, got_b, partial_b, to_b, [])
     result = finish(ids, None, arrays_a, [arrays_b[0]])
     return finish(ids, result, arrays_b, [])

time: 179 us -> 176 us (0.983)
  waiting for transfers between devices: 60.8 us -> 50.2 us
  starting transfers between devices: 62.7 us -> 70.6 us
    ppermute x27, waiting for transfers between devices: 60.8 us -> 50.2 us  [send(): return lax.ppermute(x, ('row', 'col'), [(at(*s), at(*d)) for s, d in pairs])]
    ppermute x27, starting transfers between devices: 62.7 us -> 70.6 us  [send(): return lax.ppermute(x, ('row', 'col'), [(at(*s), at(*d)) for s, d in pairs])]
    pallas_call x13 -> x12, Pallas kernels: 46.8 us -> 46.3 us  [local(): pl.pallas_call(body, out_shape=out_shape, in_specs=[pl.BlockSpec(memory_s...]
where the time goes in v5:
time: 176 us; the launch traced here: 175 us
  starting transfers between devices  70.6 us (40%)
  waiting for transfers between devices  50.2 us (29%)
  Pallas kernels  48.1 us (27%)
  local copies, waits for them, and re-layouts  5.86 us (3%)
    ppermute x27, starting transfers between devices, send(): return lax.ppermute(x, ('row', 'col'), [(at(*s), at(*d)) for s, d in pairs])  70.6 us
    ppermute x27, waiting for transfers between devices, send(): return lax.ppermute(x, ('row', 'col'), [(at(*s), at(*d)) for s, d in pairs])  50.2 us
    pallas_call x12, Pallas kernels, local(): pl.pallas_call(body, out_shape=out_shape, in_specs=[pl.BlockSpec(memory_s...  46.3 us
    unnamed x4, local copies, waits for them, and re-layouts  5.77 us
  transfers between devices with their start and end apart: 27, of which 8 were waited for; matrix products, arithmetic and copies ran while one was open for 0% of the time, Pallas kernels for 25%

profile of v5, /device:TPU:7, one launch (start us, length us, event | category | flops | bytes accessed | tf_op | source)
XLA Modules:
  0.0 175.2 jit_solution(13175026673947263018)
XLA Ops:
  0.0 4.2 %collective-permute-start = (bf16[512,512]{1,0:T(8,128)(2,1)}, bf16[512,512]{1,0:T(8,128)(2,1)S(1)}, u32[]{:S(2)}, u32[]{:S(2)}) collective-permute-start(bf16[512,512]{1,0:T(8,128)(2,1)} %refs_1_.1), channel_id=1, source_target_pairs={{4,0},{5,1},{6,2},{7,3},{12,8},{13,9},{14,10},{15,11},{16,20},{17,... | collective-permute-start | bytes 1572872 | tf_op jit(solution)/shard_map/ppermute | solution.py:349
  4.2 3.2 %collective-permute-start.1 = (bf16[512,512]{1,0:T(8,128)(2,1)}, bf16[512,512]{1,0:T(8,128)(2,1)S(1)}, u32[]{:S(2)}, u32[]{:S(2)}) collective-permute-start(bf16[512,512]{1,0:T(8,128)(2,1)} %refs_1_.1), channel_id=1, source_target_pairs={{8,10},{9,11},{16,18},{17,19},{18,20},{19,21},{24,26},{25,27},{26,... | collective-permute-start | bytes 1572872 | tf_op jit(solution)/shard_map/ppermute | solution.py:349
  8.9 5.8 %copy-done = bf16[4096,2048]{1,0:T(8,128)(2,1)S(1)} copy-done((bf16[4096,2048]{1,0:T(8,128)(2,1)S(1)}, bf16[4096,2048]{1,0:T(8,128)(2,1)}, u32[]{:S(2)}) %copy-start) | copy-done | bytes 16777240
  16.4 10.7 %collective-permute-done.refs_2_ = bf16[512,512]{1,0:T(8,128)(2,1)S(1)} collective-permute-done((bf16[512,512]{1,0:T(8,128)(2,1)}, bf16[512,512]{1,0:T(8,128)(2,1)S(1)}, u32[]{:S(2)}, u32[]{:S(2)}) %collective-permute-start) | collective-permute-done | bytes 524320 | tf_op jit(solution)/shard_map/ppermute | solution.py:349
  28.4 3.5 %collective-permute-done.2.refs_4_ = bf16[512,512]{1,0:T(8,128)(2,1)S(1)} collective-permute-done((bf16[512,512]{1,0:T(8,128)(2,1)}, bf16[512,512]{1,0:T(8,128)(2,1)S(1)}, u32[]{:S(2)}, u32[]{:S(2)}) %collective-permute-start.2) | collective-permute-done | bytes 524320 | tf_op jit(solution)/shard_map/ppermute | solution.py:349
  31.9 11.2 %collective-permute-done.3.refs_5_ = bf16[512,512]{1,0:T(8,128)(2,1)S(1)} collective-permute-done((bf16[512,512]{1,0:T(8,128)(2,1)S(1)}, bf16[512,512]{1,0:T(8,128)(2,1)S(1)}, u32[]{:S(2)}, u32[]{:S(2)}) %collective-permute-start.3) | collective-permute-done | bytes 524320 | tf_op jit(solution)/shard_map/ppermute | solution.py:349
  43.8 4.1 %collective-permute-start.4 = (bf16[2048,512]{1,0:T(8,128)(2,1)S(1)}, bf16[2048,512]{1,0:T(8,128)(2,1)S(1)}, u32[]{:S(2)}, u32[]{:S(2)}) collective-permute-start(bf16[2048,512]{1,0:T(8,128)(2,1)S(1)} %line.1.refs_1_.refs_3_), channel_id=1, source_target_pairs={{0,1},{1,0},{8,9},{9,8},{10,11},{11,10},{16,17},{17,16},{18,19},{1... | collective-permute-start | bytes 6291464 | tf_op jit(solution)/shard_map/ppermute | solution.py:349
  47.9 3.8 %collective-permute-done.4.refs_2_.refs_4_ = bf16[2048,512]{1,0:T(8,128)(2,1)S(1)} collective-permute-done((bf16[2048,512]{1,0:T(8,128)(2,1)S(1)}, bf16[2048,512]{1,0:T(8,128)(2,1)S(1)}, u32[]{:S(2)}, u32[]{:S(2)}) %collective-permute-start.4) | collective-permute-done | bytes 2097184 | tf_op jit(solution)/shard_map/ppermute | solution.py:349
  53.8 8.8 %mirrored_product.2 = (f32[2048,256]{1,0:T(8,128)S(1)}, bf16[2112,256]{1,0:T(8,128)(2,1)S(1)}) custom-call(s32[5]{0:T(128)S(1)} %stack.23.ids.refs_0_, bf16[4096,2048]{1,0:T(8,128)(2,1)S(1)} %get-tuple-element.43.refs_1_, f32[8,2048]{1,0:T(8,128)S(1)} %get-tuple-element.46.refs_2_, bf16[2048,512]{1,0:T(8,128)(2,1)S(1)} %line.1.refs_1_.refs_3_, ...), custom_call_target="tpu_custom_call" | custom-call | tf_op jit(solution)/shard_map/mirrored_product/pallas_call | solution.py:48
  64.1 8.8 %mirrored_product.3 = (f32[2048,256]{1,0:T(8,128)S(1)}, bf16[2112,256]{1,0:T(8,128)(2,1)S(1)}) custom-call(s32[5]{0:T(128)S(1)} %stack.23.ids.refs_0_, bf16[4096,2048]{1,0:T(8,128)(2,1)S(1)} %get-tuple-element.43.refs_1_, f32[8,2048]{1,0:T(8,128)S(1)} %get-tuple-element.46.refs_2_, bf16[2048,512]{1,0:T(8,128)(2,1)S(1)} %line.1.refs_1_.refs_3_, ...), custom_call_target="tpu_custom_call" | custom-call | tf_op jit(solution)/shard_map/mirrored_product/pallas_call | solution.py:48
  75.8 6.5 %collective-permute-start.13 = (bf16[2112,256]{1,0:T(8,128)(2,1)S(1)}, bf16[2112,256]{1,0:T(8,128)(2,1)S(1)}, u32[]{:S(2)}, u32[]{:S(2)}) collective-permute-start(bf16[2112,256]{1,0:T(8,128)(2,1)S(1)} %get-tuple-element.48.refs_3_), channel_id=1, source_target_pairs={{16,0},{24,8},{9,1},{25,17},{26,10},{18,2},{19,27},{29,21}} | collective-permute-start | bytes 3244040 | tf_op jit(solution)/shard_map/ppermute | solution.py:349
  82.3 2.9 %relay.2 = (f32[2048,256]{1,0:T(8,128)S(1)}, bf16[2112,256]{1,0:T(8,128)(2,1)S(1)}) custom-call(s32[5]{0:T(128)S(1)} %stack.23.ids.refs_0_, f32[2048,256]{1,0:T(8,128)S(1)} %get-tuple-element.52.refs_1_, bf16[2112,256]{1,0:T(8,128)(2,1)S(1)} %collective-permute-done.9.refs_2_, bf16[2112,256]{1,0:T(8,128)(2,1)S(1)} %get-tuple-element.48.refs_3_), custom_call_target="tpu_custom_call" | custom-call | tf_op jit(solution)/shard_map/relay/pallas_call | solution.py:48
  87.3 4.7 %collective-permute-done.8.refs_5_ = bf16[2048,256]{1,0:T(8,128)(2,1)S(1)} collective-permute-done((bf16[2048,256]{1,0:T(8,128)(2,1)S(1)}, bf16[2048,256]{1,0:T(8,128)(2,1)S(1)}, u32[]{:S(2)}, u32[]{:S(2)}) %collective-permute-start.8) | collective-permute-done | bytes 1048608 | tf_op jit(solution)/shard_map/ppermute | solution.py:349
  92.0 6.4 %direct_product.2 = (f32[2048,256]{1,0:T(8,128)S(1)}, f32[1024,256]{1,0:T(8,128)S(1)}, f32[1024,256]{1,0:T(8,128)S(1)}) custom-call(s32[5]{0:T(128)S(1)} %stack.23.ids.refs_0_, bf16[4096,2048]{1,0:T(8,128)(2,1)S(1)} %get-tuple-element.43.refs_1_, bf16[2048,256]{1,0:T(8,128)(2,1)S(1)} %get-tuple-element.50.refs_2_, ...), custom_call_target="tpu_custom_call" | custom-call | tf_op jit(solution)/shard_map/direct_product/pallas_call | solution.py:48
  98.4 3.9 %collective-permute-start.10 = (f32[1024,256]{1,0:T(8,128)S(1)}, f32[1024,256]{1,0:T(8,128)S(1)}, u32[]{:S(2)}, u32[]{:S(2)}) collective-permute-start(f32[1024,256]{1,0:T(8,128)S(1)} %get-tuple-element.55), channel_id=1, source_target_pairs={{0,1},{1,0},{8,9},{9,8},{10,11},{11,10},{16,17},{17,16},{18,19},{1... | collective-permute-start | bytes 3145736 | tf_op jit(solution)/shard_map/ppermute | solution.py:349
  102.3 1.9 %collective-permute-start.11 = (f32[1024,256]{1,0:T(8,128)S(1)}, f32[1024,256]{1,0:T(8,128)S(1)}, u32[]{:S(2)}, u32[]{:S(2)}) collective-permute-start(f32[1024,256]{1,0:T(8,128)S(1)} %get-tuple-element.56), channel_id=1, source_target_pairs={{0,1},{1,0},{8,9},{9,8},{10,11},{11,10},{16,17},{17,16},{18,19},{1... | collective-permute-start | bytes 3145736 | tf_op jit(solution)/shard_map/ppermute | solution.py:349
  104.2 6.6 %direct_product.3 = (f32[2048,256]{1,0:T(8,128)S(1)}, f32[1024,256]{1,0:T(8,128)S(1)}, f32[1024,256]{1,0:T(8,128)S(1)}) custom-call(s32[5]{0:T(128)S(1)} %stack.23.ids.refs_0_, bf16[4096,2048]{1,0:T(8,128)(2,1)S(1)} %get-tuple-element.43.refs_1_, bf16[2048,256]{1,0:T(8,128)(2,1)S(1)} %get-tuple-element.59.refs_2_, ...), custom_call_target="tpu_custom_call" | custom-call | tf_op jit(solution)/shard_map/direct_product/pallas_call | solution.py:48
  110.8 2.9 %relay.3 = (f32[2048,256]{1,0:T(8,128)S(1)}, bf16[2112,256]{1,0:T(8,128)(2,1)S(1)}) custom-call(s32[5]{0:T(128)S(1)} %stack.23.ids.refs_0_, f32[2048,256]{1,0:T(8,128)S(1)} %get-tuple-element.58.refs_1_, bf16[2112,256]{1,0:T(8,128)(2,1)S(1)} %collective-permute-done.13.refs_2_, f32[2048,256]{1,0:T(8,128)S(1)} %get-tuple-element.70.refs_3_.refs_1_, ...), custom_call_target="tpu_custom_call" | custom-call | tf_op jit(solution)/shard_map/relay/pallas_call | solution.py:48
  114.5 2.9 %collective-permute-start.20 = (f32[1024,256]{1,0:T(8,128)S(1)}, f32[1024,256]{1,0:T(8,128)S(1)}, u32[]{:S(2)}, u32[]{:S(2)}) collective-permute-start(f32[1024,256]{1,0:T(8,128)S(1)} %get-tuple-element.71), channel_id=1, source_target_pairs={{0,1},{1,0},{8,9},{9,8},{10,11},{11,10},{16,17},{17,16},{18,19},{1... | collective-permute-start | bytes 3145736 | tf_op jit(solution)/shard_map/ppermute | solution.py:349
  117.4 1.9 %collective-permute-start.21 = (f32[1024,256]{1,0:T(8,128)S(1)}, f32[1024,256]{1,0:T(8,128)S(1)}, u32[]{:S(2)}, u32[]{:S(2)}) collective-permute-start(f32[1024,256]{1,0:T(8,128)S(1)} %get-tuple-element.72), channel_id=1, source_target_pairs={{0,1},{1,0},{8,9},{9,8},{10,11},{11,10},{16,17},{17,16},{18,19},{1... | collective-permute-start | bytes 3145736 | tf_op jit(solution)/shard_map/ppermute | solution.py:349
  119.4 2.1 %pack.2 = (f32[512,256]{1,0:T(8,128)S(1)}, bf16[528,256]{1,0:T(8,128)(2,1)S(1)}, bf16[528,256]{1,0:T(8,128)(2,1)S(1)}, bf16[528,256]{1,0:T(8,128)(2,1)S(1)}, bf16[528,256]{1,0:T(8,128)(2,1)S(1)}) custom-call(s32[5]{0:T(128)S(1)} %stack.23.ids.refs_0_, f32[2048,256]{1,0:T(8,128)S(1)} %get-tuple-element.54.refs_6_.refs_1_, ...), custom_call_target="tpu_custom_call" | custom-call | tf_op jit(solution)/shard_map/pack/pallas_call | solution.py:48
  121.5 3.4 %collective-permute-start.16 = (bf16[528,256]{1,0:T(8,128)(2,1)S(1)}, bf16[528,256]{1,0:T(8,128)(2,1)S(1)}, u32[]{:S(2)}, u32[]{:S(2)}) collective-permute-start(bf16[528,256]{1,0:T(8,128)(2,1)S(1)} %get-tuple-element.64), channel_id=1, source_target_pairs={{1,4},{9,12},{10,9},{11,13},{17,20},{18,17},{19,21},{20,18},{21,22... | collective-permute-start | bytes 811016 | tf_op jit(solution)/shard_map/ppermute | solution.py:349
  126.8 2.5 %collective-permute-done.16.refs_3_ = bf16[528,256]{1,0:T(8,128)(2,1)S(1)} collective-permute-done((bf16[528,256]{1,0:T(8,128)(2,1)S(1)}, bf16[528,256]{1,0:T(8,128)(2,1)S(1)}, u32[]{:S(2)}, u32[]{:S(2)}) %collective-permute-start.16) | collective-permute-done | bytes 270368 | tf_op jit(solution)/shard_map/ppermute | solution.py:349
  129.3 2.7 %collective-permute-start.18 = (bf16[528,256]{1,0:T(8,128)(2,1)S(1)}, bf16[528,256]{1,0:T(8,128)(2,1)S(1)}, u32[]{:S(2)}, u32[]{:S(2)}) collective-permute-start(bf16[528,256]{1,0:T(8,128)(2,1)S(1)} %get-tuple-element.68), channel_id=1, source_target_pairs={{0,2},{1,6},{8,10},{9,14},{10,11},{11,15},{16,18},{17,22},{18,19},... | collective-permute-start | bytes 811016 | tf_op jit(solution)/shard_map/ppermute | solution.py:349
  132.0 11.5 %collective-permute-start.19 = (bf16[528,256]{1,0:T(8,128)(2,1)S(1)}, bf16[528,256]{1,0:T(8,128)(2,1)S(1)}, u32[]{:S(2)}, u32[]{:S(2)}) collective-permute-start(bf16[528,256]{1,0:T(8,128)(2,1)S(1)} %get-tuple-element.69), channel_id=1, source_target_pairs={{0,3},{1,7},{8,11},{9,15},{10,8},{11,12},{16,19},{17,23},{18,16},{... | collective-permute-start | bytes 811016 | tf_op jit(solution)/shard_map/ppermute | solution.py:349
  143.6 2.1 %pack.3 = (f32[512,256]{1,0:T(8,128)S(1)}, bf16[528,256]{1,0:T(8,128)(2,1)S(1)}, bf16[528,256]{1,0:T(8,128)(2,1)S(1)}, bf16[528,256]{1,0:T(8,128)(2,1)S(1)}, bf16[528,256]{1,0:T(8,128)(2,1)S(1)}) custom-call(s32[5]{0:T(128)S(1)} %stack.23.ids.refs_0_, f32[2048,256]{1,0:T(8,128)S(1)} %get-tuple-element.70.refs_3_.refs_1_, ...), custom_call_target="tpu_custom_call" | custom-call | tf_op jit(solution)/shard_map/pack/pallas_call | solution.py:48
  147.6 4.5 %collective-permute-start.24 = (bf16[528,256]{1,0:T(8,128)(2,1)S(1)}, bf16[528,256]{1,0:T(8,128)(2,1)S(1)}, u32[]{:S(2)}, u32[]{:S(2)}) collective-permute-start(bf16[528,256]{1,0:T(8,128)(2,1)S(1)} %get-tuple-element.76), channel_id=1, source_target_pairs={{0,1},{1,5},{8,9},{9,13},{11,14},{16,17},{17,21},{19,22},{20,19},{... | collective-permute-start | bytes 811016 | tf_op jit(solution)/shard_map/ppermute | solution.py:349
  152.1 1.9 %collective-permute-start.25 = (bf16[528,256]{1,0:T(8,128)(2,1)S(1)}, bf16[528,256]{1,0:T(8,128)(2,1)S(1)}, u32[]{:S(2)}, u32[]{:S(2)}) collective-permute-start(bf16[528,256]{1,0:T(8,128)(2,1)S(1)} %get-tuple-element.77), channel_id=1, source_target_pairs={{0,2},{1,6},{8,10},{9,14},{10,11},{11,15},{16,18},{17,22},{18,19},... | collective-permute-start | bytes 811016 | tf_op jit(solution)/shard_map/ppermute | solution.py:349
  154.0 3.1 %collective-permute-start.26 = (bf16[528,256]{1,0:T(8,128)(2,1)S(1)}, bf16[528,256]{1,0:T(8,128)(2,1)S(1)}, u32[]{:S(2)}, u32[]{:S(2)}) collective-permute-start(bf16[528,256]{1,0:T(8,128)(2,1)S(1)} %get-tuple-element.78), channel_id=1, source_target_pairs={{0,3},{1,7},{8,11},{9,15},{10,8},{11,12},{16,19},{17,23},{18,16},{... | collective-permute-start | bytes 811016 | tf_op jit(solution)/shard_map/ppermute | solution.py:349
  158.7 6.9 %collective-permute-done.25.refs_5_ = bf16[528,256]{1,0:T(8,128)(2,1)S(1)} collective-permute-done((bf16[528,256]{1,0:T(8,128)(2,1)S(1)}, bf16[528,256]{1,0:T(8,128)(2,1)S(1)}, u32[]{:S(2)}, u32[]{:S(2)}) %collective-permute-start.25) | collective-permute-done | bytes 270368 | tf_op jit(solution)/shard_map/ppermute | solution.py:349
  165.7 6.9 %collective-permute-done.26.refs_6_ = bf16[528,256]{1,0:T(8,128)(2,1)S(1)} collective-permute-done((bf16[528,256]{1,0:T(8,128)(2,1)S(1)}, bf16[528,256]{1,0:T(8,128)(2,1)S(1)}, u32[]{:S(2)}, u32[]{:S(2)}) %collective-permute-start.26) | collective-permute-done | bytes 270368 | tf_op jit(solution)/shard_map/ppermute | solution.py:349
  172.6 2.6 %finish.3 = f32[512,512]{1,0:T(8,128)} custom-call(s32[5]{0:T(128)S(1)} %stack.23.ids.refs_0_, f32[512,256]{1,0:T(8,128)S(1)} %finish.2.refs_1_, f32[512,256]{1,0:T(8,128)S(1)} %get-tuple-element.74.refs_7_.refs_2_, bf16[528,256]{1,0:T(8,128)(2,1)S(1)} %collective-permute-done.23.refs_3_, bf16[528,256]{1,0:T(8,128)(2,1)S(1)} %collective-permute-done.24.refs_4_, ...), custom_call_target="tpu_custom_call" | custom-call | tf_op jit(solution)/shard_map/finish/pallas_call | solution.py:48
  (40 shorter events, 19.6 us)
Async XLA Ops:
  0.0 27.1 %collective-permute-start = (bf16[512,512]{1,0:T(8,128)(2,1)}, bf16[512,512]{1,0:T(8,128)(2,1)S(1)}, u32[]{:S(2)}, u32[]{:S(2)}) collective-permute-start(bf16[512,512]{1,0:T(8,128)(2,1)} %refs_1_.1), channel_id=1, source_target_pairs={{4,0},{5,1},{6,2},{7,3},{12,8},{13,9},{14,10},{15,11},{16,20},{17,... | collective-permute-start | bytes 1572872 | tf_op jit(solution)/shard_map/ppermute | solution.py:349
  4.2 24.2 %collective-permute-start.1 = (bf16[512,512]{1,0:T(8,128)(2,1)}, bf16[512,512]{1,0:T(8,128)(2,1)S(1)}, u32[]{:S(2)}, u32[]{:S(2)}) collective-permute-start(bf16[512,512]{1,0:T(8,128)(2,1)} %refs_1_.1), channel_id=1, source_target_pairs={{8,10},{9,11},{16,18},{17,19},{18,20},{19,21},{24,26},{25,27},{26,... | collective-permute-start | bytes 1572872 | tf_op jit(solution)/shard_map/ppermute | solution.py:349
  7.5 24.4 %collective-permute-start.2 = (bf16[512,512]{1,0:T(8,128)(2,1)}, bf16[512,512]{1,0:T(8,128)(2,1)S(1)}, u32[]{:S(2)}, u32[]{:S(2)}) collective-permute-start(bf16[512,512]{1,0:T(8,128)(2,1)} %refs_1_.1), channel_id=1, source_target_pairs={{2,0},{3,1},{10,8},{11,9},{12,10},{13,11},{18,16},{19,17},{20,18},... | collective-permute-start | bytes 1572872 | tf_op jit(solution)/shard_map/ppermute | solution.py:349
  8.9 5.8 %copy-start = (bf16[4096,2048]{1,0:T(8,128)(2,1)S(1)}, bf16[4096,2048]{1,0:T(8,128)(2,1)}, u32[]{:S(2)}) copy-start(bf16[4096,2048]{1,0:T(8,128)(2,1)} %a_ref.1) | copy-start | bytes 50331652
  14.6 28.5 %copy-start.1 = (bf16[512,512]{1,0:T(8,128)(2,1)S(1)}, bf16[512,512]{1,0:T(8,128)(2,1)}, u32[]{:S(2)}) copy-start(bf16[512,512]{1,0:T(8,128)(2,1)} %refs_1_.1) | copy-start | bytes 1572868
  27.1 16.0 %collective-permute-start.3 = (bf16[512,512]{1,0:T(8,128)(2,1)S(1)}, bf16[512,512]{1,0:T(8,128)(2,1)S(1)}, u32[]{:S(2)}, u32[]{:S(2)}) collective-permute-start(bf16[512,512]{1,0:T(8,128)(2,1)S(1)} %collective-permute-done.refs_2_), channel_id=1, source_target_pairs={{2,0},{3,1},{10,8},{11,9},{18,16},{19,17},{26,24},{27,25},{28,30},... | collective-permute-start | bytes 1572872 | tf_op jit(solution)/shard_map/ppermute | solution.py:349
  43.8 7.8 %collective-permute-start.4 = (bf16[2048,512]{1,0:T(8,128)(2,1)S(1)}, bf16[2048,512]{1,0:T(8,128)(2,1)S(1)}, u32[]{:S(2)}, u32[]{:S(2)}) collective-permute-start(bf16[2048,512]{1,0:T(8,128)(2,1)S(1)} %line.1.refs_1_.refs_3_), channel_id=1, source_target_pairs={{0,1},{1,0},{8,9},{9,8},{10,11},{11,10},{16,17},{17,16},{18,19},{1... | collective-permute-start | bytes 6291464 | tf_op jit(solution)/shard_map/ppermute | solution.py:349
  52.4 20.6 %collective-permute-start.5 = (bf16[2048,256]{1,0:T(8,128)(2,1)S(1)}, bf16[2048,256]{1,0:T(8,128)(2,1)S(1)}, u32[]{:S(2)}, u32[]{:S(2)}) collective-permute-start(bf16[2048,256]{1,0:T(8,128)(2,1)S(1)} %get-tuple-element.50.refs_2_), channel_id=1, source_target_pairs={{0,8},{1,17},{10,2},{11,27},{20,28}} | collective-permute-start | bytes 3145736 | tf_op jit(solution)/shard_map/ppermute | solution.py:349
  53.1 19.9 %collective-permute-start.6 = (bf16[2048,256]{1,0:T(8,128)(2,1)S(1)}, bf16[2048,256]{1,0:T(8,128)(2,1)S(1)}, u32[]{:S(2)}, u32[]{:S(2)}) collective-permute-start(bf16[2048,256]{1,0:T(8,128)(2,1)S(1)} %get-tuple-element.59.refs_2_), channel_id=1, source_target_pairs={{0,8},{1,17},{10,2},{11,27},{20,28}} | collective-permute-start | bytes 3145736 | tf_op jit(solution)/shard_map/ppermute | solution.py:349
  62.7 19.6 %collective-permute-start.9 = (bf16[2112,256]{1,0:T(8,128)(2,1)S(1)}, bf16[2112,256]{1,0:T(8,128)(2,1)S(1)}, u32[]{:S(2)}, u32[]{:S(2)}) collective-permute-start(bf16[2112,256]{1,0:T(8,128)(2,1)S(1)} %get-tuple-element.47.refs_5_), channel_id=1, source_target_pairs={{16,0},{24,8},{9,1},{25,17},{26,10},{18,2},{19,27},{29,21}} | collective-permute-start | bytes 3244040 | tf_op jit(solution)/shard_map/ppermute | solution.py:349
  73.0 13.0 %collective-permute-start.7 = (bf16[2048,256]{1,0:T(8,128)(2,1)S(1)}, bf16[2048,256]{1,0:T(8,128)(2,1)S(1)}, u32[]{:S(2)}, u32[]{:S(2)}) collective-permute-start(bf16[2048,256]{1,0:T(8,128)(2,1)S(1)} %get-tuple-element.50.refs_2_), channel_id=1, source_target_pairs={{0,16},{1,9},{10,26},{21,29}} | collective-permute-start | bytes 3145736 | tf_op jit(solution)/shard_map/ppermute | solution.py:349
  73.7 18.2 %collective-permute-start.8 = (bf16[2048,256]{1,0:T(8,128)(2,1)S(1)}, bf16[2048,256]{1,0:T(8,128)(2,1)S(1)}, u32[]{:S(2)}, u32[]{:S(2)}) collective-permute-start(bf16[2048,256]{1,0:T(8,128)(2,1)S(1)} %collective-permute-done.5.refs_3_), channel_id=1, source_target_pairs={{8,24},{17,25},{2,18},{27,19}} | collective-permute-start | bytes 3145736 | tf_op jit(solution)/shard_map/ppermute | solution.py:349
  75.0 27.3 %collective-permute-start.14 = (bf16[2048,256]{1,0:T(8,128)(2,1)S(1)}, bf16[2048,256]{1,0:T(8,128)(2,1)S(1)}, u32[]{:S(2)}, u32[]{:S(2)}) collective-permute-start(bf16[2048,256]{1,0:T(8,128)(2,1)S(1)} %get-tuple-element.59.refs_2_), channel_id=1, source_target_pairs={{0,16},{1,9},{10,26},{21,29}} | collective-permute-start | bytes 3145736 | tf_op jit(solution)/shard_map/ppermute | solution.py:349
  75.8 35.1 %collective-permute-start.13 = (bf16[2112,256]{1,0:T(8,128)(2,1)S(1)}, bf16[2112,256]{1,0:T(8,128)(2,1)S(1)}, u32[]{:S(2)}, u32[]{:S(2)}) collective-permute-start(bf16[2112,256]{1,0:T(8,128)(2,1)S(1)} %get-tuple-element.48.refs_3_), channel_id=1, source_target_pairs={{16,0},{24,8},{9,1},{25,17},{26,10},{18,2},{19,27},{29,21}} | collective-permute-start | bytes 3244040 | tf_op jit(solution)/shard_map/ppermute | solution.py:349
  85.2 25.6 %collective-permute-start.12 = (bf16[2112,256]{1,0:T(8,128)(2,1)S(1)}, bf16[2112,256]{1,0:T(8,128)(2,1)S(1)}, u32[]{:S(2)}, u32[]{:S(2)}) collective-permute-start(bf16[2112,256]{1,0:T(8,128)(2,1)S(1)} %get-tuple-element.53.refs_6_), channel_id=1, source_target_pairs={{8,0},{17,1},{2,10},{27,11},{28,20}} | collective-permute-start | bytes 3244040 | tf_op jit(solution)/shard_map/ppermute | solution.py:349
  86.0 18.3 %collective-permute-start.15 = (bf16[2048,256]{1,0:T(8,128)(2,1)S(1)}, bf16[2048,256]{1,0:T(8,128)(2,1)S(1)}, u32[]{:S(2)}, u32[]{:S(2)}) collective-permute-start(bf16[2048,256]{1,0:T(8,128)(2,1)S(1)} %collective-permute-done.6.refs_3_), channel_id=1, source_target_pairs={{8,24},{17,25},{2,18},{27,19}} | collective-permute-start | bytes 3145736 | tf_op jit(solution)/shard_map/ppermute | solution.py:349
  98.4 21.0 %collective-permute-start.10 = (f32[1024,256]{1,0:T(8,128)S(1)}, f32[1024,256]{1,0:T(8,128)S(1)}, u32[]{:S(2)}, u32[]{:S(2)}) collective-permute-start(f32[1024,256]{1,0:T(8,128)S(1)} %get-tuple-element.55), channel_id=1, source_target_pairs={{0,1},{1,0},{8,9},{9,8},{10,11},{11,10},{16,17},{17,16},{18,19},{1... | collective-permute-start | bytes 3145736 | tf_op jit(solution)/shard_map/ppermute | solution.py:349
  102.3 17.0 %collective-permute-start.11 = (f32[1024,256]{1,0:T(8,128)S(1)}, f32[1024,256]{1,0:T(8,128)S(1)}, u32[]{:S(2)}, u32[]{:S(2)}) collective-permute-start(f32[1024,256]{1,0:T(8,128)S(1)} %get-tuple-element.56), channel_id=1, source_target_pairs={{0,1},{1,0},{8,9},{9,8},{10,11},{11,10},{16,17},{17,16},{18,19},{1... | collective-permute-start | bytes 3145736 | tf_op jit(solution)/shard_map/ppermute | solution.py:349
  113.8 29.8 %collective-permute-start.22 = (bf16[2112,256]{1,0:T(8,128)(2,1)S(1)}, bf16[2112,256]{1,0:T(8,128)(2,1)S(1)}, u32[]{:S(2)}, u32[]{:S(2)}) collective-permute-start(bf16[2112,256]{1,0:T(8,128)(2,1)S(1)} %get-tuple-element.62.refs_6_), channel_id=1, source_target_pairs={{8,0},{17,1},{2,10},{27,11},{28,20}} | collective-permute-start | bytes 3244040 | tf_op jit(solution)/shard_map/ppermute | solution.py:349
  114.5 29.0 %collective-permute-start.20 = (f32[1024,256]{1,0:T(8,128)S(1)}, f32[1024,256]{1,0:T(8,128)S(1)}, u32[]{:S(2)}, u32[]{:S(2)}) collective-permute-start(f32[1024,256]{1,0:T(8,128)S(1)} %get-tuple-element.71), channel_id=1, source_target_pairs={{0,1},{1,0},{8,9},{9,8},{10,11},{11,10},{16,17},{17,16},{18,19},{1... | collective-permute-start | bytes 3145736 | tf_op jit(solution)/shard_map/ppermute | solution.py:349
  117.4 26.1 %collective-permute-start.21 = (f32[1024,256]{1,0:T(8,128)S(1)}, f32[1024,256]{1,0:T(8,128)S(1)}, u32[]{:S(2)}, u32[]{:S(2)}) collective-permute-start(f32[1024,256]{1,0:T(8,128)S(1)} %get-tuple-element.72), channel_id=1, source_target_pairs={{0,1},{1,0},{8,9},{9,8},{10,11},{11,10},{16,17},{17,16},{18,19},{1... | collective-permute-start | bytes 3145736 | tf_op jit(solution)/shard_map/ppermute | solution.py:349
  121.5 7.8 %collective-permute-start.16 = (bf16[528,256]{1,0:T(8,128)(2,1)S(1)}, bf16[528,256]{1,0:T(8,128)(2,1)S(1)}, u32[]{:S(2)}, u32[]{:S(2)}) collective-permute-start(bf16[528,256]{1,0:T(8,128)(2,1)S(1)} %get-tuple-element.64), channel_id=1, source_target_pairs={{1,4},{9,12},{10,9},{11,13},{17,20},{18,17},{19,21},{20,18},{21,22... | collective-permute-start | bytes 811016 | tf_op jit(solution)/shard_map/ppermute | solution.py:349
  124.9 7.1 %collective-permute-start.17 = (bf16[528,256]{1,0:T(8,128)(2,1)S(1)}, bf16[528,256]{1,0:T(8,128)(2,1)S(1)}, u32[]{:S(2)}, u32[]{:S(2)}) collective-permute-start(bf16[528,256]{1,0:T(8,128)(2,1)S(1)} %get-tuple-element.65), channel_id=1, source_target_pairs={{0,1},{1,5},{8,9},{9,13},{11,14},{16,17},{17,21},{19,22},{20,19},{... | collective-permute-start | bytes 811016 | tf_op jit(solution)/shard_map/ppermute | solution.py:349
  129.3 24.7 %collective-permute-start.18 = (bf16[528,256]{1,0:T(8,128)(2,1)S(1)}, bf16[528,256]{1,0:T(8,128)(2,1)S(1)}, u32[]{:S(2)}, u32[]{:S(2)}) collective-permute-start(bf16[528,256]{1,0:T(8,128)(2,1)S(1)} %get-tuple-element.68), channel_id=1, source_target_pairs={{0,2},{1,6},{8,10},{9,14},{10,11},{11,15},{16,18},{17,22},{18,19},... | collective-permute-start | bytes 811016 | tf_op jit(solution)/shard_map/ppermute | solution.py:349
  132.0 25.1 %collective-permute-start.19 = (bf16[528,256]{1,0:T(8,128)(2,1)S(1)}, bf16[528,256]{1,0:T(8,128)(2,1)S(1)}, u32[]{:S(2)}, u32[]{:S(2)}) collective-permute-start(bf16[528,256]{1,0:T(8,128)(2,1)S(1)} %get-tuple-element.69), channel_id=1, source_target_pairs={{0,3},{1,7},{8,11},{9,15},{10,8},{11,12},{16,19},{17,23},{18,16},{... | collective-permute-start | bytes 811016 | tf_op jit(solution)/shard_map/ppermute | solution.py:349
  145.7 13.0 %collective-permute-start.23 = (bf16[528,256]{1,0:T(8,128)(2,1)S(1)}, bf16[528,256]{1,0:T(8,128)(2,1)S(1)}, u32[]{:S(2)}, u32[]{:S(2)}) collective-permute-start(bf16[528,256]{1,0:T(8,128)(2,1)S(1)} %get-tuple-element.75), channel_id=1, source_target_pairs={{1,4},{9,12},{10,9},{11,13},{17,20},{18,17},{19,21},{20,18},{21,22... | collective-permute-start | bytes 811016 | tf_op jit(solution)/shard_map/ppermute | solution.py:349
  147.6 11.1 %collective-permute-start.24 = (bf16[528,256]{1,0:T(8,128)(2,1)S(1)}, bf16[528,256]{1,0:T(8,128)(2,1)S(1)}, u32[]{:S(2)}, u32[]{:S(2)}) collective-permute-start(bf16[528,256]{1,0:T(8,128)(2,1)S(1)} %get-tuple-element.76), channel_id=1, source_target_pairs={{0,1},{1,5},{8,9},{9,13},{11,14},{16,17},{17,21},{19,22},{20,19},{... | collective-permute-start | bytes 811016 | tf_op jit(solution)/shard_map/ppermute | solution.py:349
  152.1 13.6 %collective-permute-start.25 = (bf16[528,256]{1,0:T(8,128)(2,1)S(1)}, bf16[528,256]{1,0:T(8,128)(2,1)S(1)}, u32[]{:S(2)}, u32[]{:S(2)}) collective-permute-start(bf16[528,256]{1,0:T(8,128)(2,1)S(1)} %get-tuple-element.77), channel_id=1, source_target_pairs={{0,2},{1,6},{8,10},{9,14},{10,11},{11,15},{16,18},{17,22},{18,19},... | collective-permute-start | bytes 811016 | tf_op jit(solution)/shard_map/ppermute | solution.py:349
  154.0 18.6 %collective-permute-start.26 = (bf16[528,256]{1,0:T(8,128)(2,1)S(1)}, bf16[528,256]{1,0:T(8,128)(2,1)S(1)}, u32[]{:S(2)}, u32[]{:S(2)}) collective-permute-start(bf16[528,256]{1,0:T(8,128)(2,1)S(1)} %get-tuple-element.78), channel_id=1, source_target_pairs={{0,3},{1,7},{8,11},{9,15},{10,8},{11,12},{16,19},{17,23},{18,16},{... | collective-permute-start | bytes 811016 | tf_op jit(solution)/shard_map/ppermute | solution.py:349

commit v6 on v5

--- a/solution.py
+++ b/solution.py
@@ -460,11 +460,11 @@
     partial_a, to_a, relayed = relaying(partial_a, to_a, [], [message_b])
     keep_a, *give_a = direct_product(ids, matrix, panels_a, [relayed])
     got_a = [send(x, swap) for x in give_a]
-    keep_b, *give_b = direct_product(ids, matrix, panels_b, [keep_a])
+    partial_b, to_b, relayed = relaying(partial_b, to_b, [], [keep_a, to_a, panels_b[2]])
+    arrays_a = deliver(keep_a, got_a, partial_a, to_a, [relayed, *panels_b[3:]])
+    keep_b, *give_b = direct_product(ids, matrix, panels_b, [arrays_a[0]])
+    give_b, to_b, *arrays_a[1:3] = lax.optimization_barrier((give_b, to_b, *arrays_a[1:3]))
     got_b = [send(x, swap) for x in give_b]
-    partial_b, to_b, relayed = relaying(partial_b, to_b, [], [keep_b, to_a])
-    arrays_a = deliver(keep_a, got_a, partial_a, to_a, [relayed])
-    keep_b, *arrays_a[1:3] = lax.optimization_barrier((keep_b, *arrays_a[1:3]))
     arrays_b = deliver(keep_b, got_b, partial_b, to_b, [])
     result = finish(ids, None, arrays_a, [arrays_b[0]])
     return finish(ids, result, arrays_b, [])

time: 176 us -> 173 us (0.983)
  starting transfers between devices: 70.6 us -> 60.5 us
  waiting for transfers between devices: 50.2 us -> 57.8 us
    ppermute x27, starting transfers between devices: 70.6 us -> 60.5 us  [send(): return lax.ppermute(x, ('row', 'col'), [(at(*s), at(*d)) for s, d in pairs])]
    ppermute x27, waiting for transfers between devices: 50.2 us -> 57.8 us  [send(): return lax.ppermute(x, ('row', 'col'), [(at(*s), at(*d)) for s, d in pairs])]
  transfers between devices with their start and end apart: 27 -> 27, of which waited for: 8 -> 9; matrix products, arithmetic and copies ran while one was open for 0% -> 0% of each run, Pallas kernels for 25% -> 26%
where the time goes in v6:
time: 173 us
  starting transfers between devices  60.5 us (35%)
  waiting for transfers between devices  57.8 us (33%)
  Pallas kernels  48.1 us (28%)
  local copies, waits for them, and re-layouts  5.86 us (3%)
    ppermute x27, starting transfers between devices, send(): return lax.ppermute(x, ('row', 'col'), [(at(*s), at(*d)) for s, d in pairs])  60.5 us
    ppermute x27, waiting for transfers between devices, send(): return lax.ppermute(x, ('row', 'col'), [(at(*s), at(*d)) for s, d in pairs])  57.8 us
    pallas_call x12, Pallas kernels, local(): pl.pallas_call(body, out_shape=out_shape, in_specs=[pl.BlockSpec(memory_s...  46.3 us
    unnamed x4, local copies, waits for them, and re-layouts  5.77 us
  transfers between devices with their start and end apart: 27, of which 9 were waited for; matrix products, arithmetic and copies ran while one was open for 0% of the time, Pallas kernels for 26%

profile of v6, /device:TPU:7, one launch (start us, length us, event | category | flops | bytes accessed | tf_op | source)
XLA Modules:
  0.0 172.6 jit_solution(5182600279740756190)
XLA Ops:
  0.0 4.2 %collective-permute-start = (bf16[512,512]{1,0:T(8,128)(2,1)}, bf16[512,512]{1,0:T(8,128)(2,1)S(1)}, u32[]{:S(2)}, u32[]{:S(2)}) collective-permute-start(bf16[512,512]{1,0:T(8,128)(2,1)} %refs_1_.1), channel_id=1, source_target_pairs={{4,0},{5,1},{6,2},{7,3},{12,8},{13,9},{14,10},{15,11},{16,20},{17,... | collective-permute-start | bytes 1572872 | tf_op jit(solution)/shard_map/ppermute | solution.py:349
  4.2 3.2 %collective-permute-start.1 = (bf16[512,512]{1,0:T(8,128)(2,1)}, bf16[512,512]{1,0:T(8,128)(2,1)S(1)}, u32[]{:S(2)}, u32[]{:S(2)}) collective-permute-start(bf16[512,512]{1,0:T(8,128)(2,1)} %refs_1_.1), channel_id=1, source_target_pairs={{8,10},{9,11},{16,18},{17,19},{18,20},{19,21},{24,26},{25,27},{26,... | collective-permute-start | bytes 1572872 | tf_op jit(solution)/shard_map/ppermute | solution.py:349
  8.9 5.8 %copy-done = bf16[4096,2048]{1,0:T(8,128)(2,1)S(1)} copy-done((bf16[4096,2048]{1,0:T(8,128)(2,1)S(1)}, bf16[4096,2048]{1,0:T(8,128)(2,1)}, u32[]{:S(2)}) %copy-start) | copy-done | bytes 16777240
  16.4 10.7 %collective-permute-done.refs_2_ = bf16[512,512]{1,0:T(8,128)(2,1)S(1)} collective-permute-done((bf16[512,512]{1,0:T(8,128)(2,1)}, bf16[512,512]{1,0:T(8,128)(2,1)S(1)}, u32[]{:S(2)}, u32[]{:S(2)}) %collective-permute-start) | collective-permute-done | bytes 524320 | tf_op jit(solution)/shard_map/ppermute | solution.py:349
  28.4 3.5 %collective-permute-done.2.refs_4_ = bf16[512,512]{1,0:T(8,128)(2,1)S(1)} collective-permute-done((bf16[512,512]{1,0:T(8,128)(2,1)}, bf16[512,512]{1,0:T(8,128)(2,1)S(1)}, u32[]{:S(2)}, u32[]{:S(2)}) %collective-permute-start.2) | collective-permute-done | bytes 524320 | tf_op jit(solution)/shard_map/ppermute | solution.py:349
  31.9 11.2 %collective-permute-done.3.refs_5_ = bf16[512,512]{1,0:T(8,128)(2,1)S(1)} collective-permute-done((bf16[512,512]{1,0:T(8,128)(2,1)S(1)}, bf16[512,512]{1,0:T(8,128)(2,1)S(1)}, u32[]{:S(2)}, u32[]{:S(2)}) %collective-permute-start.3) | collective-permute-done | bytes 524320 | tf_op jit(solution)/shard_map/ppermute | solution.py:349
  43.8 4.1 %collective-permute-start.4 = (bf16[2048,512]{1,0:T(8,128)(2,1)S(1)}, bf16[2048,512]{1,0:T(8,128)(2,1)S(1)}, u32[]{:S(2)}, u32[]{:S(2)}) collective-permute-start(bf16[2048,512]{1,0:T(8,128)(2,1)S(1)} %line.1.refs_1_.refs_3_), channel_id=1, source_target_pairs={{0,1},{1,0},{8,9},{9,8},{10,11},{11,10},{16,17},{17,16},{18,19},{1... | collective-permute-start | bytes 6291464 | tf_op jit(solution)/shard_map/ppermute | solution.py:349
  47.9 3.8 %collective-permute-done.4.refs_2_.refs_4_ = bf16[2048,512]{1,0:T(8,128)(2,1)S(1)} collective-permute-done((bf16[2048,512]{1,0:T(8,128)(2,1)S(1)}, bf16[2048,512]{1,0:T(8,128)(2,1)S(1)}, u32[]{:S(2)}, u32[]{:S(2)}) %collective-permute-start.4) | collective-permute-done | bytes 2097184 | tf_op jit(solution)/shard_map/ppermute | solution.py:349
  53.8 8.8 %mirrored_product.2 = (f32[2048,256]{1,0:T(8,128)S(1)}, bf16[2112,256]{1,0:T(8,128)(2,1)S(1)}) custom-call(s32[5]{0:T(128)S(1)} %stack.23.ids.refs_0_, bf16[4096,2048]{1,0:T(8,128)(2,1)S(1)} %get-tuple-element.45.refs_1_, f32[8,2048]{1,0:T(8,128)S(1)} %get-tuple-element.48.refs_2_, bf16[2048,512]{1,0:T(8,128)(2,1)S(1)} %line.1.refs_1_.refs_3_, ...), custom_call_target="tpu_custom_call" | custom-call | tf_op jit(solution)/shard_map/mirrored_product/pallas_call | solution.py:48
  64.1 8.8 %mirrored_product.3 = (f32[2048,256]{1,0:T(8,128)S(1)}, bf16[2112,256]{1,0:T(8,128)(2,1)S(1)}) custom-call(s32[5]{0:T(128)S(1)} %stack.23.ids.refs_0_, bf16[4096,2048]{1,0:T(8,128)(2,1)S(1)} %get-tuple-element.45.refs_1_, f32[8,2048]{1,0:T(8,128)S(1)} %get-tuple-element.48.refs_2_, bf16[2048,512]{1,0:T(8,128)(2,1)S(1)} %line.1.refs_1_.refs_3_, ...), custom_call_target="tpu_custom_call" | custom-call | tf_op jit(solution)/shard_map/mirrored_product/pallas_call | solution.py:48
  76.4 2.9 %relay.2 = (f32[2048,256]{1,0:T(8,128)S(1)}, bf16[2112,256]{1,0:T(8,128)(2,1)S(1)}) custom-call(s32[5]{0:T(128)S(1)} %stack.23.ids.refs_0_, f32[2048,256]{1,0:T(8,128)S(1)} %get-tuple-element.54.refs_1_, bf16[2112,256]{1,0:T(8,128)(2,1)S(1)} %collective-permute-done.9.refs_2_, bf16[2112,256]{1,0:T(8,128)(2,1)S(1)} %get-tuple-element.50.refs_3_), custom_call_target="tpu_custom_call" | custom-call | tf_op jit(solution)/shard_map/relay/pallas_call | solution.py:48
  82.1 9.8 %collective-permute-done.8.refs_5_ = bf16[2048,256]{1,0:T(8,128)(2,1)S(1)} collective-permute-done((bf16[2048,256]{1,0:T(8,128)(2,1)S(1)}, bf16[2048,256]{1,0:T(8,128)(2,1)S(1)}, u32[]{:S(2)}, u32[]{:S(2)}) %collective-permute-start.8) | collective-permute-done | bytes 1048608 | tf_op jit(solution)/shard_map/ppermute | solution.py:349
  92.0 6.4 %direct_product.2 = (f32[2048,256]{1,0:T(8,128)S(1)}, f32[1024,256]{1,0:T(8,128)S(1)}, f32[1024,256]{1,0:T(8,128)S(1)}) custom-call(s32[5]{0:T(128)S(1)} %stack.23.ids.refs_0_, bf16[4096,2048]{1,0:T(8,128)(2,1)S(1)} %get-tuple-element.45.refs_1_, bf16[2048,256]{1,0:T(8,128)(2,1)S(1)} %get-tuple-element.52.refs_2_, ...), custom_call_target="tpu_custom_call" | custom-call | tf_op jit(solution)/shard_map/direct_product/pallas_call | solution.py:48
  98.4 3.9 %collective-permute-start.10 = (f32[1024,256]{1,0:T(8,128)S(1)}, f32[1024,256]{1,0:T(8,128)S(1)}, u32[]{:S(2)}, u32[]{:S(2)}) collective-permute-start(f32[1024,256]{1,0:T(8,128)S(1)} %get-tuple-element.57), channel_id=1, source_target_pairs={{0,1},{1,0},{8,9},{9,8},{10,11},{11,10},{16,17},{17,16},{18,19},{1... | collective-permute-start | bytes 3145736 | tf_op jit(solution)/shard_map/ppermute | solution.py:349
  102.3 1.9 %collective-permute-start.11 = (f32[1024,256]{1,0:T(8,128)S(1)}, f32[1024,256]{1,0:T(8,128)S(1)}, u32[]{:S(2)}, u32[]{:S(2)}) collective-permute-start(f32[1024,256]{1,0:T(8,128)S(1)} %get-tuple-element.58), channel_id=1, source_target_pairs={{0,1},{1,0},{8,9},{9,8},{10,11},{11,10},{16,17},{17,16},{18,19},{1... | collective-permute-start | bytes 3145736 | tf_op jit(solution)/shard_map/ppermute | solution.py:349
  104.3 2.9 %relay.3 = (f32[2048,256]{1,0:T(8,128)S(1)}, bf16[2112,256]{1,0:T(8,128)(2,1)S(1)}) custom-call(s32[5]{0:T(128)S(1)} %stack.23.ids.refs_0_, f32[2048,256]{1,0:T(8,128)S(1)} %get-tuple-element.60.refs_1_, bf16[2112,256]{1,0:T(8,128)(2,1)S(1)} %collective-permute-done.13.refs_2_, f32[2048,256]{1,0:T(8,128)S(1)} %get-tuple-element.56.refs_3_.refs_1_, ...), custom_call_target="tpu_custom_call" | custom-call | tf_op jit(solution)/shard_map/relay/pallas_call | solution.py:48
  108.0 2.3 %pack.2 = (f32[512,256]{1,0:T(8,128)S(1)}, bf16[528,256]{1,0:T(8,128)(2,1)S(1)}, bf16[528,256]{1,0:T(8,128)(2,1)S(1)}, bf16[528,256]{1,0:T(8,128)(2,1)S(1)}, bf16[528,256]{1,0:T(8,128)(2,1)S(1)}) custom-call(s32[5]{0:T(128)S(1)} %stack.23.ids.refs_0_, f32[2048,256]{1,0:T(8,128)S(1)} %get-tuple-element.56.refs_3_.refs_1_, ...), custom_call_target="tpu_custom_call" | custom-call | tf_op jit(solution)/shard_map/pack/pallas_call | solution.py:48
  110.3 2.1 %collective-permute-start.17 = (bf16[528,256]{1,0:T(8,128)(2,1)S(1)}, bf16[528,256]{1,0:T(8,128)(2,1)S(1)}, u32[]{:S(2)}, u32[]{:S(2)}) collective-permute-start(bf16[528,256]{1,0:T(8,128)(2,1)S(1)} %get-tuple-element.67), channel_id=1, source_target_pairs={{1,4},{9,12},{10,9},{11,13},{17,20},{18,17},{19,21},{20,18},{21,22... | collective-permute-start | bytes 811016 | tf_op jit(solution)/shard_map/ppermute | solution.py:349
  112.4 1.9 %collective-permute-start.18 = (bf16[528,256]{1,0:T(8,128)(2,1)S(1)}, bf16[528,256]{1,0:T(8,128)(2,1)S(1)}, u32[]{:S(2)}, u32[]{:S(2)}) collective-permute-start(bf16[528,256]{1,0:T(8,128)(2,1)S(1)} %get-tuple-element.68), channel_id=1, source_target_pairs={{0,1},{1,5},{8,9},{9,13},{11,14},{16,17},{17,21},{19,22},{20,19},{... | collective-permute-start | bytes 811016 | tf_op jit(solution)/shard_map/ppermute | solution.py:349
  114.4 6.4 %direct_product.3 = (f32[2048,256]{1,0:T(8,128)S(1)}, f32[1024,256]{1,0:T(8,128)S(1)}, f32[1024,256]{1,0:T(8,128)S(1)}) custom-call(s32[5]{0:T(128)S(1)} %stack.23.ids.refs_0_, bf16[4096,2048]{1,0:T(8,128)(2,1)S(1)} %get-tuple-element.45.refs_1_, bf16[2048,256]{1,0:T(8,128)(2,1)S(1)} %get-tuple-element.61.refs_2_, ...), custom_call_target="tpu_custom_call" | custom-call | tf_op jit(solution)/shard_map/direct_product/pallas_call | solution.py:48
  120.8 6.4 %collective-permute-start.21 = (f32[1024,256]{1,0:T(8,128)S(1)}, f32[1024,256]{1,0:T(8,128)S(1)}, u32[]{:S(2)}, u32[]{:S(2)}) collective-permute-start(f32[1024,256]{1,0:T(8,128)S(1)} %get-tuple-element.74), channel_id=1, source_target_pairs={{0,1},{1,0},{8,9},{9,8},{10,11},{11,10},{16,17},{17,16},{18,19},{1... | collective-permute-start | bytes 3145736 | tf_op jit(solution)/shard_map/ppermute | solution.py:349
  127.2 1.9 %collective-permute-start.22 = (f32[1024,256]{1,0:T(8,128)S(1)}, f32[1024,256]{1,0:T(8,128)S(1)}, u32[]{:S(2)}, u32[]{:S(2)}) collective-permute-start(f32[1024,256]{1,0:T(8,128)S(1)} %get-tuple-element.75), channel_id=1, source_target_pairs={{0,1},{1,0},{8,9},{9,8},{10,11},{11,10},{16,17},{17,16},{18,19},{1... | collective-permute-start | bytes 3145736 | tf_op jit(solution)/shard_map/ppermute | solution.py:349
  129.1 4.5 %collective-permute-start.19 = (bf16[528,256]{1,0:T(8,128)(2,1)S(1)}, bf16[528,256]{1,0:T(8,128)(2,1)S(1)}, u32[]{:S(2)}, u32[]{:S(2)}) collective-permute-start(bf16[528,256]{1,0:T(8,128)(2,1)S(1)} %get-tuple-element.71), channel_id=1, source_target_pairs={{0,2},{1,6},{8,10},{9,14},{10,11},{11,15},{16,18},{17,22},{18,19},... | collective-permute-start | bytes 811016 | tf_op jit(solution)/shard_map/ppermute | solution.py:349
  133.6 1.9 %collective-permute-start.20 = (bf16[528,256]{1,0:T(8,128)(2,1)S(1)}, bf16[528,256]{1,0:T(8,128)(2,1)S(1)}, u32[]{:S(2)}, u32[]{:S(2)}) collective-permute-start(bf16[528,256]{1,0:T(8,128)(2,1)S(1)} %get-tuple-element.72), channel_id=1, source_target_pairs={{0,3},{1,7},{8,11},{9,15},{10,8},{11,12},{16,19},{17,23},{18,16},{... | collective-permute-start | bytes 811016 | tf_op jit(solution)/shard_map/ppermute | solution.py:349
  135.6 2.1 %pack.3 = (f32[512,256]{1,0:T(8,128)S(1)}, bf16[528,256]{1,0:T(8,128)(2,1)S(1)}, bf16[528,256]{1,0:T(8,128)(2,1)S(1)}, bf16[528,256]{1,0:T(8,128)(2,1)S(1)}, bf16[528,256]{1,0:T(8,128)(2,1)S(1)}) custom-call(s32[5]{0:T(128)S(1)} %stack.23.ids.refs_0_, f32[2048,256]{1,0:T(8,128)S(1)} %get-tuple-element.73.refs_1_, ...), custom_call_target="tpu_custom_call" | custom-call | tf_op jit(solution)/shard_map/pack/pallas_call | solution.py:48
  137.7 4.5 %collective-permute-start.23 = (bf16[528,256]{1,0:T(8,128)(2,1)S(1)}, bf16[528,256]{1,0:T(8,128)(2,1)S(1)}, u32[]{:S(2)}, u32[]{:S(2)}) collective-permute-start(bf16[528,256]{1,0:T(8,128)(2,1)S(1)} %get-tuple-element.79), channel_id=1, source_target_pairs={{1,4},{9,12},{10,9},{11,13},{17,20},{18,17},{19,21},{20,18},{21,22... | collective-permute-start | bytes 811016 | tf_op jit(solution)/shard_map/ppermute | solution.py:349
  142.3 2.5 %collective-permute-start.24 = (bf16[528,256]{1,0:T(8,128)(2,1)S(1)}, bf16[528,256]{1,0:T(8,128)(2,1)S(1)}, u32[]{:S(2)}, u32[]{:S(2)}) collective-permute-start(bf16[528,256]{1,0:T(8,128)(2,1)S(1)} %get-tuple-element.80), channel_id=1, source_target_pairs={{0,1},{1,5},{8,9},{9,13},{11,14},{16,17},{17,21},{19,22},{20,19},{... | collective-permute-start | bytes 811016 | tf_op jit(solution)/shard_map/ppermute | solution.py:349
  146.7 3.1 %collective-permute-start.26 = (bf16[528,256]{1,0:T(8,128)(2,1)S(1)}, bf16[528,256]{1,0:T(8,128)(2,1)S(1)}, u32[]{:S(2)}, u32[]{:S(2)}) collective-permute-start(bf16[528,256]{1,0:T(8,128)(2,1)S(1)} %get-tuple-element.82), channel_id=1, source_target_pairs={{0,3},{1,7},{8,11},{9,15},{10,8},{11,12},{16,19},{17,23},{18,16},{... | collective-permute-start | bytes 811016 | tf_op jit(solution)/shard_map/ppermute | solution.py:349
  149.8 2.8 %collective-permute-done.20.refs_6_ = bf16[528,256]{1,0:T(8,128)(2,1)S(1)} collective-permute-done((bf16[528,256]{1,0:T(8,128)(2,1)S(1)}, bf16[528,256]{1,0:T(8,128)(2,1)S(1)}, u32[]{:S(2)}, u32[]{:S(2)}) %collective-permute-start.20) | collective-permute-done | bytes 270368 | tf_op jit(solution)/shard_map/ppermute | solution.py:349
  154.8 5.0 %collective-permute-done.25.refs_5_ = bf16[528,256]{1,0:T(8,128)(2,1)S(1)} collective-permute-done((bf16[528,256]{1,0:T(8,128)(2,1)S(1)}, bf16[528,256]{1,0:T(8,128)(2,1)S(1)}, u32[]{:S(2)}, u32[]{:S(2)}) %collective-permute-start.25) | collective-permute-done | bytes 270368 | tf_op jit(solution)/shard_map/ppermute | solution.py:349
  159.8 10.3 %collective-permute-done.26.refs_6_ = bf16[528,256]{1,0:T(8,128)(2,1)S(1)} collective-permute-done((bf16[528,256]{1,0:T(8,128)(2,1)S(1)}, bf16[528,256]{1,0:T(8,128)(2,1)S(1)}, u32[]{:S(2)}, u32[]{:S(2)}) %collective-permute-start.26) | collective-permute-done | bytes 270368 | tf_op jit(solution)/shard_map/ppermute | solution.py:349
  170.1 2.6 %finish.3 = f32[512,512]{1,0:T(8,128)} custom-call(s32[5]{0:T(128)S(1)} %stack.23.ids.refs_0_, f32[512,256]{1,0:T(8,128)S(1)} %finish.2.refs_1_, f32[512,256]{1,0:T(8,128)S(1)} %get-tuple-element.78.refs_7_.refs_2_, bf16[528,256]{1,0:T(8,128)(2,1)S(1)} %collective-permute-done.23.refs_3_, bf16[528,256]{1,0:T(8,128)(2,1)S(1)} %collective-permute-done.24.refs_4_, ...), custom_call_target="tpu_custom_call" | custom-call | tf_op jit(solution)/shard_map/finish/pallas_call | solution.py:48
  (40 shorter events, 19.8 us)
Async XLA Ops:
  0.0 27.1 %collective-permute-start = (bf16[512,512]{1,0:T(8,128)(2,1)}, bf16[512,512]{1,0:T(8,128)(2,1)S(1)}, u32[]{:S(2)}, u32[]{:S(2)}) collective-permute-start(bf16[512,512]{1,0:T(8,128)(2,1)} %refs_1_.1), channel_id=1, source_target_pairs={{4,0},{5,1},{6,2},{7,3},{12,8},{13,9},{14,10},{15,11},{16,20},{17,... | collective-permute-start | bytes 1572872 | tf_op jit(solution)/shard_map/ppermute | solution.py:349
  4.2 24.2 %collective-permute-start.1 = (bf16[512,512]{1,0:T(8,128)(2,1)}, bf16[512,512]{1,0:T(8,128)(2,1)S(1)}, u32[]{:S(2)}, u32[]{:S(2)}) collective-permute-start(bf16[512,512]{1,0:T(8,128)(2,1)} %refs_1_.1), channel_id=1, source_target_pairs={{8,10},{9,11},{16,18},{17,19},{18,20},{19,21},{24,26},{25,27},{26,... | collective-permute-start | bytes 1572872 | tf_op jit(solution)/shard_map/ppermute | solution.py:349
  7.5 24.4 %collective-permute-start.2 = (bf16[512,512]{1,0:T(8,128)(2,1)}, bf16[512,512]{1,0:T(8,128)(2,1)S(1)}, u32[]{:S(2)}, u32[]{:S(2)}) collective-permute-start(bf16[512,512]{1,0:T(8,128)(2,1)} %refs_1_.1), channel_id=1, source_target_pairs={{2,0},{3,1},{10,8},{11,9},{12,10},{13,11},{18,16},{19,17},{20,18},... | collective-permute-start | bytes 1572872 | tf_op jit(solution)/shard_map/ppermute | solution.py:349
  8.9 5.8 %copy-start = (bf16[4096,2048]{1,0:T(8,128)(2,1)S(1)}, bf16[4096,2048]{1,0:T(8,128)(2,1)}, u32[]{:S(2)}) copy-start(bf16[4096,2048]{1,0:T(8,128)(2,1)} %a_ref.1) | copy-start | bytes 50331652
  14.6 28.5 %copy-start.1 = (bf16[512,512]{1,0:T(8,128)(2,1)S(1)}, bf16[512,512]{1,0:T(8,128)(2,1)}, u32[]{:S(2)}) copy-start(bf16[512,512]{1,0:T(8,128)(2,1)} %refs_1_.1) | copy-start | bytes 1572868
  27.1 16.0 %collective-permute-start.3 = (bf16[512,512]{1,0:T(8,128)(2,1)S(1)}, bf16[512,512]{1,0:T(8,128)(2,1)S(1)}, u32[]{:S(2)}, u32[]{:S(2)}) collective-permute-start(bf16[512,512]{1,0:T(8,128)(2,1)S(1)} %collective-permute-done.refs_2_), channel_id=1, source_target_pairs={{2,0},{3,1},{10,8},{11,9},{18,16},{19,17},{26,24},{27,25},{28,30},... | collective-permute-start | bytes 1572872 | tf_op jit(solution)/shard_map/ppermute | solution.py:349
  43.8 7.8 %collective-permute-start.4 = (bf16[2048,512]{1,0:T(8,128)(2,1)S(1)}, bf16[2048,512]{1,0:T(8,128)(2,1)S(1)}, u32[]{:S(2)}, u32[]{:S(2)}) collective-permute-start(bf16[2048,512]{1,0:T(8,128)(2,1)S(1)} %line.1.refs_1_.refs_3_), channel_id=1, source_target_pairs={{0,1},{1,0},{8,9},{9,8},{10,11},{11,10},{16,17},{17,16},{18,19},{1... | collective-permute-start | bytes 6291464 | tf_op jit(solution)/shard_map/ppermute | solution.py:349
  52.4 22.0 %collective-permute-start.5 = (bf16[2048,256]{1,0:T(8,128)(2,1)S(1)}, bf16[2048,256]{1,0:T(8,128)(2,1)S(1)}, u32[]{:S(2)}, u32[]{:S(2)}) collective-permute-start(bf16[2048,256]{1,0:T(8,128)(2,1)S(1)} %get-tuple-element.52.refs_2_), channel_id=1, source_target_pairs={{0,8},{1,17},{10,2},{11,27},{20,28}} | collective-permute-start | bytes 3145736 | tf_op jit(solution)/shard_map/ppermute | solution.py:349
  53.1 21.3 %collective-permute-start.6 = (bf16[2048,256]{1,0:T(8,128)(2,1)S(1)}, bf16[2048,256]{1,0:T(8,128)(2,1)S(1)}, u32[]{:S(2)}, u32[]{:S(2)}) collective-permute-start(bf16[2048,256]{1,0:T(8,128)(2,1)S(1)} %get-tuple-element.61.refs_2_), channel_id=1, source_target_pairs={{0,8},{1,17},{10,2},{11,27},{20,28}} | collective-permute-start | bytes 3145736 | tf_op jit(solution)/shard_map/ppermute | solution.py:349
  62.7 13.7 %collective-permute-start.9 = (bf16[2112,256]{1,0:T(8,128)(2,1)S(1)}, bf16[2112,256]{1,0:T(8,128)(2,1)S(1)}, u32[]{:S(2)}, u32[]{:S(2)}) collective-permute-start(bf16[2112,256]{1,0:T(8,128)(2,1)S(1)} %get-tuple-element.49.refs_5_), channel_id=1, source_target_pairs={{16,0},{24,8},{9,1},{25,17},{26,10},{18,2},{19,27},{29,21}} | collective-permute-start | bytes 3244040 | tf_op jit(solution)/shard_map/ppermute | solution.py:349
  73.0 29.3 %collective-permute-start.13 = (bf16[2112,256]{1,0:T(8,128)(2,1)S(1)}, bf16[2112,256]{1,0:T(8,128)(2,1)S(1)}, u32[]{:S(2)}, u32[]{:S(2)}) collective-permute-start(bf16[2112,256]{1,0:T(8,128)(2,1)S(1)} %get-tuple-element.50.refs_3_), channel_id=1, source_target_pairs={{16,0},{24,8},{9,1},{25,17},{26,10},{18,2},{19,27},{29,21}} | collective-permute-start | bytes 3244040 | tf_op jit(solution)/shard_map/ppermute | solution.py:349
  74.3 6.5 %collective-permute-start.7 = (bf16[2048,256]{1,0:T(8,128)(2,1)S(1)}, bf16[2048,256]{1,0:T(8,128)(2,1)S(1)}, u32[]{:S(2)}, u32[]{:S(2)}) collective-permute-start(bf16[2048,256]{1,0:T(8,128)(2,1)S(1)} %get-tuple-element.52.refs_2_), channel_id=1, source_target_pairs={{0,16},{1,9},{10,26},{21,29}} | collective-permute-start | bytes 3145736 | tf_op jit(solution)/shard_map/ppermute | solution.py:349
  75.1 16.9 %collective-permute-start.8 = (bf16[2048,256]{1,0:T(8,128)(2,1)S(1)}, bf16[2048,256]{1,0:T(8,128)(2,1)S(1)}, u32[]{:S(2)}, u32[]{:S(2)}) collective-permute-start(bf16[2048,256]{1,0:T(8,128)(2,1)S(1)} %collective-permute-done.5.refs_3_), channel_id=1, source_target_pairs={{8,24},{17,25},{2,18},{27,19}} | collective-permute-start | bytes 3145736 | tf_op jit(solution)/shard_map/ppermute | solution.py:349
  79.3 24.9 %collective-permute-start.12 = (bf16[2112,256]{1,0:T(8,128)(2,1)S(1)}, bf16[2112,256]{1,0:T(8,128)(2,1)S(1)}, u32[]{:S(2)}, u32[]{:S(2)}) collective-permute-start(bf16[2112,256]{1,0:T(8,128)(2,1)S(1)} %get-tuple-element.55.refs_6_), channel_id=1, source_target_pairs={{8,0},{17,1},{2,10},{27,11},{28,20}} | collective-permute-start | bytes 3244040 | tf_op jit(solution)/shard_map/ppermute | solution.py:349
  80.1 24.2 %collective-permute-start.14 = (bf16[2048,256]{1,0:T(8,128)(2,1)S(1)}, bf16[2048,256]{1,0:T(8,128)(2,1)S(1)}, u32[]{:S(2)}, u32[]{:S(2)}) collective-permute-start(bf16[2048,256]{1,0:T(8,128)(2,1)S(1)} %get-tuple-element.61.refs_2_), channel_id=1, source_target_pairs={{0,16},{1,9},{10,26},{21,29}} | collective-permute-start | bytes 3145736 | tf_op jit(solution)/shard_map/ppermute | solution.py:349
  80.8 27.1 %collective-permute-start.15 = (bf16[2048,256]{1,0:T(8,128)(2,1)S(1)}, bf16[2048,256]{1,0:T(8,128)(2,1)S(1)}, u32[]{:S(2)}, u32[]{:S(2)}) collective-permute-start(bf16[2048,256]{1,0:T(8,128)(2,1)S(1)} %collective-permute-done.6.refs_3_), channel_id=1, source_target_pairs={{8,24},{17,25},{2,18},{27,19}} | collective-permute-start | bytes 3145736 | tf_op jit(solution)/shard_map/ppermute | solution.py:349
  98.4 9.6 %collective-permute-start.10 = (f32[1024,256]{1,0:T(8,128)S(1)}, f32[1024,256]{1,0:T(8,128)S(1)}, u32[]{:S(2)}, u32[]{:S(2)}) collective-permute-start(f32[1024,256]{1,0:T(8,128)S(1)} %get-tuple-element.57), channel_id=1, source_target_pairs={{0,1},{1,0},{8,9},{9,8},{10,11},{11,10},{16,17},{17,16},{18,19},{1... | collective-permute-start | bytes 3145736 | tf_op jit(solution)/shard_map/ppermute | solution.py:349
  102.3 5.7 %collective-permute-start.11 = (f32[1024,256]{1,0:T(8,128)S(1)}, f32[1024,256]{1,0:T(8,128)S(1)}, u32[]{:S(2)}, u32[]{:S(2)}) collective-permute-start(f32[1024,256]{1,0:T(8,128)S(1)} %get-tuple-element.58), channel_id=1, source_target_pairs={{0,1},{1,0},{8,9},{9,8},{10,11},{11,10},{16,17},{17,16},{18,19},{1... | collective-permute-start | bytes 3145736 | tf_op jit(solution)/shard_map/ppermute | solution.py:349
  107.2 13.6 %collective-permute-start.16 = (bf16[2112,256]{1,0:T(8,128)(2,1)S(1)}, bf16[2112,256]{1,0:T(8,128)(2,1)S(1)}, u32[]{:S(2)}, u32[]{:S(2)}) collective-permute-start(bf16[2112,256]{1,0:T(8,128)(2,1)S(1)} %get-tuple-element.62.refs_6_), channel_id=1, source_target_pairs={{8,0},{17,1},{2,10},{27,11},{28,20}} | collective-permute-start | bytes 3244040 | tf_op jit(solution)/shard_map/ppermute | solution.py:349
  110.3 10.5 %collective-permute-start.17 = (bf16[528,256]{1,0:T(8,128)(2,1)S(1)}, bf16[528,256]{1,0:T(8,128)(2,1)S(1)}, u32[]{:S(2)}, u32[]{:S(2)}) collective-permute-start(bf16[528,256]{1,0:T(8,128)(2,1)S(1)} %get-tuple-element.67), channel_id=1, source_target_pairs={{1,4},{9,12},{10,9},{11,13},{17,20},{18,17},{19,21},{20,18},{21,22... | collective-permute-start | bytes 811016 | tf_op jit(solution)/shard_map/ppermute | solution.py:349
  112.4 8.4 %collective-permute-start.18 = (bf16[528,256]{1,0:T(8,128)(2,1)S(1)}, bf16[528,256]{1,0:T(8,128)(2,1)S(1)}, u32[]{:S(2)}, u32[]{:S(2)}) collective-permute-start(bf16[528,256]{1,0:T(8,128)(2,1)S(1)} %get-tuple-element.68), channel_id=1, source_target_pairs={{0,1},{1,5},{8,9},{9,13},{11,14},{16,17},{17,21},{19,22},{20,19},{... | collective-permute-start | bytes 811016 | tf_op jit(solution)/shard_map/ppermute | solution.py:349
  120.8 14.8 %collective-permute-start.21 = (f32[1024,256]{1,0:T(8,128)S(1)}, f32[1024,256]{1,0:T(8,128)S(1)}, u32[]{:S(2)}, u32[]{:S(2)}) collective-permute-start(f32[1024,256]{1,0:T(8,128)S(1)} %get-tuple-element.74), channel_id=1, source_target_pairs={{0,1},{1,0},{8,9},{9,8},{10,11},{11,10},{16,17},{17,16},{18,19},{1... | collective-permute-start | bytes 3145736 | tf_op jit(solution)/shard_map/ppermute | solution.py:349
  127.2 8.4 %collective-permute-start.22 = (f32[1024,256]{1,0:T(8,128)S(1)}, f32[1024,256]{1,0:T(8,128)S(1)}, u32[]{:S(2)}, u32[]{:S(2)}) collective-permute-start(f32[1024,256]{1,0:T(8,128)S(1)} %get-tuple-element.75), channel_id=1, source_target_pairs={{0,1},{1,0},{8,9},{9,8},{10,11},{11,10},{16,17},{17,16},{18,19},{1... | collective-permute-start | bytes 3145736 | tf_op jit(solution)/shard_map/ppermute | solution.py:349
  129.1 17.6 %collective-permute-start.19 = (bf16[528,256]{1,0:T(8,128)(2,1)S(1)}, bf16[528,256]{1,0:T(8,128)(2,1)S(1)}, u32[]{:S(2)}, u32[]{:S(2)}) collective-permute-start(bf16[528,256]{1,0:T(8,128)(2,1)S(1)} %get-tuple-element.71), channel_id=1, source_target_pairs={{0,2},{1,6},{8,10},{9,14},{10,11},{11,15},{16,18},{17,22},{18,19},... | collective-permute-start | bytes 811016 | tf_op jit(solution)/shard_map/ppermute | solution.py:349
  133.6 18.9 %collective-permute-start.20 = (bf16[528,256]{1,0:T(8,128)(2,1)S(1)}, bf16[528,256]{1,0:T(8,128)(2,1)S(1)}, u32[]{:S(2)}, u32[]{:S(2)}) collective-permute-start(bf16[528,256]{1,0:T(8,128)(2,1)S(1)} %get-tuple-element.72), channel_id=1, source_target_pairs={{0,3},{1,7},{8,11},{9,15},{10,8},{11,12},{16,19},{17,23},{18,16},{... | collective-permute-start | bytes 811016 | tf_op jit(solution)/shard_map/ppermute | solution.py:349
  137.7 16.4 %collective-permute-start.23 = (bf16[528,256]{1,0:T(8,128)(2,1)S(1)}, bf16[528,256]{1,0:T(8,128)(2,1)S(1)}, u32[]{:S(2)}, u32[]{:S(2)}) collective-permute-start(bf16[528,256]{1,0:T(8,128)(2,1)S(1)} %get-tuple-element.79), channel_id=1, source_target_pairs={{1,4},{9,12},{10,9},{11,13},{17,20},{18,17},{19,21},{20,18},{21,22... | collective-permute-start | bytes 811016 | tf_op jit(solution)/shard_map/ppermute | solution.py:349
  142.3 12.6 %collective-permute-start.24 = (bf16[528,256]{1,0:T(8,128)(2,1)S(1)}, bf16[528,256]{1,0:T(8,128)(2,1)S(1)}, u32[]{:S(2)}, u32[]{:S(2)}) collective-permute-start(bf16[528,256]{1,0:T(8,128)(2,1)S(1)} %get-tuple-element.80), channel_id=1, source_target_pairs={{0,1},{1,5},{8,9},{9,13},{11,14},{16,17},{17,21},{19,22},{20,19},{... | collective-permute-start | bytes 811016 | tf_op jit(solution)/shard_map/ppermute | solution.py:349
  144.7 15.1 %collective-permute-start.25 = (bf16[528,256]{1,0:T(8,128)(2,1)S(1)}, bf16[528,256]{1,0:T(8,128)(2,1)S(1)}, u32[]{:S(2)}, u32[]{:S(2)}) collective-permute-start(bf16[528,256]{1,0:T(8,128)(2,1)S(1)} %get-tuple-element.81), channel_id=1, source_target_pairs={{0,2},{1,6},{8,10},{9,14},{10,11},{11,15},{16,18},{17,22},{18,19},... | collective-permute-start | bytes 811016 | tf_op jit(solution)/shard_map/ppermute | solution.py:349
  146.7 23.4 %collective-permute-start.26 = (bf16[528,256]{1,0:T(8,128)(2,1)S(1)}, bf16[528,256]{1,0:T(8,128)(2,1)S(1)}, u32[]{:S(2)}, u32[]{:S(2)}) collective-permute-start(bf16[528,256]{1,0:T(8,128)(2,1)S(1)} %get-tuple-element.82), channel_id=1, source_target_pairs={{0,3},{1,7},{8,11},{9,15},{10,8},{11,12},{16,19},{17,23},{18,16},{... | collective-permute-start | bytes 811016 | tf_op jit(solution)/shard_map/ppermute | solution.py:349

commit v7 on v6

--- a/solution.py
+++ b/solution.py
@@ -397,20 +397,10 @@
     four = [
         lambda chip: (chip, chip >= 0),
         lambda chip: (chip ^ 2, chip >= 0),
-        lambda chip: (jnp.maximum(chip - 1, 0), chip > 0),
-        lambda chip: (jnp.minimum(chip + 1, 3), chip < 3),
+        lambda chip: (chip ^ 1, chip >= 0),
         lambda chip: (3 - chip, (chip == 0) | (chip == 3)),
+        lambda chip: (3 - chip, (chip == 1) | (chip == 2)),
     ]
-
-    def two_away(block):
-        return step(block, lambda k: k ^ 2, lambda r, k: k >= 2 or k + 2 <= r)
-
-    def next_ones(block):
-        up = step(block, lambda k: k + 1, lambda r, k: k + 1 <= r and k < 3)
-        return [up, step(block, lambda k: k - 1, lambda r, k: 0 <= k - 1 <= r)]
-
-    def ends(two):
-        return step(two, lambda k: 3 * (k - 1), lambda r, k: k == 1 or (k == 2 and r == 3))
 
     swap = [((r, k, c), (r, k, 1 - c)) for r, k, c in active]
 
@@ -440,10 +430,12 @@
         return arrays
 
     if chips == 4:
-        two = two_away(panel_vectors)
-        came, places = [panel_vectors, two, *next_ones(panel_vectors)], four
-        two, matrix = lax.optimization_barrier((two, matrix))
-        came.append(ends(two))
+        two = step(panel_vectors, lambda k: k ^ 2, lambda r, k: k >= 2 or k + 2 <= r)
+        near = step(panel_vectors, lambda k: k ^ 1, lambda r, k: k ^ 1 <= r)
+        two, near, own, matrix = lax.optimization_barrier((two, near, panel_vectors, matrix))
+        ends = step(two, lambda k: 3 * (k - 1), lambda r, k: k == 1 or (k == 2 and r == 3))
+        middle = step(own, lambda k: 3 - k, lambda r, k: k in (1, 2) and 3 - k <= r)
+        came, places = [panel_vectors, two, near, ends, middle], four
     else:
         came, places = by_distance(panel_vectors)
     mine = line(ids, came, places, [])
@@ -455,9 +447,9 @@
     to_a = collect(bits - 1, message_a)
     partial_b, message_b = mirrored_product(ids, matrix, diagonal, mine, other, piece, 1, [message_a])
     to_b = collect(bits - 1, message_b)
-    widen(panels_a, [message_b, panels_b[1]])
+    widen(panels_a, [message_b])
     widen(panels_b, [panels_a[1]])
-    partial_a, to_a, relayed = relaying(partial_a, to_a, [], [message_b])
+    partial_a, to_a, relayed = relaying(partial_a, to_a, [], [message_b, panels_b[1]])
     keep_a, *give_a = direct_product(ids, matrix, panels_a, [relayed])
     got_a = [send(x, swap) for x in give_a]
     partial_b, to_b, relayed = relaying(partial_b, to_b, [], [keep_a, to_a, panels_b[2]])

time: 173 us -> 177 us (1.023)
  starting transfers between devices: 60.5 us -> 65.8 us
    ppermute x27, starting transfers between devices: 60.5 us -> 65.8 us  [send(): return lax.ppermute(x, ('row', 'col'), [(at(*s), at(*d)) for s, d in pairs])]
  transfers between devices with their start and end apart: 27 -> 27, of which waited for: 9 -> 9; matrix products, arithmetic and copies ran while one was open for 0% -> 0% of each run, Pallas kernels for 26% -> 25%
where the time goes in v7:
time: 177 us
  starting transfers between devices  65.8 us (37%)
  waiting for transfers between devices  56.6 us (32%)
  Pallas kernels  48 us (27%)
  local copies, waits for them, and re-layouts  5.86 us (3%)
    ppermute x27, starting transfers between devices, send(): return lax.ppermute(x, ('row', 'col'), [(at(*s), at(*d)) for s, d in pairs])  65.8 us
    ppermute x27, waiting for transfers between devices, send(): return lax.ppermute(x, ('row', 'col'), [(at(*s), at(*d)) for s, d in pairs])  56.6 us
    pallas_call x12, Pallas kernels, local(): pl.pallas_call(body, out_shape=out_shape, in_specs=[pl.BlockSpec(memory_s...  46.3 us
    unnamed x4, local copies, waits for them, and re-layouts  5.77 us
  transfers between devices with their start and end apart: 27, of which 9 were waited for; matrix products, arithmetic and copies ran while one was open for 0% of the time, Pallas kernels for 25%

profile of v7, /device:TPU:7, one launch (start us, length us, event | category | flops | bytes accessed | tf_op | source)
XLA Modules:
  0.0 176.7 jit_solution(15445712357537743660)
XLA Ops:
  0.0 4.2 %collective-permute-start = (bf16[512,512]{1,0:T(8,128)(2,1)}, bf16[512,512]{1,0:T(8,128)(2,1)S(1)}, u32[]{:S(2)}, u32[]{:S(2)}) collective-permute-start(bf16[512,512]{1,0:T(8,128)(2,1)} %refs_1_.1), channel_id=1, source_target_pairs={{4,0},{5,1},{6,2},{7,3},{12,8},{13,9},{14,10},{15,11},{16,20},{17,... | collective-permute-start | bytes 1572872 | tf_op jit(solution)/shard_map/ppermute | solution.py:349
  4.2 3.2 %collective-permute-start.1 = (bf16[512,512]{1,0:T(8,128)(2,1)}, bf16[512,512]{1,0:T(8,128)(2,1)S(1)}, u32[]{:S(2)}, u32[]{:S(2)}) collective-permute-start(bf16[512,512]{1,0:T(8,128)(2,1)} %refs_1_.1), channel_id=1, source_target_pairs={{2,0},{3,1},{8,10},{9,11},{10,8},{11,9},{16,18},{17,19},{18,16},{1... | collective-permute-start | bytes 1572872 | tf_op jit(solution)/shard_map/ppermute | solution.py:349
  7.5 5.8 %copy-done = bf16[4096,2048]{1,0:T(8,128)(2,1)S(1)} copy-done((bf16[4096,2048]{1,0:T(8,128)(2,1)S(1)}, bf16[4096,2048]{1,0:T(8,128)(2,1)}, u32[]{:S(2)}) %copy-start) | copy-done | bytes 16777240
  15.1 12.0 %collective-permute-done.refs_2_ = bf16[512,512]{1,0:T(8,128)(2,1)S(1)} collective-permute-done((bf16[512,512]{1,0:T(8,128)(2,1)}, bf16[512,512]{1,0:T(8,128)(2,1)S(1)}, u32[]{:S(2)}, u32[]{:S(2)}) %collective-permute-start) | collective-permute-done | bytes 524320 | tf_op jit(solution)/shard_map/ppermute | solution.py:349
  30.9 11.4 %collective-permute-done.2.refs_4_ = bf16[512,512]{1,0:T(8,128)(2,1)S(1)} collective-permute-done((bf16[512,512]{1,0:T(8,128)(2,1)S(1)}, bf16[512,512]{1,0:T(8,128)(2,1)S(1)}, u32[]{:S(2)}, u32[]{:S(2)}) %collective-permute-start.2) | collective-permute-done | bytes 524320 | tf_op jit(solution)/shard_map/ppermute | solution.py:349
  43.1 4.7 %collective-permute-start.4 = (bf16[2048,512]{1,0:T(8,128)(2,1)S(1)}, bf16[2048,512]{1,0:T(8,128)(2,1)S(1)}, u32[]{:S(2)}, u32[]{:S(2)}) collective-permute-start(bf16[2048,512]{1,0:T(8,128)(2,1)S(1)} %line.1.refs_1_.refs_3_), channel_id=1, source_target_pairs={{0,1},{1,0},{8,9},{9,8},{10,11},{11,10},{16,17},{17,16},{18,19},{1... | collective-permute-start | bytes 6291464 | tf_op jit(solution)/shard_map/ppermute | solution.py:349
  47.8 3.8 %collective-permute-done.4.refs_2_.refs_4_ = bf16[2048,512]{1,0:T(8,128)(2,1)S(1)} collective-permute-done((bf16[2048,512]{1,0:T(8,128)(2,1)S(1)}, bf16[2048,512]{1,0:T(8,128)(2,1)S(1)}, u32[]{:S(2)}, u32[]{:S(2)}) %collective-permute-start.4) | collective-permute-done | bytes 2097184 | tf_op jit(solution)/shard_map/ppermute | solution.py:349
  53.0 8.8 %mirrored_product.2 = (f32[2048,256]{1,0:T(8,128)S(1)}, bf16[2112,256]{1,0:T(8,128)(2,1)S(1)}) custom-call(s32[5]{0:T(128)S(1)} %stack.23.ids.refs_0_, bf16[4096,2048]{1,0:T(8,128)(2,1)S(1)} %get-tuple-element.47.refs_1_, f32[8,2048]{1,0:T(8,128)S(1)} %get-tuple-element.52.refs_2_, bf16[2048,512]{1,0:T(8,128)(2,1)S(1)} %line.1.refs_1_.refs_3_, ...), custom_call_target="tpu_custom_call" | custom-call | tf_op jit(solution)/shard_map/mirrored_product/pallas_call | solution.py:48
  61.8 2.8 %collective-permute-start.8 = (bf16[2112,256]{1,0:T(8,128)(2,1)S(1)}, bf16[2112,256]{1,0:T(8,128)(2,1)S(1)}, u32[]{:S(2)}, u32[]{:S(2)}) collective-permute-start(bf16[2112,256]{1,0:T(8,128)(2,1)S(1)} %get-tuple-element.53.refs_5_), channel_id=1, source_target_pairs={{16,0},{24,8},{9,1},{25,17},{26,10},{18,2},{19,27},{29,21}} | collective-permute-start | bytes 3244040 | tf_op jit(solution)/shard_map/ppermute | solution.py:349
  65.3 8.8 %mirrored_product.3 = (f32[2048,256]{1,0:T(8,128)S(1)}, bf16[2112,256]{1,0:T(8,128)(2,1)S(1)}) custom-call(s32[5]{0:T(128)S(1)} %stack.23.ids.refs_0_, bf16[4096,2048]{1,0:T(8,128)(2,1)S(1)} %get-tuple-element.47.refs_1_, f32[8,2048]{1,0:T(8,128)S(1)} %get-tuple-element.52.refs_2_, bf16[2048,512]{1,0:T(8,128)(2,1)S(1)} %line.1.refs_1_.refs_3_, ...), custom_call_target="tpu_custom_call" | custom-call | tf_op jit(solution)/shard_map/mirrored_product/pallas_call | solution.py:48
  78.1 2.9 %relay.2 = (f32[2048,256]{1,0:T(8,128)S(1)}, bf16[2112,256]{1,0:T(8,128)(2,1)S(1)}) custom-call(s32[5]{0:T(128)S(1)} %stack.23.ids.refs_0_, f32[2048,256]{1,0:T(8,128)S(1)} %get-tuple-element.57.refs_1_, bf16[2112,256]{1,0:T(8,128)(2,1)S(1)} %collective-permute-done.8.refs_2_, bf16[2112,256]{1,0:T(8,128)(2,1)S(1)} %get-tuple-element.54.refs_3_, ...), custom_call_target="tpu_custom_call" | custom-call | tf_op jit(solution)/shard_map/relay/pallas_call | solution.py:48
  83.8 8.8 %collective-permute-done.7.refs_5_ = bf16[2048,256]{1,0:T(8,128)(2,1)S(1)} collective-permute-done((bf16[2048,256]{1,0:T(8,128)(2,1)S(1)}, bf16[2048,256]{1,0:T(8,128)(2,1)S(1)}, u32[]{:S(2)}, u32[]{:S(2)}) %collective-permute-start.7) | collective-permute-done | bytes 1048608 | tf_op jit(solution)/shard_map/ppermute | solution.py:349
  92.6 6.4 %direct_product.2 = (f32[2048,256]{1,0:T(8,128)S(1)}, f32[1024,256]{1,0:T(8,128)S(1)}, f32[1024,256]{1,0:T(8,128)S(1)}) custom-call(s32[5]{0:T(128)S(1)} %stack.23.ids.refs_0_, bf16[4096,2048]{1,0:T(8,128)(2,1)S(1)} %get-tuple-element.47.refs_1_, bf16[2048,256]{1,0:T(8,128)(2,1)S(1)} %get-tuple-element.55.refs_2_, ...), custom_call_target="tpu_custom_call" | custom-call | tf_op jit(solution)/shard_map/direct_product/pallas_call | solution.py:48
  99.0 1.9 %collective-permute-start.10 = (f32[1024,256]{1,0:T(8,128)S(1)}, f32[1024,256]{1,0:T(8,128)S(1)}, u32[]{:S(2)}, u32[]{:S(2)}) collective-permute-start(f32[1024,256]{1,0:T(8,128)S(1)} %get-tuple-element.62), channel_id=1, source_target_pairs={{0,1},{1,0},{8,9},{9,8},{10,11},{11,10},{16,17},{17,16},{18,19},{1... | collective-permute-start | bytes 3145736 | tf_op jit(solution)/shard_map/ppermute | solution.py:349
  101.0 2.4 %collective-permute-start.11 = (f32[1024,256]{1,0:T(8,128)S(1)}, f32[1024,256]{1,0:T(8,128)S(1)}, u32[]{:S(2)}, u32[]{:S(2)}) collective-permute-start(f32[1024,256]{1,0:T(8,128)S(1)} %get-tuple-element.63), channel_id=1, source_target_pairs={{0,1},{1,0},{8,9},{9,8},{10,11},{11,10},{16,17},{17,16},{18,19},{1... | collective-permute-start | bytes 3145736 | tf_op jit(solution)/shard_map/ppermute | solution.py:349
  103.4 2.9 %relay.3 = (f32[2048,256]{1,0:T(8,128)S(1)}, bf16[2112,256]{1,0:T(8,128)(2,1)S(1)}) custom-call(s32[5]{0:T(128)S(1)} %stack.23.ids.refs_0_, f32[2048,256]{1,0:T(8,128)S(1)} %get-tuple-element.65.refs_1_, bf16[2112,256]{1,0:T(8,128)(2,1)S(1)} %collective-permute-done.13.refs_2_, f32[2048,256]{1,0:T(8,128)S(1)} %get-tuple-element.61.refs_3_.refs_1_, ...), custom_call_target="tpu_custom_call" | custom-call | tf_op jit(solution)/shard_map/relay/pallas_call | solution.py:48
  107.1 2.3 %pack.2 = (f32[512,256]{1,0:T(8,128)S(1)}, bf16[528,256]{1,0:T(8,128)(2,1)S(1)}, bf16[528,256]{1,0:T(8,128)(2,1)S(1)}, bf16[528,256]{1,0:T(8,128)(2,1)S(1)}, bf16[528,256]{1,0:T(8,128)(2,1)S(1)}) custom-call(s32[5]{0:T(128)S(1)} %stack.23.ids.refs_0_, f32[2048,256]{1,0:T(8,128)S(1)} %get-tuple-element.61.refs_3_.refs_1_, ...), custom_call_target="tpu_custom_call" | custom-call | tf_op jit(solution)/shard_map/pack/pallas_call | solution.py:48
  109.4 7.3 %collective-permute-start.17 = (bf16[528,256]{1,0:T(8,128)(2,1)S(1)}, bf16[528,256]{1,0:T(8,128)(2,1)S(1)}, u32[]{:S(2)}, u32[]{:S(2)}) collective-permute-start(bf16[528,256]{1,0:T(8,128)(2,1)S(1)} %get-tuple-element.71), channel_id=1, source_target_pairs={{1,4},{9,12},{10,9},{11,13},{17,20},{18,17},{19,21},{20,18},{21,22... | collective-permute-start | bytes 811016 | tf_op jit(solution)/shard_map/ppermute | solution.py:349
  116.7 1.9 %collective-permute-start.18 = (bf16[528,256]{1,0:T(8,128)(2,1)S(1)}, bf16[528,256]{1,0:T(8,128)(2,1)S(1)}, u32[]{:S(2)}, u32[]{:S(2)}) collective-permute-start(bf16[528,256]{1,0:T(8,128)(2,1)S(1)} %get-tuple-element.72), channel_id=1, source_target_pairs={{0,1},{1,5},{8,9},{9,13},{11,14},{16,17},{17,21},{19,22},{20,19},{... | collective-permute-start | bytes 811016 | tf_op jit(solution)/shard_map/ppermute | solution.py:349
  118.6 6.4 %direct_product.3 = (f32[2048,256]{1,0:T(8,128)S(1)}, f32[1024,256]{1,0:T(8,128)S(1)}, f32[1024,256]{1,0:T(8,128)S(1)}) custom-call(s32[5]{0:T(128)S(1)} %stack.23.ids.refs_0_, bf16[4096,2048]{1,0:T(8,128)(2,1)S(1)} %get-tuple-element.47.refs_1_, bf16[2048,256]{1,0:T(8,128)(2,1)S(1)} %get-tuple-element.66.refs_2_, ...), custom_call_target="tpu_custom_call" | custom-call | tf_op jit(solution)/shard_map/direct_product/pallas_call | solution.py:48
  125.1 6.2 %collective-permute-start.21 = (f32[1024,256]{1,0:T(8,128)S(1)}, f32[1024,256]{1,0:T(8,128)S(1)}, u32[]{:S(2)}, u32[]{:S(2)}) collective-permute-start(f32[1024,256]{1,0:T(8,128)S(1)} %get-tuple-element.78), channel_id=1, source_target_pairs={{0,1},{1,0},{8,9},{9,8},{10,11},{11,10},{16,17},{17,16},{18,19},{1... | collective-permute-start | bytes 3145736 | tf_op jit(solution)/shard_map/ppermute | solution.py:349
  133.2 4.5 %collective-permute-start.19 = (bf16[528,256]{1,0:T(8,128)(2,1)S(1)}, bf16[528,256]{1,0:T(8,128)(2,1)S(1)}, u32[]{:S(2)}, u32[]{:S(2)}) collective-permute-start(bf16[528,256]{1,0:T(8,128)(2,1)S(1)} %get-tuple-element.75), channel_id=1, source_target_pairs={{0,2},{1,6},{8,10},{9,14},{10,11},{11,15},{16,18},{17,22},{18,19},... | collective-permute-start | bytes 811016 | tf_op jit(solution)/shard_map/ppermute | solution.py:349
  137.7 1.9 %collective-permute-start.20 = (bf16[528,256]{1,0:T(8,128)(2,1)S(1)}, bf16[528,256]{1,0:T(8,128)(2,1)S(1)}, u32[]{:S(2)}, u32[]{:S(2)}) collective-permute-start(bf16[528,256]{1,0:T(8,128)(2,1)S(1)} %get-tuple-element.76), channel_id=1, source_target_pairs={{0,3},{1,7},{8,11},{9,15},{10,8},{11,12},{16,19},{17,23},{18,16},{... | collective-permute-start | bytes 811016 | tf_op jit(solution)/shard_map/ppermute | solution.py:349
  139.7 2.1 %pack.3 = (f32[512,256]{1,0:T(8,128)S(1)}, bf16[528,256]{1,0:T(8,128)(2,1)S(1)}, bf16[528,256]{1,0:T(8,128)(2,1)S(1)}, bf16[528,256]{1,0:T(8,128)(2,1)S(1)}, bf16[528,256]{1,0:T(8,128)(2,1)S(1)}) custom-call(s32[5]{0:T(128)S(1)} %stack.23.ids.refs_0_, f32[2048,256]{1,0:T(8,128)S(1)} %get-tuple-element.77.refs_1_, ...), custom_call_target="tpu_custom_call" | custom-call | tf_op jit(solution)/shard_map/pack/pallas_call | solution.py:48
  141.8 4.5 %collective-permute-start.23 = (bf16[528,256]{1,0:T(8,128)(2,1)S(1)}, bf16[528,256]{1,0:T(8,128)(2,1)S(1)}, u32[]{:S(2)}, u32[]{:S(2)}) collective-permute-start(bf16[528,256]{1,0:T(8,128)(2,1)S(1)} %get-tuple-element.83), channel_id=1, source_target_pairs={{1,4},{9,12},{10,9},{11,13},{17,20},{18,17},{19,21},{20,18},{21,22... | collective-permute-start | bytes 811016 | tf_op jit(solution)/shard_map/ppermute | solution.py:349
  146.4 2.5 %collective-permute-start.24 = (bf16[528,256]{1,0:T(8,128)(2,1)S(1)}, bf16[528,256]{1,0:T(8,128)(2,1)S(1)}, u32[]{:S(2)}, u32[]{:S(2)}) collective-permute-start(bf16[528,256]{1,0:T(8,128)(2,1)S(1)} %get-tuple-element.84), channel_id=1, source_target_pairs={{0,1},{1,5},{8,9},{9,13},{11,14},{16,17},{17,21},{19,22},{20,19},{... | collective-permute-start | bytes 811016 | tf_op jit(solution)/shard_map/ppermute | solution.py:349
  148.8 1.9 %collective-permute-start.25 = (bf16[528,256]{1,0:T(8,128)(2,1)S(1)}, bf16[528,256]{1,0:T(8,128)(2,1)S(1)}, u32[]{:S(2)}, u32[]{:S(2)}) collective-permute-start(bf16[528,256]{1,0:T(8,128)(2,1)S(1)} %get-tuple-element.85), channel_id=1, source_target_pairs={{0,2},{1,6},{8,10},{9,14},{10,11},{11,15},{16,18},{17,22},{18,19},... | collective-permute-start | bytes 811016 | tf_op jit(solution)/shard_map/ppermute | solution.py:349
  150.8 3.1 %collective-permute-start.26 = (bf16[528,256]{1,0:T(8,128)(2,1)S(1)}, bf16[528,256]{1,0:T(8,128)(2,1)S(1)}, u32[]{:S(2)}, u32[]{:S(2)}) collective-permute-start(bf16[528,256]{1,0:T(8,128)(2,1)S(1)} %get-tuple-element.86), channel_id=1, source_target_pairs={{0,3},{1,7},{8,11},{9,15},{10,8},{11,12},{16,19},{17,23},{18,16},{... | collective-permute-start | bytes 811016 | tf_op jit(solution)/shard_map/ppermute | solution.py:349
  153.9 2.8 %collective-permute-done.20.refs_6_ = bf16[528,256]{1,0:T(8,128)(2,1)S(1)} collective-permute-done((bf16[528,256]{1,0:T(8,128)(2,1)S(1)}, bf16[528,256]{1,0:T(8,128)(2,1)S(1)}, u32[]{:S(2)}, u32[]{:S(2)}) %collective-permute-start.20) | collective-permute-done | bytes 270368 | tf_op jit(solution)/shard_map/ppermute | solution.py:349
  158.9 5.0 %collective-permute-done.25.refs_5_ = bf16[528,256]{1,0:T(8,128)(2,1)S(1)} collective-permute-done((bf16[528,256]{1,0:T(8,128)(2,1)S(1)}, bf16[528,256]{1,0:T(8,128)(2,1)S(1)}, u32[]{:S(2)}, u32[]{:S(2)}) %collective-permute-start.25) | collective-permute-done | bytes 270368 | tf_op jit(solution)/shard_map/ppermute | solution.py:349
  163.9 10.3 %collective-permute-done.26.refs_6_ = bf16[528,256]{1,0:T(8,128)(2,1)S(1)} collective-permute-done((bf16[528,256]{1,0:T(8,128)(2,1)S(1)}, bf16[528,256]{1,0:T(8,128)(2,1)S(1)}, u32[]{:S(2)}, u32[]{:S(2)}) %collective-permute-start.26) | collective-permute-done | bytes 270368 | tf_op jit(solution)/shard_map/ppermute | solution.py:349
  174.2 2.6 %finish.3 = f32[512,512]{1,0:T(8,128)} custom-call(s32[5]{0:T(128)S(1)} %stack.23.ids.refs_0_, f32[512,256]{1,0:T(8,128)S(1)} %finish.2.refs_1_, f32[512,256]{1,0:T(8,128)S(1)} %get-tuple-element.82.refs_7_.refs_2_, bf16[528,256]{1,0:T(8,128)(2,1)S(1)} %collective-permute-done.23.refs_3_, bf16[528,256]{1,0:T(8,128)(2,1)S(1)} %collective-permute-done.24.refs_4_, ...), custom_call_target="tpu_custom_call" | custom-call | tf_op jit(solution)/shard_map/finish/pallas_call | solution.py:48
  (40 shorter events, 20.1 us)
Async XLA Ops:
  0.0 27.1 %collective-permute-start = (bf16[512,512]{1,0:T(8,128)(2,1)}, bf16[512,512]{1,0:T(8,128)(2,1)S(1)}, u32[]{:S(2)}, u32[]{:S(2)}) collective-permute-start(bf16[512,512]{1,0:T(8,128)(2,1)} %refs_1_.1), channel_id=1, source_target_pairs={{4,0},{5,1},{6,2},{7,3},{12,8},{13,9},{14,10},{15,11},{16,20},{17,... | collective-permute-start | bytes 1572872 | tf_op jit(solution)/shard_map/ppermute | solution.py:349
  4.2 24.7 %collective-permute-start.1 = (bf16[512,512]{1,0:T(8,128)(2,1)}, bf16[512,512]{1,0:T(8,128)(2,1)S(1)}, u32[]{:S(2)}, u32[]{:S(2)}) collective-permute-start(bf16[512,512]{1,0:T(8,128)(2,1)} %refs_1_.1), channel_id=1, source_target_pairs={{2,0},{3,1},{8,10},{9,11},{10,8},{11,9},{16,18},{17,19},{18,16},{1... | collective-permute-start | bytes 1572872 | tf_op jit(solution)/shard_map/ppermute | solution.py:349
  7.5 5.8 %copy-start = (bf16[4096,2048]{1,0:T(8,128)(2,1)S(1)}, bf16[4096,2048]{1,0:T(8,128)(2,1)}, u32[]{:S(2)}) copy-start(bf16[4096,2048]{1,0:T(8,128)(2,1)} %a_ref.1) | copy-start | bytes 50331652
  13.3 16.9 %copy-start.1 = (bf16[512,512]{1,0:T(8,128)(2,1)S(1)}, bf16[512,512]{1,0:T(8,128)(2,1)}, u32[]{:S(2)}) copy-start(bf16[512,512]{1,0:T(8,128)(2,1)} %refs_1_.1) | copy-start | bytes 1572868
  28.9 13.4 %collective-permute-start.2 = (bf16[512,512]{1,0:T(8,128)(2,1)S(1)}, bf16[512,512]{1,0:T(8,128)(2,1)S(1)}, u32[]{:S(2)}, u32[]{:S(2)}) collective-permute-start(bf16[512,512]{1,0:T(8,128)(2,1)S(1)} %collective-permute-done.refs_2_), channel_id=1, source_target_pairs={{2,0},{3,1},{10,8},{11,9},{18,16},{19,17},{26,24},{27,25},{28,30},... | collective-permute-start | bytes 1572872 | tf_op jit(solution)/shard_map/ppermute | solution.py:349
  30.2 12.1 %collective-permute-start.3 = (bf16[512,512]{1,0:T(8,128)(2,1)S(1)}, bf16[512,512]{1,0:T(8,128)(2,1)S(1)}, u32[]{:S(2)}, u32[]{:S(2)}) collective-permute-start(bf16[512,512]{1,0:T(8,128)(2,1)S(1)} %copy-done.1), channel_id=1, source_target_pairs={{12,10},{13,11},{18,20},{19,21},{20,18},{21,19},{26,28},{27,29},{2... | collective-permute-start | bytes 1572872 | tf_op jit(solution)/shard_map/ppermute | solution.py:349
  43.1 8.5 %collective-permute-start.4 = (bf16[2048,512]{1,0:T(8,128)(2,1)S(1)}, bf16[2048,512]{1,0:T(8,128)(2,1)S(1)}, u32[]{:S(2)}, u32[]{:S(2)}) collective-permute-start(bf16[2048,512]{1,0:T(8,128)(2,1)S(1)} %line.1.refs_1_.refs_3_), channel_id=1, source_target_pairs={{0,1},{1,0},{8,9},{9,8},{10,11},{11,10},{16,17},{17,16},{18,19},{1... | collective-permute-start | bytes 6291464 | tf_op jit(solution)/shard_map/ppermute | solution.py:349
  52.2 23.8 %collective-permute-start.5 = (bf16[2048,256]{1,0:T(8,128)(2,1)S(1)}, bf16[2048,256]{1,0:T(8,128)(2,1)S(1)}, u32[]{:S(2)}, u32[]{:S(2)}) collective-permute-start(bf16[2048,256]{1,0:T(8,128)(2,1)S(1)} %get-tuple-element.55.refs_2_), channel_id=1, source_target_pairs={{0,8},{1,17},{10,2},{11,27},{20,28}} | collective-permute-start | bytes 3145736 | tf_op jit(solution)/shard_map/ppermute | solution.py:349
  61.8 16.3 %collective-permute-start.8 = (bf16[2112,256]{1,0:T(8,128)(2,1)S(1)}, bf16[2112,256]{1,0:T(8,128)(2,1)S(1)}, u32[]{:S(2)}, u32[]{:S(2)}) collective-permute-start(bf16[2112,256]{1,0:T(8,128)(2,1)S(1)} %get-tuple-element.53.refs_5_), channel_id=1, source_target_pairs={{16,0},{24,8},{9,1},{25,17},{26,10},{18,2},{19,27},{29,21}} | collective-permute-start | bytes 3244040 | tf_op jit(solution)/shard_map/ppermute | solution.py:349
  64.6 13.5 %collective-permute-start.9 = (bf16[2048,256]{1,0:T(8,128)(2,1)S(1)}, bf16[2048,256]{1,0:T(8,128)(2,1)S(1)}, u32[]{:S(2)}, u32[]{:S(2)}) collective-permute-start(bf16[2048,256]{1,0:T(8,128)(2,1)S(1)} %get-tuple-element.66.refs_2_), channel_id=1, source_target_pairs={{0,8},{1,17},{10,2},{11,27},{20,28}} | collective-permute-start | bytes 3145736 | tf_op jit(solution)/shard_map/ppermute | solution.py:349
  74.2 26.8 %collective-permute-start.13 = (bf16[2112,256]{1,0:T(8,128)(2,1)S(1)}, bf16[2112,256]{1,0:T(8,128)(2,1)S(1)}, u32[]{:S(2)}, u32[]{:S(2)}) collective-permute-start(bf16[2112,256]{1,0:T(8,128)(2,1)S(1)} %get-tuple-element.54.refs_3_), channel_id=1, source_target_pairs={{16,0},{24,8},{9,1},{25,17},{26,10},{18,2},{19,27},{29,21}} | collective-permute-start | bytes 3244040 | tf_op jit(solution)/shard_map/ppermute | solution.py:349
  76.0 6.5 %collective-permute-start.6 = (bf16[2048,256]{1,0:T(8,128)(2,1)S(1)}, bf16[2048,256]{1,0:T(8,128)(2,1)S(1)}, u32[]{:S(2)}, u32[]{:S(2)}) collective-permute-start(bf16[2048,256]{1,0:T(8,128)(2,1)S(1)} %get-tuple-element.55.refs_2_), channel_id=1, source_target_pairs={{0,16},{1,9},{10,26},{21,29}} | collective-permute-start | bytes 3145736 | tf_op jit(solution)/shard_map/ppermute | solution.py:349
  76.8 15.8 %collective-permute-start.7 = (bf16[2048,256]{1,0:T(8,128)(2,1)S(1)}, bf16[2048,256]{1,0:T(8,128)(2,1)S(1)}, u32[]{:S(2)}, u32[]{:S(2)}) collective-permute-start(bf16[2048,256]{1,0:T(8,128)(2,1)S(1)} %collective-permute-done.5.refs_3_), channel_id=1, source_target_pairs={{8,24},{17,25},{2,18},{27,19}} | collective-permute-start | bytes 3145736 | tf_op jit(solution)/shard_map/ppermute | solution.py:349
  81.0 22.3 %collective-permute-start.12 = (bf16[2112,256]{1,0:T(8,128)(2,1)S(1)}, bf16[2112,256]{1,0:T(8,128)(2,1)S(1)}, u32[]{:S(2)}, u32[]{:S(2)}) collective-permute-start(bf16[2112,256]{1,0:T(8,128)(2,1)S(1)} %get-tuple-element.60.refs_6_), channel_id=1, source_target_pairs={{8,0},{17,1},{2,10},{27,11},{28,20}} | collective-permute-start | bytes 3244040 | tf_op jit(solution)/shard_map/ppermute | solution.py:349
  81.8 21.6 %collective-permute-start.14 = (bf16[2048,256]{1,0:T(8,128)(2,1)S(1)}, bf16[2048,256]{1,0:T(8,128)(2,1)S(1)}, u32[]{:S(2)}, u32[]{:S(2)}) collective-permute-start(bf16[2048,256]{1,0:T(8,128)(2,1)S(1)} %get-tuple-element.66.refs_2_), channel_id=1, source_target_pairs={{0,16},{1,9},{10,26},{21,29}} | collective-permute-start | bytes 3145736 | tf_op jit(solution)/shard_map/ppermute | solution.py:349
  82.5 24.5 %collective-permute-start.15 = (bf16[2048,256]{1,0:T(8,128)(2,1)S(1)}, bf16[2048,256]{1,0:T(8,128)(2,1)S(1)}, u32[]{:S(2)}, u32[]{:S(2)}) collective-permute-start(bf16[2048,256]{1,0:T(8,128)(2,1)S(1)} %collective-permute-done.9.refs_4_.refs_3_), channel_id=1, source_target_pairs={{8,24},{17,25},{2,18},{27,19}} | collective-permute-start | bytes 3145736 | tf_op jit(solution)/shard_map/ppermute | solution.py:349
  99.0 8.1 %collective-permute-start.10 = (f32[1024,256]{1,0:T(8,128)S(1)}, f32[1024,256]{1,0:T(8,128)S(1)}, u32[]{:S(2)}, u32[]{:S(2)}) collective-permute-start(f32[1024,256]{1,0:T(8,128)S(1)} %get-tuple-element.62), channel_id=1, source_target_pairs={{0,1},{1,0},{8,9},{9,8},{10,11},{11,10},{16,17},{17,16},{18,19},{1... | collective-permute-start | bytes 3145736 | tf_op jit(solution)/shard_map/ppermute | solution.py:349
  101.0 6.1 %collective-permute-start.11 = (f32[1024,256]{1,0:T(8,128)S(1)}, f32[1024,256]{1,0:T(8,128)S(1)}, u32[]{:S(2)}, u32[]{:S(2)}) collective-permute-start(f32[1024,256]{1,0:T(8,128)S(1)} %get-tuple-element.63), channel_id=1, source_target_pairs={{0,1},{1,0},{8,9},{9,8},{10,11},{11,10},{16,17},{17,16},{18,19},{1... | collective-permute-start | bytes 3145736 | tf_op jit(solution)/shard_map/ppermute | solution.py:349
  106.3 18.7 %collective-permute-start.16 = (bf16[2112,256]{1,0:T(8,128)(2,1)S(1)}, bf16[2112,256]{1,0:T(8,128)(2,1)S(1)}, u32[]{:S(2)}, u32[]{:S(2)}) collective-permute-start(bf16[2112,256]{1,0:T(8,128)(2,1)S(1)} %get-tuple-element.67.refs_6_), channel_id=1, source_target_pairs={{8,0},{17,1},{2,10},{27,11},{28,20}} | collective-permute-start | bytes 3244040 | tf_op jit(solution)/shard_map/ppermute | solution.py:349
  109.4 15.6 %collective-permute-start.17 = (bf16[528,256]{1,0:T(8,128)(2,1)S(1)}, bf16[528,256]{1,0:T(8,128)(2,1)S(1)}, u32[]{:S(2)}, u32[]{:S(2)}) collective-permute-start(bf16[528,256]{1,0:T(8,128)(2,1)S(1)} %get-tuple-element.71), channel_id=1, source_target_pairs={{1,4},{9,12},{10,9},{11,13},{17,20},{18,17},{19,21},{20,18},{21,22... | collective-permute-start | bytes 811016 | tf_op jit(solution)/shard_map/ppermute | solution.py:349
  116.7 8.4 %collective-permute-start.18 = (bf16[528,256]{1,0:T(8,128)(2,1)S(1)}, bf16[528,256]{1,0:T(8,128)(2,1)S(1)}, u32[]{:S(2)}, u32[]{:S(2)}) collective-permute-start(bf16[528,256]{1,0:T(8,128)(2,1)S(1)} %get-tuple-element.72), channel_id=1, source_target_pairs={{0,1},{1,5},{8,9},{9,13},{11,14},{16,17},{17,21},{19,22},{20,19},{... | collective-permute-start | bytes 811016 | tf_op jit(solution)/shard_map/ppermute | solution.py:349
  125.1 14.6 %collective-permute-start.21 = (f32[1024,256]{1,0:T(8,128)S(1)}, f32[1024,256]{1,0:T(8,128)S(1)}, u32[]{:S(2)}, u32[]{:S(2)}) collective-permute-start(f32[1024,256]{1,0:T(8,128)S(1)} %get-tuple-element.78), channel_id=1, source_target_pairs={{0,1},{1,0},{8,9},{9,8},{10,11},{11,10},{16,17},{17,16},{18,19},{1... | collective-permute-start | bytes 3145736 | tf_op jit(solution)/shard_map/ppermute | solution.py:349
  131.3 8.4 %collective-permute-start.22 = (f32[1024,256]{1,0:T(8,128)S(1)}, f32[1024,256]{1,0:T(8,128)S(1)}, u32[]{:S(2)}, u32[]{:S(2)}) collective-permute-start(f32[1024,256]{1,0:T(8,128)S(1)} %get-tuple-element.79), channel_id=1, source_target_pairs={{0,1},{1,0},{8,9},{9,8},{10,11},{11,10},{16,17},{17,16},{18,19},{1... | collective-permute-start | bytes 3145736 | tf_op jit(solution)/shard_map/ppermute | solution.py:349
  133.2 17.6 %collective-permute-start.19 = (bf16[528,256]{1,0:T(8,128)(2,1)S(1)}, bf16[528,256]{1,0:T(8,128)(2,1)S(1)}, u32[]{:S(2)}, u32[]{:S(2)}) collective-permute-start(bf16[528,256]{1,0:T(8,128)(2,1)S(1)} %get-tuple-element.75), channel_id=1, source_target_pairs={{0,2},{1,6},{8,10},{9,14},{10,11},{11,15},{16,18},{17,22},{18,19},... | collective-permute-start | bytes 811016 | tf_op jit(solution)/shard_map/ppermute | solution.py:349
  137.7 18.9 %collective-permute-start.20 = (bf16[528,256]{1,0:T(8,128)(2,1)S(1)}, bf16[528,256]{1,0:T(8,128)(2,1)S(1)}, u32[]{:S(2)}, u32[]{:S(2)}) collective-permute-start(bf16[528,256]{1,0:T(8,128)(2,1)S(1)} %get-tuple-element.76), channel_id=1, source_target_pairs={{0,3},{1,7},{8,11},{9,15},{10,8},{11,12},{16,19},{17,23},{18,16},{... | collective-permute-start | bytes 811016 | tf_op jit(solution)/shard_map/ppermute | solution.py:349
  141.8 16.4 %collective-permute-start.23 = (bf16[528,256]{1,0:T(8,128)(2,1)S(1)}, bf16[528,256]{1,0:T(8,128)(2,1)S(1)}, u32[]{:S(2)}, u32[]{:S(2)}) collective-permute-start(bf16[528,256]{1,0:T(8,128)(2,1)S(1)} %get-tuple-element.83), channel_id=1, source_target_pairs={{1,4},{9,12},{10,9},{11,13},{17,20},{18,17},{19,21},{20,18},{21,22... | collective-permute-start | bytes 811016 | tf_op jit(solution)/shard_map/ppermute | solution.py:349
  146.4 12.6 %collective-permute-start.24 = (bf16[528,256]{1,0:T(8,128)(2,1)S(1)}, bf16[528,256]{1,0:T(8,128)(2,1)S(1)}, u32[]{:S(2)}, u32[]{:S(2)}) collective-permute-start(bf16[528,256]{1,0:T(8,128)(2,1)S(1)} %get-tuple-element.84), channel_id=1, source_target_pairs={{0,1},{1,5},{8,9},{9,13},{11,14},{16,17},{17,21},{19,22},{20,19},{... | collective-permute-start | bytes 811016 | tf_op jit(solution)/shard_map/ppermute | solution.py:349
  148.8 15.1 %collective-permute-start.25 = (bf16[528,256]{1,0:T(8,128)(2,1)S(1)}, bf16[528,256]{1,0:T(8,128)(2,1)S(1)}, u32[]{:S(2)}, u32[]{:S(2)}) collective-permute-start(bf16[528,256]{1,0:T(8,128)(2,1)S(1)} %get-tuple-element.85), channel_id=1, source_target_pairs={{0,2},{1,6},{8,10},{9,14},{10,11},{11,15},{16,18},{17,22},{18,19},... | collective-permute-start | bytes 811016 | tf_op jit(solution)/shard_map/ppermute | solution.py:349
  150.8 23.4 %collective-permute-start.26 = (bf16[528,256]{1,0:T(8,128)(2,1)S(1)}, bf16[528,256]{1,0:T(8,128)(2,1)S(1)}, u32[]{:S(2)}, u32[]{:S(2)}) collective-permute-start(bf16[528,256]{1,0:T(8,128)(2,1)S(1)} %get-tuple-element.86), channel_id=1, source_target_pairs={{0,3},{1,7},{8,11},{9,15},{10,8},{11,12},{16,19},{17,23},{18,16},{... | collective-permute-start | bytes 811016 | tf_op jit(solution)/shard_map/ppermute | solution.py:349

commit v8 on v6

--- a/solution.py
+++ b/solution.py
@@ -455,9 +455,9 @@
     to_a = collect(bits - 1, message_a)
     partial_b, message_b = mirrored_product(ids, matrix, diagonal, mine, other, piece, 1, [message_a])
     to_b = collect(bits - 1, message_b)
-    widen(panels_a, [message_b, panels_b[1]])
+    widen(panels_a, [message_b])
     widen(panels_b, [panels_a[1]])
-    partial_a, to_a, relayed = relaying(partial_a, to_a, [], [message_b])
+    partial_a, to_a, relayed = relaying(partial_a, to_a, [], [message_b, panels_b[1]])
     keep_a, *give_a = direct_product(ids, matrix, panels_a, [relayed])
     got_a = [send(x, swap) for x in give_a]
     partial_b, to_b, relayed = relaying(partial_b, to_b, [], [keep_a, to_a, panels_b[2]])

time: 173 us -> 173 us (level)
  no operation moved by 1% of the time
where the time goes in v8:
time: 173 us
  starting transfers between devices  61.5 us (36%)
  waiting for transfers between devices  56.7 us (33%)
  Pallas kernels  48.1 us (28%)
  local copies, waits for them, and re-layouts  5.86 us (3%)
    ppermute x27, starting transfers between devices, send(): return lax.ppermute(x, ('row', 'col'), [(at(*s), at(*d)) for s, d in pairs])  61.5 us
    ppermute x27, waiting for transfers between devices, send(): return lax.ppermute(x, ('row', 'col'), [(at(*s), at(*d)) for s, d in pairs])  56.7 us
    pallas_call x12, Pallas kernels, local(): pl.pallas_call(body, out_shape=out_shape, in_specs=[pl.BlockSpec(memory_s...  46.3 us
    unnamed x4, local copies, waits for them, and re-layouts  5.77 us
  transfers between devices with their start and end apart: 27, of which 9 were waited for; matrix products, arithmetic and copies ran while one was open for 0% of the time, Pallas kernels for 26%

profile of v8, /device:TPU:7, one launch (start us, length us, event | category | flops | bytes accessed | tf_op | source)
XLA Modules:
  0.0 172.7 jit_solution(11052183365327563583)
XLA Ops:
  0.0 4.2 %collective-permute-start = (bf16[512,512]{1,0:T(8,128)(2,1)}, bf16[512,512]{1,0:T(8,128)(2,1)S(1)}, u32[]{:S(2)}, u32[]{:S(2)}) collective-permute-start(bf16[512,512]{1,0:T(8,128)(2,1)} %refs_1_.1), channel_id=1, source_target_pairs={{4,0},{5,1},{6,2},{7,3},{12,8},{13,9},{14,10},{15,11},{16,20},{17,... | collective-permute-start | bytes 1572872 | tf_op jit(solution)/shard_map/ppermute | solution.py:349
  4.2 3.2 %collective-permute-start.1 = (bf16[512,512]{1,0:T(8,128)(2,1)}, bf16[512,512]{1,0:T(8,128)(2,1)S(1)}, u32[]{:S(2)}, u32[]{:S(2)}) collective-permute-start(bf16[512,512]{1,0:T(8,128)(2,1)} %refs_1_.1), channel_id=1, source_target_pairs={{8,10},{9,11},{16,18},{17,19},{18,20},{19,21},{24,26},{25,27},{26,... | collective-permute-start | bytes 1572872 | tf_op jit(solution)/shard_map/ppermute | solution.py:349
  8.9 5.8 %copy-done = bf16[4096,2048]{1,0:T(8,128)(2,1)S(1)} copy-done((bf16[4096,2048]{1,0:T(8,128)(2,1)S(1)}, bf16[4096,2048]{1,0:T(8,128)(2,1)}, u32[]{:S(2)}) %copy-start) | copy-done | bytes 16777240
  16.4 10.7 %collective-permute-done.refs_2_ = bf16[512,512]{1,0:T(8,128)(2,1)S(1)} collective-permute-done((bf16[512,512]{1,0:T(8,128)(2,1)}, bf16[512,512]{1,0:T(8,128)(2,1)S(1)}, u32[]{:S(2)}, u32[]{:S(2)}) %collective-permute-start) | collective-permute-done | bytes 524320 | tf_op jit(solution)/shard_map/ppermute | solution.py:349
  28.4 3.5 %collective-permute-done.2.refs_4_ = bf16[512,512]{1,0:T(8,128)(2,1)S(1)} collective-permute-done((bf16[512,512]{1,0:T(8,128)(2,1)}, bf16[512,512]{1,0:T(8,128)(2,1)S(1)}, u32[]{:S(2)}, u32[]{:S(2)}) %collective-permute-start.2) | collective-permute-done | bytes 524320 | tf_op jit(solution)/shard_map/ppermute | solution.py:349
  31.9 11.2 %collective-permute-done.3.refs_5_ = bf16[512,512]{1,0:T(8,128)(2,1)S(1)} collective-permute-done((bf16[512,512]{1,0:T(8,128)(2,1)S(1)}, bf16[512,512]{1,0:T(8,128)(2,1)S(1)}, u32[]{:S(2)}, u32[]{:S(2)}) %collective-permute-start.3) | collective-permute-done | bytes 524320 | tf_op jit(solution)/shard_map/ppermute | solution.py:349
  43.8 4.1 %collective-permute-start.4 = (bf16[2048,512]{1,0:T(8,128)(2,1)S(1)}, bf16[2048,512]{1,0:T(8,128)(2,1)S(1)}, u32[]{:S(2)}, u32[]{:S(2)}) collective-permute-start(bf16[2048,512]{1,0:T(8,128)(2,1)S(1)} %line.1.refs_1_.refs_3_), channel_id=1, source_target_pairs={{0,1},{1,0},{8,9},{9,8},{10,11},{11,10},{16,17},{17,16},{18,19},{1... | collective-permute-start | bytes 6291464 | tf_op jit(solution)/shard_map/ppermute | solution.py:349
  47.9 3.8 %collective-permute-done.4.refs_2_.refs_4_ = bf16[2048,512]{1,0:T(8,128)(2,1)S(1)} collective-permute-done((bf16[2048,512]{1,0:T(8,128)(2,1)S(1)}, bf16[2048,512]{1,0:T(8,128)(2,1)S(1)}, u32[]{:S(2)}, u32[]{:S(2)}) %collective-permute-start.4) | collective-permute-done | bytes 2097184 | tf_op jit(solution)/shard_map/ppermute | solution.py:349
  53.1 8.8 %mirrored_product.2 = (f32[2048,256]{1,0:T(8,128)S(1)}, bf16[2112,256]{1,0:T(8,128)(2,1)S(1)}) custom-call(s32[5]{0:T(128)S(1)} %stack.23.ids.refs_0_, bf16[4096,2048]{1,0:T(8,128)(2,1)S(1)} %get-tuple-element.45.refs_1_, f32[8,2048]{1,0:T(8,128)S(1)} %get-tuple-element.48.refs_2_, bf16[2048,512]{1,0:T(8,128)(2,1)S(1)} %line.1.refs_1_.refs_3_, ...), custom_call_target="tpu_custom_call" | custom-call | tf_op jit(solution)/shard_map/mirrored_product/pallas_call | solution.py:48
  64.0 8.8 %mirrored_product.3 = (f32[2048,256]{1,0:T(8,128)S(1)}, bf16[2112,256]{1,0:T(8,128)(2,1)S(1)}) custom-call(s32[5]{0:T(128)S(1)} %stack.23.ids.refs_0_, bf16[4096,2048]{1,0:T(8,128)(2,1)S(1)} %get-tuple-element.45.refs_1_, f32[8,2048]{1,0:T(8,128)S(1)} %get-tuple-element.48.refs_2_, bf16[2048,512]{1,0:T(8,128)(2,1)S(1)} %line.1.refs_1_.refs_3_, ...), custom_call_target="tpu_custom_call" | custom-call | tf_op jit(solution)/shard_map/mirrored_product/pallas_call | solution.py:48
  76.3 2.9 %relay.2 = (f32[2048,256]{1,0:T(8,128)S(1)}, bf16[2112,256]{1,0:T(8,128)(2,1)S(1)}) custom-call(s32[5]{0:T(128)S(1)} %stack.23.ids.refs_0_, f32[2048,256]{1,0:T(8,128)S(1)} %get-tuple-element.53.refs_1_, bf16[2112,256]{1,0:T(8,128)(2,1)S(1)} %collective-permute-done.8.refs_2_, bf16[2112,256]{1,0:T(8,128)(2,1)S(1)} %get-tuple-element.50.refs_3_, ...), custom_call_target="tpu_custom_call" | custom-call | tf_op jit(solution)/shard_map/relay/pallas_call | solution.py:48
  82.0 8.8 %collective-permute-done.7.refs_5_ = bf16[2048,256]{1,0:T(8,128)(2,1)S(1)} collective-permute-done((bf16[2048,256]{1,0:T(8,128)(2,1)S(1)}, bf16[2048,256]{1,0:T(8,128)(2,1)S(1)}, u32[]{:S(2)}, u32[]{:S(2)}) %collective-permute-start.7) | collective-permute-done | bytes 1048608 | tf_op jit(solution)/shard_map/ppermute | solution.py:349
  90.8 6.4 %direct_product.2 = (f32[2048,256]{1,0:T(8,128)S(1)}, f32[1024,256]{1,0:T(8,128)S(1)}, f32[1024,256]{1,0:T(8,128)S(1)}) custom-call(s32[5]{0:T(128)S(1)} %stack.23.ids.refs_0_, bf16[4096,2048]{1,0:T(8,128)(2,1)S(1)} %get-tuple-element.45.refs_1_, bf16[2048,256]{1,0:T(8,128)(2,1)S(1)} %get-tuple-element.51.refs_2_, ...), custom_call_target="tpu_custom_call" | custom-call | tf_op jit(solution)/shard_map/direct_product/pallas_call | solution.py:48
  97.2 3.4 %collective-permute-start.10 = (f32[1024,256]{1,0:T(8,128)S(1)}, f32[1024,256]{1,0:T(8,128)S(1)}, u32[]{:S(2)}, u32[]{:S(2)}) collective-permute-start(f32[1024,256]{1,0:T(8,128)S(1)} %get-tuple-element.58), channel_id=1, source_target_pairs={{0,1},{1,0},{8,9},{9,8},{10,11},{11,10},{16,17},{17,16},{18,19},{1... | collective-permute-start | bytes 3145736 | tf_op jit(solution)/shard_map/ppermute | solution.py:349
  100.6 1.9 %collective-permute-start.11 = (f32[1024,256]{1,0:T(8,128)S(1)}, f32[1024,256]{1,0:T(8,128)S(1)}, u32[]{:S(2)}, u32[]{:S(2)}) collective-permute-start(f32[1024,256]{1,0:T(8,128)S(1)} %get-tuple-element.59), channel_id=1, source_target_pairs={{0,1},{1,0},{8,9},{9,8},{10,11},{11,10},{16,17},{17,16},{18,19},{1... | collective-permute-start | bytes 3145736 | tf_op jit(solution)/shard_map/ppermute | solution.py:349
  102.5 2.9 %relay.3 = (f32[2048,256]{1,0:T(8,128)S(1)}, bf16[2112,256]{1,0:T(8,128)(2,1)S(1)}) custom-call(s32[5]{0:T(128)S(1)} %stack.23.ids.refs_0_, f32[2048,256]{1,0:T(8,128)S(1)} %get-tuple-element.61.refs_1_, bf16[2112,256]{1,0:T(8,128)(2,1)S(1)} %collective-permute-done.13.refs_2_, f32[2048,256]{1,0:T(8,128)S(1)} %get-tuple-element.57.refs_3_.refs_1_, ...), custom_call_target="tpu_custom_call" | custom-call | tf_op jit(solution)/shard_map/relay/pallas_call | solution.py:48
  106.3 2.3 %pack.2 = (f32[512,256]{1,0:T(8,128)S(1)}, bf16[528,256]{1,0:T(8,128)(2,1)S(1)}, bf16[528,256]{1,0:T(8,128)(2,1)S(1)}, bf16[528,256]{1,0:T(8,128)(2,1)S(1)}, bf16[528,256]{1,0:T(8,128)(2,1)S(1)}) custom-call(s32[5]{0:T(128)S(1)} %stack.23.ids.refs_0_, f32[2048,256]{1,0:T(8,128)S(1)} %get-tuple-element.57.refs_3_.refs_1_, ...), custom_call_target="tpu_custom_call" | custom-call | tf_op jit(solution)/shard_map/pack/pallas_call | solution.py:48
  108.6 4.0 %collective-permute-start.17 = (bf16[528,256]{1,0:T(8,128)(2,1)S(1)}, bf16[528,256]{1,0:T(8,128)(2,1)S(1)}, u32[]{:S(2)}, u32[]{:S(2)}) collective-permute-start(bf16[528,256]{1,0:T(8,128)(2,1)S(1)} %get-tuple-element.67), channel_id=1, source_target_pairs={{1,4},{9,12},{10,9},{11,13},{17,20},{18,17},{19,21},{20,18},{21,22... | collective-permute-start | bytes 811016 | tf_op jit(solution)/shard_map/ppermute | solution.py:349
  112.6 1.9 %collective-permute-start.18 = (bf16[528,256]{1,0:T(8,128)(2,1)S(1)}, bf16[528,256]{1,0:T(8,128)(2,1)S(1)}, u32[]{:S(2)}, u32[]{:S(2)}) collective-permute-start(bf16[528,256]{1,0:T(8,128)(2,1)S(1)} %get-tuple-element.68), channel_id=1, source_target_pairs={{0,1},{1,5},{8,9},{9,13},{11,14},{16,17},{17,21},{19,22},{20,19},{... | collective-permute-start | bytes 811016 | tf_op jit(solution)/shard_map/ppermute | solution.py:349
  114.5 6.4 %direct_product.3 = (f32[2048,256]{1,0:T(8,128)S(1)}, f32[1024,256]{1,0:T(8,128)S(1)}, f32[1024,256]{1,0:T(8,128)S(1)}) custom-call(s32[5]{0:T(128)S(1)} %stack.23.ids.refs_0_, bf16[4096,2048]{1,0:T(8,128)(2,1)S(1)} %get-tuple-element.45.refs_1_, bf16[2048,256]{1,0:T(8,128)(2,1)S(1)} %get-tuple-element.62.refs_2_, ...), custom_call_target="tpu_custom_call" | custom-call | tf_op jit(solution)/shard_map/direct_product/pallas_call | solution.py:48
  120.9 6.3 %collective-permute-start.21 = (f32[1024,256]{1,0:T(8,128)S(1)}, f32[1024,256]{1,0:T(8,128)S(1)}, u32[]{:S(2)}, u32[]{:S(2)}) collective-permute-start(f32[1024,256]{1,0:T(8,128)S(1)} %get-tuple-element.74), channel_id=1, source_target_pairs={{0,1},{1,0},{8,9},{9,8},{10,11},{11,10},{16,17},{17,16},{18,19},{1... | collective-permute-start | bytes 3145736 | tf_op jit(solution)/shard_map/ppermute | solution.py:349
  127.2 1.9 %collective-permute-start.22 = (f32[1024,256]{1,0:T(8,128)S(1)}, f32[1024,256]{1,0:T(8,128)S(1)}, u32[]{:S(2)}, u32[]{:S(2)}) collective-permute-start(f32[1024,256]{1,0:T(8,128)S(1)} %get-tuple-element.75), channel_id=1, source_target_pairs={{0,1},{1,0},{8,9},{9,8},{10,11},{11,10},{16,17},{17,16},{18,19},{1... | collective-permute-start | bytes 3145736 | tf_op jit(solution)/shard_map/ppermute | solution.py:349
  129.1 4.5 %collective-permute-start.19 = (bf16[528,256]{1,0:T(8,128)(2,1)S(1)}, bf16[528,256]{1,0:T(8,128)(2,1)S(1)}, u32[]{:S(2)}, u32[]{:S(2)}) collective-permute-start(bf16[528,256]{1,0:T(8,128)(2,1)S(1)} %get-tuple-element.71), channel_id=1, source_target_pairs={{0,2},{1,6},{8,10},{9,14},{10,11},{11,15},{16,18},{17,22},{18,19},... | collective-permute-start | bytes 811016 | tf_op jit(solution)/shard_map/ppermute | solution.py:349
  133.6 1.9 %collective-permute-start.20 = (bf16[528,256]{1,0:T(8,128)(2,1)S(1)}, bf16[528,256]{1,0:T(8,128)(2,1)S(1)}, u32[]{:S(2)}, u32[]{:S(2)}) collective-permute-start(bf16[528,256]{1,0:T(8,128)(2,1)S(1)} %get-tuple-element.72), channel_id=1, source_target_pairs={{0,3},{1,7},{8,11},{9,15},{10,8},{11,12},{16,19},{17,23},{18,16},{... | collective-permute-start | bytes 811016 | tf_op jit(solution)/shard_map/ppermute | solution.py:349
  135.6 2.1 %pack.3 = (f32[512,256]{1,0:T(8,128)S(1)}, bf16[528,256]{1,0:T(8,128)(2,1)S(1)}, bf16[528,256]{1,0:T(8,128)(2,1)S(1)}, bf16[528,256]{1,0:T(8,128)(2,1)S(1)}, bf16[528,256]{1,0:T(8,128)(2,1)S(1)}) custom-call(s32[5]{0:T(128)S(1)} %stack.23.ids.refs_0_, f32[2048,256]{1,0:T(8,128)S(1)} %get-tuple-element.73.refs_1_, ...), custom_call_target="tpu_custom_call" | custom-call | tf_op jit(solution)/shard_map/pack/pallas_call | solution.py:48
  137.7 4.5 %collective-permute-start.23 = (bf16[528,256]{1,0:T(8,128)(2,1)S(1)}, bf16[528,256]{1,0:T(8,128)(2,1)S(1)}, u32[]{:S(2)}, u32[]{:S(2)}) collective-permute-start(bf16[528,256]{1,0:T(8,128)(2,1)S(1)} %get-tuple-element.79), channel_id=1, source_target_pairs={{1,4},{9,12},{10,9},{11,13},{17,20},{18,17},{19,21},{20,18},{21,22... | collective-permute-start | bytes 811016 | tf_op jit(solution)/shard_map/ppermute | solution.py:349
  142.3 2.5 %collective-permute-start.24 = (bf16[528,256]{1,0:T(8,128)(2,1)S(1)}, bf16[528,256]{1,0:T(8,128)(2,1)S(1)}, u32[]{:S(2)}, u32[]{:S(2)}) collective-permute-start(bf16[528,256]{1,0:T(8,128)(2,1)S(1)} %get-tuple-element.80), channel_id=1, source_target_pairs={{0,1},{1,5},{8,9},{9,13},{11,14},{16,17},{17,21},{19,22},{20,19},{... | collective-permute-start | bytes 811016 | tf_op jit(solution)/shard_map/ppermute | solution.py:349
  146.7 3.1 %collective-permute-start.26 = (bf16[528,256]{1,0:T(8,128)(2,1)S(1)}, bf16[528,256]{1,0:T(8,128)(2,1)S(1)}, u32[]{:S(2)}, u32[]{:S(2)}) collective-permute-start(bf16[528,256]{1,0:T(8,128)(2,1)S(1)} %get-tuple-element.82), channel_id=1, source_target_pairs={{0,3},{1,7},{8,11},{9,15},{10,8},{11,12},{16,19},{17,23},{18,16},{... | collective-permute-start | bytes 811016 | tf_op jit(solution)/shard_map/ppermute | solution.py:349
  149.8 2.8 %collective-permute-done.20.refs_6_ = bf16[528,256]{1,0:T(8,128)(2,1)S(1)} collective-permute-done((bf16[528,256]{1,0:T(8,128)(2,1)S(1)}, bf16[528,256]{1,0:T(8,128)(2,1)S(1)}, u32[]{:S(2)}, u32[]{:S(2)}) %collective-permute-start.20) | collective-permute-done | bytes 270368 | tf_op jit(solution)/shard_map/ppermute | solution.py:349
  154.8 5.0 %collective-permute-done.25.refs_5_ = bf16[528,256]{1,0:T(8,128)(2,1)S(1)} collective-permute-done((bf16[528,256]{1,0:T(8,128)(2,1)S(1)}, bf16[528,256]{1,0:T(8,128)(2,1)S(1)}, u32[]{:S(2)}, u32[]{:S(2)}) %collective-permute-start.25) | collective-permute-done | bytes 270368 | tf_op jit(solution)/shard_map/ppermute | solution.py:349
  159.8 10.3 %collective-permute-done.26.refs_6_ = bf16[528,256]{1,0:T(8,128)(2,1)S(1)} collective-permute-done((bf16[528,256]{1,0:T(8,128)(2,1)S(1)}, bf16[528,256]{1,0:T(8,128)(2,1)S(1)}, u32[]{:S(2)}, u32[]{:S(2)}) %collective-permute-start.26) | collective-permute-done | bytes 270368 | tf_op jit(solution)/shard_map/ppermute | solution.py:349
  170.1 2.6 %finish.3 = f32[512,512]{1,0:T(8,128)} custom-call(s32[5]{0:T(128)S(1)} %stack.23.ids.refs_0_, f32[512,256]{1,0:T(8,128)S(1)} %finish.2.refs_1_, f32[512,256]{1,0:T(8,128)S(1)} %get-tuple-element.78.refs_7_.refs_2_, bf16[528,256]{1,0:T(8,128)(2,1)S(1)} %collective-permute-done.23.refs_3_, bf16[528,256]{1,0:T(8,128)(2,1)S(1)} %collective-permute-done.24.refs_4_, ...), custom_call_target="tpu_custom_call" | custom-call | tf_op jit(solution)/shard_map/finish/pallas_call | solution.py:48
  (40 shorter events, 19.7 us)
Async XLA Ops:
  0.0 27.1 %collective-permute-start = (bf16[512,512]{1,0:T(8,128)(2,1)}, bf16[512,512]{1,0:T(8,128)(2,1)S(1)}, u32[]{:S(2)}, u32[]{:S(2)}) collective-permute-start(bf16[512,512]{1,0:T(8,128)(2,1)} %refs_1_.1), channel_id=1, source_target_pairs={{4,0},{5,1},{6,2},{7,3},{12,8},{13,9},{14,10},{15,11},{16,20},{17,... | collective-permute-start | bytes 1572872 | tf_op jit(solution)/shard_map/ppermute | solution.py:349
  4.2 24.2 %collective-permute-start.1 = (bf16[512,512]{1,0:T(8,128)(2,1)}, bf16[512,512]{1,0:T(8,128)(2,1)S(1)}, u32[]{:S(2)}, u32[]{:S(2)}) collective-permute-start(bf16[512,512]{1,0:T(8,128)(2,1)} %refs_1_.1), channel_id=1, source_target_pairs={{8,10},{9,11},{16,18},{17,19},{18,20},{19,21},{24,26},{25,27},{26,... | collective-permute-start | bytes 1572872 | tf_op jit(solution)/shard_map/ppermute | solution.py:349
  7.5 24.4 %collective-permute-start.2 = (bf16[512,512]{1,0:T(8,128)(2,1)}, bf16[512,512]{1,0:T(8,128)(2,1)S(1)}, u32[]{:S(2)}, u32[]{:S(2)}) collective-permute-start(bf16[512,512]{1,0:T(8,128)(2,1)} %refs_1_.1), channel_id=1, source_target_pairs={{2,0},{3,1},{10,8},{11,9},{12,10},{13,11},{18,16},{19,17},{20,18},... | collective-permute-start | bytes 1572872 | tf_op jit(solution)/shard_map/ppermute | solution.py:349
  8.9 5.8 %copy-start = (bf16[4096,2048]{1,0:T(8,128)(2,1)S(1)}, bf16[4096,2048]{1,0:T(8,128)(2,1)}, u32[]{:S(2)}) copy-start(bf16[4096,2048]{1,0:T(8,128)(2,1)} %a_ref.1) | copy-start | bytes 50331652
  14.6 28.5 %copy-start.1 = (bf16[512,512]{1,0:T(8,128)(2,1)S(1)}, bf16[512,512]{1,0:T(8,128)(2,1)}, u32[]{:S(2)}) copy-start(bf16[512,512]{1,0:T(8,128)(2,1)} %refs_1_.1) | copy-start | bytes 1572868
  27.1 16.0 %collective-permute-start.3 = (bf16[512,512]{1,0:T(8,128)(2,1)S(1)}, bf16[512,512]{1,0:T(8,128)(2,1)S(1)}, u32[]{:S(2)}, u32[]{:S(2)}) collective-permute-start(bf16[512,512]{1,0:T(8,128)(2,1)S(1)} %collective-permute-done.refs_2_), channel_id=1, source_target_pairs={{2,0},{3,1},{10,8},{11,9},{18,16},{19,17},{26,24},{27,25},{28,30},... | collective-permute-start | bytes 1572872 | tf_op jit(solution)/shard_map/ppermute | solution.py:349
  43.8 7.8 %collective-permute-start.4 = (bf16[2048,512]{1,0:T(8,128)(2,1)S(1)}, bf16[2048,512]{1,0:T(8,128)(2,1)S(1)}, u32[]{:S(2)}, u32[]{:S(2)}) collective-permute-start(bf16[2048,512]{1,0:T(8,128)(2,1)S(1)} %line.1.refs_1_.refs_3_), channel_id=1, source_target_pairs={{0,1},{1,0},{8,9},{9,8},{10,11},{11,10},{16,17},{17,16},{18,19},{1... | collective-permute-start | bytes 6291464 | tf_op jit(solution)/shard_map/ppermute | solution.py:349
  52.4 21.9 %collective-permute-start.5 = (bf16[2048,256]{1,0:T(8,128)(2,1)S(1)}, bf16[2048,256]{1,0:T(8,128)(2,1)S(1)}, u32[]{:S(2)}, u32[]{:S(2)}) collective-permute-start(bf16[2048,256]{1,0:T(8,128)(2,1)S(1)} %get-tuple-element.51.refs_2_), channel_id=1, source_target_pairs={{0,8},{1,17},{10,2},{11,27},{20,28}} | collective-permute-start | bytes 3145736 | tf_op jit(solution)/shard_map/ppermute | solution.py:349
  61.9 14.4 %collective-permute-start.8 = (bf16[2112,256]{1,0:T(8,128)(2,1)S(1)}, bf16[2112,256]{1,0:T(8,128)(2,1)S(1)}, u32[]{:S(2)}, u32[]{:S(2)}) collective-permute-start(bf16[2112,256]{1,0:T(8,128)(2,1)S(1)} %get-tuple-element.49.refs_5_), channel_id=1, source_target_pairs={{16,0},{24,8},{9,1},{25,17},{26,10},{18,2},{19,27},{29,21}} | collective-permute-start | bytes 3244040 | tf_op jit(solution)/shard_map/ppermute | solution.py:349
  63.3 13.0 %collective-permute-start.9 = (bf16[2048,256]{1,0:T(8,128)(2,1)S(1)}, bf16[2048,256]{1,0:T(8,128)(2,1)S(1)}, u32[]{:S(2)}, u32[]{:S(2)}) collective-permute-start(bf16[2048,256]{1,0:T(8,128)(2,1)S(1)} %get-tuple-element.62.refs_2_), channel_id=1, source_target_pairs={{0,8},{1,17},{10,2},{11,27},{20,28}} | collective-permute-start | bytes 3145736 | tf_op jit(solution)/shard_map/ppermute | solution.py:349
  72.9 27.7 %collective-permute-start.13 = (bf16[2112,256]{1,0:T(8,128)(2,1)S(1)}, bf16[2112,256]{1,0:T(8,128)(2,1)S(1)}, u32[]{:S(2)}, u32[]{:S(2)}) collective-permute-start(bf16[2112,256]{1,0:T(8,128)(2,1)S(1)} %get-tuple-element.50.refs_3_), channel_id=1, source_target_pairs={{16,0},{24,8},{9,1},{25,17},{26,10},{18,2},{19,27},{29,21}} | collective-permute-start | bytes 3244040 | tf_op jit(solution)/shard_map/ppermute | solution.py:349
  74.3 6.5 %collective-permute-start.6 = (bf16[2048,256]{1,0:T(8,128)(2,1)S(1)}, bf16[2048,256]{1,0:T(8,128)(2,1)S(1)}, u32[]{:S(2)}, u32[]{:S(2)}) collective-permute-start(bf16[2048,256]{1,0:T(8,128)(2,1)S(1)} %get-tuple-element.51.refs_2_), channel_id=1, source_target_pairs={{0,16},{1,9},{10,26},{21,29}} | collective-permute-start | bytes 3145736 | tf_op jit(solution)/shard_map/ppermute | solution.py:349
  75.0 15.8 %collective-permute-start.7 = (bf16[2048,256]{1,0:T(8,128)(2,1)S(1)}, bf16[2048,256]{1,0:T(8,128)(2,1)S(1)}, u32[]{:S(2)}, u32[]{:S(2)}) collective-permute-start(bf16[2048,256]{1,0:T(8,128)(2,1)S(1)} %collective-permute-done.5.refs_3_), channel_id=1, source_target_pairs={{8,24},{17,25},{2,18},{27,19}} | collective-permute-start | bytes 3145736 | tf_op jit(solution)/shard_map/ppermute | solution.py:349
  79.2 23.3 %collective-permute-start.12 = (bf16[2112,256]{1,0:T(8,128)(2,1)S(1)}, bf16[2112,256]{1,0:T(8,128)(2,1)S(1)}, u32[]{:S(2)}, u32[]{:S(2)}) collective-permute-start(bf16[2112,256]{1,0:T(8,128)(2,1)S(1)} %get-tuple-element.56.refs_6_), channel_id=1, source_target_pairs={{8,0},{17,1},{2,10},{27,11},{28,20}} | collective-permute-start | bytes 3244040 | tf_op jit(solution)/shard_map/ppermute | solution.py:349
  80.0 22.5 %collective-permute-start.14 = (bf16[2048,256]{1,0:T(8,128)(2,1)S(1)}, bf16[2048,256]{1,0:T(8,128)(2,1)S(1)}, u32[]{:S(2)}, u32[]{:S(2)}) collective-permute-start(bf16[2048,256]{1,0:T(8,128)(2,1)S(1)} %get-tuple-element.62.refs_2_), channel_id=1, source_target_pairs={{0,16},{1,9},{10,26},{21,29}} | collective-permute-start | bytes 3145736 | tf_op jit(solution)/shard_map/ppermute | solution.py:349
  80.7 25.5 %collective-permute-start.15 = (bf16[2048,256]{1,0:T(8,128)(2,1)S(1)}, bf16[2048,256]{1,0:T(8,128)(2,1)S(1)}, u32[]{:S(2)}, u32[]{:S(2)}) collective-permute-start(bf16[2048,256]{1,0:T(8,128)(2,1)S(1)} %collective-permute-done.9.refs_4_.refs_3_), channel_id=1, source_target_pairs={{8,24},{17,25},{2,18},{27,19}} | collective-permute-start | bytes 3145736 | tf_op jit(solution)/shard_map/ppermute | solution.py:349
  97.2 9.0 %collective-permute-start.10 = (f32[1024,256]{1,0:T(8,128)S(1)}, f32[1024,256]{1,0:T(8,128)S(1)}, u32[]{:S(2)}, u32[]{:S(2)}) collective-permute-start(f32[1024,256]{1,0:T(8,128)S(1)} %get-tuple-element.58), channel_id=1, source_target_pairs={{0,1},{1,0},{8,9},{9,8},{10,11},{11,10},{16,17},{17,16},{18,19},{1... | collective-permute-start | bytes 3145736 | tf_op jit(solution)/shard_map/ppermute | solution.py:349
  100.6 5.7 %collective-permute-start.11 = (f32[1024,256]{1,0:T(8,128)S(1)}, f32[1024,256]{1,0:T(8,128)S(1)}, u32[]{:S(2)}, u32[]{:S(2)}) collective-permute-start(f32[1024,256]{1,0:T(8,128)S(1)} %get-tuple-element.59), channel_id=1, source_target_pairs={{0,1},{1,0},{8,9},{9,8},{10,11},{11,10},{16,17},{17,16},{18,19},{1... | collective-permute-start | bytes 3145736 | tf_op jit(solution)/shard_map/ppermute | solution.py:349
  105.5 15.4 %collective-permute-start.16 = (bf16[2112,256]{1,0:T(8,128)(2,1)S(1)}, bf16[2112,256]{1,0:T(8,128)(2,1)S(1)}, u32[]{:S(2)}, u32[]{:S(2)}) collective-permute-start(bf16[2112,256]{1,0:T(8,128)(2,1)S(1)} %get-tuple-element.63.refs_6_), channel_id=1, source_target_pairs={{8,0},{17,1},{2,10},{27,11},{28,20}} | collective-permute-start | bytes 3244040 | tf_op jit(solution)/shard_map/ppermute | solution.py:349
  108.6 12.3 %collective-permute-start.17 = (bf16[528,256]{1,0:T(8,128)(2,1)S(1)}, bf16[528,256]{1,0:T(8,128)(2,1)S(1)}, u32[]{:S(2)}, u32[]{:S(2)}) collective-permute-start(bf16[528,256]{1,0:T(8,128)(2,1)S(1)} %get-tuple-element.67), channel_id=1, source_target_pairs={{1,4},{9,12},{10,9},{11,13},{17,20},{18,17},{19,21},{20,18},{21,22... | collective-permute-start | bytes 811016 | tf_op jit(solution)/shard_map/ppermute | solution.py:349
  112.6 8.4 %collective-permute-start.18 = (bf16[528,256]{1,0:T(8,128)(2,1)S(1)}, bf16[528,256]{1,0:T(8,128)(2,1)S(1)}, u32[]{:S(2)}, u32[]{:S(2)}) collective-permute-start(bf16[528,256]{1,0:T(8,128)(2,1)S(1)} %get-tuple-element.68), channel_id=1, source_target_pairs={{0,1},{1,5},{8,9},{9,13},{11,14},{16,17},{17,21},{19,22},{20,19},{... | collective-permute-start | bytes 811016 | tf_op jit(solution)/shard_map/ppermute | solution.py:349
  120.9 14.6 %collective-permute-start.21 = (f32[1024,256]{1,0:T(8,128)S(1)}, f32[1024,256]{1,0:T(8,128)S(1)}, u32[]{:S(2)}, u32[]{:S(2)}) collective-permute-start(f32[1024,256]{1,0:T(8,128)S(1)} %get-tuple-element.74), channel_id=1, source_target_pairs={{0,1},{1,0},{8,9},{9,8},{10,11},{11,10},{16,17},{17,16},{18,19},{1... | collective-permute-start | bytes 3145736 | tf_op jit(solution)/shard_map/ppermute | solution.py:349
  127.2 8.4 %collective-permute-start.22 = (f32[1024,256]{1,0:T(8,128)S(1)}, f32[1024,256]{1,0:T(8,128)S(1)}, u32[]{:S(2)}, u32[]{:S(2)}) collective-permute-start(f32[1024,256]{1,0:T(8,128)S(1)} %get-tuple-element.75), channel_id=1, source_target_pairs={{0,1},{1,0},{8,9},{9,8},{10,11},{11,10},{16,17},{17,16},{18,19},{1... | collective-permute-start | bytes 3145736 | tf_op jit(solution)/shard_map/ppermute | solution.py:349
  129.1 17.6 %collective-permute-start.19 = (bf16[528,256]{1,0:T(8,128)(2,1)S(1)}, bf16[528,256]{1,0:T(8,128)(2,1)S(1)}, u32[]{:S(2)}, u32[]{:S(2)}) collective-permute-start(bf16[528,256]{1,0:T(8,128)(2,1)S(1)} %get-tuple-element.71), channel_id=1, source_target_pairs={{0,2},{1,6},{8,10},{9,14},{10,11},{11,15},{16,18},{17,22},{18,19},... | collective-permute-start | bytes 811016 | tf_op jit(solution)/shard_map/ppermute | solution.py:349
  133.6 18.9 %collective-permute-start.20 = (bf16[528,256]{1,0:T(8,128)(2,1)S(1)}, bf16[528,256]{1,0:T(8,128)(2,1)S(1)}, u32[]{:S(2)}, u32[]{:S(2)}) collective-permute-start(bf16[528,256]{1,0:T(8,128)(2,1)S(1)} %get-tuple-element.72), channel_id=1, source_target_pairs={{0,3},{1,7},{8,11},{9,15},{10,8},{11,12},{16,19},{17,23},{18,16},{... | collective-permute-start | bytes 811016 | tf_op jit(solution)/shard_map/ppermute | solution.py:349
  137.7 16.4 %collective-permute-start.23 = (bf16[528,256]{1,0:T(8,128)(2,1)S(1)}, bf16[528,256]{1,0:T(8,128)(2,1)S(1)}, u32[]{:S(2)}, u32[]{:S(2)}) collective-permute-start(bf16[528,256]{1,0:T(8,128)(2,1)S(1)} %get-tuple-element.79), channel_id=1, source_target_pairs={{1,4},{9,12},{10,9},{11,13},{17,20},{18,17},{19,21},{20,18},{21,22... | collective-permute-start | bytes 811016 | tf_op jit(solution)/shard_map/ppermute | solution.py:349
  142.3 12.6 %collective-permute-start.24 = (bf16[528,256]{1,0:T(8,128)(2,1)S(1)}, bf16[528,256]{1,0:T(8,128)(2,1)S(1)}, u32[]{:S(2)}, u32[]{:S(2)}) collective-permute-start(bf16[528,256]{1,0:T(8,128)(2,1)S(1)} %get-tuple-element.80), channel_id=1, source_target_pairs={{0,1},{1,5},{8,9},{9,13},{11,14},{16,17},{17,21},{19,22},{20,19},{... | collective-permute-start | bytes 811016 | tf_op jit(solution)/shard_map/ppermute | solution.py:349
  144.7 15.1 %collective-permute-start.25 = (bf16[528,256]{1,0:T(8,128)(2,1)S(1)}, bf16[528,256]{1,0:T(8,128)(2,1)S(1)}, u32[]{:S(2)}, u32[]{:S(2)}) collective-permute-start(bf16[528,256]{1,0:T(8,128)(2,1)S(1)} %get-tuple-element.81), channel_id=1, source_target_pairs={{0,2},{1,6},{8,10},{9,14},{10,11},{11,15},{16,18},{17,22},{18,19},... | collective-permute-start | bytes 811016 | tf_op jit(solution)/shard_map/ppermute | solution.py:349
  146.7 23.4 %collective-permute-start.26 = (bf16[528,256]{1,0:T(8,128)(2,1)S(1)}, bf16[528,256]{1,0:T(8,128)(2,1)S(1)}, u32[]{:S(2)}, u32[]{:S(2)}) collective-permute-start(bf16[528,256]{1,0:T(8,128)(2,1)S(1)} %get-tuple-element.82), channel_id=1, source_target_pairs={{0,3},{1,7},{8,11},{9,15},{10,8},{11,12},{16,19},{17,23},{18,16},{... | collective-permute-start | bytes 811016 | tf_op jit(solution)/shard_map/ppermute | solution.py:349

commit v9 on v4

--- a/solution.py
+++ b/solution.py
@@ -479,22 +479,22 @@
     other = send(mine, swap)
     panels_a, panels_b = ([x] for x in half(ids, mine, other, piece))
     panels_a.append(spread(1, panels_a[0]))
+    panels_b.append(spread(1, panels_b[0]))
     partial_a, message_a = mirrored_product(ids, matrix, diagonal, mine, other, piece, 0, [])
     to_a = collect(bits - 1, message_a)
     partial_b, message_b = mirrored_product(ids, matrix, diagonal, mine, other, piece, 1, [message_a])
     to_b = collect(bits - 1, message_b)
     widen(panels_a, [message_b])
-    panels_b.append(spread(1, panels_b[0]))
-    partial_a, to_a, relayed = relaying(partial_a, to_a, [], [message_b])
+    widen(panels_b, [panels_a[1]])
+    partial_a, to_a, relayed = relaying(partial_a, to_a, [], [message_b, panels_b[1]])
     keep_a, *give_a = direct_product(ids, matrix, panels_a, [relayed])
     got_a = [send(x, swap) for x in give_a]
-    partial_b, to_b, relayed = relaying(partial_b, to_b, [], [keep_a, to_a])
-    widen(panels_b, [])
-    arrays_a = deliver(keep_a, got_a, partial_a, to_a, [relayed])
+    partial_b, to_b, relayed = relaying(partial_b, to_b, [], [keep_a, to_a, panels_b[2]])
+    arrays_a = deliver(keep_a, got_a, partial_a, to_a, [relayed, *panels_b[3:]])
     *give_b, panel_b = give_product(ids, matrix, panels_b, [arrays_a[0]])
-    give_b, to_b, *arrays_a[1:3] = lax.optimization_barrier((give_b, to_b, *arrays_a[1:3]))
     got_b = [send(x, swap) for x in give_b]
-    keep_b = keep_product(ids, matrix, panel_b, [])
+    keep_b = keep_product(ids, matrix, panel_b, [to_b])
+    keep_b, *arrays_a[1:3] = lax.optimization_barrier((keep_b, *arrays_a[1:3]))
     arrays_b = deliver(keep_b, got_b, partial_b, to_b, [])
     result = finish(ids, None, arrays_a, [arrays_b[0]])
     return finish(ids, result, arrays_b, [])

time: 179 us -> 172 us (0.961)
  waiting for transfers between devices: 60.8 us -> 52.6 us
    ppermute x27, waiting for transfers between devices: 60.8 us -> 52.6 us  [send(): return lax.ppermute(x, ('row', 'col'), [(at(*s), at(*d)) for s, d in pairs])]
  transfers between devices with their start and end apart: 27 -> 27, of which waited for: 8 -> 7; matrix products, arithmetic and copies ran while one was open for 0% -> 0% of each run, Pallas kernels for 25% -> 26%
where the time goes in v9:
time: 172 us
  starting transfers between devices  64.2 us (37%)
  waiting for transfers between devices  52.6 us (31%)
  Pallas kernels  48.6 us (28%)
  local copies, waits for them, and re-layouts  5.86 us (3%)
    ppermute x27, starting transfers between devices, send(): return lax.ppermute(x, ('row', 'col'), [(at(*s), at(*d)) for s, d in pairs])  64.2 us
    ppermute x27, waiting for transfers between devices, send(): return lax.ppermute(x, ('row', 'col'), [(at(*s), at(*d)) for s, d in pairs])  52.6 us
    pallas_call x13, Pallas kernels, local(): pl.pallas_call(body, out_shape=out_shape, in_specs=[pl.BlockSpec(memory_s...  46.8 us
    unnamed x4, local copies, waits for them, and re-layouts  5.77 us
  transfers between devices with their start and end apart: 27, of which 7 were waited for; matrix products, arithmetic and copies ran while one was open for 0% of the time, Pallas kernels for 26%

profile of v9, /device:TPU:7, one launch (start us, length us, event | category | flops | bytes accessed | tf_op | source)
XLA Modules:
  0.0 171.7 jit_solution(17871206280003134728)
XLA Ops:
  0.0 4.2 %collective-permute-start = (bf16[512,512]{1,0:T(8,128)(2,1)}, bf16[512,512]{1,0:T(8,128)(2,1)S(1)}, u32[]{:S(2)}, u32[]{:S(2)}) collective-permute-start(bf16[512,512]{1,0:T(8,128)(2,1)} %refs_1_.1), channel_id=1, source_target_pairs={{4,0},{5,1},{6,2},{7,3},{12,8},{13,9},{14,10},{15,11},{16,20},{17,... | collective-permute-start | bytes 1572872 | tf_op jit(solution)/shard_map/ppermute | solution.py:378
  4.2 3.2 %collective-permute-start.1 = (bf16[512,512]{1,0:T(8,128)(2,1)}, bf16[512,512]{1,0:T(8,128)(2,1)S(1)}, u32[]{:S(2)}, u32[]{:S(2)}) collective-permute-start(bf16[512,512]{1,0:T(8,128)(2,1)} %refs_1_.1), channel_id=1, source_target_pairs={{8,10},{9,11},{16,18},{17,19},{18,20},{19,21},{24,26},{25,27},{26,... | collective-permute-start | bytes 1572872 | tf_op jit(solution)/shard_map/ppermute | solution.py:378
  8.9 5.8 %copy-done = bf16[4096,2048]{1,0:T(8,128)(2,1)S(1)} copy-done((bf16[4096,2048]{1,0:T(8,128)(2,1)S(1)}, bf16[4096,2048]{1,0:T(8,128)(2,1)}, u32[]{:S(2)}) %copy-start) | copy-done | bytes 16777240
  16.4 10.7 %collective-permute-done.refs_2_ = bf16[512,512]{1,0:T(8,128)(2,1)S(1)} collective-permute-done((bf16[512,512]{1,0:T(8,128)(2,1)}, bf16[512,512]{1,0:T(8,128)(2,1)S(1)}, u32[]{:S(2)}, u32[]{:S(2)}) %collective-permute-start) | collective-permute-done | bytes 524320 | tf_op jit(solution)/shard_map/ppermute | solution.py:378
  28.4 3.5 %collective-permute-done.2.refs_4_ = bf16[512,512]{1,0:T(8,128)(2,1)S(1)} collective-permute-done((bf16[512,512]{1,0:T(8,128)(2,1)}, bf16[512,512]{1,0:T(8,128)(2,1)S(1)}, u32[]{:S(2)}, u32[]{:S(2)}) %collective-permute-start.2) | collective-permute-done | bytes 524320 | tf_op jit(solution)/shard_map/ppermute | solution.py:378
  31.9 11.2 %collective-permute-done.3.refs_5_ = bf16[512,512]{1,0:T(8,128)(2,1)S(1)} collective-permute-done((bf16[512,512]{1,0:T(8,128)(2,1)S(1)}, bf16[512,512]{1,0:T(8,128)(2,1)S(1)}, u32[]{:S(2)}, u32[]{:S(2)}) %collective-permute-start.3) | collective-permute-done | bytes 524320 | tf_op jit(solution)/shard_map/ppermute | solution.py:378
  43.8 4.1 %collective-permute-start.4 = (bf16[2048,512]{1,0:T(8,128)(2,1)S(1)}, bf16[2048,512]{1,0:T(8,128)(2,1)S(1)}, u32[]{:S(2)}, u32[]{:S(2)}) collective-permute-start(bf16[2048,512]{1,0:T(8,128)(2,1)S(1)} %line.1.refs_1_.refs_3_), channel_id=1, source_target_pairs={{0,1},{1,0},{8,9},{9,8},{10,11},{11,10},{16,17},{17,16},{18,19},{1... | collective-permute-start | bytes 6291464 | tf_op jit(solution)/shard_map/ppermute | solution.py:378
  47.9 3.8 %collective-permute-done.4.refs_2_.refs_4_ = bf16[2048,512]{1,0:T(8,128)(2,1)S(1)} collective-permute-done((bf16[2048,512]{1,0:T(8,128)(2,1)S(1)}, bf16[2048,512]{1,0:T(8,128)(2,1)S(1)}, u32[]{:S(2)}, u32[]{:S(2)}) %collective-permute-start.4) | collective-permute-done | bytes 2097184 | tf_op jit(solution)/shard_map/ppermute | solution.py:378
  53.1 8.8 %mirrored_product.2 = (f32[2048,256]{1,0:T(8,128)S(1)}, bf16[2112,256]{1,0:T(8,128)(2,1)S(1)}) custom-call(s32[5]{0:T(128)S(1)} %stack.23.ids.refs_0_, bf16[4096,2048]{1,0:T(8,128)(2,1)S(1)} %get-tuple-element.43.refs_1_, f32[8,2048]{1,0:T(8,128)S(1)} %get-tuple-element.46.refs_2_, bf16[2048,512]{1,0:T(8,128)(2,1)S(1)} %line.1.refs_1_.refs_3_, ...), custom_call_target="tpu_custom_call" | custom-call | tf_op jit(solution)/shard_map/mirrored_product/pallas_call | solution.py:48
  64.0 8.8 %mirrored_product.3 = (f32[2048,256]{1,0:T(8,128)S(1)}, bf16[2112,256]{1,0:T(8,128)(2,1)S(1)}) custom-call(s32[5]{0:T(128)S(1)} %stack.23.ids.refs_0_, bf16[4096,2048]{1,0:T(8,128)(2,1)S(1)} %get-tuple-element.43.refs_1_, f32[8,2048]{1,0:T(8,128)S(1)} %get-tuple-element.46.refs_2_, bf16[2048,512]{1,0:T(8,128)(2,1)S(1)} %line.1.refs_1_.refs_3_, ...), custom_call_target="tpu_custom_call" | custom-call | tf_op jit(solution)/shard_map/mirrored_product/pallas_call | solution.py:48
  76.3 2.9 %relay.2 = (f32[2048,256]{1,0:T(8,128)S(1)}, bf16[2112,256]{1,0:T(8,128)(2,1)S(1)}) custom-call(s32[5]{0:T(128)S(1)} %stack.23.ids.refs_0_, f32[2048,256]{1,0:T(8,128)S(1)} %get-tuple-element.51.refs_1_, bf16[2112,256]{1,0:T(8,128)(2,1)S(1)} %collective-permute-done.8.refs_2_, bf16[2112,256]{1,0:T(8,128)(2,1)S(1)} %get-tuple-element.48.refs_3_, ...), custom_call_target="tpu_custom_call" | custom-call | tf_op jit(solution)/shard_map/relay/pallas_call | solution.py:48
  82.0 8.8 %collective-permute-done.7.refs_5_ = bf16[2048,256]{1,0:T(8,128)(2,1)S(1)} collective-permute-done((bf16[2048,256]{1,0:T(8,128)(2,1)S(1)}, bf16[2048,256]{1,0:T(8,128)(2,1)S(1)}, u32[]{:S(2)}, u32[]{:S(2)}) %collective-permute-start.7) | collective-permute-done | bytes 1048608 | tf_op jit(solution)/shard_map/ppermute | solution.py:378
  90.8 6.4 %direct_product.1 = (f32[2048,256]{1,0:T(8,128)S(1)}, f32[1024,256]{1,0:T(8,128)S(1)}, f32[1024,256]{1,0:T(8,128)S(1)}) custom-call(s32[5]{0:T(128)S(1)} %stack.23.ids.refs_0_, bf16[4096,2048]{1,0:T(8,128)(2,1)S(1)} %get-tuple-element.43.refs_1_, bf16[2048,256]{1,0:T(8,128)(2,1)S(1)} %get-tuple-element.49.refs_2_, ...), custom_call_target="tpu_custom_call" | custom-call | tf_op jit(solution)/shard_map/direct_product/pallas_call | solution.py:48
  97.2 3.4 %collective-permute-start.10 = (f32[1024,256]{1,0:T(8,128)S(1)}, f32[1024,256]{1,0:T(8,128)S(1)}, u32[]{:S(2)}, u32[]{:S(2)}) collective-permute-start(f32[1024,256]{1,0:T(8,128)S(1)} %get-tuple-element.56), channel_id=1, source_target_pairs={{0,1},{1,0},{8,9},{9,8},{10,11},{11,10},{16,17},{17,16},{18,19},{1... | collective-permute-start | bytes 3145736 | tf_op jit(solution)/shard_map/ppermute | solution.py:378
  100.6 1.9 %collective-permute-start.11 = (f32[1024,256]{1,0:T(8,128)S(1)}, f32[1024,256]{1,0:T(8,128)S(1)}, u32[]{:S(2)}, u32[]{:S(2)}) collective-permute-start(f32[1024,256]{1,0:T(8,128)S(1)} %get-tuple-element.57), channel_id=1, source_target_pairs={{0,1},{1,0},{8,9},{9,8},{10,11},{11,10},{16,17},{17,16},{18,19},{1... | collective-permute-start | bytes 3145736 | tf_op jit(solution)/shard_map/ppermute | solution.py:378
  102.5 2.9 %relay.3 = (f32[2048,256]{1,0:T(8,128)S(1)}, bf16[2112,256]{1,0:T(8,128)(2,1)S(1)}) custom-call(s32[5]{0:T(128)S(1)} %stack.23.ids.refs_0_, f32[2048,256]{1,0:T(8,128)S(1)} %get-tuple-element.59.refs_1_, bf16[2112,256]{1,0:T(8,128)(2,1)S(1)} %collective-permute-done.13.refs_2_, f32[2048,256]{1,0:T(8,128)S(1)} %get-tuple-element.55.refs_3_.refs_1_, ...), custom_call_target="tpu_custom_call" | custom-call | tf_op jit(solution)/shard_map/relay/pallas_call | solution.py:48
  106.3 2.3 %pack.2 = (f32[512,256]{1,0:T(8,128)S(1)}, bf16[528,256]{1,0:T(8,128)(2,1)S(1)}, bf16[528,256]{1,0:T(8,128)(2,1)S(1)}, bf16[528,256]{1,0:T(8,128)(2,1)S(1)}, bf16[528,256]{1,0:T(8,128)(2,1)S(1)}) custom-call(s32[5]{0:T(128)S(1)} %stack.23.ids.refs_0_, f32[2048,256]{1,0:T(8,128)S(1)} %get-tuple-element.55.refs_3_.refs_1_, ...), custom_call_target="tpu_custom_call" | custom-call | tf_op jit(solution)/shard_map/pack/pallas_call | solution.py:48
  108.6 3.5 %give_product.1 = (f32[1024,256]{1,0:T(8,128)S(1)}, f32[1024,256]{1,0:T(8,128)S(1)}, bf16[2048,256]{1,0:T(8,128)(2,1)S(1)}) custom-call(s32[5]{0:T(128)S(1)} %stack.23.ids.refs_0_, bf16[4096,2048]{1,0:T(8,128)(2,1)S(1)} %get-tuple-element.43.refs_1_, bf16[2048,256]{1,0:T(8,128)(2,1)S(1)} %get-tuple-element.60.refs_2_, ...), custom_call_target="tpu_custom_call" | custom-call | tf_op jit(solution)/shard_map/give_product/pallas_call | solution.py:48
  112.1 2.4 %collective-permute-start.21 = (f32[1024,256]{1,0:T(8,128)S(1)}, f32[1024,256]{1,0:T(8,128)S(1)}, u32[]{:S(2)}, u32[]{:S(2)}) collective-permute-start(f32[1024,256]{1,0:T(8,128)S(1)} %get-tuple-element.71), channel_id=1, source_target_pairs={{0,1},{1,0},{8,9},{9,8},{10,11},{11,10},{16,17},{17,16},{18,19},{1... | collective-permute-start | bytes 3145736 | tf_op jit(solution)/shard_map/ppermute | solution.py:378
  114.5 1.9 %collective-permute-start.22 = (f32[1024,256]{1,0:T(8,128)S(1)}, f32[1024,256]{1,0:T(8,128)S(1)}, u32[]{:S(2)}, u32[]{:S(2)}) collective-permute-start(f32[1024,256]{1,0:T(8,128)S(1)} %get-tuple-element.72), channel_id=1, source_target_pairs={{0,1},{1,0},{8,9},{9,8},{10,11},{11,10},{16,17},{17,16},{18,19},{1... | collective-permute-start | bytes 3145736 | tf_op jit(solution)/shard_map/ppermute | solution.py:378
  116.5 4.0 %collective-permute-start.17 = (bf16[528,256]{1,0:T(8,128)(2,1)S(1)}, bf16[528,256]{1,0:T(8,128)(2,1)S(1)}, u32[]{:S(2)}, u32[]{:S(2)}) collective-permute-start(bf16[528,256]{1,0:T(8,128)(2,1)S(1)} %get-tuple-element.64), channel_id=1, source_target_pairs={{1,4},{9,12},{10,9},{11,13},{17,20},{18,17},{19,21},{20,18},{21,22... | collective-permute-start | bytes 811016 | tf_op jit(solution)/shard_map/ppermute | solution.py:378
  120.4 1.9 %collective-permute-start.18 = (bf16[528,256]{1,0:T(8,128)(2,1)S(1)}, bf16[528,256]{1,0:T(8,128)(2,1)S(1)}, u32[]{:S(2)}, u32[]{:S(2)}) collective-permute-start(bf16[528,256]{1,0:T(8,128)(2,1)S(1)} %get-tuple-element.65), channel_id=1, source_target_pairs={{0,1},{1,5},{8,9},{9,13},{11,14},{16,17},{17,21},{19,22},{20,19},{... | collective-permute-start | bytes 811016 | tf_op jit(solution)/shard_map/ppermute | solution.py:378
  122.4 3.9 %collective-permute-start.19 = (bf16[528,256]{1,0:T(8,128)(2,1)S(1)}, bf16[528,256]{1,0:T(8,128)(2,1)S(1)}, u32[]{:S(2)}, u32[]{:S(2)}) collective-permute-start(bf16[528,256]{1,0:T(8,128)(2,1)S(1)} %get-tuple-element.68), channel_id=1, source_target_pairs={{0,2},{1,6},{8,10},{9,14},{10,11},{11,15},{16,18},{17,22},{18,19},... | collective-permute-start | bytes 811016 | tf_op jit(solution)/shard_map/ppermute | solution.py:378
  126.3 3.4 %keep_product.1.refs_1_ = f32[2048,256]{1,0:T(8,128)S(1)} custom-call(s32[5]{0:T(128)S(1)} %stack.23.ids.refs_0_, bf16[4096,2048]{1,0:T(8,128)(2,1)S(1)} %get-tuple-element.43.refs_1_, bf16[2048,256]{1,0:T(8,128)(2,1)S(1)} %get-tuple-element.63.refs_2_, bf16[2112,256]{1,0:T(8,128)(2,1)S(1)} %collective-permute-done.16.refs_3_.refs_5_), custom_call_target="tpu_custom_call" | custom-call | tf_op jit(solution)/shard_map/keep_product/pallas_call | solution.py:48
  129.7 2.1 %collective-permute-start.20 = (bf16[528,256]{1,0:T(8,128)(2,1)S(1)}, bf16[528,256]{1,0:T(8,128)(2,1)S(1)}, u32[]{:S(2)}, u32[]{:S(2)}) collective-permute-start(bf16[528,256]{1,0:T(8,128)(2,1)S(1)} %get-tuple-element.69), channel_id=1, source_target_pairs={{0,3},{1,7},{8,11},{9,15},{10,8},{11,12},{16,19},{17,23},{18,16},{... | collective-permute-start | bytes 811016 | tf_op jit(solution)/shard_map/ppermute | solution.py:378
  131.8 2.1 %pack.3 = (f32[512,256]{1,0:T(8,128)S(1)}, bf16[528,256]{1,0:T(8,128)(2,1)S(1)}, bf16[528,256]{1,0:T(8,128)(2,1)S(1)}, bf16[528,256]{1,0:T(8,128)(2,1)S(1)}, bf16[528,256]{1,0:T(8,128)(2,1)S(1)}) custom-call(s32[5]{0:T(128)S(1)} %stack.23.ids.refs_0_, f32[2048,256]{1,0:T(8,128)S(1)} %keep_product.1.refs_1_, f32[1024,256]{1,0:T(8,128)S(1)} %collective-permute-done.21.refs_2_, ...), custom_call_target="tpu_custom_call" | custom-call | tf_op jit(solution)/shard_map/pack/pallas_call | solution.py:48
  134.0 4.8 %collective-permute-start.23 = (bf16[528,256]{1,0:T(8,128)(2,1)S(1)}, bf16[528,256]{1,0:T(8,128)(2,1)S(1)}, u32[]{:S(2)}, u32[]{:S(2)}) collective-permute-start(bf16[528,256]{1,0:T(8,128)(2,1)S(1)} %get-tuple-element.75), channel_id=1, source_target_pairs={{1,4},{9,12},{10,9},{11,13},{17,20},{18,17},{19,21},{20,18},{21,22... | collective-permute-start | bytes 811016 | tf_op jit(solution)/shard_map/ppermute | solution.py:378
  138.8 9.1 %collective-permute-start.24 = (bf16[528,256]{1,0:T(8,128)(2,1)S(1)}, bf16[528,256]{1,0:T(8,128)(2,1)S(1)}, u32[]{:S(2)}, u32[]{:S(2)}) collective-permute-start(bf16[528,256]{1,0:T(8,128)(2,1)S(1)} %get-tuple-element.76), channel_id=1, source_target_pairs={{0,1},{1,5},{8,9},{9,13},{11,14},{16,17},{17,21},{19,22},{20,19},{... | collective-permute-start | bytes 811016 | tf_op jit(solution)/shard_map/ppermute | solution.py:378
  149.8 3.1 %collective-permute-start.26 = (bf16[528,256]{1,0:T(8,128)(2,1)S(1)}, bf16[528,256]{1,0:T(8,128)(2,1)S(1)}, u32[]{:S(2)}, u32[]{:S(2)}) collective-permute-start(bf16[528,256]{1,0:T(8,128)(2,1)S(1)} %get-tuple-element.78), channel_id=1, source_target_pairs={{0,3},{1,7},{8,11},{9,15},{10,8},{11,12},{16,19},{17,23},{18,16},{... | collective-permute-start | bytes 811016 | tf_op jit(solution)/shard_map/ppermute | solution.py:378
  154.5 4.2 %collective-permute-done.25.refs_5_ = bf16[528,256]{1,0:T(8,128)(2,1)S(1)} collective-permute-done((bf16[528,256]{1,0:T(8,128)(2,1)S(1)}, bf16[528,256]{1,0:T(8,128)(2,1)S(1)}, u32[]{:S(2)}, u32[]{:S(2)}) %collective-permute-start.25) | collective-permute-done | bytes 270368 | tf_op jit(solution)/shard_map/ppermute | solution.py:378
  158.7 10.4 %collective-permute-done.26.refs_6_ = bf16[528,256]{1,0:T(8,128)(2,1)S(1)} collective-permute-done((bf16[528,256]{1,0:T(8,128)(2,1)S(1)}, bf16[528,256]{1,0:T(8,128)(2,1)S(1)}, u32[]{:S(2)}, u32[]{:S(2)}) %collective-permute-start.26) | collective-permute-done | bytes 270368 | tf_op jit(solution)/shard_map/ppermute | solution.py:378
  169.1 2.6 %finish.3 = f32[512,512]{1,0:T(8,128)} custom-call(s32[5]{0:T(128)S(1)} %stack.23.ids.refs_0_, f32[512,256]{1,0:T(8,128)S(1)} %finish.2.refs_1_, f32[512,256]{1,0:T(8,128)S(1)} %get-tuple-element.74.refs_7_.refs_2_, bf16[528,256]{1,0:T(8,128)(2,1)S(1)} %collective-permute-done.23.refs_3_, bf16[528,256]{1,0:T(8,128)(2,1)S(1)} %collective-permute-done.24.refs_4_, ...), custom_call_target="tpu_custom_call" | custom-call | tf_op jit(solution)/shard_map/finish/pallas_call | solution.py:48
  (41 shorter events, 19.0 us)
Async XLA Ops:
  0.0 27.1 %collective-permute-start = (bf16[512,512]{1,0:T(8,128)(2,1)}, bf16[512,512]{1,0:T(8,128)(2,1)S(1)}, u32[]{:S(2)}, u32[]{:S(2)}) collective-permute-start(bf16[512,512]{1,0:T(8,128)(2,1)} %refs_1_.1), channel_id=1, source_target_pairs={{4,0},{5,1},{6,2},{7,3},{12,8},{13,9},{14,10},{15,11},{16,20},{17,... | collective-permute-start | bytes 1572872 | tf_op jit(solution)/shard_map/ppermute | solution.py:378
  4.2 24.2 %collective-permute-start.1 = (bf16[512,512]{1,0:T(8,128)(2,1)}, bf16[512,512]{1,0:T(8,128)(2,1)S(1)}, u32[]{:S(2)}, u32[]{:S(2)}) collective-permute-start(bf16[512,512]{1,0:T(8,128)(2,1)} %refs_1_.1), channel_id=1, source_target_pairs={{8,10},{9,11},{16,18},{17,19},{18,20},{19,21},{24,26},{25,27},{26,... | collective-permute-start | bytes 1572872 | tf_op jit(solution)/shard_map/ppermute | solution.py:378
  7.5 24.4 %collective-permute-start.2 = (bf16[512,512]{1,0:T(8,128)(2,1)}, bf16[512,512]{1,0:T(8,128)(2,1)S(1)}, u32[]{:S(2)}, u32[]{:S(2)}) collective-permute-start(bf16[512,512]{1,0:T(8,128)(2,1)} %refs_1_.1), channel_id=1, source_target_pairs={{2,0},{3,1},{10,8},{11,9},{12,10},{13,11},{18,16},{19,17},{20,18},... | collective-permute-start | bytes 1572872 | tf_op jit(solution)/shard_map/ppermute | solution.py:378
  8.9 5.8 %copy-start = (bf16[4096,2048]{1,0:T(8,128)(2,1)S(1)}, bf16[4096,2048]{1,0:T(8,128)(2,1)}, u32[]{:S(2)}) copy-start(bf16[4096,2048]{1,0:T(8,128)(2,1)} %a_ref.1) | copy-start | bytes 50331652
  14.6 28.5 %copy-start.1 = (bf16[512,512]{1,0:T(8,128)(2,1)S(1)}, bf16[512,512]{1,0:T(8,128)(2,1)}, u32[]{:S(2)}) copy-start(bf16[512,512]{1,0:T(8,128)(2,1)} %refs_1_.1) | copy-start | bytes 1572868
  27.1 16.0 %collective-permute-start.3 = (bf16[512,512]{1,0:T(8,128)(2,1)S(1)}, bf16[512,512]{1,0:T(8,128)(2,1)S(1)}, u32[]{:S(2)}, u32[]{:S(2)}) collective-permute-start(bf16[512,512]{1,0:T(8,128)(2,1)S(1)} %collective-permute-done.refs_2_), channel_id=1, source_target_pairs={{2,0},{3,1},{10,8},{11,9},{18,16},{19,17},{26,24},{27,25},{28,30},... | collective-permute-start | bytes 1572872 | tf_op jit(solution)/shard_map/ppermute | solution.py:378
  43.8 7.8 %collective-permute-start.4 = (bf16[2048,512]{1,0:T(8,128)(2,1)S(1)}, bf16[2048,512]{1,0:T(8,128)(2,1)S(1)}, u32[]{:S(2)}, u32[]{:S(2)}) collective-permute-start(bf16[2048,512]{1,0:T(8,128)(2,1)S(1)} %line.1.refs_1_.refs_3_), channel_id=1, source_target_pairs={{0,1},{1,0},{8,9},{9,8},{10,11},{11,10},{16,17},{17,16},{18,19},{1... | collective-permute-start | bytes 6291464 | tf_op jit(solution)/shard_map/ppermute | solution.py:378
  52.4 21.9 %collective-permute-start.5 = (bf16[2048,256]{1,0:T(8,128)(2,1)S(1)}, bf16[2048,256]{1,0:T(8,128)(2,1)S(1)}, u32[]{:S(2)}, u32[]{:S(2)}) collective-permute-start(bf16[2048,256]{1,0:T(8,128)(2,1)S(1)} %get-tuple-element.49.refs_2_), channel_id=1, source_target_pairs={{0,8},{1,17},{10,2},{11,27},{20,28}} | collective-permute-start | bytes 3145736 | tf_op jit(solution)/shard_map/ppermute | solution.py:378
  61.9 14.4 %collective-permute-start.8 = (bf16[2112,256]{1,0:T(8,128)(2,1)S(1)}, bf16[2112,256]{1,0:T(8,128)(2,1)S(1)}, u32[]{:S(2)}, u32[]{:S(2)}) collective-permute-start(bf16[2112,256]{1,0:T(8,128)(2,1)S(1)} %get-tuple-element.47.refs_5_), channel_id=1, source_target_pairs={{16,0},{24,8},{9,1},{25,17},{26,10},{18,2},{19,27},{29,21}} | collective-permute-start | bytes 3244040 | tf_op jit(solution)/shard_map/ppermute | solution.py:378
  63.3 13.0 %collective-permute-start.9 = (bf16[2048,256]{1,0:T(8,128)(2,1)S(1)}, bf16[2048,256]{1,0:T(8,128)(2,1)S(1)}, u32[]{:S(2)}, u32[]{:S(2)}) collective-permute-start(bf16[2048,256]{1,0:T(8,128)(2,1)S(1)} %get-tuple-element.60.refs_2_), channel_id=1, source_target_pairs={{0,8},{1,17},{10,2},{11,27},{20,28}} | collective-permute-start | bytes 3145736 | tf_op jit(solution)/shard_map/ppermute | solution.py:378
  72.9 27.7 %collective-permute-start.13 = (bf16[2112,256]{1,0:T(8,128)(2,1)S(1)}, bf16[2112,256]{1,0:T(8,128)(2,1)S(1)}, u32[]{:S(2)}, u32[]{:S(2)}) collective-permute-start(bf16[2112,256]{1,0:T(8,128)(2,1)S(1)} %get-tuple-element.48.refs_3_), channel_id=1, source_target_pairs={{16,0},{24,8},{9,1},{25,17},{26,10},{18,2},{19,27},{29,21}} | collective-permute-start | bytes 3244040 | tf_op jit(solution)/shard_map/ppermute | solution.py:378
  74.3 6.5 %collective-permute-start.6 = (bf16[2048,256]{1,0:T(8,128)(2,1)S(1)}, bf16[2048,256]{1,0:T(8,128)(2,1)S(1)}, u32[]{:S(2)}, u32[]{:S(2)}) collective-permute-start(bf16[2048,256]{1,0:T(8,128)(2,1)S(1)} %get-tuple-element.49.refs_2_), channel_id=1, source_target_pairs={{0,16},{1,9},{10,26},{21,29}} | collective-permute-start | bytes 3145736 | tf_op jit(solution)/shard_map/ppermute | solution.py:378
  75.0 15.8 %collective-permute-start.7 = (bf16[2048,256]{1,0:T(8,128)(2,1)S(1)}, bf16[2048,256]{1,0:T(8,128)(2,1)S(1)}, u32[]{:S(2)}, u32[]{:S(2)}) collective-permute-start(bf16[2048,256]{1,0:T(8,128)(2,1)S(1)} %collective-permute-done.5.refs_3_), channel_id=1, source_target_pairs={{8,24},{17,25},{2,18},{27,19}} | collective-permute-start | bytes 3145736 | tf_op jit(solution)/shard_map/ppermute | solution.py:378
  79.2 23.3 %collective-permute-start.12 = (bf16[2112,256]{1,0:T(8,128)(2,1)S(1)}, bf16[2112,256]{1,0:T(8,128)(2,1)S(1)}, u32[]{:S(2)}, u32[]{:S(2)}) collective-permute-start(bf16[2112,256]{1,0:T(8,128)(2,1)S(1)} %get-tuple-element.54.refs_6_), channel_id=1, source_target_pairs={{8,0},{17,1},{2,10},{27,11},{28,20}} | collective-permute-start | bytes 3244040 | tf_op jit(solution)/shard_map/ppermute | solution.py:378
  80.0 22.5 %collective-permute-start.14 = (bf16[2048,256]{1,0:T(8,128)(2,1)S(1)}, bf16[2048,256]{1,0:T(8,128)(2,1)S(1)}, u32[]{:S(2)}, u32[]{:S(2)}) collective-permute-start(bf16[2048,256]{1,0:T(8,128)(2,1)S(1)} %get-tuple-element.60.refs_2_), channel_id=1, source_target_pairs={{0,16},{1,9},{10,26},{21,29}} | collective-permute-start | bytes 3145736 | tf_op jit(solution)/shard_map/ppermute | solution.py:378
  80.7 25.5 %collective-permute-start.15 = (bf16[2048,256]{1,0:T(8,128)(2,1)S(1)}, bf16[2048,256]{1,0:T(8,128)(2,1)S(1)}, u32[]{:S(2)}, u32[]{:S(2)}) collective-permute-start(bf16[2048,256]{1,0:T(8,128)(2,1)S(1)} %collective-permute-done.9.refs_4_.refs_3_), channel_id=1, source_target_pairs={{8,24},{17,25},{2,18},{27,19}} | collective-permute-start | bytes 3145736 | tf_op jit(solution)/shard_map/ppermute | solution.py:378
  97.2 9.0 %collective-permute-start.10 = (f32[1024,256]{1,0:T(8,128)S(1)}, f32[1024,256]{1,0:T(8,128)S(1)}, u32[]{:S(2)}, u32[]{:S(2)}) collective-permute-start(f32[1024,256]{1,0:T(8,128)S(1)} %get-tuple-element.56), channel_id=1, source_target_pairs={{0,1},{1,0},{8,9},{9,8},{10,11},{11,10},{16,17},{17,16},{18,19},{1... | collective-permute-start | bytes 3145736 | tf_op jit(solution)/shard_map/ppermute | solution.py:378
  100.6 5.7 %collective-permute-start.11 = (f32[1024,256]{1,0:T(8,128)S(1)}, f32[1024,256]{1,0:T(8,128)S(1)}, u32[]{:S(2)}, u32[]{:S(2)}) collective-permute-start(f32[1024,256]{1,0:T(8,128)S(1)} %get-tuple-element.57), channel_id=1, source_target_pairs={{0,1},{1,0},{8,9},{9,8},{10,11},{11,10},{16,17},{17,16},{18,19},{1... | collective-permute-start | bytes 3145736 | tf_op jit(solution)/shard_map/ppermute | solution.py:378
  105.5 16.9 %collective-permute-start.16 = (bf16[2112,256]{1,0:T(8,128)(2,1)S(1)}, bf16[2112,256]{1,0:T(8,128)(2,1)S(1)}, u32[]{:S(2)}, u32[]{:S(2)}) collective-permute-start(bf16[2112,256]{1,0:T(8,128)(2,1)S(1)} %get-tuple-element.61.refs_6_), channel_id=1, source_target_pairs={{8,0},{17,1},{2,10},{27,11},{28,20}} | collective-permute-start | bytes 3244040 | tf_op jit(solution)/shard_map/ppermute | solution.py:378
  112.1 19.7 %collective-permute-start.21 = (f32[1024,256]{1,0:T(8,128)S(1)}, f32[1024,256]{1,0:T(8,128)S(1)}, u32[]{:S(2)}, u32[]{:S(2)}) collective-permute-start(f32[1024,256]{1,0:T(8,128)S(1)} %get-tuple-element.71), channel_id=1, source_target_pairs={{0,1},{1,0},{8,9},{9,8},{10,11},{11,10},{16,17},{17,16},{18,19},{1... | collective-permute-start | bytes 3145736 | tf_op jit(solution)/shard_map/ppermute | solution.py:378
  114.5 17.3 %collective-permute-start.22 = (f32[1024,256]{1,0:T(8,128)S(1)}, f32[1024,256]{1,0:T(8,128)S(1)}, u32[]{:S(2)}, u32[]{:S(2)}) collective-permute-start(f32[1024,256]{1,0:T(8,128)S(1)} %get-tuple-element.72), channel_id=1, source_target_pairs={{0,1},{1,0},{8,9},{9,8},{10,11},{11,10},{16,17},{17,16},{18,19},{1... | collective-permute-start | bytes 3145736 | tf_op jit(solution)/shard_map/ppermute | solution.py:378
  116.5 13.2 %collective-permute-start.17 = (bf16[528,256]{1,0:T(8,128)(2,1)S(1)}, bf16[528,256]{1,0:T(8,128)(2,1)S(1)}, u32[]{:S(2)}, u32[]{:S(2)}) collective-permute-start(bf16[528,256]{1,0:T(8,128)(2,1)S(1)} %get-tuple-element.64), channel_id=1, source_target_pairs={{1,4},{9,12},{10,9},{11,13},{17,20},{18,17},{19,21},{20,18},{21,22... | collective-permute-start | bytes 811016 | tf_op jit(solution)/shard_map/ppermute | solution.py:378
  120.4 11.4 %collective-permute-start.18 = (bf16[528,256]{1,0:T(8,128)(2,1)S(1)}, bf16[528,256]{1,0:T(8,128)(2,1)S(1)}, u32[]{:S(2)}, u32[]{:S(2)}) collective-permute-start(bf16[528,256]{1,0:T(8,128)(2,1)S(1)} %get-tuple-element.65), channel_id=1, source_target_pairs={{0,1},{1,5},{8,9},{9,13},{11,14},{16,17},{17,21},{19,22},{20,19},{... | collective-permute-start | bytes 811016 | tf_op jit(solution)/shard_map/ppermute | solution.py:378
  122.4 27.5 %collective-permute-start.19 = (bf16[528,256]{1,0:T(8,128)(2,1)S(1)}, bf16[528,256]{1,0:T(8,128)(2,1)S(1)}, u32[]{:S(2)}, u32[]{:S(2)}) collective-permute-start(bf16[528,256]{1,0:T(8,128)(2,1)S(1)} %get-tuple-element.68), channel_id=1, source_target_pairs={{0,2},{1,6},{8,10},{9,14},{10,11},{11,15},{16,18},{17,22},{18,19},... | collective-permute-start | bytes 811016 | tf_op jit(solution)/shard_map/ppermute | solution.py:378
  129.7 23.2 %collective-permute-start.20 = (bf16[528,256]{1,0:T(8,128)(2,1)S(1)}, bf16[528,256]{1,0:T(8,128)(2,1)S(1)}, u32[]{:S(2)}, u32[]{:S(2)}) collective-permute-start(bf16[528,256]{1,0:T(8,128)(2,1)S(1)} %get-tuple-element.69), channel_id=1, source_target_pairs={{0,3},{1,7},{8,11},{9,15},{10,8},{11,12},{16,19},{17,23},{18,16},{... | collective-permute-start | bytes 811016 | tf_op jit(solution)/shard_map/ppermute | solution.py:378
  134.0 20.5 %collective-permute-start.23 = (bf16[528,256]{1,0:T(8,128)(2,1)S(1)}, bf16[528,256]{1,0:T(8,128)(2,1)S(1)}, u32[]{:S(2)}, u32[]{:S(2)}) collective-permute-start(bf16[528,256]{1,0:T(8,128)(2,1)S(1)} %get-tuple-element.75), channel_id=1, source_target_pairs={{1,4},{9,12},{10,9},{11,13},{17,20},{18,17},{19,21},{20,18},{21,22... | collective-permute-start | bytes 811016 | tf_op jit(solution)/shard_map/ppermute | solution.py:378
  138.8 15.8 %collective-permute-start.24 = (bf16[528,256]{1,0:T(8,128)(2,1)S(1)}, bf16[528,256]{1,0:T(8,128)(2,1)S(1)}, u32[]{:S(2)}, u32[]{:S(2)}) collective-permute-start(bf16[528,256]{1,0:T(8,128)(2,1)S(1)} %get-tuple-element.76), channel_id=1, source_target_pairs={{0,1},{1,5},{8,9},{9,13},{11,14},{16,17},{17,21},{19,22},{20,19},{... | collective-permute-start | bytes 811016 | tf_op jit(solution)/shard_map/ppermute | solution.py:378
  147.9 10.8 %collective-permute-start.25 = (bf16[528,256]{1,0:T(8,128)(2,1)S(1)}, bf16[528,256]{1,0:T(8,128)(2,1)S(1)}, u32[]{:S(2)}, u32[]{:S(2)}) collective-permute-start(bf16[528,256]{1,0:T(8,128)(2,1)S(1)} %get-tuple-element.77), channel_id=1, source_target_pairs={{0,2},{1,6},{8,10},{9,14},{10,11},{11,15},{16,18},{17,22},{18,19},... | collective-permute-start | bytes 811016 | tf_op jit(solution)/shard_map/ppermute | solution.py:378
  149.8 19.3 %collective-permute-start.26 = (bf16[528,256]{1,0:T(8,128)(2,1)S(1)}, bf16[528,256]{1,0:T(8,128)(2,1)S(1)}, u32[]{:S(2)}, u32[]{:S(2)}) collective-permute-start(bf16[528,256]{1,0:T(8,128)(2,1)S(1)} %get-tuple-element.78), channel_id=1, source_target_pairs={{0,3},{1,7},{8,11},{9,15},{10,8},{11,12},{16,19},{17,23},{18,16},{... | collective-permute-start | bytes 811016 | tf_op jit(solution)/shard_map/ppermute | solution.py:378

commit v10 on v9

--- a/solution.py
+++ b/solution.py
@@ -110,52 +110,51 @@
 
 
 def line_kernel(places, ids, *refs):
-    *came, out_ref = refs
+    *came, out_a, out_b = refs
     height = came[0].shape[0]
+    width = out_a.shape[1]
     for place, piece in zip(places, came):
         chip, there = place(ids[1])
 
         @pl.when(there)
         def _():
-            out_ref[pl.ds(pl.multiple_of(chip * height, height), height), :] = piece[...]
+            to = pl.ds(pl.multiple_of(chip * height, height), height)
+            out_a[to, :] = piece[:, pl.ds(0, width)]
+            out_b[to, :] = piece[:, pl.ds(width, width)]
 
 
 def line(ids, came, places, after):
     height, width = came[0].shape
     chips = 4 if len(came) == 5 else len(came)
-    out_shape = jax.ShapeDtypeStruct((height * chips, width), came[0].dtype)
+    out_shape = [jax.ShapeDtypeStruct((height * chips, width // 2), came[0].dtype)] * 2
     return local(functools.partial(line_kernel, places), out_shape, "line", ids, *came, after=after)
 
 
-def half_kernel(height, ids, mine, other, *outs):
-    rows, width = outs[0].shape
-    count = rows // height
+def half_kernel(height, ids, mine, other, out_ref):
+    count = out_ref.shape[0] // height
     for at in range(count // 2):
         chip = ids[2] * (count // 2) + at
         here = pl.ds(pl.multiple_of(chip * height, height), height)
         for core, ref in ((ids[2], mine), (1 - ids[2], other)):
             to = pl.ds(pl.multiple_of((2 * at + core) * height, height), height)
-            for part, out_ref in enumerate(outs):
-                out_ref[to, :] = ref[here, pl.ds(part * width, width)]
+            out_ref[to, :] = ref[here, :]
 
 
 def half(ids, mine, other, height):
-    rows, width = mine.shape
-    out_shape = [jax.ShapeDtypeStruct((rows, width // 2), mine.dtype)] * 2
+    out_shape = jax.ShapeDtypeStruct(mine.shape, mine.dtype)
     return local(functools.partial(half_kernel, height), out_shape, "half", ids, mine, other)
 
 
-def mirrored_kernel(piece, part_at, ids, a_ref, diagonal, mine, other, m_ref, msg_ref, turned):
+def mirrored_kernel(piece, ids, a_ref, diagonal, mine, other, m_ref, msg_ref, turned):
     height, cols = a_ref.shape
     block = cols // 4
     used = ids[1] <= ids[0]
-    these = pl.ds(part_at * m_ref.shape[1], m_ref.shape[1])
 
     @pl.loop(0, height // piece // 2)
     def _(at):
         rows = pl.ds(pl.multiple_of(at * piece, piece), piece)
         for core, ref in ((ids[2], mine), (1 - ids[2], other)):
-            turned[:, pl.ds(pl.multiple_of((2 * at + core) * piece, piece), piece)] = ref[rows, these].T
+            turned[:, pl.ds(pl.multiple_of((2 * at + core) * piece, piece), piece)] = ref[rows, :].T
 
     @pl.loop(0, 4)
     def _(part):
@@ -180,15 +179,15 @@
         put_scale(msg_ref, cols, part, scale)
 
 
-def mirrored_product(ids, matrix, diagonal, mine, other, piece, part_at, after):
+def mirrored_product(ids, matrix, diagonal, mine, other, piece, after):
     rows, cols = matrix.shape
-    width = mine.shape[1] // 2
+    width = mine.shape[1]
     out_shape = [
         jax.ShapeDtypeStruct((cols, width), jnp.float32),
         jax.ShapeDtypeStruct((cols + 4 * TAIL, width), jnp.bfloat16),
     ]
     return local(
-        functools.partial(mirrored_kernel, piece, part_at), out_shape, "mirrored_product",
+        functools.partial(mirrored_kernel, piece), out_shape, "mirrored_product",
         ids, matrix, diagonal, mine, other, after=after,
         scratch_shapes=[pltpu.VMEM((width, rows), jnp.bfloat16)],
     )
@@ -475,14 +474,14 @@
         came.append(ends(two))
     else:
         came, places = by_distance(panel_vectors)
-    mine = line(ids, came, places, [])
-    other = send(mine, swap)
-    panels_a, panels_b = ([x] for x in half(ids, mine, other, piece))
+    mine_a, mine_b = line(ids, came, places, [])
+    other_a, other_b = send(mine_a, swap), send(mine_b, swap)
+    panels_a, panels_b = [half(ids, mine_a, other_a, piece)], [half(ids, mine_b, other_b, piece)]
     panels_a.append(spread(1, panels_a[0]))
     panels_b.append(spread(1, panels_b[0]))
-    partial_a, message_a = mirrored_product(ids, matrix, diagonal, mine, other, piece, 0, [])
+    partial_a, message_a = mirrored_product(ids, matrix, diagonal, mine_a, other_a, piece, [])
     to_a = collect(bits - 1, message_a)
-    partial_b, message_b = mirrored_product(ids, matrix, diagonal, mine, other, piece, 1, [message_a])
+    partial_b, message_b = mirrored_product(ids, matrix, diagonal, mine_b, other_b, piece, [message_a])
     to_b = collect(bits - 1, message_b)
     widen(panels_a, [message_b])
     widen(panels_b, [panels_a[1]])
@@ -494,7 +493,7 @@
     *give_b, panel_b = give_product(ids, matrix, panels_b, [arrays_a[0]])
     got_b = [send(x, swap) for x in give_b]
     keep_b = keep_product(ids, matrix, panel_b, [to_b])
-    keep_b, *arrays_a[1:3] = lax.optimization_barrier((keep_b, *arrays_a[1:3]))
+    keep_b, arrays_a[1] = lax.optimization_barrier((keep_b, arrays_a[1]))
     arrays_b = deliver(keep_b, got_b, partial_b, to_b, [])
     result = finish(ids, None, arrays_a, [arrays_b[0]])
     return finish(ids, result, arrays_b, [])

time: 172 us -> 171 us (level)
    ppermute x27 -> x28, starting transfers between devices: 64.2 us -> 62.9 us  [send(): return lax.ppermute(x, ('row', 'col'), [(at(*s), at(*d)) for s, d in pairs])]
    pallas_call x13 -> x14, Pallas kernels: 46.8 us -> 47.4 us  [local(): pl.pallas_call(body, out_shape=out_shape, in_specs=[pl.BlockSpec(memory_s...]
    ppermute x27 -> x28, waiting for transfers between devices: 52.6 us -> 52.3 us  [send(): return lax.ppermute(x, ('row', 'col'), [(at(*s), at(*d)) for s, d in pairs])]
  transfers between devices with their start and end apart: 27 -> 28, of which waited for: 7 -> 8; matrix products, arithmetic and copies ran while one was open for 0% -> 0% of each run, Pallas kernels for 26% -> 27%
where the time goes in v10:
time: 171 us
  starting transfers between devices  62.9 us (37%)
  waiting for transfers between devices  52.3 us (31%)
  Pallas kernels  49.1 us (29%)
  local copies, waits for them, and re-layouts  5.86 us (3%)
    ppermute x28, starting transfers between devices, send(): return lax.ppermute(x, ('row', 'col'), [(at(*s), at(*d)) for s, d in pairs])  62.9 us
    ppermute x28, waiting for transfers between devices, send(): return lax.ppermute(x, ('row', 'col'), [(at(*s), at(*d)) for s, d in pairs])  52.3 us
    pallas_call x14, Pallas kernels, local(): pl.pallas_call(body, out_shape=out_shape, in_specs=[pl.BlockSpec(memory_s...  47.4 us
    unnamed x4, local copies, waits for them, and re-layouts  5.77 us
  transfers between devices with their start and end apart: 28, of which 8 were waited for; matrix products, arithmetic and copies ran while one was open for 0% of the time, Pallas kernels for 27%

profile of v10, /device:TPU:7, one launch (start us, length us, event | category | flops | bytes accessed | tf_op | source)
XLA Modules:
  0.0 170.7 jit_solution(14584596921931182207)
XLA Ops:
  0.0 4.2 %collective-permute-start = (bf16[512,512]{1,0:T(8,128)(2,1)}, bf16[512,512]{1,0:T(8,128)(2,1)S(1)}, u32[]{:S(2)}, u32[]{:S(2)}) collective-permute-start(bf16[512,512]{1,0:T(8,128)(2,1)} %refs_1_.1), channel_id=1, source_target_pairs={{4,0},{5,1},{6,2},{7,3},{12,8},{13,9},{14,10},{15,11},{16,20},{17,... | collective-permute-start | bytes 1572872 | tf_op jit(solution)/shard_map/ppermute | solution.py:377
  4.2 3.2 %collective-permute-start.1 = (bf16[512,512]{1,0:T(8,128)(2,1)}, bf16[512,512]{1,0:T(8,128)(2,1)S(1)}, u32[]{:S(2)}, u32[]{:S(2)}) collective-permute-start(bf16[512,512]{1,0:T(8,128)(2,1)} %refs_1_.1), channel_id=1, source_target_pairs={{8,10},{9,11},{16,18},{17,19},{18,20},{19,21},{24,26},{25,27},{26,... | collective-permute-start | bytes 1572872 | tf_op jit(solution)/shard_map/ppermute | solution.py:377
  8.9 5.8 %copy-done = bf16[4096,2048]{1,0:T(8,128)(2,1)S(1)} copy-done((bf16[4096,2048]{1,0:T(8,128)(2,1)S(1)}, bf16[4096,2048]{1,0:T(8,128)(2,1)}, u32[]{:S(2)}) %copy-start) | copy-done | bytes 16777240
  16.4 10.7 %collective-permute-done.refs_2_ = bf16[512,512]{1,0:T(8,128)(2,1)S(1)} collective-permute-done((bf16[512,512]{1,0:T(8,128)(2,1)}, bf16[512,512]{1,0:T(8,128)(2,1)S(1)}, u32[]{:S(2)}, u32[]{:S(2)}) %collective-permute-start) | collective-permute-done | bytes 524320 | tf_op jit(solution)/shard_map/ppermute | solution.py:377
  28.4 3.5 %collective-permute-done.2.refs_4_ = bf16[512,512]{1,0:T(8,128)(2,1)S(1)} collective-permute-done((bf16[512,512]{1,0:T(8,128)(2,1)}, bf16[512,512]{1,0:T(8,128)(2,1)S(1)}, u32[]{:S(2)}, u32[]{:S(2)}) %collective-permute-start.2) | collective-permute-done | bytes 524320 | tf_op jit(solution)/shard_map/ppermute | solution.py:377
  31.9 11.2 %collective-permute-done.3.refs_5_ = bf16[512,512]{1,0:T(8,128)(2,1)S(1)} collective-permute-done((bf16[512,512]{1,0:T(8,128)(2,1)S(1)}, bf16[512,512]{1,0:T(8,128)(2,1)S(1)}, u32[]{:S(2)}, u32[]{:S(2)}) %collective-permute-start.3) | collective-permute-done | bytes 524320 | tf_op jit(solution)/shard_map/ppermute | solution.py:377
  43.8 4.1 %collective-permute-start.4 = (bf16[2048,256]{1,0:T(8,128)(2,1)S(1)}, bf16[2048,256]{1,0:T(8,128)(2,1)S(1)}, u32[]{:S(2)}, u32[]{:S(2)}) collective-permute-start(bf16[2048,256]{1,0:T(8,128)(2,1)S(1)} %get-tuple-element.44.refs_1_.refs_3_), channel_id=1, source_target_pairs={{0,1},{1,0},{8,9},{9,8},{10,11},{11,10},{16,17},{17,16},{18,19},{1... | collective-permute-start | bytes 3145736 | tf_op jit(solution)/shard_map/ppermute | solution.py:377
  47.9 1.9 %collective-permute-start.6 = (bf16[2048,256]{1,0:T(8,128)(2,1)S(1)}, bf16[2048,256]{1,0:T(8,128)(2,1)S(1)}, u32[]{:S(2)}, u32[]{:S(2)}) collective-permute-start(bf16[2048,256]{1,0:T(8,128)(2,1)S(1)} %get-tuple-element.46.refs_3_.refs_1_), channel_id=1, source_target_pairs={{0,1},{1,0},{8,9},{9,8},{10,11},{11,10},{16,17},{17,16},{18,19},{1... | collective-permute-start | bytes 3145736 | tf_op jit(solution)/shard_map/ppermute | solution.py:377
  51.5 8.8 %mirrored_product.2 = (f32[2048,256]{1,0:T(8,128)S(1)}, bf16[2112,256]{1,0:T(8,128)(2,1)S(1)}) custom-call(s32[5]{0:T(128)S(1)} %stack.23.ids.refs_0_, bf16[4096,2048]{1,0:T(8,128)(2,1)S(1)} %get-tuple-element.42.refs_1_, f32[8,2048]{1,0:T(8,128)S(1)} %get-tuple-element.45.refs_2_, bf16[2048,256]{1,0:T(8,128)(2,1)S(1)} %get-tuple-element.44.refs_1_.refs_3_, ...), custom_call_target="tpu_custom_call" | custom-call | tf_op jit(solution)/shard_map/mirrored_product/pallas_call | solution.py:48
  63.1 8.8 %mirrored_product.3 = (f32[2048,256]{1,0:T(8,128)S(1)}, bf16[2112,256]{1,0:T(8,128)(2,1)S(1)}) custom-call(s32[5]{0:T(128)S(1)} %stack.23.ids.refs_0_, bf16[4096,2048]{1,0:T(8,128)(2,1)S(1)} %get-tuple-element.42.refs_1_, f32[8,2048]{1,0:T(8,128)S(1)} %get-tuple-element.45.refs_2_, bf16[2048,256]{1,0:T(8,128)(2,1)S(1)} %get-tuple-element.46.refs_3_.refs_1_, ...), custom_call_target="tpu_custom_call" | custom-call | tf_op jit(solution)/shard_map/mirrored_product/pallas_call | solution.py:48
  75.4 2.9 %relay.2 = (f32[2048,256]{1,0:T(8,128)S(1)}, bf16[2112,256]{1,0:T(8,128)(2,1)S(1)}) custom-call(s32[5]{0:T(128)S(1)} %stack.23.ids.refs_0_, f32[2048,256]{1,0:T(8,128)S(1)} %get-tuple-element.51.refs_1_, bf16[2112,256]{1,0:T(8,128)(2,1)S(1)} %collective-permute-done.9.refs_2_, bf16[2112,256]{1,0:T(8,128)(2,1)S(1)} %get-tuple-element.48.refs_3_, ...), custom_call_target="tpu_custom_call" | custom-call | tf_op jit(solution)/shard_map/relay/pallas_call | solution.py:48
  81.1 8.8 %collective-permute-done.8.refs_5_ = bf16[2048,256]{1,0:T(8,128)(2,1)S(1)} collective-permute-done((bf16[2048,256]{1,0:T(8,128)(2,1)S(1)}, bf16[2048,256]{1,0:T(8,128)(2,1)S(1)}, u32[]{:S(2)}, u32[]{:S(2)}) %collective-permute-start.8) | collective-permute-done | bytes 1048608 | tf_op jit(solution)/shard_map/ppermute | solution.py:377
  89.9 6.4 %direct_product.1 = (f32[2048,256]{1,0:T(8,128)S(1)}, f32[1024,256]{1,0:T(8,128)S(1)}, f32[1024,256]{1,0:T(8,128)S(1)}) custom-call(s32[5]{0:T(128)S(1)} %stack.23.ids.refs_0_, bf16[4096,2048]{1,0:T(8,128)(2,1)S(1)} %get-tuple-element.42.refs_1_, bf16[2048,256]{1,0:T(8,128)(2,1)S(1)} %half.2.refs_2_, bf16[2048,256]{1,0:T(8,128)(2,1)S(1)} %collective-permute-done.5.refs_3_, ...), custom_call_target="tpu_custom_call" | custom-call | tf_op jit(solution)/shard_map/direct_product/pallas_call | solution.py:48
  96.3 3.3 %collective-permute-start.11 = (f32[1024,256]{1,0:T(8,128)S(1)}, f32[1024,256]{1,0:T(8,128)S(1)}, u32[]{:S(2)}, u32[]{:S(2)}) collective-permute-start(f32[1024,256]{1,0:T(8,128)S(1)} %get-tuple-element.55), channel_id=1, source_target_pairs={{0,1},{1,0},{8,9},{9,8},{10,11},{11,10},{16,17},{17,16},{18,19},{1... | collective-permute-start | bytes 3145736 | tf_op jit(solution)/shard_map/ppermute | solution.py:377
  99.6 1.9 %collective-permute-start.12 = (f32[1024,256]{1,0:T(8,128)S(1)}, f32[1024,256]{1,0:T(8,128)S(1)}, u32[]{:S(2)}, u32[]{:S(2)}) collective-permute-start(f32[1024,256]{1,0:T(8,128)S(1)} %get-tuple-element.56), channel_id=1, source_target_pairs={{0,1},{1,0},{8,9},{9,8},{10,11},{11,10},{16,17},{17,16},{18,19},{1... | collective-permute-start | bytes 3145736 | tf_op jit(solution)/shard_map/ppermute | solution.py:377
  101.6 2.9 %relay.3 = (f32[2048,256]{1,0:T(8,128)S(1)}, bf16[2112,256]{1,0:T(8,128)(2,1)S(1)}) custom-call(s32[5]{0:T(128)S(1)} %stack.23.ids.refs_0_, f32[2048,256]{1,0:T(8,128)S(1)} %get-tuple-element.58.refs_1_, bf16[2112,256]{1,0:T(8,128)(2,1)S(1)} %collective-permute-done.14.refs_2_, f32[2048,256]{1,0:T(8,128)S(1)} %get-tuple-element.54.refs_3_.refs_1_, ...), custom_call_target="tpu_custom_call" | custom-call | tf_op jit(solution)/shard_map/relay/pallas_call | solution.py:48
  105.3 2.3 %pack.2 = (f32[512,256]{1,0:T(8,128)S(1)}, bf16[528,256]{1,0:T(8,128)(2,1)S(1)}, bf16[528,256]{1,0:T(8,128)(2,1)S(1)}, bf16[528,256]{1,0:T(8,128)(2,1)S(1)}, bf16[528,256]{1,0:T(8,128)(2,1)S(1)}) custom-call(s32[5]{0:T(128)S(1)} %stack.23.ids.refs_0_, f32[2048,256]{1,0:T(8,128)S(1)} %get-tuple-element.54.refs_3_.refs_1_, ...), custom_call_target="tpu_custom_call" | custom-call | tf_op jit(solution)/shard_map/pack/pallas_call | solution.py:48
  107.6 3.5 %give_product.1 = (f32[1024,256]{1,0:T(8,128)S(1)}, f32[1024,256]{1,0:T(8,128)S(1)}, bf16[2048,256]{1,0:T(8,128)(2,1)S(1)}) custom-call(s32[5]{0:T(128)S(1)} %stack.23.ids.refs_0_, bf16[4096,2048]{1,0:T(8,128)(2,1)S(1)} %get-tuple-element.42.refs_1_, bf16[2048,256]{1,0:T(8,128)(2,1)S(1)} %half.3.refs_2_, ...), custom_call_target="tpu_custom_call" | custom-call | tf_op jit(solution)/shard_map/give_product/pallas_call | solution.py:48
  111.2 2.4 %collective-permute-start.22 = (f32[1024,256]{1,0:T(8,128)S(1)}, f32[1024,256]{1,0:T(8,128)S(1)}, u32[]{:S(2)}, u32[]{:S(2)}) collective-permute-start(f32[1024,256]{1,0:T(8,128)S(1)} %get-tuple-element.69), channel_id=1, source_target_pairs={{0,1},{1,0},{8,9},{9,8},{10,11},{11,10},{16,17},{17,16},{18,19},{1... | collective-permute-start | bytes 3145736 | tf_op jit(solution)/shard_map/ppermute | solution.py:377
  113.6 1.9 %collective-permute-start.23 = (f32[1024,256]{1,0:T(8,128)S(1)}, f32[1024,256]{1,0:T(8,128)S(1)}, u32[]{:S(2)}, u32[]{:S(2)}) collective-permute-start(f32[1024,256]{1,0:T(8,128)S(1)} %get-tuple-element.70), channel_id=1, source_target_pairs={{0,1},{1,0},{8,9},{9,8},{10,11},{11,10},{16,17},{17,16},{18,19},{1... | collective-permute-start | bytes 3145736 | tf_op jit(solution)/shard_map/ppermute | solution.py:377
  115.5 4.0 %collective-permute-start.18 = (bf16[528,256]{1,0:T(8,128)(2,1)S(1)}, bf16[528,256]{1,0:T(8,128)(2,1)S(1)}, u32[]{:S(2)}, u32[]{:S(2)}) collective-permute-start(bf16[528,256]{1,0:T(8,128)(2,1)S(1)} %get-tuple-element.63), channel_id=1, source_target_pairs={{1,4},{9,12},{10,9},{11,13},{17,20},{18,17},{19,21},{20,18},{21,22... | collective-permute-start | bytes 811016 | tf_op jit(solution)/shard_map/ppermute | solution.py:377
  121.4 3.9 %collective-permute-start.20 = (bf16[528,256]{1,0:T(8,128)(2,1)S(1)}, bf16[528,256]{1,0:T(8,128)(2,1)S(1)}, u32[]{:S(2)}, u32[]{:S(2)}) collective-permute-start(bf16[528,256]{1,0:T(8,128)(2,1)S(1)} %get-tuple-element.66), channel_id=1, source_target_pairs={{0,2},{1,6},{8,10},{9,14},{10,11},{11,15},{16,18},{17,22},{18,19},... | collective-permute-start | bytes 811016 | tf_op jit(solution)/shard_map/ppermute | solution.py:377
  125.3 3.4 %keep_product.1.refs_1_ = f32[2048,256]{1,0:T(8,128)S(1)} custom-call(s32[5]{0:T(128)S(1)} %stack.23.ids.refs_0_, bf16[4096,2048]{1,0:T(8,128)(2,1)S(1)} %get-tuple-element.42.refs_1_, bf16[2048,256]{1,0:T(8,128)(2,1)S(1)} %get-tuple-element.62.refs_2_, bf16[2112,256]{1,0:T(8,128)(2,1)S(1)} %collective-permute-done.17.refs_3_.refs_5_), custom_call_target="tpu_custom_call" | custom-call | tf_op jit(solution)/shard_map/keep_product/pallas_call | solution.py:48
  128.7 2.1 %collective-permute-start.21 = (bf16[528,256]{1,0:T(8,128)(2,1)S(1)}, bf16[528,256]{1,0:T(8,128)(2,1)S(1)}, u32[]{:S(2)}, u32[]{:S(2)}) collective-permute-start(bf16[528,256]{1,0:T(8,128)(2,1)S(1)} %get-tuple-element.67), channel_id=1, source_target_pairs={{0,3},{1,7},{8,11},{9,15},{10,8},{11,12},{16,19},{17,23},{18,16},{... | collective-permute-start | bytes 811016 | tf_op jit(solution)/shard_map/ppermute | solution.py:377
  130.9 2.1 %pack.3 = (f32[512,256]{1,0:T(8,128)S(1)}, bf16[528,256]{1,0:T(8,128)(2,1)S(1)}, bf16[528,256]{1,0:T(8,128)(2,1)S(1)}, bf16[528,256]{1,0:T(8,128)(2,1)S(1)}, bf16[528,256]{1,0:T(8,128)(2,1)S(1)}) custom-call(s32[5]{0:T(128)S(1)} %stack.23.ids.refs_0_, f32[2048,256]{1,0:T(8,128)S(1)} %keep_product.1.refs_1_, f32[1024,256]{1,0:T(8,128)S(1)} %collective-permute-done.22.refs_2_, ...), custom_call_target="tpu_custom_call" | custom-call | tf_op jit(solution)/shard_map/pack/pallas_call | solution.py:48
  133.0 4.4 %collective-permute-start.24 = (bf16[528,256]{1,0:T(8,128)(2,1)S(1)}, bf16[528,256]{1,0:T(8,128)(2,1)S(1)}, u32[]{:S(2)}, u32[]{:S(2)}) collective-permute-start(bf16[528,256]{1,0:T(8,128)(2,1)S(1)} %get-tuple-element.73), channel_id=1, source_target_pairs={{1,4},{9,12},{10,9},{11,13},{17,20},{18,17},{19,21},{20,18},{21,22... | collective-permute-start | bytes 811016 | tf_op jit(solution)/shard_map/ppermute | solution.py:377
  137.4 3.6 %collective-permute-start.25 = (bf16[528,256]{1,0:T(8,128)(2,1)S(1)}, bf16[528,256]{1,0:T(8,128)(2,1)S(1)}, u32[]{:S(2)}, u32[]{:S(2)}) collective-permute-start(bf16[528,256]{1,0:T(8,128)(2,1)S(1)} %get-tuple-element.74), channel_id=1, source_target_pairs={{0,1},{1,5},{8,9},{9,13},{11,14},{16,17},{17,21},{19,22},{20,19},{... | collective-permute-start | bytes 811016 | tf_op jit(solution)/shard_map/ppermute | solution.py:377
  142.9 5.9 %collective-permute-start.27 = (bf16[528,256]{1,0:T(8,128)(2,1)S(1)}, bf16[528,256]{1,0:T(8,128)(2,1)S(1)}, u32[]{:S(2)}, u32[]{:S(2)}) collective-permute-start(bf16[528,256]{1,0:T(8,128)(2,1)S(1)} %get-tuple-element.76), channel_id=1, source_target_pairs={{0,3},{1,7},{8,11},{9,15},{10,8},{11,12},{16,19},{17,23},{18,16},{... | collective-permute-start | bytes 811016 | tf_op jit(solution)/shard_map/ppermute | solution.py:377
  148.8 2.3 %collective-permute-done.21.refs_6_ = bf16[528,256]{1,0:T(8,128)(2,1)S(1)} collective-permute-done((bf16[528,256]{1,0:T(8,128)(2,1)S(1)}, bf16[528,256]{1,0:T(8,128)(2,1)S(1)}, u32[]{:S(2)}, u32[]{:S(2)}) %collective-permute-start.21) | collective-permute-done | bytes 270368 | tf_op jit(solution)/shard_map/ppermute | solution.py:377
  152.7 2.0 %collective-permute-done.26.refs_5_ = bf16[528,256]{1,0:T(8,128)(2,1)S(1)} collective-permute-done((bf16[528,256]{1,0:T(8,128)(2,1)S(1)}, bf16[528,256]{1,0:T(8,128)(2,1)S(1)}, u32[]{:S(2)}, u32[]{:S(2)}) %collective-permute-start.26) | collective-permute-done | bytes 270368 | tf_op jit(solution)/shard_map/ppermute | solution.py:377
  154.7 13.4 %collective-permute-done.27.refs_6_ = bf16[528,256]{1,0:T(8,128)(2,1)S(1)} collective-permute-done((bf16[528,256]{1,0:T(8,128)(2,1)S(1)}, bf16[528,256]{1,0:T(8,128)(2,1)S(1)}, u32[]{:S(2)}, u32[]{:S(2)}) %collective-permute-start.27) | collective-permute-done | bytes 270368 | tf_op jit(solution)/shard_map/ppermute | solution.py:377
  168.1 2.6 %finish.3 = f32[512,512]{1,0:T(8,128)} custom-call(s32[5]{0:T(128)S(1)} %stack.23.ids.refs_0_, f32[512,256]{1,0:T(8,128)S(1)} %finish.2.refs_1_, f32[512,256]{1,0:T(8,128)S(1)} %get-tuple-element.72.refs_7_.refs_2_, bf16[528,256]{1,0:T(8,128)(2,1)S(1)} %collective-permute-done.24.refs_3_, bf16[528,256]{1,0:T(8,128)(2,1)S(1)} %collective-permute-done.25.refs_4_, ...), custom_call_target="tpu_custom_call" | custom-call | tf_op jit(solution)/shard_map/finish/pallas_call | solution.py:48
  (44 shorter events, 21.8 us)
Async XLA Ops:
  0.0 27.1 %collective-permute-start = (bf16[512,512]{1,0:T(8,128)(2,1)}, bf16[512,512]{1,0:T(8,128)(2,1)S(1)}, u32[]{:S(2)}, u32[]{:S(2)}) collective-permute-start(bf16[512,512]{1,0:T(8,128)(2,1)} %refs_1_.1), channel_id=1, source_target_pairs={{4,0},{5,1},{6,2},{7,3},{12,8},{13,9},{14,10},{15,11},{16,20},{17,... | collective-permute-start | bytes 1572872 | tf_op jit(solution)/shard_map/ppermute | solution.py:377
  4.2 24.2 %collective-permute-start.1 = (bf16[512,512]{1,0:T(8,128)(2,1)}, bf16[512,512]{1,0:T(8,128)(2,1)S(1)}, u32[]{:S(2)}, u32[]{:S(2)}) collective-permute-start(bf16[512,512]{1,0:T(8,128)(2,1)} %refs_1_.1), channel_id=1, source_target_pairs={{8,10},{9,11},{16,18},{17,19},{18,20},{19,21},{24,26},{25,27},{26,... | collective-permute-start | bytes 1572872 | tf_op jit(solution)/shard_map/ppermute | solution.py:377
  7.5 24.4 %collective-permute-start.2 = (bf16[512,512]{1,0:T(8,128)(2,1)}, bf16[512,512]{1,0:T(8,128)(2,1)S(1)}, u32[]{:S(2)}, u32[]{:S(2)}) collective-permute-start(bf16[512,512]{1,0:T(8,128)(2,1)} %refs_1_.1), channel_id=1, source_target_pairs={{2,0},{3,1},{10,8},{11,9},{12,10},{13,11},{18,16},{19,17},{20,18},... | collective-permute-start | bytes 1572872 | tf_op jit(solution)/shard_map/ppermute | solution.py:377
  8.9 5.8 %copy-start = (bf16[4096,2048]{1,0:T(8,128)(2,1)S(1)}, bf16[4096,2048]{1,0:T(8,128)(2,1)}, u32[]{:S(2)}) copy-start(bf16[4096,2048]{1,0:T(8,128)(2,1)} %a_ref.1) | copy-start | bytes 50331652
  14.6 28.5 %copy-start.1 = (bf16[512,512]{1,0:T(8,128)(2,1)S(1)}, bf16[512,512]{1,0:T(8,128)(2,1)}, u32[]{:S(2)}) copy-start(bf16[512,512]{1,0:T(8,128)(2,1)} %refs_1_.1) | copy-start | bytes 1572868
  27.1 16.0 %collective-permute-start.3 = (bf16[512,512]{1,0:T(8,128)(2,1)S(1)}, bf16[512,512]{1,0:T(8,128)(2,1)S(1)}, u32[]{:S(2)}, u32[]{:S(2)}) collective-permute-start(bf16[512,512]{1,0:T(8,128)(2,1)S(1)} %collective-permute-done.refs_2_), channel_id=1, source_target_pairs={{2,0},{3,1},{10,8},{11,9},{18,16},{19,17},{26,24},{27,25},{28,30},... | collective-permute-start | bytes 1572872 | tf_op jit(solution)/shard_map/ppermute | solution.py:377
  43.8 6.3 %collective-permute-start.4 = (bf16[2048,256]{1,0:T(8,128)(2,1)S(1)}, bf16[2048,256]{1,0:T(8,128)(2,1)S(1)}, u32[]{:S(2)}, u32[]{:S(2)}) collective-permute-start(bf16[2048,256]{1,0:T(8,128)(2,1)S(1)} %get-tuple-element.44.refs_1_.refs_3_), channel_id=1, source_target_pairs={{0,1},{1,0},{8,9},{9,8},{10,11},{11,10},{16,17},{17,16},{18,19},{1... | collective-permute-start | bytes 3145736 | tf_op jit(solution)/shard_map/ppermute | solution.py:377
  47.9 13.8 %collective-permute-start.6 = (bf16[2048,256]{1,0:T(8,128)(2,1)S(1)}, bf16[2048,256]{1,0:T(8,128)(2,1)S(1)}, u32[]{:S(2)}, u32[]{:S(2)}) collective-permute-start(bf16[2048,256]{1,0:T(8,128)(2,1)S(1)} %get-tuple-element.46.refs_3_.refs_1_), channel_id=1, source_target_pairs={{0,1},{1,0},{8,9},{9,8},{10,11},{11,10},{16,17},{17,16},{18,19},{1... | collective-permute-start | bytes 3145736 | tf_op jit(solution)/shard_map/ppermute | solution.py:377
  50.8 22.5 %collective-permute-start.5 = (bf16[2048,256]{1,0:T(8,128)(2,1)S(1)}, bf16[2048,256]{1,0:T(8,128)(2,1)S(1)}, u32[]{:S(2)}, u32[]{:S(2)}) collective-permute-start(bf16[2048,256]{1,0:T(8,128)(2,1)S(1)} %half.2.refs_2_), channel_id=1, source_target_pairs={{0,8},{1,17},{10,2},{11,27},{20,28}} | collective-permute-start | bytes 3145736 | tf_op jit(solution)/shard_map/ppermute | solution.py:377
  60.4 15.0 %collective-permute-start.9 = (bf16[2112,256]{1,0:T(8,128)(2,1)S(1)}, bf16[2112,256]{1,0:T(8,128)(2,1)S(1)}, u32[]{:S(2)}, u32[]{:S(2)}) collective-permute-start(bf16[2112,256]{1,0:T(8,128)(2,1)S(1)} %get-tuple-element.47.refs_5_), channel_id=1, source_target_pairs={{16,0},{24,8},{9,1},{25,17},{26,10},{18,2},{19,27},{29,21}} | collective-permute-start | bytes 3244040 | tf_op jit(solution)/shard_map/ppermute | solution.py:377
  62.4 13.0 %collective-permute-start.10 = (bf16[2048,256]{1,0:T(8,128)(2,1)S(1)}, bf16[2048,256]{1,0:T(8,128)(2,1)S(1)}, u32[]{:S(2)}, u32[]{:S(2)}) collective-permute-start(bf16[2048,256]{1,0:T(8,128)(2,1)S(1)} %half.3.refs_2_), channel_id=1, source_target_pairs={{0,8},{1,17},{10,2},{11,27},{20,28}} | collective-permute-start | bytes 3145736 | tf_op jit(solution)/shard_map/ppermute | solution.py:377
  71.9 27.7 %collective-permute-start.14 = (bf16[2112,256]{1,0:T(8,128)(2,1)S(1)}, bf16[2112,256]{1,0:T(8,128)(2,1)S(1)}, u32[]{:S(2)}, u32[]{:S(2)}) collective-permute-start(bf16[2112,256]{1,0:T(8,128)(2,1)S(1)} %get-tuple-element.48.refs_3_), channel_id=1, source_target_pairs={{16,0},{24,8},{9,1},{25,17},{26,10},{18,2},{19,27},{29,21}} | collective-permute-start | bytes 3244040 | tf_op jit(solution)/shard_map/ppermute | solution.py:377
  73.3 6.5 %collective-permute-start.7 = (bf16[2048,256]{1,0:T(8,128)(2,1)S(1)}, bf16[2048,256]{1,0:T(8,128)(2,1)S(1)}, u32[]{:S(2)}, u32[]{:S(2)}) collective-permute-start(bf16[2048,256]{1,0:T(8,128)(2,1)S(1)} %half.2.refs_2_), channel_id=1, source_target_pairs={{0,16},{1,9},{10,26},{21,29}} | collective-permute-start | bytes 3145736 | tf_op jit(solution)/shard_map/ppermute | solution.py:377
  74.1 15.8 %collective-permute-start.8 = (bf16[2048,256]{1,0:T(8,128)(2,1)S(1)}, bf16[2048,256]{1,0:T(8,128)(2,1)S(1)}, u32[]{:S(2)}, u32[]{:S(2)}) collective-permute-start(bf16[2048,256]{1,0:T(8,128)(2,1)S(1)} %collective-permute-done.5.refs_3_), channel_id=1, source_target_pairs={{8,24},{17,25},{2,18},{27,19}} | collective-permute-start | bytes 3145736 | tf_op jit(solution)/shard_map/ppermute | solution.py:377
  78.3 23.3 %collective-permute-start.13 = (bf16[2112,256]{1,0:T(8,128)(2,1)S(1)}, bf16[2112,256]{1,0:T(8,128)(2,1)S(1)}, u32[]{:S(2)}, u32[]{:S(2)}) collective-permute-start(bf16[2112,256]{1,0:T(8,128)(2,1)S(1)} %get-tuple-element.53.refs_6_), channel_id=1, source_target_pairs={{8,0},{17,1},{2,10},{27,11},{28,20}} | collective-permute-start | bytes 3244040 | tf_op jit(solution)/shard_map/ppermute | solution.py:377
  79.1 22.5 %collective-permute-start.15 = (bf16[2048,256]{1,0:T(8,128)(2,1)S(1)}, bf16[2048,256]{1,0:T(8,128)(2,1)S(1)}, u32[]{:S(2)}, u32[]{:S(2)}) collective-permute-start(bf16[2048,256]{1,0:T(8,128)(2,1)S(1)} %half.3.refs_2_), channel_id=1, source_target_pairs={{0,16},{1,9},{10,26},{21,29}} | collective-permute-start | bytes 3145736 | tf_op jit(solution)/shard_map/ppermute | solution.py:377
  79.8 25.5 %collective-permute-start.16 = (bf16[2048,256]{1,0:T(8,128)(2,1)S(1)}, bf16[2048,256]{1,0:T(8,128)(2,1)S(1)}, u32[]{:S(2)}, u32[]{:S(2)}) collective-permute-start(bf16[2048,256]{1,0:T(8,128)(2,1)S(1)} %collective-permute-done.10.refs_4_.refs_3_), channel_id=1, source_target_pairs={{8,24},{17,25},{2,18},{27,19}} | collective-permute-start | bytes 3145736 | tf_op jit(solution)/shard_map/ppermute | solution.py:377
  96.3 9.0 %collective-permute-start.11 = (f32[1024,256]{1,0:T(8,128)S(1)}, f32[1024,256]{1,0:T(8,128)S(1)}, u32[]{:S(2)}, u32[]{:S(2)}) collective-permute-start(f32[1024,256]{1,0:T(8,128)S(1)} %get-tuple-element.55), channel_id=1, source_target_pairs={{0,1},{1,0},{8,9},{9,8},{10,11},{11,10},{16,17},{17,16},{18,19},{1... | collective-permute-start | bytes 3145736 | tf_op jit(solution)/shard_map/ppermute | solution.py:377
  99.6 5.7 %collective-permute-start.12 = (f32[1024,256]{1,0:T(8,128)S(1)}, f32[1024,256]{1,0:T(8,128)S(1)}, u32[]{:S(2)}, u32[]{:S(2)}) collective-permute-start(f32[1024,256]{1,0:T(8,128)S(1)} %get-tuple-element.56), channel_id=1, source_target_pairs={{0,1},{1,0},{8,9},{9,8},{10,11},{11,10},{16,17},{17,16},{18,19},{1... | collective-permute-start | bytes 3145736 | tf_op jit(solution)/shard_map/ppermute | solution.py:377
  104.5 16.9 %collective-permute-start.17 = (bf16[2112,256]{1,0:T(8,128)(2,1)S(1)}, bf16[2112,256]{1,0:T(8,128)(2,1)S(1)}, u32[]{:S(2)}, u32[]{:S(2)}) collective-permute-start(bf16[2112,256]{1,0:T(8,128)(2,1)S(1)} %get-tuple-element.60.refs_6_), channel_id=1, source_target_pairs={{8,0},{17,1},{2,10},{27,11},{28,20}} | collective-permute-start | bytes 3244040 | tf_op jit(solution)/shard_map/ppermute | solution.py:377
  111.2 19.7 %collective-permute-start.22 = (f32[1024,256]{1,0:T(8,128)S(1)}, f32[1024,256]{1,0:T(8,128)S(1)}, u32[]{:S(2)}, u32[]{:S(2)}) collective-permute-start(f32[1024,256]{1,0:T(8,128)S(1)} %get-tuple-element.69), channel_id=1, source_target_pairs={{0,1},{1,0},{8,9},{9,8},{10,11},{11,10},{16,17},{17,16},{18,19},{1... | collective-permute-start | bytes 3145736 | tf_op jit(solution)/shard_map/ppermute | solution.py:377
  113.6 17.3 %collective-permute-start.23 = (f32[1024,256]{1,0:T(8,128)S(1)}, f32[1024,256]{1,0:T(8,128)S(1)}, u32[]{:S(2)}, u32[]{:S(2)}) collective-permute-start(f32[1024,256]{1,0:T(8,128)S(1)} %get-tuple-element.70), channel_id=1, source_target_pairs={{0,1},{1,0},{8,9},{9,8},{10,11},{11,10},{16,17},{17,16},{18,19},{1... | collective-permute-start | bytes 3145736 | tf_op jit(solution)/shard_map/ppermute | solution.py:377
  115.5 13.2 %collective-permute-start.18 = (bf16[528,256]{1,0:T(8,128)(2,1)S(1)}, bf16[528,256]{1,0:T(8,128)(2,1)S(1)}, u32[]{:S(2)}, u32[]{:S(2)}) collective-permute-start(bf16[528,256]{1,0:T(8,128)(2,1)S(1)} %get-tuple-element.63), channel_id=1, source_target_pairs={{1,4},{9,12},{10,9},{11,13},{17,20},{18,17},{19,21},{20,18},{21,22... | collective-permute-start | bytes 811016 | tf_op jit(solution)/shard_map/ppermute | solution.py:377
  119.5 21.5 %collective-permute-start.19 = (bf16[528,256]{1,0:T(8,128)(2,1)S(1)}, bf16[528,256]{1,0:T(8,128)(2,1)S(1)}, u32[]{:S(2)}, u32[]{:S(2)}) collective-permute-start(bf16[528,256]{1,0:T(8,128)(2,1)S(1)} %get-tuple-element.65), channel_id=1, source_target_pairs={{0,1},{1,5},{8,9},{9,13},{11,14},{16,17},{17,21},{19,22},{20,19},{... | collective-permute-start | bytes 811016 | tf_op jit(solution)/shard_map/ppermute | solution.py:377
  121.4 21.5 %collective-permute-start.20 = (bf16[528,256]{1,0:T(8,128)(2,1)S(1)}, bf16[528,256]{1,0:T(8,128)(2,1)S(1)}, u32[]{:S(2)}, u32[]{:S(2)}) collective-permute-start(bf16[528,256]{1,0:T(8,128)(2,1)S(1)} %get-tuple-element.66), channel_id=1, source_target_pairs={{0,2},{1,6},{8,10},{9,14},{10,11},{11,15},{16,18},{17,22},{18,19},... | collective-permute-start | bytes 811016 | tf_op jit(solution)/shard_map/ppermute | solution.py:377
  128.7 22.4 %collective-permute-start.21 = (bf16[528,256]{1,0:T(8,128)(2,1)S(1)}, bf16[528,256]{1,0:T(8,128)(2,1)S(1)}, u32[]{:S(2)}, u32[]{:S(2)}) collective-permute-start(bf16[528,256]{1,0:T(8,128)(2,1)S(1)} %get-tuple-element.67), channel_id=1, source_target_pairs={{0,3},{1,7},{8,11},{9,15},{10,8},{11,12},{16,19},{17,23},{18,16},{... | collective-permute-start | bytes 811016 | tf_op jit(solution)/shard_map/ppermute | solution.py:377
  133.0 19.7 %collective-permute-start.24 = (bf16[528,256]{1,0:T(8,128)(2,1)S(1)}, bf16[528,256]{1,0:T(8,128)(2,1)S(1)}, u32[]{:S(2)}, u32[]{:S(2)}) collective-permute-start(bf16[528,256]{1,0:T(8,128)(2,1)S(1)} %get-tuple-element.73), channel_id=1, source_target_pairs={{1,4},{9,12},{10,9},{11,13},{17,20},{18,17},{19,21},{20,18},{21,22... | collective-permute-start | bytes 811016 | tf_op jit(solution)/shard_map/ppermute | solution.py:377
  137.4 15.3 %collective-permute-start.25 = (bf16[528,256]{1,0:T(8,128)(2,1)S(1)}, bf16[528,256]{1,0:T(8,128)(2,1)S(1)}, u32[]{:S(2)}, u32[]{:S(2)}) collective-permute-start(bf16[528,256]{1,0:T(8,128)(2,1)S(1)} %get-tuple-element.74), channel_id=1, source_target_pairs={{0,1},{1,5},{8,9},{9,13},{11,14},{16,17},{17,21},{19,22},{20,19},{... | collective-permute-start | bytes 811016 | tf_op jit(solution)/shard_map/ppermute | solution.py:377
  141.0 13.7 %collective-permute-start.26 = (bf16[528,256]{1,0:T(8,128)(2,1)S(1)}, bf16[528,256]{1,0:T(8,128)(2,1)S(1)}, u32[]{:S(2)}, u32[]{:S(2)}) collective-permute-start(bf16[528,256]{1,0:T(8,128)(2,1)S(1)} %get-tuple-element.75), channel_id=1, source_target_pairs={{0,2},{1,6},{8,10},{9,14},{10,11},{11,15},{16,18},{17,22},{18,19},... | collective-permute-start | bytes 811016 | tf_op jit(solution)/shard_map/ppermute | solution.py:377
  142.9 25.1 %collective-permute-start.27 = (bf16[528,256]{1,0:T(8,128)(2,1)S(1)}, bf16[528,256]{1,0:T(8,128)(2,1)S(1)}, u32[]{:S(2)}, u32[]{:S(2)}) collective-permute-start(bf16[528,256]{1,0:T(8,128)(2,1)S(1)} %get-tuple-element.76), channel_id=1, source_target_pairs={{0,3},{1,7},{8,11},{9,15},{10,8},{11,12},{16,19},{17,23},{18,16},{... | collective-permute-start | bytes 811016 | tf_op jit(solution)/shard_map/ppermute | solution.py:377

commit v11 on v10

--- a/solution.py
+++ b/solution.py
@@ -469,7 +469,8 @@
 
     if chips == 4:
         two = two_away(panel_vectors)
-        came, places = [panel_vectors, two, *next_ones(panel_vectors)], four
+        later, matrix = lax.optimization_barrier((panel_vectors, matrix))
+        came, places = [panel_vectors, two, *next_ones(later)], four
         two, matrix = lax.optimization_barrier((two, matrix))
         came.append(ends(two))
     else:

time: 171 us -> 179 us (1.047)
  waiting for transfers between devices: 52.3 us -> 61.6 us
    ppermute x28, waiting for transfers between devices: 52.3 us -> 61.6 us  [send(): return lax.ppermute(x, ('row', 'col'), [(at(*s), at(*d)) for s, d in pairs])]
  transfers between devices with their start and end apart: 28 -> 28, of which waited for: 8 -> 8; matrix products, arithmetic and copies ran while one was open for 0% -> 0% of each run, Pallas kernels for 27% -> 26%
where the time goes in v11:
time: 179 us; the launch traced here: 178 us
  waiting for transfers between devices  61.6 us (34%)
  starting transfers between devices  61.3 us (34%)
  Pallas kernels  49.1 us (27%)
  local copies, waits for them, and re-layouts  5.86 us (3%)
    ppermute x28, waiting for transfers between devices, send(): return lax.ppermute(x, ('row', 'col'), [(at(*s), at(*d)) for s, d in pairs])  61.6 us
    ppermute x28, starting transfers between devices, send(): return lax.ppermute(x, ('row', 'col'), [(at(*s), at(*d)) for s, d in pairs])  61.3 us
    pallas_call x14, Pallas kernels, local(): pl.pallas_call(body, out_shape=out_shape, in_specs=[pl.BlockSpec(memory_s...  47.3 us
    unnamed x4, local copies, waits for them, and re-layouts  5.77 us
  transfers between devices with their start and end apart: 28, of which 8 were waited for; matrix products, arithmetic and copies ran while one was open for 0% of the time, Pallas kernels for 26%

profile of v11, /device:TPU:7, one launch (start us, length us, event | category | flops | bytes accessed | tf_op | source)
XLA Modules:
  0.0 178.4 jit_solution(157599785560537061)
XLA Ops:
  0.0 4.2 %collective-permute-start = (bf16[512,512]{1,0:T(8,128)(2,1)}, bf16[512,512]{1,0:T(8,128)(2,1)S(1)}, u32[]{:S(2)}, u32[]{:S(2)}) collective-permute-start(bf16[512,512]{1,0:T(8,128)(2,1)} %refs_1_.1), channel_id=1, source_target_pairs={{4,0},{5,1},{6,2},{7,3},{12,8},{13,9},{14,10},{15,11},{16,20},{17,... | collective-permute-start | bytes 1572872 | tf_op jit(solution)/shard_map/ppermute | solution.py:377
  4.3 5.8 %copy-done = bf16[4096,2048]{1,0:T(8,128)(2,1)S(1)} copy-done((bf16[4096,2048]{1,0:T(8,128)(2,1)S(1)}, bf16[4096,2048]{1,0:T(8,128)(2,1)}, u32[]{:S(2)}) %copy-start) | copy-done | bytes 16777240
  11.9 3.2 %collective-permute-start.1 = (bf16[512,512]{1,0:T(8,128)(2,1)S(1)}, bf16[512,512]{1,0:T(8,128)(2,1)S(1)}, u32[]{:S(2)}, u32[]{:S(2)}) collective-permute-start(bf16[512,512]{1,0:T(8,128)(2,1)S(1)} %copy-done.1), channel_id=1, source_target_pairs={{8,10},{9,11},{16,18},{17,19},{18,20},{19,21},{24,26},{25,27},{26,... | collective-permute-start | bytes 1572872 | tf_op jit(solution)/shard_map/ppermute | solution.py:377
  16.4 10.7 %collective-permute-done.refs_2_ = bf16[512,512]{1,0:T(8,128)(2,1)S(1)} collective-permute-done((bf16[512,512]{1,0:T(8,128)(2,1)}, bf16[512,512]{1,0:T(8,128)(2,1)S(1)}, u32[]{:S(2)}, u32[]{:S(2)}) %collective-permute-start) | collective-permute-done | bytes 524320 | tf_op jit(solution)/shard_map/ppermute | solution.py:377
  28.4 10.9 %collective-permute-done.2.refs_4_ = bf16[512,512]{1,0:T(8,128)(2,1)S(1)} collective-permute-done((bf16[512,512]{1,0:T(8,128)(2,1)S(1)}, bf16[512,512]{1,0:T(8,128)(2,1)S(1)}, u32[]{:S(2)}, u32[]{:S(2)}) %collective-permute-start.2) | collective-permute-done | bytes 524320 | tf_op jit(solution)/shard_map/ppermute | solution.py:377
  39.3 11.2 %collective-permute-done.3.refs_5_ = bf16[512,512]{1,0:T(8,128)(2,1)S(1)} collective-permute-done((bf16[512,512]{1,0:T(8,128)(2,1)S(1)}, bf16[512,512]{1,0:T(8,128)(2,1)S(1)}, u32[]{:S(2)}, u32[]{:S(2)}) %collective-permute-start.3) | collective-permute-done | bytes 524320 | tf_op jit(solution)/shard_map/ppermute | solution.py:377
  51.3 2.4 %collective-permute-start.4 = (bf16[2048,256]{1,0:T(8,128)(2,1)S(1)}, bf16[2048,256]{1,0:T(8,128)(2,1)S(1)}, u32[]{:S(2)}, u32[]{:S(2)}) collective-permute-start(bf16[2048,256]{1,0:T(8,128)(2,1)S(1)} %get-tuple-element.48.refs_1_.refs_3_), channel_id=1, source_target_pairs={{0,1},{1,0},{8,9},{9,8},{10,11},{11,10},{16,17},{17,16},{18,19},{1... | collective-permute-start | bytes 3145736 | tf_op jit(solution)/shard_map/ppermute | solution.py:377
  53.7 1.9 %collective-permute-start.6 = (bf16[2048,256]{1,0:T(8,128)(2,1)S(1)}, bf16[2048,256]{1,0:T(8,128)(2,1)S(1)}, u32[]{:S(2)}, u32[]{:S(2)}) collective-permute-start(bf16[2048,256]{1,0:T(8,128)(2,1)S(1)} %get-tuple-element.50.refs_3_.refs_1_), channel_id=1, source_target_pairs={{0,1},{1,0},{8,9},{9,8},{10,11},{11,10},{16,17},{17,16},{18,19},{1... | collective-permute-start | bytes 3145736 | tf_op jit(solution)/shard_map/ppermute | solution.py:377
  57.3 8.8 %mirrored_product.2 = (f32[2048,256]{1,0:T(8,128)S(1)}, bf16[2112,256]{1,0:T(8,128)(2,1)S(1)}) custom-call(s32[5]{0:T(128)S(1)} %stack.23.ids.refs_0_, bf16[4096,2048]{1,0:T(8,128)(2,1)S(1)} %get-tuple-element.45.refs_1_, f32[8,2048]{1,0:T(8,128)S(1)} %get-tuple-element.49.refs_2_, bf16[2048,256]{1,0:T(8,128)(2,1)S(1)} %get-tuple-element.48.refs_1_.refs_3_, ...), custom_call_target="tpu_custom_call" | custom-call | tf_op jit(solution)/shard_map/mirrored_product/pallas_call | solution.py:48
  66.1 2.8 %collective-permute-start.9 = (bf16[2112,256]{1,0:T(8,128)(2,1)S(1)}, bf16[2112,256]{1,0:T(8,128)(2,1)S(1)}, u32[]{:S(2)}, u32[]{:S(2)}) collective-permute-start(bf16[2112,256]{1,0:T(8,128)(2,1)S(1)} %get-tuple-element.51.refs_5_), channel_id=1, source_target_pairs={{16,0},{24,8},{9,1},{25,17},{26,10},{18,2},{19,27},{29,21}} | collective-permute-start | bytes 3244040 | tf_op jit(solution)/shard_map/ppermute | solution.py:377
  70.3 8.8 %mirrored_product.3 = (f32[2048,256]{1,0:T(8,128)S(1)}, bf16[2112,256]{1,0:T(8,128)(2,1)S(1)}) custom-call(s32[5]{0:T(128)S(1)} %stack.23.ids.refs_0_, bf16[4096,2048]{1,0:T(8,128)(2,1)S(1)} %get-tuple-element.45.refs_1_, f32[8,2048]{1,0:T(8,128)S(1)} %get-tuple-element.49.refs_2_, bf16[2048,256]{1,0:T(8,128)(2,1)S(1)} %get-tuple-element.50.refs_3_.refs_1_, ...), custom_call_target="tpu_custom_call" | custom-call | tf_op jit(solution)/shard_map/mirrored_product/pallas_call | solution.py:48
  83.1 2.9 %relay.2 = (f32[2048,256]{1,0:T(8,128)S(1)}, bf16[2112,256]{1,0:T(8,128)(2,1)S(1)}) custom-call(s32[5]{0:T(128)S(1)} %stack.23.ids.refs_0_, f32[2048,256]{1,0:T(8,128)S(1)} %get-tuple-element.55.refs_1_, bf16[2112,256]{1,0:T(8,128)(2,1)S(1)} %collective-permute-done.9.refs_2_, bf16[2112,256]{1,0:T(8,128)(2,1)S(1)} %get-tuple-element.52.refs_3_, ...), custom_call_target="tpu_custom_call" | custom-call | tf_op jit(solution)/shard_map/relay/pallas_call | solution.py:48
  88.8 8.8 %collective-permute-done.8.refs_5_ = bf16[2048,256]{1,0:T(8,128)(2,1)S(1)} collective-permute-done((bf16[2048,256]{1,0:T(8,128)(2,1)S(1)}, bf16[2048,256]{1,0:T(8,128)(2,1)S(1)}, u32[]{:S(2)}, u32[]{:S(2)}) %collective-permute-start.8) | collective-permute-done | bytes 1048608 | tf_op jit(solution)/shard_map/ppermute | solution.py:377
  97.6 6.4 %direct_product.1 = (f32[2048,256]{1,0:T(8,128)S(1)}, f32[1024,256]{1,0:T(8,128)S(1)}, f32[1024,256]{1,0:T(8,128)S(1)}) custom-call(s32[5]{0:T(128)S(1)} %stack.23.ids.refs_0_, bf16[4096,2048]{1,0:T(8,128)(2,1)S(1)} %get-tuple-element.45.refs_1_, bf16[2048,256]{1,0:T(8,128)(2,1)S(1)} %half.2.refs_2_, bf16[2048,256]{1,0:T(8,128)(2,1)S(1)} %collective-permute-done.5.refs_3_, ...), custom_call_target="tpu_custom_call" | custom-call | tf_op jit(solution)/shard_map/direct_product/pallas_call | solution.py:48
  104.0 3.4 %collective-permute-start.11 = (f32[1024,256]{1,0:T(8,128)S(1)}, f32[1024,256]{1,0:T(8,128)S(1)}, u32[]{:S(2)}, u32[]{:S(2)}) collective-permute-start(f32[1024,256]{1,0:T(8,128)S(1)} %get-tuple-element.59), channel_id=1, source_target_pairs={{0,1},{1,0},{8,9},{9,8},{10,11},{11,10},{16,17},{17,16},{18,19},{1... | collective-permute-start | bytes 3145736 | tf_op jit(solution)/shard_map/ppermute | solution.py:377
  107.4 1.9 %collective-permute-start.12 = (f32[1024,256]{1,0:T(8,128)S(1)}, f32[1024,256]{1,0:T(8,128)S(1)}, u32[]{:S(2)}, u32[]{:S(2)}) collective-permute-start(f32[1024,256]{1,0:T(8,128)S(1)} %get-tuple-element.60), channel_id=1, source_target_pairs={{0,1},{1,0},{8,9},{9,8},{10,11},{11,10},{16,17},{17,16},{18,19},{1... | collective-permute-start | bytes 3145736 | tf_op jit(solution)/shard_map/ppermute | solution.py:377
  109.3 2.9 %relay.3 = (f32[2048,256]{1,0:T(8,128)S(1)}, bf16[2112,256]{1,0:T(8,128)(2,1)S(1)}) custom-call(s32[5]{0:T(128)S(1)} %stack.23.ids.refs_0_, f32[2048,256]{1,0:T(8,128)S(1)} %get-tuple-element.62.refs_1_, bf16[2112,256]{1,0:T(8,128)(2,1)S(1)} %collective-permute-done.14.refs_2_, f32[2048,256]{1,0:T(8,128)S(1)} %get-tuple-element.58.refs_3_.refs_1_, ...), custom_call_target="tpu_custom_call" | custom-call | tf_op jit(solution)/shard_map/relay/pallas_call | solution.py:48
  113.0 2.3 %pack.2 = (f32[512,256]{1,0:T(8,128)S(1)}, bf16[528,256]{1,0:T(8,128)(2,1)S(1)}, bf16[528,256]{1,0:T(8,128)(2,1)S(1)}, bf16[528,256]{1,0:T(8,128)(2,1)S(1)}, bf16[528,256]{1,0:T(8,128)(2,1)S(1)}) custom-call(s32[5]{0:T(128)S(1)} %stack.23.ids.refs_0_, f32[2048,256]{1,0:T(8,128)S(1)} %get-tuple-element.58.refs_3_.refs_1_, ...), custom_call_target="tpu_custom_call" | custom-call | tf_op jit(solution)/shard_map/pack/pallas_call | solution.py:48
  115.4 3.5 %give_product.1 = (f32[1024,256]{1,0:T(8,128)S(1)}, f32[1024,256]{1,0:T(8,128)S(1)}, bf16[2048,256]{1,0:T(8,128)(2,1)S(1)}) custom-call(s32[5]{0:T(128)S(1)} %stack.23.ids.refs_0_, bf16[4096,2048]{1,0:T(8,128)(2,1)S(1)} %get-tuple-element.45.refs_1_, bf16[2048,256]{1,0:T(8,128)(2,1)S(1)} %half.3.refs_2_, ...), custom_call_target="tpu_custom_call" | custom-call | tf_op jit(solution)/shard_map/give_product/pallas_call | solution.py:48
  118.9 2.4 %collective-permute-start.22 = (f32[1024,256]{1,0:T(8,128)S(1)}, f32[1024,256]{1,0:T(8,128)S(1)}, u32[]{:S(2)}, u32[]{:S(2)}) collective-permute-start(f32[1024,256]{1,0:T(8,128)S(1)} %get-tuple-element.73), channel_id=1, source_target_pairs={{0,1},{1,0},{8,9},{9,8},{10,11},{11,10},{16,17},{17,16},{18,19},{1... | collective-permute-start | bytes 3145736 | tf_op jit(solution)/shard_map/ppermute | solution.py:377
  123.2 2.0 %collective-permute-start.18 = (bf16[528,256]{1,0:T(8,128)(2,1)S(1)}, bf16[528,256]{1,0:T(8,128)(2,1)S(1)}, u32[]{:S(2)}, u32[]{:S(2)}) collective-permute-start(bf16[528,256]{1,0:T(8,128)(2,1)S(1)} %get-tuple-element.67), channel_id=1, source_target_pairs={{1,4},{9,12},{10,9},{11,13},{17,20},{18,17},{19,21},{20,18},{21,22... | collective-permute-start | bytes 811016 | tf_op jit(solution)/shard_map/ppermute | solution.py:377
  127.2 5.9 %collective-permute-start.20 = (bf16[528,256]{1,0:T(8,128)(2,1)S(1)}, bf16[528,256]{1,0:T(8,128)(2,1)S(1)}, u32[]{:S(2)}, u32[]{:S(2)}) collective-permute-start(bf16[528,256]{1,0:T(8,128)(2,1)S(1)} %get-tuple-element.70), channel_id=1, source_target_pairs={{0,2},{1,6},{8,10},{9,14},{10,11},{11,15},{16,18},{17,22},{18,19},... | collective-permute-start | bytes 811016 | tf_op jit(solution)/shard_map/ppermute | solution.py:377
  133.1 3.4 %keep_product.1.refs_1_ = f32[2048,256]{1,0:T(8,128)S(1)} custom-call(s32[5]{0:T(128)S(1)} %stack.23.ids.refs_0_, bf16[4096,2048]{1,0:T(8,128)(2,1)S(1)} %get-tuple-element.45.refs_1_, bf16[2048,256]{1,0:T(8,128)(2,1)S(1)} %get-tuple-element.66.refs_2_, bf16[2112,256]{1,0:T(8,128)(2,1)S(1)} %collective-permute-done.17.refs_3_.refs_5_), custom_call_target="tpu_custom_call" | custom-call | tf_op jit(solution)/shard_map/keep_product/pallas_call | solution.py:48
  136.5 2.1 %collective-permute-start.21 = (bf16[528,256]{1,0:T(8,128)(2,1)S(1)}, bf16[528,256]{1,0:T(8,128)(2,1)S(1)}, u32[]{:S(2)}, u32[]{:S(2)}) collective-permute-start(bf16[528,256]{1,0:T(8,128)(2,1)S(1)} %get-tuple-element.71), channel_id=1, source_target_pairs={{0,3},{1,7},{8,11},{9,15},{10,8},{11,12},{16,19},{17,23},{18,16},{... | collective-permute-start | bytes 811016 | tf_op jit(solution)/shard_map/ppermute | solution.py:377
  138.6 2.1 %pack.3 = (f32[512,256]{1,0:T(8,128)S(1)}, bf16[528,256]{1,0:T(8,128)(2,1)S(1)}, bf16[528,256]{1,0:T(8,128)(2,1)S(1)}, bf16[528,256]{1,0:T(8,128)(2,1)S(1)}, bf16[528,256]{1,0:T(8,128)(2,1)S(1)}) custom-call(s32[5]{0:T(128)S(1)} %stack.23.ids.refs_0_, f32[2048,256]{1,0:T(8,128)S(1)} %keep_product.1.refs_1_, f32[1024,256]{1,0:T(8,128)S(1)} %collective-permute-done.22.refs_2_, ...), custom_call_target="tpu_custom_call" | custom-call | tf_op jit(solution)/shard_map/pack/pallas_call | solution.py:48
  140.7 4.4 %collective-permute-start.24 = (bf16[528,256]{1,0:T(8,128)(2,1)S(1)}, bf16[528,256]{1,0:T(8,128)(2,1)S(1)}, u32[]{:S(2)}, u32[]{:S(2)}) collective-permute-start(bf16[528,256]{1,0:T(8,128)(2,1)S(1)} %get-tuple-element.77), channel_id=1, source_target_pairs={{1,4},{9,12},{10,9},{11,13},{17,20},{18,17},{19,21},{20,18},{21,22... | collective-permute-start | bytes 811016 | tf_op jit(solution)/shard_map/ppermute | solution.py:377
  145.1 3.6 %collective-permute-start.25 = (bf16[528,256]{1,0:T(8,128)(2,1)S(1)}, bf16[528,256]{1,0:T(8,128)(2,1)S(1)}, u32[]{:S(2)}, u32[]{:S(2)}) collective-permute-start(bf16[528,256]{1,0:T(8,128)(2,1)S(1)} %get-tuple-element.78), channel_id=1, source_target_pairs={{0,1},{1,5},{8,9},{9,13},{11,14},{16,17},{17,21},{19,22},{20,19},{... | collective-permute-start | bytes 811016 | tf_op jit(solution)/shard_map/ppermute | solution.py:377
  150.7 3.9 %collective-permute-start.27 = (bf16[528,256]{1,0:T(8,128)(2,1)S(1)}, bf16[528,256]{1,0:T(8,128)(2,1)S(1)}, u32[]{:S(2)}, u32[]{:S(2)}) collective-permute-start(bf16[528,256]{1,0:T(8,128)(2,1)S(1)} %get-tuple-element.80), channel_id=1, source_target_pairs={{0,3},{1,7},{8,11},{9,15},{10,8},{11,12},{16,19},{17,23},{18,16},{... | collective-permute-start | bytes 811016 | tf_op jit(solution)/shard_map/ppermute | solution.py:377
  154.6 4.2 %collective-permute-done.21.refs_6_ = bf16[528,256]{1,0:T(8,128)(2,1)S(1)} collective-permute-done((bf16[528,256]{1,0:T(8,128)(2,1)S(1)}, bf16[528,256]{1,0:T(8,128)(2,1)S(1)}, u32[]{:S(2)}, u32[]{:S(2)}) %collective-permute-start.21) | collective-permute-done | bytes 270368 | tf_op jit(solution)/shard_map/ppermute | solution.py:377
  160.4 2.0 %collective-permute-done.26.refs_5_ = bf16[528,256]{1,0:T(8,128)(2,1)S(1)} collective-permute-done((bf16[528,256]{1,0:T(8,128)(2,1)S(1)}, bf16[528,256]{1,0:T(8,128)(2,1)S(1)}, u32[]{:S(2)}, u32[]{:S(2)}) %collective-permute-start.26) | collective-permute-done | bytes 270368 | tf_op jit(solution)/shard_map/ppermute | solution.py:377
  162.5 13.4 %collective-permute-done.27.refs_6_ = bf16[528,256]{1,0:T(8,128)(2,1)S(1)} collective-permute-done((bf16[528,256]{1,0:T(8,128)(2,1)S(1)}, bf16[528,256]{1,0:T(8,128)(2,1)S(1)}, u32[]{:S(2)}, u32[]{:S(2)}) %collective-permute-start.27) | collective-permute-done | bytes 270368 | tf_op jit(solution)/shard_map/ppermute | solution.py:377
  175.8 2.6 %finish.3 = f32[512,512]{1,0:T(8,128)} custom-call(s32[5]{0:T(128)S(1)} %stack.23.ids.refs_0_, f32[512,256]{1,0:T(8,128)S(1)} %finish.2.refs_1_, f32[512,256]{1,0:T(8,128)S(1)} %get-tuple-element.76.refs_7_.refs_2_, bf16[528,256]{1,0:T(8,128)(2,1)S(1)} %collective-permute-done.24.refs_3_, bf16[528,256]{1,0:T(8,128)(2,1)S(1)} %collective-permute-done.25.refs_4_, ...), custom_call_target="tpu_custom_call" | custom-call | tf_op jit(solution)/shard_map/finish/pallas_call | solution.py:48
  (44 shorter events, 22.9 us)
Async XLA Ops:
  0.0 27.1 %collective-permute-start = (bf16[512,512]{1,0:T(8,128)(2,1)}, bf16[512,512]{1,0:T(8,128)(2,1)S(1)}, u32[]{:S(2)}, u32[]{:S(2)}) collective-permute-start(bf16[512,512]{1,0:T(8,128)(2,1)} %refs_1_.1), channel_id=1, source_target_pairs={{4,0},{5,1},{6,2},{7,3},{12,8},{13,9},{14,10},{15,11},{16,20},{17,... | collective-permute-start | bytes 1572872 | tf_op jit(solution)/shard_map/ppermute | solution.py:377
  4.3 5.8 %copy-start = (bf16[4096,2048]{1,0:T(8,128)(2,1)S(1)}, bf16[4096,2048]{1,0:T(8,128)(2,1)}, u32[]{:S(2)}) copy-start(bf16[4096,2048]{1,0:T(8,128)(2,1)} %a_ref.1) | copy-start | bytes 50331652
  10.1 1.7 copy-start.1
  11.9 16.5 %collective-permute-start.1 = (bf16[512,512]{1,0:T(8,128)(2,1)S(1)}, bf16[512,512]{1,0:T(8,128)(2,1)S(1)}, u32[]{:S(2)}, u32[]{:S(2)}) collective-permute-start(bf16[512,512]{1,0:T(8,128)(2,1)S(1)} %copy-done.1), channel_id=1, source_target_pairs={{8,10},{9,11},{16,18},{17,19},{18,20},{19,21},{24,26},{25,27},{26,... | collective-permute-start | bytes 1572872 | tf_op jit(solution)/shard_map/ppermute | solution.py:377
  15.1 24.2 %collective-permute-start.2 = (bf16[512,512]{1,0:T(8,128)(2,1)S(1)}, bf16[512,512]{1,0:T(8,128)(2,1)S(1)}, u32[]{:S(2)}, u32[]{:S(2)}) collective-permute-start(bf16[512,512]{1,0:T(8,128)(2,1)S(1)} %copy-done.1), channel_id=1, source_target_pairs={{2,0},{3,1},{10,8},{11,9},{12,10},{13,11},{18,16},{19,17},{20,18},... | collective-permute-start | bytes 1572872 | tf_op jit(solution)/shard_map/ppermute | solution.py:377
  27.1 23.5 %collective-permute-start.3 = (bf16[512,512]{1,0:T(8,128)(2,1)S(1)}, bf16[512,512]{1,0:T(8,128)(2,1)S(1)}, u32[]{:S(2)}, u32[]{:S(2)}) collective-permute-start(bf16[512,512]{1,0:T(8,128)(2,1)S(1)} %collective-permute-done.refs_2_), channel_id=1, source_target_pairs={{2,0},{3,1},{10,8},{11,9},{18,16},{19,17},{26,24},{27,25},{28,30},... | collective-permute-start | bytes 1572872 | tf_op jit(solution)/shard_map/ppermute | solution.py:377
  51.3 4.7 %collective-permute-start.4 = (bf16[2048,256]{1,0:T(8,128)(2,1)S(1)}, bf16[2048,256]{1,0:T(8,128)(2,1)S(1)}, u32[]{:S(2)}, u32[]{:S(2)}) collective-permute-start(bf16[2048,256]{1,0:T(8,128)(2,1)S(1)} %get-tuple-element.48.refs_1_.refs_3_), channel_id=1, source_target_pairs={{0,1},{1,0},{8,9},{9,8},{10,11},{11,10},{16,17},{17,16},{18,19},{1... | collective-permute-start | bytes 3145736 | tf_op jit(solution)/shard_map/ppermute | solution.py:377
  53.7 15.2 %collective-permute-start.6 = (bf16[2048,256]{1,0:T(8,128)(2,1)S(1)}, bf16[2048,256]{1,0:T(8,128)(2,1)S(1)}, u32[]{:S(2)}, u32[]{:S(2)}) collective-permute-start(bf16[2048,256]{1,0:T(8,128)(2,1)S(1)} %get-tuple-element.50.refs_3_.refs_1_), channel_id=1, source_target_pairs={{0,1},{1,0},{8,9},{9,8},{10,11},{11,10},{16,17},{17,16},{18,19},{1... | collective-permute-start | bytes 3145736 | tf_op jit(solution)/shard_map/ppermute | solution.py:377
  56.6 24.4 %collective-permute-start.5 = (bf16[2048,256]{1,0:T(8,128)(2,1)S(1)}, bf16[2048,256]{1,0:T(8,128)(2,1)S(1)}, u32[]{:S(2)}, u32[]{:S(2)}) collective-permute-start(bf16[2048,256]{1,0:T(8,128)(2,1)S(1)} %half.2.refs_2_), channel_id=1, source_target_pairs={{0,8},{1,17},{10,2},{11,27},{20,28}} | collective-permute-start | bytes 3145736 | tf_op jit(solution)/shard_map/ppermute | solution.py:377
  66.1 16.9 %collective-permute-start.9 = (bf16[2112,256]{1,0:T(8,128)(2,1)S(1)}, bf16[2112,256]{1,0:T(8,128)(2,1)S(1)}, u32[]{:S(2)}, u32[]{:S(2)}) collective-permute-start(bf16[2112,256]{1,0:T(8,128)(2,1)S(1)} %get-tuple-element.51.refs_5_), channel_id=1, source_target_pairs={{16,0},{24,8},{9,1},{25,17},{26,10},{18,2},{19,27},{29,21}} | collective-permute-start | bytes 3244040 | tf_op jit(solution)/shard_map/ppermute | solution.py:377
  69.5 13.5 %collective-permute-start.10 = (bf16[2048,256]{1,0:T(8,128)(2,1)S(1)}, bf16[2048,256]{1,0:T(8,128)(2,1)S(1)}, u32[]{:S(2)}, u32[]{:S(2)}) collective-permute-start(bf16[2048,256]{1,0:T(8,128)(2,1)S(1)} %half.3.refs_2_), channel_id=1, source_target_pairs={{0,8},{1,17},{10,2},{11,27},{20,28}} | collective-permute-start | bytes 3145736 | tf_op jit(solution)/shard_map/ppermute | solution.py:377
  79.1 28.3 %collective-permute-start.14 = (bf16[2112,256]{1,0:T(8,128)(2,1)S(1)}, bf16[2112,256]{1,0:T(8,128)(2,1)S(1)}, u32[]{:S(2)}, u32[]{:S(2)}) collective-permute-start(bf16[2112,256]{1,0:T(8,128)(2,1)S(1)} %get-tuple-element.52.refs_3_), channel_id=1, source_target_pairs={{16,0},{24,8},{9,1},{25,17},{26,10},{18,2},{19,27},{29,21}} | collective-permute-start | bytes 3244040 | tf_op jit(solution)/shard_map/ppermute | solution.py:377
  81.0 6.5 %collective-permute-start.7 = (bf16[2048,256]{1,0:T(8,128)(2,1)S(1)}, bf16[2048,256]{1,0:T(8,128)(2,1)S(1)}, u32[]{:S(2)}, u32[]{:S(2)}) collective-permute-start(bf16[2048,256]{1,0:T(8,128)(2,1)S(1)} %half.2.refs_2_), channel_id=1, source_target_pairs={{0,16},{1,9},{10,26},{21,29}} | collective-permute-start | bytes 3145736 | tf_op jit(solution)/shard_map/ppermute | solution.py:377
  81.7 15.8 %collective-permute-start.8 = (bf16[2048,256]{1,0:T(8,128)(2,1)S(1)}, bf16[2048,256]{1,0:T(8,128)(2,1)S(1)}, u32[]{:S(2)}, u32[]{:S(2)}) collective-permute-start(bf16[2048,256]{1,0:T(8,128)(2,1)S(1)} %collective-permute-done.5.refs_3_), channel_id=1, source_target_pairs={{8,24},{17,25},{2,18},{27,19}} | collective-permute-start | bytes 3145736 | tf_op jit(solution)/shard_map/ppermute | solution.py:377
  86.0 23.3 %collective-permute-start.13 = (bf16[2112,256]{1,0:T(8,128)(2,1)S(1)}, bf16[2112,256]{1,0:T(8,128)(2,1)S(1)}, u32[]{:S(2)}, u32[]{:S(2)}) collective-permute-start(bf16[2112,256]{1,0:T(8,128)(2,1)S(1)} %get-tuple-element.57.refs_6_), channel_id=1, source_target_pairs={{8,0},{17,1},{2,10},{27,11},{28,20}} | collective-permute-start | bytes 3244040 | tf_op jit(solution)/shard_map/ppermute | solution.py:377
  86.7 22.6 %collective-permute-start.15 = (bf16[2048,256]{1,0:T(8,128)(2,1)S(1)}, bf16[2048,256]{1,0:T(8,128)(2,1)S(1)}, u32[]{:S(2)}, u32[]{:S(2)}) collective-permute-start(bf16[2048,256]{1,0:T(8,128)(2,1)S(1)} %half.3.refs_2_), channel_id=1, source_target_pairs={{0,16},{1,9},{10,26},{21,29}} | collective-permute-start | bytes 3145736 | tf_op jit(solution)/shard_map/ppermute | solution.py:377
  87.5 25.5 %collective-permute-start.16 = (bf16[2048,256]{1,0:T(8,128)(2,1)S(1)}, bf16[2048,256]{1,0:T(8,128)(2,1)S(1)}, u32[]{:S(2)}, u32[]{:S(2)}) collective-permute-start(bf16[2048,256]{1,0:T(8,128)(2,1)S(1)} %collective-permute-done.10.refs_4_.refs_3_), channel_id=1, source_target_pairs={{8,24},{17,25},{2,18},{27,19}} | collective-permute-start | bytes 3145736 | tf_op jit(solution)/shard_map/ppermute | solution.py:377
  104.0 9.1 %collective-permute-start.11 = (f32[1024,256]{1,0:T(8,128)S(1)}, f32[1024,256]{1,0:T(8,128)S(1)}, u32[]{:S(2)}, u32[]{:S(2)}) collective-permute-start(f32[1024,256]{1,0:T(8,128)S(1)} %get-tuple-element.59), channel_id=1, source_target_pairs={{0,1},{1,0},{8,9},{9,8},{10,11},{11,10},{16,17},{17,16},{18,19},{1... | collective-permute-start | bytes 3145736 | tf_op jit(solution)/shard_map/ppermute | solution.py:377
  107.4 5.7 %collective-permute-start.12 = (f32[1024,256]{1,0:T(8,128)S(1)}, f32[1024,256]{1,0:T(8,128)S(1)}, u32[]{:S(2)}, u32[]{:S(2)}) collective-permute-start(f32[1024,256]{1,0:T(8,128)S(1)} %get-tuple-element.60), channel_id=1, source_target_pairs={{0,1},{1,0},{8,9},{9,8},{10,11},{11,10},{16,17},{17,16},{18,19},{1... | collective-permute-start | bytes 3145736 | tf_op jit(solution)/shard_map/ppermute | solution.py:377
  112.3 14.9 %collective-permute-start.17 = (bf16[2112,256]{1,0:T(8,128)(2,1)S(1)}, bf16[2112,256]{1,0:T(8,128)(2,1)S(1)}, u32[]{:S(2)}, u32[]{:S(2)}) collective-permute-start(bf16[2112,256]{1,0:T(8,128)(2,1)S(1)} %get-tuple-element.64.refs_6_), channel_id=1, source_target_pairs={{8,0},{17,1},{2,10},{27,11},{28,20}} | collective-permute-start | bytes 3244040 | tf_op jit(solution)/shard_map/ppermute | solution.py:377
  118.9 19.7 %collective-permute-start.22 = (f32[1024,256]{1,0:T(8,128)S(1)}, f32[1024,256]{1,0:T(8,128)S(1)}, u32[]{:S(2)}, u32[]{:S(2)}) collective-permute-start(f32[1024,256]{1,0:T(8,128)S(1)} %get-tuple-element.73), channel_id=1, source_target_pairs={{0,1},{1,0},{8,9},{9,8},{10,11},{11,10},{16,17},{17,16},{18,19},{1... | collective-permute-start | bytes 3145736 | tf_op jit(solution)/shard_map/ppermute | solution.py:377
  121.3 17.3 %collective-permute-start.23 = (f32[1024,256]{1,0:T(8,128)S(1)}, f32[1024,256]{1,0:T(8,128)S(1)}, u32[]{:S(2)}, u32[]{:S(2)}) collective-permute-start(f32[1024,256]{1,0:T(8,128)S(1)} %get-tuple-element.74), channel_id=1, source_target_pairs={{0,1},{1,0},{8,9},{9,8},{10,11},{11,10},{16,17},{17,16},{18,19},{1... | collective-permute-start | bytes 3145736 | tf_op jit(solution)/shard_map/ppermute | solution.py:377
  123.2 13.2 %collective-permute-start.18 = (bf16[528,256]{1,0:T(8,128)(2,1)S(1)}, bf16[528,256]{1,0:T(8,128)(2,1)S(1)}, u32[]{:S(2)}, u32[]{:S(2)}) collective-permute-start(bf16[528,256]{1,0:T(8,128)(2,1)S(1)} %get-tuple-element.67), channel_id=1, source_target_pairs={{1,4},{9,12},{10,9},{11,13},{17,20},{18,17},{19,21},{20,18},{21,22... | collective-permute-start | bytes 811016 | tf_op jit(solution)/shard_map/ppermute | solution.py:377
  125.3 23.5 %collective-permute-start.19 = (bf16[528,256]{1,0:T(8,128)(2,1)S(1)}, bf16[528,256]{1,0:T(8,128)(2,1)S(1)}, u32[]{:S(2)}, u32[]{:S(2)}) collective-permute-start(bf16[528,256]{1,0:T(8,128)(2,1)S(1)} %get-tuple-element.69), channel_id=1, source_target_pairs={{0,1},{1,5},{8,9},{9,13},{11,14},{16,17},{17,21},{19,22},{20,19},{... | collective-permute-start | bytes 811016 | tf_op jit(solution)/shard_map/ppermute | solution.py:377
  127.2 23.5 %collective-permute-start.20 = (bf16[528,256]{1,0:T(8,128)(2,1)S(1)}, bf16[528,256]{1,0:T(8,128)(2,1)S(1)}, u32[]{:S(2)}, u32[]{:S(2)}) collective-permute-start(bf16[528,256]{1,0:T(8,128)(2,1)S(1)} %get-tuple-element.70), channel_id=1, source_target_pairs={{0,2},{1,6},{8,10},{9,14},{10,11},{11,15},{16,18},{17,22},{18,19},... | collective-permute-start | bytes 811016 | tf_op jit(solution)/shard_map/ppermute | solution.py:377
  136.5 22.4 %collective-permute-start.21 = (bf16[528,256]{1,0:T(8,128)(2,1)S(1)}, bf16[528,256]{1,0:T(8,128)(2,1)S(1)}, u32[]{:S(2)}, u32[]{:S(2)}) collective-permute-start(bf16[528,256]{1,0:T(8,128)(2,1)S(1)} %get-tuple-element.71), channel_id=1, source_target_pairs={{0,3},{1,7},{8,11},{9,15},{10,8},{11,12},{16,19},{17,23},{18,16},{... | collective-permute-start | bytes 811016 | tf_op jit(solution)/shard_map/ppermute | solution.py:377
  140.7 19.7 %collective-permute-start.24 = (bf16[528,256]{1,0:T(8,128)(2,1)S(1)}, bf16[528,256]{1,0:T(8,128)(2,1)S(1)}, u32[]{:S(2)}, u32[]{:S(2)}) collective-permute-start(bf16[528,256]{1,0:T(8,128)(2,1)S(1)} %get-tuple-element.77), channel_id=1, source_target_pairs={{1,4},{9,12},{10,9},{11,13},{17,20},{18,17},{19,21},{20,18},{21,22... | collective-permute-start | bytes 811016 | tf_op jit(solution)/shard_map/ppermute | solution.py:377
  145.1 15.3 %collective-permute-start.25 = (bf16[528,256]{1,0:T(8,128)(2,1)S(1)}, bf16[528,256]{1,0:T(8,128)(2,1)S(1)}, u32[]{:S(2)}, u32[]{:S(2)}) collective-permute-start(bf16[528,256]{1,0:T(8,128)(2,1)S(1)} %get-tuple-element.78), channel_id=1, source_target_pairs={{0,1},{1,5},{8,9},{9,13},{11,14},{16,17},{17,21},{19,22},{20,19},{... | collective-permute-start | bytes 811016 | tf_op jit(solution)/shard_map/ppermute | solution.py:377
  148.7 13.7 %collective-permute-start.26 = (bf16[528,256]{1,0:T(8,128)(2,1)S(1)}, bf16[528,256]{1,0:T(8,128)(2,1)S(1)}, u32[]{:S(2)}, u32[]{:S(2)}) collective-permute-start(bf16[528,256]{1,0:T(8,128)(2,1)S(1)} %get-tuple-element.79), channel_id=1, source_target_pairs={{0,2},{1,6},{8,10},{9,14},{10,11},{11,15},{16,18},{17,22},{18,19},... | collective-permute-start | bytes 811016 | tf_op jit(solution)/shard_map/ppermute | solution.py:377
  150.7 25.1 %collective-permute-start.27 = (bf16[528,256]{1,0:T(8,128)(2,1)S(1)}, bf16[528,256]{1,0:T(8,128)(2,1)S(1)}, u32[]{:S(2)}, u32[]{:S(2)}) collective-permute-start(bf16[528,256]{1,0:T(8,128)(2,1)S(1)} %get-tuple-element.80), channel_id=1, source_target_pairs={{0,3},{1,7},{8,11},{9,15},{10,8},{11,12},{16,19},{17,23},{18,16},{... | collective-permute-start | bytes 811016 | tf_op jit(solution)/shard_map/ppermute | solution.py:377

commit v12 on v10

--- a/solution.py
+++ b/solution.py
@@ -284,7 +284,7 @@
     )
 
 
-def pack_kernel(count, ids, a_ref, *refs):
+def pack_kernel(count, sides, ids, a_ref, *refs):
     theirs, (sum_ref, in_ref, own_ref, *msgs, total) = refs[:count], refs[count:]
     height = own_ref.shape[0]
     rounds = len(msgs)
@@ -311,11 +311,12 @@
         msg[pl.ds(0, height), :] = encode(values, scale)
         put_scale(msg, height, 0, scale)
 
-    stays = (chip <= ids[0]) & (lax.div(chip, rounds // 2) == core)
+    each = rounds // sides
+    stays = (chip <= ids[0]) & (lax.div(chip, sides) == core)
 
     @pl.when(stays)
     def _():
-        place = 2 * lax.rem(chip, rounds // 2) + core
+        place = each * lax.rem(chip, sides) + (core if each > 1 else 0)
         own_ref[...] = total[pl.ds(pl.multiple_of(place * height, height), height), :]
 
     @pl.when(jnp.logical_not(stays))
@@ -323,7 +324,7 @@
         own_ref[...] = jnp.zeros_like(own_ref)
 
 
-def pack(ids, mine, theirs, partial, message, rounds, after):
+def pack(ids, mine, theirs, partial, message, rounds, sides, after):
     rows, width = mine.shape
     height = rows // rounds
     out_shape = [
@@ -331,28 +332,45 @@
         *[jax.ShapeDtypeStruct((height + TAIL, width), jnp.bfloat16)] * rounds,
     ]
     return local(
-        functools.partial(pack_kernel, len(theirs)), out_shape, "pack", ids, mine, *theirs, partial, message, after=after,
+        functools.partial(pack_kernel, len(theirs), sides), out_shape, "pack", ids, mine, *theirs, partial, message, after=after,
         scratch_shapes=[pltpu.VMEM((rows, width), jnp.float32)],
     )
 
 
-def finish_kernel(ids, before, own, *refs):
+def add_kernel(ids, own, *refs):
+    *messages, keep_ref, give_ref, give_too = refs
+    height, half_way = keep_ref.shape[0], give_ref.shape[0]
+    for core, first, out_ref in ((ids[2], 0, keep_ref), (1 - ids[2], 0, give_ref), (1 - ids[2], half_way, give_too)):
+        at = pl.ds(pl.multiple_of(core * height + first, half_way), out_ref.shape[0])
+        total = own[at, :]
+        for message in messages:
+            total += decode(message[at, :], scale_of(message, own.shape[0], 0))
+        out_ref[...] = total
+
+
+def add(ids, arrays, after):
+    rows, width = arrays[0].shape
+    out_shape = [jax.ShapeDtypeStruct((rows // parts, width), jnp.float32) for parts in (2, 4, 4)]
+    return local(add_kernel, out_shape, "add", ids, *arrays, after=after)
+
+
+def finish_kernel(ids, mine, other, other_too, own, *refs):
     *messages, out_ref = refs
     height, width = own.shape
+    half_way = other.shape[0]
+    for first, ref in ((0, other), (half_way, other_too)):
+        at = pl.ds(first, half_way)
+        out_ref[at, pl.ds(0, width)] = mine[at, :] + ref[...]
     total = own[...]
     for message in messages:
         total += decode(message[pl.ds(0, height), :], scale_of(message, height, 0))
-    done = out_ref.shape[1] - width
-    if done:
-        out_ref[:, pl.ds(0, done)] = before[:, pl.ds(0, done)]
-    out_ref[:, pl.ds(done, width)] = total
-
-
-def finish(ids, before, arrays, after):
-    height, width = arrays[0].shape
-    done = 0 if before is None else before.shape[1]
-    out_shape = jax.ShapeDtypeStruct((height, done + width), jnp.float32)
-    return local(finish_kernel, out_shape, "finish", ids, arrays[0] if before is None else before, *arrays, after=after)
+    out_ref[:, pl.ds(width, width)] = total
+
+
+def finish(ids, mine, others, arrays):
+    height, width = mine.shape
+    out_shape = jax.ShapeDtypeStruct((height, 2 * width), jnp.float32)
+    return local(finish_kernel, out_shape, "finish", ids, mine, *others, *arrays)
 
 
 def shards(trailing, panel_vectors):
@@ -455,17 +473,21 @@
             came = collect(bit, message)
         return partial, came, message
 
-    def deliver(keep, got, partial, came, after):
-        own, *out = pack(ids, keep, got, partial, came, chips, after)
+    def deliver(keep, got, partial, came, rounds, after):
+        sides = chips // 2
+        own, *out = pack(ids, keep, got, partial, came, rounds, sides, after)
         arrays = [own]
         for step, x in enumerate(out):
             pairs = []
             for r, k, c in active:
-                at = c * chips + (k + step) % chips
-                if (at // 2, at % 2) != (k, c):
-                    pairs.append(((r, k, c), (r, at // 2, at % 2)))
+                at = (k + step) % rounds
+                to = (c * sides + at // 2, at % 2) if rounds > sides else (c * sides + at, k // sides)
+                if to != (k, c):
+                    pairs.append(((r, k, c), (r, *to)))
             arrays.append(send(x, pairs))
         return arrays
+
+    all_swap = [((r, k, c), (r, k, 1 - c)) for r, k, c in line_of]
 
     if chips == 4:
         two = two_away(panel_vectors)
@@ -489,14 +511,13 @@
     keep_a, *give_a = direct_product(ids, matrix, panels_a, [relayed])
     got_a = [send(x, swap) for x in give_a]
     partial_b, to_b, relayed = relaying(partial_b, to_b, [], [keep_a, to_a, panels_b[2]])
-    arrays_a = deliver(keep_a, got_a, partial_a, to_a, [relayed, *panels_b[3:]])
+    arrays_a = deliver(keep_a, got_a, partial_a, to_a, chips // 2, [relayed, *panels_b[3:]])
     *give_b, panel_b = give_product(ids, matrix, panels_b, [arrays_a[0]])
     got_b = [send(x, swap) for x in give_b]
     keep_b = keep_product(ids, matrix, panel_b, [to_b])
-    keep_b, arrays_a[1] = lax.optimization_barrier((keep_b, arrays_a[1]))
-    arrays_b = deliver(keep_b, got_b, partial_b, to_b, [])
-    result = finish(ids, None, arrays_a, [arrays_b[0]])
-    return finish(ids, result, arrays_b, [])
+    arrays_b = deliver(keep_b, got_b, partial_b, to_b, chips, [])
+    mine_sum, *gives = add(ids, arrays_a, [arrays_b[1]])
+    return finish(ids, mine_sum, [send(x, all_swap) for x in gives], arrays_b)
 
 
 def solution(mesh):

time: 171 us -> 171 us (level)
  starting transfers between devices: 62.9 us -> 55.4 us
  waiting for transfers between devices: 52.3 us -> 59 us
    ppermute x28, starting transfers between devices: 62.9 us -> 55.4 us  [send(): return lax.ppermute(x, ('row', 'col'), [(at(*s), at(*d)) for s, d in pairs])]
    ppermute x28, waiting for transfers between devices: 52.3 us -> 59 us  [send(): return lax.ppermute(x, ('row', 'col'), [(at(*s), at(*d)) for s, d in pairs])]
  transfers between devices with their start and end apart: 28 -> 28, of which waited for: 8 -> 9; matrix products, arithmetic and copies ran while one was open for 0% -> 0% of each run, Pallas kernels for 27% -> 27%
where the time goes in v12:
time: 171 us; the launch traced here: 170 us
  waiting for transfers between devices  59 us (35%)
  starting transfers between devices  55.4 us (32%)
  Pallas kernels  49.2 us (29%)
  local copies, waits for them, and re-layouts  5.86 us (3%)
    ppermute x28, waiting for transfers between devices, send(): return lax.ppermute(x, ('row', 'col'), [(at(*s), at(*d)) for s, d in pairs])  59 us
    ppermute x28, starting transfers between devices, send(): return lax.ppermute(x, ('row', 'col'), [(at(*s), at(*d)) for s, d in pairs])  55.4 us
    pallas_call x14, Pallas kernels, local(): pl.pallas_call(body, out_shape=out_shape, in_specs=[pl.BlockSpec(memory_s...  47.5 us
    unnamed x4, local copies, waits for them, and re-layouts  5.77 us
  transfers between devices with their start and end apart: 28, of which 9 were waited for; matrix products, arithmetic and copies ran while one was open for 0% of the time, Pallas kernels for 27%

profile of v12, /device:TPU:7, one launch (start us, length us, event | category | flops | bytes accessed | tf_op | source)
XLA Modules:
  0.0 170.0 jit_solution(2729674084873274765)
XLA Ops:
  0.0 4.2 %collective-permute-start = (bf16[512,512]{1,0:T(8,128)(2,1)}, bf16[512,512]{1,0:T(8,128)(2,1)S(1)}, u32[]{:S(2)}, u32[]{:S(2)}) collective-permute-start(bf16[512,512]{1,0:T(8,128)(2,1)} %refs_1_.1), channel_id=1, source_target_pairs={{4,0},{5,1},{6,2},{7,3},{12,8},{13,9},{14,10},{15,11},{16,20},{17,... | collective-permute-start | bytes 1572872 | tf_op jit(solution)/shard_map/ppermute | solution.py:395
  4.2 3.2 %collective-permute-start.1 = (bf16[512,512]{1,0:T(8,128)(2,1)}, bf16[512,512]{1,0:T(8,128)(2,1)S(1)}, u32[]{:S(2)}, u32[]{:S(2)}) collective-permute-start(bf16[512,512]{1,0:T(8,128)(2,1)} %refs_1_.1), channel_id=1, source_target_pairs={{8,10},{9,11},{16,18},{17,19},{18,20},{19,21},{24,26},{25,27},{26,... | collective-permute-start | bytes 1572872 | tf_op jit(solution)/shard_map/ppermute | solution.py:395
  8.9 5.8 %copy-done = bf16[4096,2048]{1,0:T(8,128)(2,1)S(1)} copy-done((bf16[4096,2048]{1,0:T(8,128)(2,1)S(1)}, bf16[4096,2048]{1,0:T(8,128)(2,1)}, u32[]{:S(2)}) %copy-start) | copy-done | bytes 16777240
  16.4 10.7 %collective-permute-done.refs_2_ = bf16[512,512]{1,0:T(8,128)(2,1)S(1)} collective-permute-done((bf16[512,512]{1,0:T(8,128)(2,1)}, bf16[512,512]{1,0:T(8,128)(2,1)S(1)}, u32[]{:S(2)}, u32[]{:S(2)}) %collective-permute-start) | collective-permute-done | bytes 524320 | tf_op jit(solution)/shard_map/ppermute | solution.py:395
  28.4 3.5 %collective-permute-done.2.refs_4_ = bf16[512,512]{1,0:T(8,128)(2,1)S(1)} collective-permute-done((bf16[512,512]{1,0:T(8,128)(2,1)}, bf16[512,512]{1,0:T(8,128)(2,1)S(1)}, u32[]{:S(2)}, u32[]{:S(2)}) %collective-permute-start.2) | collective-permute-done | bytes 524320 | tf_op jit(solution)/shard_map/ppermute | solution.py:395
  31.9 11.2 %collective-permute-done.3.refs_5_ = bf16[512,512]{1,0:T(8,128)(2,1)S(1)} collective-permute-done((bf16[512,512]{1,0:T(8,128)(2,1)S(1)}, bf16[512,512]{1,0:T(8,128)(2,1)S(1)}, u32[]{:S(2)}, u32[]{:S(2)}) %collective-permute-start.3) | collective-permute-done | bytes 524320 | tf_op jit(solution)/shard_map/ppermute | solution.py:395
  43.8 4.1 %collective-permute-start.4 = (bf16[2048,256]{1,0:T(8,128)(2,1)S(1)}, bf16[2048,256]{1,0:T(8,128)(2,1)S(1)}, u32[]{:S(2)}, u32[]{:S(2)}) collective-permute-start(bf16[2048,256]{1,0:T(8,128)(2,1)S(1)} %get-tuple-element.43.refs_1_.refs_3_), channel_id=1, source_target_pairs={{0,1},{1,0},{8,9},{9,8},{10,11},{11,10},{16,17},{17,16},{18,19},{1... | collective-permute-start | bytes 3145736 | tf_op jit(solution)/shard_map/ppermute | solution.py:395
  47.9 1.9 %collective-permute-start.6 = (bf16[2048,256]{1,0:T(8,128)(2,1)S(1)}, bf16[2048,256]{1,0:T(8,128)(2,1)S(1)}, u32[]{:S(2)}, u32[]{:S(2)}) collective-permute-start(bf16[2048,256]{1,0:T(8,128)(2,1)S(1)} %get-tuple-element.45.refs_3_.refs_1_), channel_id=1, source_target_pairs={{0,1},{1,0},{8,9},{9,8},{10,11},{11,10},{16,17},{17,16},{18,19},{1... | collective-permute-start | bytes 3145736 | tf_op jit(solution)/shard_map/ppermute | solution.py:395
  51.5 8.8 %mirrored_product.2 = (f32[2048,256]{1,0:T(8,128)S(1)}, bf16[2112,256]{1,0:T(8,128)(2,1)S(1)}) custom-call(s32[5]{0:T(128)S(1)} %stack.23.ids.refs_0_, bf16[4096,2048]{1,0:T(8,128)(2,1)S(1)} %get-tuple-element.41.refs_1_, f32[8,2048]{1,0:T(8,128)S(1)} %get-tuple-element.44.refs_2_, bf16[2048,256]{1,0:T(8,128)(2,1)S(1)} %get-tuple-element.43.refs_1_.refs_3_, ...), custom_call_target="tpu_custom_call" | custom-call | tf_op jit(solution)/shard_map/mirrored_product/pallas_call | solution.py:48
  63.1 8.8 %mirrored_product.3 = (f32[2048,256]{1,0:T(8,128)S(1)}, bf16[2112,256]{1,0:T(8,128)(2,1)S(1)}) custom-call(s32[5]{0:T(128)S(1)} %stack.23.ids.refs_0_, bf16[4096,2048]{1,0:T(8,128)(2,1)S(1)} %get-tuple-element.41.refs_1_, f32[8,2048]{1,0:T(8,128)S(1)} %get-tuple-element.44.refs_2_, bf16[2048,256]{1,0:T(8,128)(2,1)S(1)} %get-tuple-element.45.refs_3_.refs_1_, ...), custom_call_target="tpu_custom_call" | custom-call | tf_op jit(solution)/shard_map/mirrored_product/pallas_call | solution.py:48
  75.4 2.9 %relay.2 = (f32[2048,256]{1,0:T(8,128)S(1)}, bf16[2112,256]{1,0:T(8,128)(2,1)S(1)}) custom-call(s32[5]{0:T(128)S(1)} %stack.23.ids.refs_0_, f32[2048,256]{1,0:T(8,128)S(1)} %get-tuple-element.50.refs_1_, bf16[2112,256]{1,0:T(8,128)(2,1)S(1)} %collective-permute-done.9.refs_2_, bf16[2112,256]{1,0:T(8,128)(2,1)S(1)} %get-tuple-element.47.refs_3_, ...), custom_call_target="tpu_custom_call" | custom-call | tf_op jit(solution)/shard_map/relay/pallas_call | solution.py:48
  81.1 8.8 %collective-permute-done.8.refs_5_ = bf16[2048,256]{1,0:T(8,128)(2,1)S(1)} collective-permute-done((bf16[2048,256]{1,0:T(8,128)(2,1)S(1)}, bf16[2048,256]{1,0:T(8,128)(2,1)S(1)}, u32[]{:S(2)}, u32[]{:S(2)}) %collective-permute-start.8) | collective-permute-done | bytes 1048608 | tf_op jit(solution)/shard_map/ppermute | solution.py:395
  89.9 6.4 %direct_product.1 = (f32[2048,256]{1,0:T(8,128)S(1)}, f32[1024,256]{1,0:T(8,128)S(1)}, f32[1024,256]{1,0:T(8,128)S(1)}) custom-call(s32[5]{0:T(128)S(1)} %stack.23.ids.refs_0_, bf16[4096,2048]{1,0:T(8,128)(2,1)S(1)} %get-tuple-element.41.refs_1_, bf16[2048,256]{1,0:T(8,128)(2,1)S(1)} %half.2.refs_2_, bf16[2048,256]{1,0:T(8,128)(2,1)S(1)} %collective-permute-done.5.refs_3_, ...), custom_call_target="tpu_custom_call" | custom-call | tf_op jit(solution)/shard_map/direct_product/pallas_call | solution.py:48
  96.3 3.3 %collective-permute-start.11 = (f32[1024,256]{1,0:T(8,128)S(1)}, f32[1024,256]{1,0:T(8,128)S(1)}, u32[]{:S(2)}, u32[]{:S(2)}) collective-permute-start(f32[1024,256]{1,0:T(8,128)S(1)} %get-tuple-element.54), channel_id=1, source_target_pairs={{0,1},{1,0},{8,9},{9,8},{10,11},{11,10},{16,17},{17,16},{18,19},{1... | collective-permute-start | bytes 3145736 | tf_op jit(solution)/shard_map/ppermute | solution.py:395
  99.6 1.9 %collective-permute-start.12 = (f32[1024,256]{1,0:T(8,128)S(1)}, f32[1024,256]{1,0:T(8,128)S(1)}, u32[]{:S(2)}, u32[]{:S(2)}) collective-permute-start(f32[1024,256]{1,0:T(8,128)S(1)} %get-tuple-element.55), channel_id=1, source_target_pairs={{0,1},{1,0},{8,9},{9,8},{10,11},{11,10},{16,17},{17,16},{18,19},{1... | collective-permute-start | bytes 3145736 | tf_op jit(solution)/shard_map/ppermute | solution.py:395
  101.6 2.9 %relay.3 = (f32[2048,256]{1,0:T(8,128)S(1)}, bf16[2112,256]{1,0:T(8,128)(2,1)S(1)}) custom-call(s32[5]{0:T(128)S(1)} %stack.23.ids.refs_0_, f32[2048,256]{1,0:T(8,128)S(1)} %get-tuple-element.57.refs_1_, bf16[2112,256]{1,0:T(8,128)(2,1)S(1)} %collective-permute-done.14.refs_2_, f32[2048,256]{1,0:T(8,128)S(1)} %get-tuple-element.53.refs_3_.refs_1_, ...), custom_call_target="tpu_custom_call" | custom-call | tf_op jit(solution)/shard_map/relay/pallas_call | solution.py:48
  105.3 2.4 %pack.2 = (f32[1024,256]{1,0:T(8,128)S(1)}, bf16[1040,256]{1,0:T(8,128)(2,1)S(1)}, bf16[1040,256]{1,0:T(8,128)(2,1)S(1)}) custom-call(s32[5]{0:T(128)S(1)} %stack.23.ids.refs_0_, f32[2048,256]{1,0:T(8,128)S(1)} %get-tuple-element.53.refs_3_.refs_1_, f32[1024,256]{1,0:T(8,128)S(1)} %collective-permute-done.11.refs_2_, ...), custom_call_target="tpu_custom_call" | custom-call | tf_op jit(solution)/shard_map/pack/pallas_call | solution.py:48
  107.8 3.5 %give_product.1 = (f32[1024,256]{1,0:T(8,128)S(1)}, f32[1024,256]{1,0:T(8,128)S(1)}, bf16[2048,256]{1,0:T(8,128)(2,1)S(1)}) custom-call(s32[5]{0:T(128)S(1)} %stack.23.ids.refs_0_, bf16[4096,2048]{1,0:T(8,128)(2,1)S(1)} %get-tuple-element.41.refs_1_, bf16[2048,256]{1,0:T(8,128)(2,1)S(1)} %half.3.refs_2_, ...), custom_call_target="tpu_custom_call" | custom-call | tf_op jit(solution)/shard_map/give_product/pallas_call | solution.py:48
  111.3 2.4 %collective-permute-start.20 = (f32[1024,256]{1,0:T(8,128)S(1)}, f32[1024,256]{1,0:T(8,128)S(1)}, u32[]{:S(2)}, u32[]{:S(2)}) collective-permute-start(f32[1024,256]{1,0:T(8,128)S(1)} %get-tuple-element.64), channel_id=1, source_target_pairs={{0,1},{1,0},{8,9},{9,8},{10,11},{11,10},{16,17},{17,16},{18,19},{1... | collective-permute-start | bytes 3145736 | tf_op jit(solution)/shard_map/ppermute | solution.py:395
  113.7 1.9 %collective-permute-start.21 = (f32[1024,256]{1,0:T(8,128)S(1)}, f32[1024,256]{1,0:T(8,128)S(1)}, u32[]{:S(2)}, u32[]{:S(2)}) collective-permute-start(f32[1024,256]{1,0:T(8,128)S(1)} %get-tuple-element.65), channel_id=1, source_target_pairs={{0,1},{1,0},{8,9},{9,8},{10,11},{11,10},{16,17},{17,16},{18,19},{1... | collective-permute-start | bytes 3145736 | tf_op jit(solution)/shard_map/ppermute | solution.py:395
  115.6 4.0 %collective-permute-start.17 = (bf16[1040,256]{1,0:T(8,128)(2,1)S(1)}, bf16[1040,256]{1,0:T(8,128)(2,1)S(1)}, u32[]{:S(2)}, u32[]{:S(2)}) collective-permute-start(bf16[1040,256]{1,0:T(8,128)(2,1)S(1)} %get-tuple-element.61), channel_id=1, source_target_pairs={{1,4},{9,12},{11,14},{17,20},{19,22},{20,17},{25,28},{27,30},{28,2... | collective-permute-start | bytes 1597448 | tf_op jit(solution)/shard_map/ppermute | solution.py:395
  119.6 3.9 %collective-permute-start.18 = (bf16[1040,256]{1,0:T(8,128)(2,1)S(1)}, bf16[1040,256]{1,0:T(8,128)(2,1)S(1)}, u32[]{:S(2)}, u32[]{:S(2)}) collective-permute-start(bf16[1040,256]{1,0:T(8,128)(2,1)S(1)} %get-tuple-element.62), channel_id=1, source_target_pairs={{0,2},{1,6},{8,10},{9,14},{10,8},{11,12},{16,18},{17,22},{18,16},{... | collective-permute-start | bytes 1597448 | tf_op jit(solution)/shard_map/ppermute | solution.py:395
  123.5 3.4 %keep_product.1.refs_1_ = f32[2048,256]{1,0:T(8,128)S(1)} custom-call(s32[5]{0:T(128)S(1)} %stack.23.ids.refs_0_, bf16[4096,2048]{1,0:T(8,128)(2,1)S(1)} %get-tuple-element.41.refs_1_, bf16[2048,256]{1,0:T(8,128)(2,1)S(1)} %get-tuple-element.63.refs_2_, bf16[2112,256]{1,0:T(8,128)(2,1)S(1)} %collective-permute-done.19.refs_3_.refs_5_), custom_call_target="tpu_custom_call" | custom-call | tf_op jit(solution)/shard_map/keep_product/pallas_call | solution.py:48
  126.9 2.1 %pack.3 = (f32[512,256]{1,0:T(8,128)S(1)}, bf16[528,256]{1,0:T(8,128)(2,1)S(1)}, bf16[528,256]{1,0:T(8,128)(2,1)S(1)}, bf16[528,256]{1,0:T(8,128)(2,1)S(1)}, bf16[528,256]{1,0:T(8,128)(2,1)S(1)}) custom-call(s32[5]{0:T(128)S(1)} %stack.23.ids.refs_0_, f32[2048,256]{1,0:T(8,128)S(1)} %keep_product.1.refs_1_, f32[1024,256]{1,0:T(8,128)S(1)} %collective-permute-done.20.refs_2_, ...), custom_call_target="tpu_custom_call" | custom-call | tf_op jit(solution)/shard_map/pack/pallas_call | solution.py:48
  131.0 4.8 %collective-permute-start.25 = (bf16[528,256]{1,0:T(8,128)(2,1)S(1)}, bf16[528,256]{1,0:T(8,128)(2,1)S(1)}, u32[]{:S(2)}, u32[]{:S(2)}) collective-permute-start(bf16[528,256]{1,0:T(8,128)(2,1)S(1)} %get-tuple-element.72), channel_id=1, source_target_pairs={{0,1},{1,5},{8,9},{9,13},{11,14},{16,17},{17,21},{19,22},{20,19},{... | collective-permute-start | bytes 811016 | tf_op jit(solution)/shard_map/ppermute | solution.py:395
  135.8 1.9 %collective-permute-start.26 = (bf16[528,256]{1,0:T(8,128)(2,1)S(1)}, bf16[528,256]{1,0:T(8,128)(2,1)S(1)}, u32[]{:S(2)}, u32[]{:S(2)}) collective-permute-start(bf16[528,256]{1,0:T(8,128)(2,1)S(1)} %get-tuple-element.73), channel_id=1, source_target_pairs={{0,2},{1,6},{8,10},{9,14},{10,11},{11,15},{16,18},{17,22},{18,19},... | collective-permute-start | bytes 811016 | tf_op jit(solution)/shard_map/ppermute | solution.py:395
  137.7 3.1 %collective-permute-start.27 = (bf16[528,256]{1,0:T(8,128)(2,1)S(1)}, bf16[528,256]{1,0:T(8,128)(2,1)S(1)}, u32[]{:S(2)}, u32[]{:S(2)}) collective-permute-start(bf16[528,256]{1,0:T(8,128)(2,1)S(1)} %get-tuple-element.74), channel_id=1, source_target_pairs={{0,3},{1,7},{8,11},{9,15},{10,8},{11,12},{16,19},{17,23},{18,16},{... | collective-permute-start | bytes 811016 | tf_op jit(solution)/shard_map/ppermute | solution.py:395
  140.8 3.3 %collective-permute-done.18.refs_3_ = bf16[1040,256]{1,0:T(8,128)(2,1)S(1)} collective-permute-done((bf16[1040,256]{1,0:T(8,128)(2,1)S(1)}, bf16[1040,256]{1,0:T(8,128)(2,1)S(1)}, u32[]{:S(2)}, u32[]{:S(2)}) %collective-permute-start.18) | collective-permute-done | bytes 532512 | tf_op jit(solution)/shard_map/ppermute | solution.py:395
  146.2 2.6 %collective-permute-done.25.refs_6_ = bf16[528,256]{1,0:T(8,128)(2,1)S(1)} collective-permute-done((bf16[528,256]{1,0:T(8,128)(2,1)S(1)}, bf16[528,256]{1,0:T(8,128)(2,1)S(1)}, u32[]{:S(2)}, u32[]{:S(2)}) %collective-permute-start.25) | collective-permute-done | bytes 270368 | tf_op jit(solution)/shard_map/ppermute | solution.py:395
  148.8 4.9 %collective-permute-done.26.refs_7_ = bf16[528,256]{1,0:T(8,128)(2,1)S(1)} collective-permute-done((bf16[528,256]{1,0:T(8,128)(2,1)S(1)}, bf16[528,256]{1,0:T(8,128)(2,1)S(1)}, u32[]{:S(2)}, u32[]{:S(2)}) %collective-permute-start.26) | collective-permute-done | bytes 270368 | tf_op jit(solution)/shard_map/ppermute | solution.py:395
  153.7 13.7 %collective-permute-done.27.refs_8_ = bf16[528,256]{1,0:T(8,128)(2,1)S(1)} collective-permute-done((bf16[528,256]{1,0:T(8,128)(2,1)S(1)}, bf16[528,256]{1,0:T(8,128)(2,1)S(1)}, u32[]{:S(2)}, u32[]{:S(2)}) %collective-permute-start.27) | collective-permute-done | bytes 270368 | tf_op jit(solution)/shard_map/ppermute | solution.py:395
  167.4 2.6 %finish.1 = f32[512,512]{1,0:T(8,128)} custom-call(s32[5]{0:T(128)S(1)} %stack.23.ids.refs_0_, f32[512,256]{1,0:T(8,128)S(1)} %get-tuple-element.68.refs_1_, f32[256,256]{1,0:T(8,128)S(1)} %collective-permute-done.23.refs_2_, f32[256,256]{1,0:T(8,128)S(1)} %collective-permute-done.24.refs_3_, f32[512,256]{1,0:T(8,128)S(1)} %get-tuple-element.71.refs_4_, ...), custom_call_target="tpu_custom_call" | custom-call | tf_op jit(solution)/shard_map/finish/pallas_call | solution.py:48
  (44 shorter events, 20.4 us)
Async XLA Ops:
  0.0 27.1 %collective-permute-start = (bf16[512,512]{1,0:T(8,128)(2,1)}, bf16[512,512]{1,0:T(8,128)(2,1)S(1)}, u32[]{:S(2)}, u32[]{:S(2)}) collective-permute-start(bf16[512,512]{1,0:T(8,128)(2,1)} %refs_1_.1), channel_id=1, source_target_pairs={{4,0},{5,1},{6,2},{7,3},{12,8},{13,9},{14,10},{15,11},{16,20},{17,... | collective-permute-start | bytes 1572872 | tf_op jit(solution)/shard_map/ppermute | solution.py:395
  4.2 24.2 %collective-permute-start.1 = (bf16[512,512]{1,0:T(8,128)(2,1)}, bf16[512,512]{1,0:T(8,128)(2,1)S(1)}, u32[]{:S(2)}, u32[]{:S(2)}) collective-permute-start(bf16[512,512]{1,0:T(8,128)(2,1)} %refs_1_.1), channel_id=1, source_target_pairs={{8,10},{9,11},{16,18},{17,19},{18,20},{19,21},{24,26},{25,27},{26,... | collective-permute-start | bytes 1572872 | tf_op jit(solution)/shard_map/ppermute | solution.py:395
  7.5 24.4 %collective-permute-start.2 = (bf16[512,512]{1,0:T(8,128)(2,1)}, bf16[512,512]{1,0:T(8,128)(2,1)S(1)}, u32[]{:S(2)}, u32[]{:S(2)}) collective-permute-start(bf16[512,512]{1,0:T(8,128)(2,1)} %refs_1_.1), channel_id=1, source_target_pairs={{2,0},{3,1},{10,8},{11,9},{12,10},{13,11},{18,16},{19,17},{20,18},... | collective-permute-start | bytes 1572872 | tf_op jit(solution)/shard_map/ppermute | solution.py:395
  8.9 5.8 %copy-start = (bf16[4096,2048]{1,0:T(8,128)(2,1)S(1)}, bf16[4096,2048]{1,0:T(8,128)(2,1)}, u32[]{:S(2)}) copy-start(bf16[4096,2048]{1,0:T(8,128)(2,1)} %a_ref.1) | copy-start | bytes 50331652
  14.6 28.5 %copy-start.1 = (bf16[512,512]{1,0:T(8,128)(2,1)S(1)}, bf16[512,512]{1,0:T(8,128)(2,1)}, u32[]{:S(2)}) copy-start(bf16[512,512]{1,0:T(8,128)(2,1)} %refs_1_.1) | copy-start | bytes 1572868
  27.1 16.0 %collective-permute-start.3 = (bf16[512,512]{1,0:T(8,128)(2,1)S(1)}, bf16[512,512]{1,0:T(8,128)(2,1)S(1)}, u32[]{:S(2)}, u32[]{:S(2)}) collective-permute-start(bf16[512,512]{1,0:T(8,128)(2,1)S(1)} %collective-permute-done.refs_2_), channel_id=1, source_target_pairs={{2,0},{3,1},{10,8},{11,9},{18,16},{19,17},{26,24},{27,25},{28,30},... | collective-permute-start | bytes 1572872 | tf_op jit(solution)/shard_map/ppermute | solution.py:395
  43.8 6.3 %collective-permute-start.4 = (bf16[2048,256]{1,0:T(8,128)(2,1)S(1)}, bf16[2048,256]{1,0:T(8,128)(2,1)S(1)}, u32[]{:S(2)}, u32[]{:S(2)}) collective-permute-start(bf16[2048,256]{1,0:T(8,128)(2,1)S(1)} %get-tuple-element.43.refs_1_.refs_3_), channel_id=1, source_target_pairs={{0,1},{1,0},{8,9},{9,8},{10,11},{11,10},{16,17},{17,16},{18,19},{1... | collective-permute-start | bytes 3145736 | tf_op jit(solution)/shard_map/ppermute | solution.py:395
  47.9 13.8 %collective-permute-start.6 = (bf16[2048,256]{1,0:T(8,128)(2,1)S(1)}, bf16[2048,256]{1,0:T(8,128)(2,1)S(1)}, u32[]{:S(2)}, u32[]{:S(2)}) collective-permute-start(bf16[2048,256]{1,0:T(8,128)(2,1)S(1)} %get-tuple-element.45.refs_3_.refs_1_), channel_id=1, source_target_pairs={{0,1},{1,0},{8,9},{9,8},{10,11},{11,10},{16,17},{17,16},{18,19},{1... | collective-permute-start | bytes 3145736 | tf_op jit(solution)/shard_map/ppermute | solution.py:395
  50.8 22.5 %collective-permute-start.5 = (bf16[2048,256]{1,0:T(8,128)(2,1)S(1)}, bf16[2048,256]{1,0:T(8,128)(2,1)S(1)}, u32[]{:S(2)}, u32[]{:S(2)}) collective-permute-start(bf16[2048,256]{1,0:T(8,128)(2,1)S(1)} %half.2.refs_2_), channel_id=1, source_target_pairs={{0,8},{1,17},{10,2},{11,27},{20,28}} | collective-permute-start | bytes 3145736 | tf_op jit(solution)/shard_map/ppermute | solution.py:395
  60.4 15.0 %collective-permute-start.9 = (bf16[2112,256]{1,0:T(8,128)(2,1)S(1)}, bf16[2112,256]{1,0:T(8,128)(2,1)S(1)}, u32[]{:S(2)}, u32[]{:S(2)}) collective-permute-start(bf16[2112,256]{1,0:T(8,128)(2,1)S(1)} %get-tuple-element.46.refs_5_), channel_id=1, source_target_pairs={{16,0},{24,8},{9,1},{25,17},{26,10},{18,2},{19,27},{29,21}} | collective-permute-start | bytes 3244040 | tf_op jit(solution)/shard_map/ppermute | solution.py:395
  62.4 13.0 %collective-permute-start.10 = (bf16[2048,256]{1,0:T(8,128)(2,1)S(1)}, bf16[2048,256]{1,0:T(8,128)(2,1)S(1)}, u32[]{:S(2)}, u32[]{:S(2)}) collective-permute-start(bf16[2048,256]{1,0:T(8,128)(2,1)S(1)} %half.3.refs_2_), channel_id=1, source_target_pairs={{0,8},{1,17},{10,2},{11,27},{20,28}} | collective-permute-start | bytes 3145736 | tf_op jit(solution)/shard_map/ppermute | solution.py:395
  71.9 27.7 %collective-permute-start.14 = (bf16[2112,256]{1,0:T(8,128)(2,1)S(1)}, bf16[2112,256]{1,0:T(8,128)(2,1)S(1)}, u32[]{:S(2)}, u32[]{:S(2)}) collective-permute-start(bf16[2112,256]{1,0:T(8,128)(2,1)S(1)} %get-tuple-element.47.refs_3_), channel_id=1, source_target_pairs={{16,0},{24,8},{9,1},{25,17},{26,10},{18,2},{19,27},{29,21}} | collective-permute-start | bytes 3244040 | tf_op jit(solution)/shard_map/ppermute | solution.py:395
  73.3 6.5 %collective-permute-start.7 = (bf16[2048,256]{1,0:T(8,128)(2,1)S(1)}, bf16[2048,256]{1,0:T(8,128)(2,1)S(1)}, u32[]{:S(2)}, u32[]{:S(2)}) collective-permute-start(bf16[2048,256]{1,0:T(8,128)(2,1)S(1)} %half.2.refs_2_), channel_id=1, source_target_pairs={{0,16},{1,9},{10,26},{21,29}} | collective-permute-start | bytes 3145736 | tf_op jit(solution)/shard_map/ppermute | solution.py:395
  74.1 15.8 %collective-permute-start.8 = (bf16[2048,256]{1,0:T(8,128)(2,1)S(1)}, bf16[2048,256]{1,0:T(8,128)(2,1)S(1)}, u32[]{:S(2)}, u32[]{:S(2)}) collective-permute-start(bf16[2048,256]{1,0:T(8,128)(2,1)S(1)} %collective-permute-done.5.refs_3_), channel_id=1, source_target_pairs={{8,24},{17,25},{2,18},{27,19}} | collective-permute-start | bytes 3145736 | tf_op jit(solution)/shard_map/ppermute | solution.py:395
  78.3 23.3 %collective-permute-start.13 = (bf16[2112,256]{1,0:T(8,128)(2,1)S(1)}, bf16[2112,256]{1,0:T(8,128)(2,1)S(1)}, u32[]{:S(2)}, u32[]{:S(2)}) collective-permute-start(bf16[2112,256]{1,0:T(8,128)(2,1)S(1)} %get-tuple-element.52.refs_6_), channel_id=1, source_target_pairs={{8,0},{17,1},{2,10},{27,11},{28,20}} | collective-permute-start | bytes 3244040 | tf_op jit(solution)/shard_map/ppermute | solution.py:395
  79.1 22.5 %collective-permute-start.15 = (bf16[2048,256]{1,0:T(8,128)(2,1)S(1)}, bf16[2048,256]{1,0:T(8,128)(2,1)S(1)}, u32[]{:S(2)}, u32[]{:S(2)}) collective-permute-start(bf16[2048,256]{1,0:T(8,128)(2,1)S(1)} %half.3.refs_2_), channel_id=1, source_target_pairs={{0,16},{1,9},{10,26},{21,29}} | collective-permute-start | bytes 3145736 | tf_op jit(solution)/shard_map/ppermute | solution.py:395
  79.8 25.5 %collective-permute-start.16 = (bf16[2048,256]{1,0:T(8,128)(2,1)S(1)}, bf16[2048,256]{1,0:T(8,128)(2,1)S(1)}, u32[]{:S(2)}, u32[]{:S(2)}) collective-permute-start(bf16[2048,256]{1,0:T(8,128)(2,1)S(1)} %collective-permute-done.10.refs_4_.refs_3_), channel_id=1, source_target_pairs={{8,24},{17,25},{2,18},{27,19}} | collective-permute-start | bytes 3145736 | tf_op jit(solution)/shard_map/ppermute | solution.py:395
  96.3 9.0 %collective-permute-start.11 = (f32[1024,256]{1,0:T(8,128)S(1)}, f32[1024,256]{1,0:T(8,128)S(1)}, u32[]{:S(2)}, u32[]{:S(2)}) collective-permute-start(f32[1024,256]{1,0:T(8,128)S(1)} %get-tuple-element.54), channel_id=1, source_target_pairs={{0,1},{1,0},{8,9},{9,8},{10,11},{11,10},{16,17},{17,16},{18,19},{1... | collective-permute-start | bytes 3145736 | tf_op jit(solution)/shard_map/ppermute | solution.py:395
  99.6 5.7 %collective-permute-start.12 = (f32[1024,256]{1,0:T(8,128)S(1)}, f32[1024,256]{1,0:T(8,128)S(1)}, u32[]{:S(2)}, u32[]{:S(2)}) collective-permute-start(f32[1024,256]{1,0:T(8,128)S(1)} %get-tuple-element.55), channel_id=1, source_target_pairs={{0,1},{1,0},{8,9},{9,8},{10,11},{11,10},{16,17},{17,16},{18,19},{1... | collective-permute-start | bytes 3145736 | tf_op jit(solution)/shard_map/ppermute | solution.py:395
  104.5 19.0 %collective-permute-start.19 = (bf16[2112,256]{1,0:T(8,128)(2,1)S(1)}, bf16[2112,256]{1,0:T(8,128)(2,1)S(1)}, u32[]{:S(2)}, u32[]{:S(2)}) collective-permute-start(bf16[2112,256]{1,0:T(8,128)(2,1)S(1)} %get-tuple-element.59.refs_6_), channel_id=1, source_target_pairs={{8,0},{17,1},{2,10},{27,11},{28,20}} | collective-permute-start | bytes 3244040 | tf_op jit(solution)/shard_map/ppermute | solution.py:395
  111.3 15.6 %collective-permute-start.20 = (f32[1024,256]{1,0:T(8,128)S(1)}, f32[1024,256]{1,0:T(8,128)S(1)}, u32[]{:S(2)}, u32[]{:S(2)}) collective-permute-start(f32[1024,256]{1,0:T(8,128)S(1)} %get-tuple-element.64), channel_id=1, source_target_pairs={{0,1},{1,0},{8,9},{9,8},{10,11},{11,10},{16,17},{17,16},{18,19},{1... | collective-permute-start | bytes 3145736 | tf_op jit(solution)/shard_map/ppermute | solution.py:395
  113.7 13.2 %collective-permute-start.21 = (f32[1024,256]{1,0:T(8,128)S(1)}, f32[1024,256]{1,0:T(8,128)S(1)}, u32[]{:S(2)}, u32[]{:S(2)}) collective-permute-start(f32[1024,256]{1,0:T(8,128)S(1)} %get-tuple-element.65), channel_id=1, source_target_pairs={{0,1},{1,0},{8,9},{9,8},{10,11},{11,10},{16,17},{17,16},{18,19},{1... | collective-permute-start | bytes 3145736 | tf_op jit(solution)/shard_map/ppermute | solution.py:395
  115.6 22.1 %collective-permute-start.17 = (bf16[1040,256]{1,0:T(8,128)(2,1)S(1)}, bf16[1040,256]{1,0:T(8,128)(2,1)S(1)}, u32[]{:S(2)}, u32[]{:S(2)}) collective-permute-start(bf16[1040,256]{1,0:T(8,128)(2,1)S(1)} %get-tuple-element.61), channel_id=1, source_target_pairs={{1,4},{9,12},{11,14},{17,20},{19,22},{20,17},{25,28},{27,30},{28,2... | collective-permute-start | bytes 1597448 | tf_op jit(solution)/shard_map/ppermute | solution.py:395
  119.6 24.5 %collective-permute-start.18 = (bf16[1040,256]{1,0:T(8,128)(2,1)S(1)}, bf16[1040,256]{1,0:T(8,128)(2,1)S(1)}, u32[]{:S(2)}, u32[]{:S(2)}) collective-permute-start(bf16[1040,256]{1,0:T(8,128)(2,1)S(1)} %get-tuple-element.62), channel_id=1, source_target_pairs={{0,2},{1,6},{8,10},{9,14},{10,8},{11,12},{16,18},{17,22},{18,16},{... | collective-permute-start | bytes 1597448 | tf_op jit(solution)/shard_map/ppermute | solution.py:395
  129.1 15.0 %collective-permute-start.22 = (bf16[528,256]{1,0:T(8,128)(2,1)S(1)}, bf16[528,256]{1,0:T(8,128)(2,1)S(1)}, u32[]{:S(2)}, u32[]{:S(2)}) collective-permute-start(bf16[528,256]{1,0:T(8,128)(2,1)S(1)} %get-tuple-element.67), channel_id=1, source_target_pairs={{1,4},{9,12},{10,9},{11,13},{17,20},{18,17},{19,21},{20,18},{21,22... | collective-permute-start | bytes 811016 | tf_op jit(solution)/shard_map/ppermute | solution.py:395
  131.0 17.8 %collective-permute-start.25 = (bf16[528,256]{1,0:T(8,128)(2,1)S(1)}, bf16[528,256]{1,0:T(8,128)(2,1)S(1)}, u32[]{:S(2)}, u32[]{:S(2)}) collective-permute-start(bf16[528,256]{1,0:T(8,128)(2,1)S(1)} %get-tuple-element.72), channel_id=1, source_target_pairs={{0,1},{1,5},{8,9},{9,13},{11,14},{16,17},{17,21},{19,22},{20,19},{... | collective-permute-start | bytes 811016 | tf_op jit(solution)/shard_map/ppermute | solution.py:395
  135.8 17.9 %collective-permute-start.26 = (bf16[528,256]{1,0:T(8,128)(2,1)S(1)}, bf16[528,256]{1,0:T(8,128)(2,1)S(1)}, u32[]{:S(2)}, u32[]{:S(2)}) collective-permute-start(bf16[528,256]{1,0:T(8,128)(2,1)S(1)} %get-tuple-element.73), channel_id=1, source_target_pairs={{0,2},{1,6},{8,10},{9,14},{10,11},{11,15},{16,18},{17,22},{18,19},... | collective-permute-start | bytes 811016 | tf_op jit(solution)/shard_map/ppermute | solution.py:395
  137.7 29.7 %collective-permute-start.27 = (bf16[528,256]{1,0:T(8,128)(2,1)S(1)}, bf16[528,256]{1,0:T(8,128)(2,1)S(1)}, u32[]{:S(2)}, u32[]{:S(2)}) collective-permute-start(bf16[528,256]{1,0:T(8,128)(2,1)S(1)} %get-tuple-element.74), channel_id=1, source_target_pairs={{0,3},{1,7},{8,11},{9,15},{10,8},{11,12},{16,19},{17,23},{18,16},{... | collective-permute-start | bytes 811016 | tf_op jit(solution)/shard_map/ppermute | solution.py:395
  145.6 21.8 %collective-permute-start.23 = (f32[256,256]{1,0:T(8,128)S(1)}, f32[256,256]{1,0:T(8,128)S(1)}, u32[]{:S(2)}, u32[]{:S(2)}) collective-permute-start(f32[256,256]{1,0:T(8,128)S(1)} %get-tuple-element.69), channel_id=1, source_target_pairs={{0,1},{1,0},{2,3},{3,2},{4,5},{5,4},{6,7},{7,6},{8,9},{9,8},{10,11... | collective-permute-start | bytes 786440 | tf_op jit(solution)/shard_map/ppermute | solution.py:395
  145.7 21.7 %collective-permute-start.24 = (f32[256,256]{1,0:T(8,128)S(1)}, f32[256,256]{1,0:T(8,128)S(1)}, u32[]{:S(2)}, u32[]{:S(2)}) collective-permute-start(f32[256,256]{1,0:T(8,128)S(1)} %get-tuple-element.70), channel_id=1, source_target_pairs={{0,1},{1,0},{2,3},{3,2},{4,5},{5,4},{6,7},{7,6},{8,9},{9,8},{10,11... | collective-permute-start | bytes 786440 | tf_op jit(solution)/shard_map/ppermute | solution.py:395

commit v13 on v12

--- a/solution.py
+++ b/solution.py
@@ -160,18 +160,19 @@
     def _(part):
         here = pl.ds(pl.multiple_of(part * block, block), block)
 
-        @pl.when(used)
+        @pl.when(used & (ids[1] != ids[0]))
         def _():
             m_ref[here, :] = jnp.dot(turned[...], a_ref[:, here], preferred_element_type=jnp.float32).T
+
+        @pl.when(ids[1] == ids[0])
+        def _():
+            rows = pl.ds(pl.multiple_of(part * block - ids[3], block), block)
+            total = jnp.dot(turned[...], a_ref[:, here], preferred_element_type=jnp.float32)
+            m_ref[here, :] = (total - turned[:, rows].astype(jnp.float32) * diagonal[0:1, here]).T
 
         @pl.when(jnp.logical_not(used))
         def _():
             m_ref[here, :] = jnp.zeros((block, m_ref.shape[1]), jnp.float32)
-
-        @pl.when(ids[1] == ids[0])
-        def _():
-            rows = pl.ds(pl.multiple_of(part * block - ids[3], block), block)
-            m_ref[here, :] -= (turned[:, rows].astype(jnp.float32) * diagonal[0:1, here]).T
 
         total = m_ref[here, :]
         scale = scale_for(jnp.max(jnp.abs(total), keepdims=True))

time: 171 us -> 171 us (level)
  transfers between devices with their start and end apart: 28 -> 28, of which waited for: 9 -> 10; matrix products, arithmetic and copies ran while one was open for 0% -> 0% of each run, Pallas kernels for 27% -> 27%
where the time goes in v13:
time: 171 us; the launch traced here: 170 us
  waiting for transfers between devices  59.7 us (35%)
  starting transfers between devices  54.8 us (32%)
  Pallas kernels  49 us (29%)
  local copies, waits for them, and re-layouts  5.86 us (3%)
    ppermute x28, waiting for transfers between devices, send(): return lax.ppermute(x, ('row', 'col'), [(at(*s), at(*d)) for s, d in pairs])  59.7 us
    ppermute x28, starting transfers between devices, send(): return lax.ppermute(x, ('row', 'col'), [(at(*s), at(*d)) for s, d in pairs])  54.8 us
    pallas_call x14, Pallas kernels, local(): pl.pallas_call(body, out_shape=out_shape, in_specs=[pl.BlockSpec(memory_s...  47.3 us
    unnamed x4, local copies, waits for them, and re-layouts  5.77 us
  transfers between devices with their start and end apart: 28, of which 10 were waited for; matrix products, arithmetic and copies ran while one was open for 0% of the time, Pallas kernels for 27%

profile of v13, /device:TPU:7, one launch (start us, length us, event | category | flops | bytes accessed | tf_op | source)
XLA Modules:
  0.0 169.9 jit_solution(18050755506087936374)
XLA Ops:
  0.0 4.2 %collective-permute-start = (bf16[512,512]{1,0:T(8,128)(2,1)}, bf16[512,512]{1,0:T(8,128)(2,1)S(1)}, u32[]{:S(2)}, u32[]{:S(2)}) collective-permute-start(bf16[512,512]{1,0:T(8,128)(2,1)} %refs_1_.1), channel_id=1, source_target_pairs={{4,0},{5,1},{6,2},{7,3},{12,8},{13,9},{14,10},{15,11},{16,20},{17,... | collective-permute-start | bytes 1572872 | tf_op jit(solution)/shard_map/ppermute | solution.py:396
  4.2 3.2 %collective-permute-start.1 = (bf16[512,512]{1,0:T(8,128)(2,1)}, bf16[512,512]{1,0:T(8,128)(2,1)S(1)}, u32[]{:S(2)}, u32[]{:S(2)}) collective-permute-start(bf16[512,512]{1,0:T(8,128)(2,1)} %refs_1_.1), channel_id=1, source_target_pairs={{8,10},{9,11},{16,18},{17,19},{18,20},{19,21},{24,26},{25,27},{26,... | collective-permute-start | bytes 1572872 | tf_op jit(solution)/shard_map/ppermute | solution.py:396
  8.9 5.8 %copy-done = bf16[4096,2048]{1,0:T(8,128)(2,1)S(1)} copy-done((bf16[4096,2048]{1,0:T(8,128)(2,1)S(1)}, bf16[4096,2048]{1,0:T(8,128)(2,1)}, u32[]{:S(2)}) %copy-start) | copy-done | bytes 16777240
  16.4 10.7 %collective-permute-done.refs_2_ = bf16[512,512]{1,0:T(8,128)(2,1)S(1)} collective-permute-done((bf16[512,512]{1,0:T(8,128)(2,1)}, bf16[512,512]{1,0:T(8,128)(2,1)S(1)}, u32[]{:S(2)}, u32[]{:S(2)}) %collective-permute-start) | collective-permute-done | bytes 524320 | tf_op jit(solution)/shard_map/ppermute | solution.py:396
  28.4 3.5 %collective-permute-done.2.refs_4_ = bf16[512,512]{1,0:T(8,128)(2,1)S(1)} collective-permute-done((bf16[512,512]{1,0:T(8,128)(2,1)}, bf16[512,512]{1,0:T(8,128)(2,1)S(1)}, u32[]{:S(2)}, u32[]{:S(2)}) %collective-permute-start.2) | collective-permute-done | bytes 524320 | tf_op jit(solution)/shard_map/ppermute | solution.py:396
  31.9 11.2 %collective-permute-done.3.refs_5_ = bf16[512,512]{1,0:T(8,128)(2,1)S(1)} collective-permute-done((bf16[512,512]{1,0:T(8,128)(2,1)S(1)}, bf16[512,512]{1,0:T(8,128)(2,1)S(1)}, u32[]{:S(2)}, u32[]{:S(2)}) %collective-permute-start.3) | collective-permute-done | bytes 524320 | tf_op jit(solution)/shard_map/ppermute | solution.py:396
  43.8 4.1 %collective-permute-start.4 = (bf16[2048,256]{1,0:T(8,128)(2,1)S(1)}, bf16[2048,256]{1,0:T(8,128)(2,1)S(1)}, u32[]{:S(2)}, u32[]{:S(2)}) collective-permute-start(bf16[2048,256]{1,0:T(8,128)(2,1)S(1)} %get-tuple-element.43.refs_1_.refs_3_), channel_id=1, source_target_pairs={{0,1},{1,0},{8,9},{9,8},{10,11},{11,10},{16,17},{17,16},{18,19},{1... | collective-permute-start | bytes 3145736 | tf_op jit(solution)/shard_map/ppermute | solution.py:396
  47.9 1.9 %collective-permute-start.6 = (bf16[2048,256]{1,0:T(8,128)(2,1)S(1)}, bf16[2048,256]{1,0:T(8,128)(2,1)S(1)}, u32[]{:S(2)}, u32[]{:S(2)}) collective-permute-start(bf16[2048,256]{1,0:T(8,128)(2,1)S(1)} %get-tuple-element.45.refs_3_.refs_1_), channel_id=1, source_target_pairs={{0,1},{1,0},{8,9},{9,8},{10,11},{11,10},{16,17},{17,16},{18,19},{1... | collective-permute-start | bytes 3145736 | tf_op jit(solution)/shard_map/ppermute | solution.py:396
  51.5 8.8 %mirrored_product.2 = (f32[2048,256]{1,0:T(8,128)S(1)}, bf16[2112,256]{1,0:T(8,128)(2,1)S(1)}) custom-call(s32[5]{0:T(128)S(1)} %stack.23.ids.refs_0_, bf16[4096,2048]{1,0:T(8,128)(2,1)S(1)} %get-tuple-element.41.refs_1_, f32[8,2048]{1,0:T(8,128)S(1)} %get-tuple-element.44.refs_2_, bf16[2048,256]{1,0:T(8,128)(2,1)S(1)} %get-tuple-element.43.refs_1_.refs_3_, ...), custom_call_target="tpu_custom_call" | custom-call | tf_op jit(solution)/shard_map/mirrored_product/pallas_call | solution.py:48
  63.1 8.8 %mirrored_product.3 = (f32[2048,256]{1,0:T(8,128)S(1)}, bf16[2112,256]{1,0:T(8,128)(2,1)S(1)}) custom-call(s32[5]{0:T(128)S(1)} %stack.23.ids.refs_0_, bf16[4096,2048]{1,0:T(8,128)(2,1)S(1)} %get-tuple-element.41.refs_1_, f32[8,2048]{1,0:T(8,128)S(1)} %get-tuple-element.44.refs_2_, bf16[2048,256]{1,0:T(8,128)(2,1)S(1)} %get-tuple-element.45.refs_3_.refs_1_, ...), custom_call_target="tpu_custom_call" | custom-call | tf_op jit(solution)/shard_map/mirrored_product/pallas_call | solution.py:48
  75.4 2.9 %relay.2 = (f32[2048,256]{1,0:T(8,128)S(1)}, bf16[2112,256]{1,0:T(8,128)(2,1)S(1)}) custom-call(s32[5]{0:T(128)S(1)} %stack.23.ids.refs_0_, f32[2048,256]{1,0:T(8,128)S(1)} %get-tuple-element.50.refs_1_, bf16[2112,256]{1,0:T(8,128)(2,1)S(1)} %collective-permute-done.9.refs_2_, bf16[2112,256]{1,0:T(8,128)(2,1)S(1)} %get-tuple-element.47.refs_3_, ...), custom_call_target="tpu_custom_call" | custom-call | tf_op jit(solution)/shard_map/relay/pallas_call | solution.py:48
  81.1 8.8 %collective-permute-done.8.refs_5_ = bf16[2048,256]{1,0:T(8,128)(2,1)S(1)} collective-permute-done((bf16[2048,256]{1,0:T(8,128)(2,1)S(1)}, bf16[2048,256]{1,0:T(8,128)(2,1)S(1)}, u32[]{:S(2)}, u32[]{:S(2)}) %collective-permute-start.8) | collective-permute-done | bytes 1048608 | tf_op jit(solution)/shard_map/ppermute | solution.py:396
  89.9 6.4 %direct_product.1 = (f32[2048,256]{1,0:T(8,128)S(1)}, f32[1024,256]{1,0:T(8,128)S(1)}, f32[1024,256]{1,0:T(8,128)S(1)}) custom-call(s32[5]{0:T(128)S(1)} %stack.23.ids.refs_0_, bf16[4096,2048]{1,0:T(8,128)(2,1)S(1)} %get-tuple-element.41.refs_1_, bf16[2048,256]{1,0:T(8,128)(2,1)S(1)} %half.2.refs_2_, bf16[2048,256]{1,0:T(8,128)(2,1)S(1)} %collective-permute-done.5.refs_3_, ...), custom_call_target="tpu_custom_call" | custom-call | tf_op jit(solution)/shard_map/direct_product/pallas_call | solution.py:48
  96.3 3.3 %collective-permute-start.11 = (f32[1024,256]{1,0:T(8,128)S(1)}, f32[1024,256]{1,0:T(8,128)S(1)}, u32[]{:S(2)}, u32[]{:S(2)}) collective-permute-start(f32[1024,256]{1,0:T(8,128)S(1)} %get-tuple-element.54), channel_id=1, source_target_pairs={{0,1},{1,0},{8,9},{9,8},{10,11},{11,10},{16,17},{17,16},{18,19},{1... | collective-permute-start | bytes 3145736 | tf_op jit(solution)/shard_map/ppermute | solution.py:396
  99.6 2.1 %collective-permute-start.12 = (f32[1024,256]{1,0:T(8,128)S(1)}, f32[1024,256]{1,0:T(8,128)S(1)}, u32[]{:S(2)}, u32[]{:S(2)}) collective-permute-start(f32[1024,256]{1,0:T(8,128)S(1)} %get-tuple-element.55), channel_id=1, source_target_pairs={{0,1},{1,0},{8,9},{9,8},{10,11},{11,10},{16,17},{17,16},{18,19},{1... | collective-permute-start | bytes 3145736 | tf_op jit(solution)/shard_map/ppermute | solution.py:396
  101.8 2.9 %relay.3 = (f32[2048,256]{1,0:T(8,128)S(1)}, bf16[2112,256]{1,0:T(8,128)(2,1)S(1)}) custom-call(s32[5]{0:T(128)S(1)} %stack.23.ids.refs_0_, f32[2048,256]{1,0:T(8,128)S(1)} %get-tuple-element.57.refs_1_, bf16[2112,256]{1,0:T(8,128)(2,1)S(1)} %collective-permute-done.14.refs_2_, f32[2048,256]{1,0:T(8,128)S(1)} %get-tuple-element.53.refs_3_.refs_1_, ...), custom_call_target="tpu_custom_call" | custom-call | tf_op jit(solution)/shard_map/relay/pallas_call | solution.py:48
  105.5 2.3 %pack.2 = (f32[1024,256]{1,0:T(8,128)S(1)}, bf16[1040,256]{1,0:T(8,128)(2,1)S(1)}, bf16[1040,256]{1,0:T(8,128)(2,1)S(1)}) custom-call(s32[5]{0:T(128)S(1)} %stack.23.ids.refs_0_, f32[2048,256]{1,0:T(8,128)S(1)} %get-tuple-element.53.refs_3_.refs_1_, f32[1024,256]{1,0:T(8,128)S(1)} %collective-permute-done.11.refs_2_, ...), custom_call_target="tpu_custom_call" | custom-call | tf_op jit(solution)/shard_map/pack/pallas_call | solution.py:48
  107.7 3.5 %give_product.1 = (f32[1024,256]{1,0:T(8,128)S(1)}, f32[1024,256]{1,0:T(8,128)S(1)}, bf16[2048,256]{1,0:T(8,128)(2,1)S(1)}) custom-call(s32[5]{0:T(128)S(1)} %stack.23.ids.refs_0_, bf16[4096,2048]{1,0:T(8,128)(2,1)S(1)} %get-tuple-element.41.refs_1_, bf16[2048,256]{1,0:T(8,128)(2,1)S(1)} %half.3.refs_2_, ...), custom_call_target="tpu_custom_call" | custom-call | tf_op jit(solution)/shard_map/give_product/pallas_call | solution.py:48
  111.3 2.4 %collective-permute-start.20 = (f32[1024,256]{1,0:T(8,128)S(1)}, f32[1024,256]{1,0:T(8,128)S(1)}, u32[]{:S(2)}, u32[]{:S(2)}) collective-permute-start(f32[1024,256]{1,0:T(8,128)S(1)} %get-tuple-element.64), channel_id=1, source_target_pairs={{0,1},{1,0},{8,9},{9,8},{10,11},{11,10},{16,17},{17,16},{18,19},{1... | collective-permute-start | bytes 3145736 | tf_op jit(solution)/shard_map/ppermute | solution.py:396
  113.7 1.9 %collective-permute-start.21 = (f32[1024,256]{1,0:T(8,128)S(1)}, f32[1024,256]{1,0:T(8,128)S(1)}, u32[]{:S(2)}, u32[]{:S(2)}) collective-permute-start(f32[1024,256]{1,0:T(8,128)S(1)} %get-tuple-element.65), channel_id=1, source_target_pairs={{0,1},{1,0},{8,9},{9,8},{10,11},{11,10},{16,17},{17,16},{18,19},{1... | collective-permute-start | bytes 3145736 | tf_op jit(solution)/shard_map/ppermute | solution.py:396
  115.6 3.1 %collective-permute-start.17 = (bf16[1040,256]{1,0:T(8,128)(2,1)S(1)}, bf16[1040,256]{1,0:T(8,128)(2,1)S(1)}, u32[]{:S(2)}, u32[]{:S(2)}) collective-permute-start(bf16[1040,256]{1,0:T(8,128)(2,1)S(1)} %get-tuple-element.61), channel_id=1, source_target_pairs={{1,4},{9,12},{11,14},{17,20},{19,22},{20,17},{25,28},{27,30},{28,2... | collective-permute-start | bytes 1597448 | tf_op jit(solution)/shard_map/ppermute | solution.py:396
  118.8 3.1 %collective-permute-start.18 = (bf16[1040,256]{1,0:T(8,128)(2,1)S(1)}, bf16[1040,256]{1,0:T(8,128)(2,1)S(1)}, u32[]{:S(2)}, u32[]{:S(2)}) collective-permute-start(bf16[1040,256]{1,0:T(8,128)(2,1)S(1)} %get-tuple-element.62), channel_id=1, source_target_pairs={{0,2},{1,6},{8,10},{9,14},{10,8},{11,12},{16,18},{17,22},{18,16},{... | collective-permute-start | bytes 1597448 | tf_op jit(solution)/shard_map/ppermute | solution.py:396
  121.9 3.4 %keep_product.1.refs_1_ = f32[2048,256]{1,0:T(8,128)S(1)} custom-call(s32[5]{0:T(128)S(1)} %stack.23.ids.refs_0_, bf16[4096,2048]{1,0:T(8,128)(2,1)S(1)} %get-tuple-element.41.refs_1_, bf16[2048,256]{1,0:T(8,128)(2,1)S(1)} %get-tuple-element.63.refs_2_, bf16[2112,256]{1,0:T(8,128)(2,1)S(1)} %collective-permute-done.19.refs_3_.refs_5_), custom_call_target="tpu_custom_call" | custom-call | tf_op jit(solution)/shard_map/keep_product/pallas_call | solution.py:48
  125.3 2.1 %pack.3 = (f32[512,256]{1,0:T(8,128)S(1)}, bf16[528,256]{1,0:T(8,128)(2,1)S(1)}, bf16[528,256]{1,0:T(8,128)(2,1)S(1)}, bf16[528,256]{1,0:T(8,128)(2,1)S(1)}, bf16[528,256]{1,0:T(8,128)(2,1)S(1)}) custom-call(s32[5]{0:T(128)S(1)} %stack.23.ids.refs_0_, f32[2048,256]{1,0:T(8,128)S(1)} %keep_product.1.refs_1_, f32[1024,256]{1,0:T(8,128)S(1)} %collective-permute-done.20.refs_2_, ...), custom_call_target="tpu_custom_call" | custom-call | tf_op jit(solution)/shard_map/pack/pallas_call | solution.py:48
  127.4 2.2 %collective-permute-start.22 = (bf16[528,256]{1,0:T(8,128)(2,1)S(1)}, bf16[528,256]{1,0:T(8,128)(2,1)S(1)}, u32[]{:S(2)}, u32[]{:S(2)}) collective-permute-start(bf16[528,256]{1,0:T(8,128)(2,1)S(1)} %get-tuple-element.67), channel_id=1, source_target_pairs={{1,4},{9,12},{10,9},{11,13},{17,20},{18,17},{19,21},{20,18},{21,22... | collective-permute-start | bytes 811016 | tf_op jit(solution)/shard_map/ppermute | solution.py:396
  129.6 5.3 %collective-permute-start.25 = (bf16[528,256]{1,0:T(8,128)(2,1)S(1)}, bf16[528,256]{1,0:T(8,128)(2,1)S(1)}, u32[]{:S(2)}, u32[]{:S(2)}) collective-permute-start(bf16[528,256]{1,0:T(8,128)(2,1)S(1)} %get-tuple-element.72), channel_id=1, source_target_pairs={{0,1},{1,5},{8,9},{9,13},{11,14},{16,17},{17,21},{19,22},{20,19},{... | collective-permute-start | bytes 811016 | tf_op jit(solution)/shard_map/ppermute | solution.py:396
  136.9 3.1 %collective-permute-start.27 = (bf16[528,256]{1,0:T(8,128)(2,1)S(1)}, bf16[528,256]{1,0:T(8,128)(2,1)S(1)}, u32[]{:S(2)}, u32[]{:S(2)}) collective-permute-start(bf16[528,256]{1,0:T(8,128)(2,1)S(1)} %get-tuple-element.74), channel_id=1, source_target_pairs={{0,3},{1,7},{8,11},{9,15},{10,8},{11,12},{16,19},{17,23},{18,16},{... | collective-permute-start | bytes 811016 | tf_op jit(solution)/shard_map/ppermute | solution.py:396
  140.0 2.9 %collective-permute-done.18.refs_3_ = bf16[1040,256]{1,0:T(8,128)(2,1)S(1)} collective-permute-done((bf16[1040,256]{1,0:T(8,128)(2,1)S(1)}, bf16[1040,256]{1,0:T(8,128)(2,1)S(1)}, u32[]{:S(2)}, u32[]{:S(2)}) %collective-permute-start.18) | collective-permute-done | bytes 532512 | tf_op jit(solution)/shard_map/ppermute | solution.py:396
  145.9 2.1 %collective-permute-done.25.refs_6_ = bf16[528,256]{1,0:T(8,128)(2,1)S(1)} collective-permute-done((bf16[528,256]{1,0:T(8,128)(2,1)S(1)}, bf16[528,256]{1,0:T(8,128)(2,1)S(1)}, u32[]{:S(2)}, u32[]{:S(2)}) %collective-permute-start.25) | collective-permute-done | bytes 270368 | tf_op jit(solution)/shard_map/ppermute | solution.py:396
  148.0 4.8 %collective-permute-done.26.refs_7_ = bf16[528,256]{1,0:T(8,128)(2,1)S(1)} collective-permute-done((bf16[528,256]{1,0:T(8,128)(2,1)S(1)}, bf16[528,256]{1,0:T(8,128)(2,1)S(1)}, u32[]{:S(2)}, u32[]{:S(2)}) %collective-permute-start.26) | collective-permute-done | bytes 270368 | tf_op jit(solution)/shard_map/ppermute | solution.py:396
  152.8 14.4 %collective-permute-done.27.refs_8_ = bf16[528,256]{1,0:T(8,128)(2,1)S(1)} collective-permute-done((bf16[528,256]{1,0:T(8,128)(2,1)S(1)}, bf16[528,256]{1,0:T(8,128)(2,1)S(1)}, u32[]{:S(2)}, u32[]{:S(2)}) %collective-permute-start.27) | collective-permute-done | bytes 270368 | tf_op jit(solution)/shard_map/ppermute | solution.py:396
  167.3 2.6 %finish.1 = f32[512,512]{1,0:T(8,128)} custom-call(s32[5]{0:T(128)S(1)} %stack.23.ids.refs_0_, f32[512,256]{1,0:T(8,128)S(1)} %get-tuple-element.68.refs_1_, f32[256,256]{1,0:T(8,128)S(1)} %collective-permute-done.23.refs_2_, f32[256,256]{1,0:T(8,128)S(1)} %collective-permute-done.24.refs_3_, f32[512,256]{1,0:T(8,128)S(1)} %get-tuple-element.71.refs_4_, ...), custom_call_target="tpu_custom_call" | custom-call | tf_op jit(solution)/shard_map/finish/pallas_call | solution.py:48
  (44 shorter events, 21.3 us)
Async XLA Ops:
  0.0 27.1 %collective-permute-start = (bf16[512,512]{1,0:T(8,128)(2,1)}, bf16[512,512]{1,0:T(8,128)(2,1)S(1)}, u32[]{:S(2)}, u32[]{:S(2)}) collective-permute-start(bf16[512,512]{1,0:T(8,128)(2,1)} %refs_1_.1), channel_id=1, source_target_pairs={{4,0},{5,1},{6,2},{7,3},{12,8},{13,9},{14,10},{15,11},{16,20},{17,... | collective-permute-start | bytes 1572872 | tf_op jit(solution)/shard_map/ppermute | solution.py:396
  4.2 24.2 %collective-permute-start.1 = (bf16[512,512]{1,0:T(8,128)(2,1)}, bf16[512,512]{1,0:T(8,128)(2,1)S(1)}, u32[]{:S(2)}, u32[]{:S(2)}) collective-permute-start(bf16[512,512]{1,0:T(8,128)(2,1)} %refs_1_.1), channel_id=1, source_target_pairs={{8,10},{9,11},{16,18},{17,19},{18,20},{19,21},{24,26},{25,27},{26,... | collective-permute-start | bytes 1572872 | tf_op jit(solution)/shard_map/ppermute | solution.py:396
  7.5 24.4 %collective-permute-start.2 = (bf16[512,512]{1,0:T(8,128)(2,1)}, bf16[512,512]{1,0:T(8,128)(2,1)S(1)}, u32[]{:S(2)}, u32[]{:S(2)}) collective-permute-start(bf16[512,512]{1,0:T(8,128)(2,1)} %refs_1_.1), channel_id=1, source_target_pairs={{2,0},{3,1},{10,8},{11,9},{12,10},{13,11},{18,16},{19,17},{20,18},... | collective-permute-start | bytes 1572872 | tf_op jit(solution)/shard_map/ppermute | solution.py:396
  8.9 5.8 %copy-start = (bf16[4096,2048]{1,0:T(8,128)(2,1)S(1)}, bf16[4096,2048]{1,0:T(8,128)(2,1)}, u32[]{:S(2)}) copy-start(bf16[4096,2048]{1,0:T(8,128)(2,1)} %a_ref.1) | copy-start | bytes 50331652
  14.6 28.5 %copy-start.1 = (bf16[512,512]{1,0:T(8,128)(2,1)S(1)}, bf16[512,512]{1,0:T(8,128)(2,1)}, u32[]{:S(2)}) copy-start(bf16[512,512]{1,0:T(8,128)(2,1)} %refs_1_.1) | copy-start | bytes 1572868
  27.1 16.0 %collective-permute-start.3 = (bf16[512,512]{1,0:T(8,128)(2,1)S(1)}, bf16[512,512]{1,0:T(8,128)(2,1)S(1)}, u32[]{:S(2)}, u32[]{:S(2)}) collective-permute-start(bf16[512,512]{1,0:T(8,128)(2,1)S(1)} %collective-permute-done.refs_2_), channel_id=1, source_target_pairs={{2,0},{3,1},{10,8},{11,9},{18,16},{19,17},{26,24},{27,25},{28,30},... | collective-permute-start | bytes 1572872 | tf_op jit(solution)/shard_map/ppermute | solution.py:396
  43.8 6.3 %collective-permute-start.4 = (bf16[2048,256]{1,0:T(8,128)(2,1)S(1)}, bf16[2048,256]{1,0:T(8,128)(2,1)S(1)}, u32[]{:S(2)}, u32[]{:S(2)}) collective-permute-start(bf16[2048,256]{1,0:T(8,128)(2,1)S(1)} %get-tuple-element.43.refs_1_.refs_3_), channel_id=1, source_target_pairs={{0,1},{1,0},{8,9},{9,8},{10,11},{11,10},{16,17},{17,16},{18,19},{1... | collective-permute-start | bytes 3145736 | tf_op jit(solution)/shard_map/ppermute | solution.py:396
  47.9 13.8 %collective-permute-start.6 = (bf16[2048,256]{1,0:T(8,128)(2,1)S(1)}, bf16[2048,256]{1,0:T(8,128)(2,1)S(1)}, u32[]{:S(2)}, u32[]{:S(2)}) collective-permute-start(bf16[2048,256]{1,0:T(8,128)(2,1)S(1)} %get-tuple-element.45.refs_3_.refs_1_), channel_id=1, source_target_pairs={{0,1},{1,0},{8,9},{9,8},{10,11},{11,10},{16,17},{17,16},{18,19},{1... | collective-permute-start | bytes 3145736 | tf_op jit(solution)/shard_map/ppermute | solution.py:396
  50.8 22.5 %collective-permute-start.5 = (bf16[2048,256]{1,0:T(8,128)(2,1)S(1)}, bf16[2048,256]{1,0:T(8,128)(2,1)S(1)}, u32[]{:S(2)}, u32[]{:S(2)}) collective-permute-start(bf16[2048,256]{1,0:T(8,128)(2,1)S(1)} %half.2.refs_2_), channel_id=1, source_target_pairs={{0,8},{1,17},{10,2},{11,27},{20,28}} | collective-permute-start | bytes 3145736 | tf_op jit(solution)/shard_map/ppermute | solution.py:396
  60.3 15.0 %collective-permute-start.9 = (bf16[2112,256]{1,0:T(8,128)(2,1)S(1)}, bf16[2112,256]{1,0:T(8,128)(2,1)S(1)}, u32[]{:S(2)}, u32[]{:S(2)}) collective-permute-start(bf16[2112,256]{1,0:T(8,128)(2,1)S(1)} %get-tuple-element.46.refs_5_), channel_id=1, source_target_pairs={{16,0},{24,8},{9,1},{25,17},{26,10},{18,2},{19,27},{29,21}} | collective-permute-start | bytes 3244040 | tf_op jit(solution)/shard_map/ppermute | solution.py:396
  62.3 13.0 %collective-permute-start.10 = (bf16[2048,256]{1,0:T(8,128)(2,1)S(1)}, bf16[2048,256]{1,0:T(8,128)(2,1)S(1)}, u32[]{:S(2)}, u32[]{:S(2)}) collective-permute-start(bf16[2048,256]{1,0:T(8,128)(2,1)S(1)} %half.3.refs_2_), channel_id=1, source_target_pairs={{0,8},{1,17},{10,2},{11,27},{20,28}} | collective-permute-start | bytes 3145736 | tf_op jit(solution)/shard_map/ppermute | solution.py:396
  71.9 27.7 %collective-permute-start.14 = (bf16[2112,256]{1,0:T(8,128)(2,1)S(1)}, bf16[2112,256]{1,0:T(8,128)(2,1)S(1)}, u32[]{:S(2)}, u32[]{:S(2)}) collective-permute-start(bf16[2112,256]{1,0:T(8,128)(2,1)S(1)} %get-tuple-element.47.refs_3_), channel_id=1, source_target_pairs={{16,0},{24,8},{9,1},{25,17},{26,10},{18,2},{19,27},{29,21}} | collective-permute-start | bytes 3244040 | tf_op jit(solution)/shard_map/ppermute | solution.py:396
  73.3 6.5 %collective-permute-start.7 = (bf16[2048,256]{1,0:T(8,128)(2,1)S(1)}, bf16[2048,256]{1,0:T(8,128)(2,1)S(1)}, u32[]{:S(2)}, u32[]{:S(2)}) collective-permute-start(bf16[2048,256]{1,0:T(8,128)(2,1)S(1)} %half.2.refs_2_), channel_id=1, source_target_pairs={{0,16},{1,9},{10,26},{21,29}} | collective-permute-start | bytes 3145736 | tf_op jit(solution)/shard_map/ppermute | solution.py:396
  74.1 15.8 %collective-permute-start.8 = (bf16[2048,256]{1,0:T(8,128)(2,1)S(1)}, bf16[2048,256]{1,0:T(8,128)(2,1)S(1)}, u32[]{:S(2)}, u32[]{:S(2)}) collective-permute-start(bf16[2048,256]{1,0:T(8,128)(2,1)S(1)} %collective-permute-done.5.refs_3_), channel_id=1, source_target_pairs={{8,24},{17,25},{2,18},{27,19}} | collective-permute-start | bytes 3145736 | tf_op jit(solution)/shard_map/ppermute | solution.py:396
  78.3 23.4 %collective-permute-start.13 = (bf16[2112,256]{1,0:T(8,128)(2,1)S(1)}, bf16[2112,256]{1,0:T(8,128)(2,1)S(1)}, u32[]{:S(2)}, u32[]{:S(2)}) collective-permute-start(bf16[2112,256]{1,0:T(8,128)(2,1)S(1)} %get-tuple-element.52.refs_6_), channel_id=1, source_target_pairs={{8,0},{17,1},{2,10},{27,11},{28,20}} | collective-permute-start | bytes 3244040 | tf_op jit(solution)/shard_map/ppermute | solution.py:396
  79.1 22.7 %collective-permute-start.15 = (bf16[2048,256]{1,0:T(8,128)(2,1)S(1)}, bf16[2048,256]{1,0:T(8,128)(2,1)S(1)}, u32[]{:S(2)}, u32[]{:S(2)}) collective-permute-start(bf16[2048,256]{1,0:T(8,128)(2,1)S(1)} %half.3.refs_2_), channel_id=1, source_target_pairs={{0,16},{1,9},{10,26},{21,29}} | collective-permute-start | bytes 3145736 | tf_op jit(solution)/shard_map/ppermute | solution.py:396
  79.8 25.6 %collective-permute-start.16 = (bf16[2048,256]{1,0:T(8,128)(2,1)S(1)}, bf16[2048,256]{1,0:T(8,128)(2,1)S(1)}, u32[]{:S(2)}, u32[]{:S(2)}) collective-permute-start(bf16[2048,256]{1,0:T(8,128)(2,1)S(1)} %collective-permute-done.10.refs_4_.refs_3_), channel_id=1, source_target_pairs={{8,24},{17,25},{2,18},{27,19}} | collective-permute-start | bytes 3145736 | tf_op jit(solution)/shard_map/ppermute | solution.py:396
  96.3 9.2 %collective-permute-start.11 = (f32[1024,256]{1,0:T(8,128)S(1)}, f32[1024,256]{1,0:T(8,128)S(1)}, u32[]{:S(2)}, u32[]{:S(2)}) collective-permute-start(f32[1024,256]{1,0:T(8,128)S(1)} %get-tuple-element.54), channel_id=1, source_target_pairs={{0,1},{1,0},{8,9},{9,8},{10,11},{11,10},{16,17},{17,16},{18,19},{1... | collective-permute-start | bytes 3145736 | tf_op jit(solution)/shard_map/ppermute | solution.py:396
  99.6 5.8 %collective-permute-start.12 = (f32[1024,256]{1,0:T(8,128)S(1)}, f32[1024,256]{1,0:T(8,128)S(1)}, u32[]{:S(2)}, u32[]{:S(2)}) collective-permute-start(f32[1024,256]{1,0:T(8,128)S(1)} %get-tuple-element.55), channel_id=1, source_target_pairs={{0,1},{1,0},{8,9},{9,8},{10,11},{11,10},{16,17},{17,16},{18,19},{1... | collective-permute-start | bytes 3145736 | tf_op jit(solution)/shard_map/ppermute | solution.py:396
  104.7 17.1 %collective-permute-start.19 = (bf16[2112,256]{1,0:T(8,128)(2,1)S(1)}, bf16[2112,256]{1,0:T(8,128)(2,1)S(1)}, u32[]{:S(2)}, u32[]{:S(2)}) collective-permute-start(bf16[2112,256]{1,0:T(8,128)(2,1)S(1)} %get-tuple-element.59.refs_6_), channel_id=1, source_target_pairs={{8,0},{17,1},{2,10},{27,11},{28,20}} | collective-permute-start | bytes 3244040 | tf_op jit(solution)/shard_map/ppermute | solution.py:396
  111.3 14.0 %collective-permute-start.20 = (f32[1024,256]{1,0:T(8,128)S(1)}, f32[1024,256]{1,0:T(8,128)S(1)}, u32[]{:S(2)}, u32[]{:S(2)}) collective-permute-start(f32[1024,256]{1,0:T(8,128)S(1)} %get-tuple-element.64), channel_id=1, source_target_pairs={{0,1},{1,0},{8,9},{9,8},{10,11},{11,10},{16,17},{17,16},{18,19},{1... | collective-permute-start | bytes 3145736 | tf_op jit(solution)/shard_map/ppermute | solution.py:396
  113.7 11.6 %collective-permute-start.21 = (f32[1024,256]{1,0:T(8,128)S(1)}, f32[1024,256]{1,0:T(8,128)S(1)}, u32[]{:S(2)}, u32[]{:S(2)}) collective-permute-start(f32[1024,256]{1,0:T(8,128)S(1)} %get-tuple-element.65), channel_id=1, source_target_pairs={{0,1},{1,0},{8,9},{9,8},{10,11},{11,10},{16,17},{17,16},{18,19},{1... | collective-permute-start | bytes 3145736 | tf_op jit(solution)/shard_map/ppermute | solution.py:396
  115.6 21.3 %collective-permute-start.17 = (bf16[1040,256]{1,0:T(8,128)(2,1)S(1)}, bf16[1040,256]{1,0:T(8,128)(2,1)S(1)}, u32[]{:S(2)}, u32[]{:S(2)}) collective-permute-start(bf16[1040,256]{1,0:T(8,128)(2,1)S(1)} %get-tuple-element.61), channel_id=1, source_target_pairs={{1,4},{9,12},{11,14},{17,20},{19,22},{20,17},{25,28},{27,30},{28,2... | collective-permute-start | bytes 1597448 | tf_op jit(solution)/shard_map/ppermute | solution.py:396
  118.8 24.2 %collective-permute-start.18 = (bf16[1040,256]{1,0:T(8,128)(2,1)S(1)}, bf16[1040,256]{1,0:T(8,128)(2,1)S(1)}, u32[]{:S(2)}, u32[]{:S(2)}) collective-permute-start(bf16[1040,256]{1,0:T(8,128)(2,1)S(1)} %get-tuple-element.62), channel_id=1, source_target_pairs={{0,2},{1,6},{8,10},{9,14},{10,8},{11,12},{16,18},{17,22},{18,16},{... | collective-permute-start | bytes 1597448 | tf_op jit(solution)/shard_map/ppermute | solution.py:396
  127.4 16.4 %collective-permute-start.22 = (bf16[528,256]{1,0:T(8,128)(2,1)S(1)}, bf16[528,256]{1,0:T(8,128)(2,1)S(1)}, u32[]{:S(2)}, u32[]{:S(2)}) collective-permute-start(bf16[528,256]{1,0:T(8,128)(2,1)S(1)} %get-tuple-element.67), channel_id=1, source_target_pairs={{1,4},{9,12},{10,9},{11,13},{17,20},{18,17},{19,21},{20,18},{21,22... | collective-permute-start | bytes 811016 | tf_op jit(solution)/shard_map/ppermute | solution.py:396
  129.6 18.4 %collective-permute-start.25 = (bf16[528,256]{1,0:T(8,128)(2,1)S(1)}, bf16[528,256]{1,0:T(8,128)(2,1)S(1)}, u32[]{:S(2)}, u32[]{:S(2)}) collective-permute-start(bf16[528,256]{1,0:T(8,128)(2,1)S(1)} %get-tuple-element.72), channel_id=1, source_target_pairs={{0,1},{1,5},{8,9},{9,13},{11,14},{16,17},{17,21},{19,22},{20,19},{... | collective-permute-start | bytes 811016 | tf_op jit(solution)/shard_map/ppermute | solution.py:396
  134.9 17.9 %collective-permute-start.26 = (bf16[528,256]{1,0:T(8,128)(2,1)S(1)}, bf16[528,256]{1,0:T(8,128)(2,1)S(1)}, u32[]{:S(2)}, u32[]{:S(2)}) collective-permute-start(bf16[528,256]{1,0:T(8,128)(2,1)S(1)} %get-tuple-element.73), channel_id=1, source_target_pairs={{0,2},{1,6},{8,10},{9,14},{10,11},{11,15},{16,18},{17,22},{18,19},... | collective-permute-start | bytes 811016 | tf_op jit(solution)/shard_map/ppermute | solution.py:396
  136.9 30.4 %collective-permute-start.27 = (bf16[528,256]{1,0:T(8,128)(2,1)S(1)}, bf16[528,256]{1,0:T(8,128)(2,1)S(1)}, u32[]{:S(2)}, u32[]{:S(2)}) collective-permute-start(bf16[528,256]{1,0:T(8,128)(2,1)S(1)} %get-tuple-element.74), channel_id=1, source_target_pairs={{0,3},{1,7},{8,11},{9,15},{10,8},{11,12},{16,19},{17,23},{18,16},{... | collective-permute-start | bytes 811016 | tf_op jit(solution)/shard_map/ppermute | solution.py:396
  145.3 21.9 %collective-permute-start.23 = (f32[256,256]{1,0:T(8,128)S(1)}, f32[256,256]{1,0:T(8,128)S(1)}, u32[]{:S(2)}, u32[]{:S(2)}) collective-permute-start(f32[256,256]{1,0:T(8,128)S(1)} %get-tuple-element.69), channel_id=1, source_target_pairs={{0,1},{1,0},{2,3},{3,2},{4,5},{5,4},{6,7},{7,6},{8,9},{9,8},{10,11... | collective-permute-start | bytes 786440 | tf_op jit(solution)/shard_map/ppermute | solution.py:396
  145.4 21.8 %collective-permute-start.24 = (f32[256,256]{1,0:T(8,128)S(1)}, f32[256,256]{1,0:T(8,128)S(1)}, u32[]{:S(2)}, u32[]{:S(2)}) collective-permute-start(f32[256,256]{1,0:T(8,128)S(1)} %get-tuple-element.70), channel_id=1, source_target_pairs={{0,1},{1,0},{2,3},{3,2},{4,5},{5,4},{6,7},{7,6},{8,9},{9,8},{10,11... | collective-permute-start | bytes 786440 | tf_op jit(solution)/shard_map/ppermute | solution.py:396
